TPU v7x, 512 devices: a whole 4x4x16 slice. The times are simulated.
512 devices in a mesh: angle: 16 (over z_lo, core), slab: 4 (over x), tile: 8 (over y, z_hi).
Axes of the slice: x: 4, y: 4, z: 16 (z_hi: 2, z_lo: 8; z = z_hi * 8 + z_lo), core: 2. Of those that a mesh axis runs over, the one named last changes fastest.
Arguments:
- volume: bfloat16 [2, 4, 1536, 1536], P(None, 'slab', 'tile'), may hold values from -2 to 2
- probe_wave: float32 [2, 256, 256], replicated, may hold values from -6 to 6
- amplitudes: bfloat16 [16, 8, 4, 2, 256, 256], P('angle', 'tile', 'slab'), may hold values from 0.099609375 to 3
- offsets: int32 [16, 8, 4, 2], P('angle', 'tile', 'slab'), may hold values from 0 to 128
- column_starts: int32 [16, 8, 4, 2], P('angle', 'tile', 'slab'), may hold values from 0 to 1280
- counts: int32 [16, 8, 4], P('angle', 'tile', 'slab'), may hold values from 1 to 2, as said below
- angle_ids: int32 [16], P('angle'), may hold values from 0 to 1199
Outputs:
- new_volume: float32 [2, 4, 1536, 1536], P(None, 'slab', 'tile')
Inputs may be any that keep to these rules, and one draw needn't show every extreme that they name: counts gives the live slots of one device; slots at or beyond it are ignored; in every draw some device has 2.
All inputs are finite; a program needn't handle non-finite values.
Results may differ from a plain program's by a relative error of at most 0.04.
Values may be sent and summed in bfloat16 or wider, within the bound.
No kernel may reach another device: no remote copies, remote signals or barrier semaphores. Data moves between devices by JAX's collectives and lax.ppermute only.
A program may use at most 64 MiB of HBM per device.

v0:
```python
import jax
import jax.numpy as jnp
from jax import lax
from jax.sharding import PartitionSpec as P

angle_center = 600
shear_divisor = 64
step_size = 0.03
floor_square = 0.25


def passed_along(value, axis, steps):
    count = lax.axis_size(axis)
    initial, last = (max(0, -steps), min(count, count - steps))
    return lax.ppermute(value, axis, [(source, source + steps) for source in range(initial, last)])


def dft_tables(plane_width):
    index_line = jnp.arange(plane_width, dtype=jnp.int32)
    product_mod = jnp.mod(index_line[:, None] * index_line[None, :], plane_width)
    phase_table = product_mod.astype(jnp.float32) * (2.0 * 3.141592653589793 / plane_width)
    scale_factor = plane_width ** (-0.5)
    table_real = (jnp.cos(phase_table) * scale_factor).astype(jnp.bfloat16)
    table_imag = (-jnp.sin(phase_table) * scale_factor).astype(jnp.bfloat16)
    return (table_real, table_imag)


def shear_shifts(angle_value, first_layer, layer_count, total_depth, column_count):
    layer_index = first_layer + jnp.arange(layer_count, dtype=jnp.int32)
    offset_layer = layer_index - total_depth // 2
    sheared = jnp.floor_divide((angle_value - angle_center) * offset_layer, shear_divisor)
    return jnp.mod(sheared, column_count)


def roll_columns(field, amount):
    return jnp.roll(field, amount, axis=-1)


def twodot(left_matrix, right_matrix):
    return jnp.dot(left_matrix, right_matrix, preferred_element_type=jnp.float32)


def patch_gradient(window, probe_wave, pattern, table_real, table_imag):
    window_wide = window.astype(jnp.float32)
    trans_mag = jnp.exp(-window_wide[1])
    trans_real = trans_mag * jnp.cos(window_wide[0])
    trans_imag = trans_mag * jnp.sin(window_wide[0])
    wave_real = (probe_wave[0] * trans_real - probe_wave[1] * trans_imag).astype(jnp.bfloat16)
    wave_imag = (probe_wave[0] * trans_imag + probe_wave[1] * trans_real).astype(jnp.bfloat16)
    left_real = (twodot(table_real, wave_real) - twodot(table_imag, wave_imag)).astype(jnp.bfloat16)
    left_imag = (twodot(table_real, wave_imag) + twodot(table_imag, wave_real)).astype(jnp.bfloat16)
    far_real = twodot(left_real, table_real) - twodot(left_imag, table_imag)
    far_imag = twodot(left_real, table_imag) + twodot(left_imag, table_real)
    ratio = pattern.astype(jnp.float32) / jnp.sqrt(
        far_real * far_real + far_imag * far_imag + floor_square
    )
    keeping = 1.0 - ratio
    resid_real = (far_real * keeping).astype(jnp.bfloat16)
    resid_imag = (far_imag * keeping).astype(jnp.bfloat16)
    back_real = (twodot(table_real, resid_real) + twodot(table_imag, resid_imag)).astype(
        jnp.bfloat16
    )
    back_imag = (twodot(table_real, resid_imag) - twodot(table_imag, resid_real)).astype(
        jnp.bfloat16
    )
    exit_real = twodot(back_real, table_real) + twodot(back_imag, table_imag)
    exit_imag = twodot(back_imag, table_real) - twodot(back_real, table_imag)
    mixed_real = probe_wave[0] * exit_real + probe_wave[1] * exit_imag
    mixed_imag = probe_wave[0] * exit_imag - probe_wave[1] * exit_real
    final_real = trans_real * mixed_real + trans_imag * mixed_imag
    final_imag = trans_real * mixed_imag - trans_imag * mixed_real
    return jnp.stack([final_imag, -final_real])


def slot_update(
    buffer, extended, start_row, start_column, pattern, probe_wave, table_real, table_imag
):
    plane_width = pattern.shape[-1]
    zero_index = jnp.zeros((), jnp.int32)
    corner = (zero_index, start_row, start_column)
    window = lax.dynamic_slice(extended, corner, (2, plane_width, plane_width))
    gradient = patch_gradient(window, probe_wave, pattern, table_real, table_imag)
    previous = lax.dynamic_slice(buffer, corner, (2, plane_width, plane_width))
    return lax.dynamic_update_slice(buffer, previous + gradient, corner)


def per_device(volume, probe_wave, amplitudes, offsets, column_starts, counts, angle_ids):
    layer_count = volume.shape[1]
    tile_rows = volume.shape[2]
    column_count = volume.shape[3]
    plane_width = amplitudes.shape[-1]
    capacity = offsets.shape[3]
    slab_total = lax.axis_size("slab")
    slab_number = lax.axis_index("slab")
    table_real, table_imag = dft_tables(plane_width)
    shifts = shear_shifts(
        angle_ids[0], slab_number * layer_count, layer_count, layer_count * slab_total, column_count
    )
    rolled = jax.vmap(roll_columns, in_axes=(1, 0))(volume, -shifts)
    partial_sum = jnp.sum(rolled.astype(jnp.float32), axis=0)
    projection = lax.psum(partial_sum.astype(jnp.bfloat16), "slab")
    rows_after = passed_along(projection, "tile", -1)
    extended = jnp.concatenate([projection, rows_after], axis=1)
    own_patterns = amplitudes.reshape(capacity, plane_width, plane_width)
    own_starts = offsets.reshape(capacity)
    own_columns = column_starts.reshape(capacity)
    own_count = counts.reshape(1)
    zero_buffer = jnp.zeros(extended.shape, jnp.float32)

    def visit_own(position, current):
        return slot_update(
            current,
            extended,
            own_starts[position],
            own_columns[position],
            own_patterns[position],
            probe_wave,
            table_real,
            table_imag,
        )

    buffer = lax.fori_loop(0, own_count[0], visit_own, zero_buffer)
    spilled = passed_along(buffer[:, tile_rows:].astype(jnp.bfloat16), "tile", 1).astype(
        jnp.float32
    )
    tile_gradient = buffer[:, :tile_rows] + spilled
    plane_gradient = lax.psum(tile_gradient.astype(jnp.bfloat16), "slab").astype(jnp.float32)
    layer_gradient = jnp.moveaxis(
        jax.vmap(roll_columns, in_axes=(None, 0))(plane_gradient, shifts), 0, 1
    )
    summed_gradient = lax.psum(layer_gradient.astype(jnp.bfloat16), "angle").astype(jnp.float32)
    return volume.astype(jnp.float32) - step_size * summed_gradient


def solution(mesh):
    in_specs = (
        P(None, "slab", "tile", None),
        P(),
        P("angle", "tile", "slab", None, None, None),
        P("angle", "tile", "slab", None),
        P("angle", "tile", "slab", None),
        P("angle", "tile", "slab"),
        P("angle"),
    )
    out_specs = P(None, "slab", "tile", None)
    return jax.shard_map(
        per_device, mesh=mesh, in_specs=in_specs, out_specs=out_specs, check_vma=False
    )
```

profile of v0, /device:TPU:1, one launch (start us, length us, event | category | flops | bytes accessed | tf_op | source)
XLA Modules:
  0.0 612.6 jit_solution(4029603987470485382)
XLA Ops:
  7.2 3.4 fusion.118
  10.8 66.1 %all-reduce.6.cloned.1.call-done = bf16[2,192,1536]{2,1,0:T(8,128)(2,1)} async-done(((bf16[2,192,1536]{2,1,0:T(8,128)(2,1)}), bf16[2,192,1536]{2,1,0:T(8,128)(2,1)}) %all-reduce.6.cloned.1.call-update) | async-done | bytes 1179664 | tf_op jit(solution)/shard_map/psum | solution.py:101
  76.9 1.3 collective-permute-start
  78.2 35.9 %collective-permute-done = bf16[2,192,1536]{2,1,0:T(8,128)(2,1)S(1)} collective-permute-done((bf16[2,192,1536]{2,1,0:T(8,128)(2,1)}, bf16[2,192,1536]{2,1,0:T(8,128)(2,1)S(1)}, u32[]{:S(2)}, u32[]{:S(2)}) %collective-permute-start) | collective-permute-done | bytes 1179680 | tf_op jit(solution)/shard_map/ppermute | solution.py:15
  114.1 1.4 pad_maximum_fusion
  115.6 2.7 broadcast_in_dim.13
  118.3 35.1 %while.14 = (s32[]{:T(128)}, f32[2,384,1536]{2,1,0:T(8,128)}, s32[]{:T(128)}, s32[2]{0:T(128)S(1)}, s32[2]{0:T(128)S(1)}, /*index=5*/bf16[2,384,1536]{2,1,0:T(8,...) while((s32[]{:T(128)}, f32[2,384,1536]{2,1,0:T(8,128)}, ...), condition=%wide.region_2.3_spmd.clone.clone, body=%wide.region_1.2_spmd.clone.clone.sunk | while | flops 557645824 | bytes 17695004 | solution.py:122
  125.6 1.1 fusion.187
  126.8 1.1 fusion.188
  127.9 1.1 fusion.190
  129.1 1.1 fusion.191
  130.2 1.1 fusion.192
  131.3 1.1 fusion.189
  132.5 1.1 convolution_add_fusion.6
  133.6 2.1 multiply_convert_fusion.53
  135.8 1.1 fusion.193
  136.9 1.1 fusion.194
  139.2 1.1 fusion.197
  140.3 1.1 fusion.198
  141.5 1.1 fusion.195
  142.6 1.2 convolution_add_fusion.7
  143.8 1.2 fusion.199
  145.1 1.4 maximum_add_fusion.2
  146.5 6.3 %dynamic_update_slice.6 = f32[2,384,1536]{2,1,0:T(8,128)} dynamic-update-slice(f32[2,384,1536]{2,1,0:T(8,128)} %get-tuple-element.287, f32[2,256,256]{2,1,0:T(8,128)S(1)} %maximum_add_fusion.2, s32[]{:T(128)} %constant.108.clone.1..sunk, s32[]{:T(128)S(6)} %select_n.172, s32[]{:T(128)S(6)} %select_n.173) | dynamic-update-slice | bytes 1048580 | tf_op jit(solution)/shard_map/while/body/dynamic_update_slice | solution.py:84
  153.4 1.8 slice.94
  155.2 55.3 %collective-permute-start.1 = (bf16[2,192,1536]{2,1,0:T(8,128)(2,1)S(1)}, bf16[2,192,1536]{2,1,0:T(8,128)(2,1)S(1)}, u32[]{:S(2)}, u32[]{:S(2)}) collective-permute-start(bf16[2,192,1536]{2,1,0:T(8,128)(2,1)S(1)} %slice.94), channel_id=1, source_target_pairs={{0,1},{1,2},{2,3},{3,4},{4,5},{5,6},{6,7},{8,9},{9,10},{10,11},{11... | collective-permute-start | bytes 3538952 | tf_op jit(solution)/shard_map/ppermute | solution.py:15
  210.5 13.1 %collective-permute-done.1 = bf16[2,192,1536]{2,1,0:T(8,128)(2,1)S(1)} collective-permute-done((bf16[2,192,1536]{2,1,0:T(8,128)(2,1)S(1)}, bf16[2,192,1536]{2,1,0:T(8,128)(2,1)S(1)}, u32[]{:S(2)}, u32[]{:S(2)}) %collective-permute-start.1) | collective-permute-done | bytes 1179680 | tf_op jit(solution)/shard_map/ppermute | solution.py:15
  223.5 3.1 add_convert_fusion
  226.7 170.4 %all-reduce.8.cloned.1.call-done = bf16[2,192,1536]{2,1,0:T(8,128)(2,1)} async-done(((bf16[2,192,1536]{2,1,0:T(8,128)(2,1)}), bf16[2,192,1536]{2,1,0:T(8,128)(2,1)}) %all-reduce.8.cloned.1.call-update) | async-done | bytes 1179664 | tf_op jit(solution)/shard_map/psum | solution.py:127
  397.1 3.3 fusion.115
  400.5 202.6 %all-reduce.10.cloned.1.call-done = bf16[2,1,192,1536]{3,2,1,0:T(8,128)(2,1)} async-done(((bf16[2,1,192,1536]{3,2,1,0:T(8,128)(2,1)}), bf16[2,1,192,1536]{3,2,1,0:T(8,128)(2,1)}) %all-reduce.10.cloned.1.call-update) | async-done | bytes 1179664 | tf_op jit(solution)/shard_map/psum | solution.py:131
  603.0 3.0 multiply_subtract_fusion
  (21 shorter events, 3.9 us)
Async XLA Ops:
  6.5 70.4 %all-reduce.6.cloned.1.call-start = ((), (), s32[]{:S(2)}) async-start(), calls=%async_computation | async-start | bytes 2359296 | tf_op jit(solution)/shard_map/psum | solution.py:101
  10.7 386.4 %all-reduce.8.cloned.1.call-start = ((), (), s32[]{:S(2)}) async-start(), calls=%async_computation.1 | async-start | bytes 2359296 | tf_op jit(solution)/shard_map/psum | solution.py:127
  76.9 37.2 %collective-permute-start = (bf16[2,192,1536]{2,1,0:T(8,128)(2,1)}, bf16[2,192,1536]{2,1,0:T(8,128)(2,1)S(1)}, u32[]{:S(2)}, u32[]{:S(2)}) collective-permute-start(bf16[2,192,1536]{2,1,0:T(8,128)(2,1)} %all-reduce.6.cloned.1.call-done), channel_id=1, source_target_pairs={{1,0},{2,1},{3,2},{4,3},{5,4},{6,5},{7,6},{9,8},{10,9},{11,10},{12... | collective-permute-start | bytes 3538952 | tf_op jit(solution)/shard_map/ppermute | solution.py:15
  115.5 2.8 copy-start
  115.6 2.8 copy-start.2
  115.6 2.8 copy-start.3
  155.2 68.3 %collective-permute-start.1 = (bf16[2,192,1536]{2,1,0:T(8,128)(2,1)S(1)}, bf16[2,192,1536]{2,1,0:T(8,128)(2,1)S(1)}, u32[]{:S(2)}, u32[]{:S(2)}) collective-permute-start(bf16[2,192,1536]{2,1,0:T(8,128)(2,1)S(1)} %slice.94), channel_id=1, source_target_pairs={{0,1},{1,2},{2,3},{3,4},{4,5},{5,6},{6,7},{8,9},{9,10},{10,11},{11... | collective-permute-start | bytes 3538952 | tf_op jit(solution)/shard_map/ppermute | solution.py:15
  226.6 376.4 %copy-start.1 = (bf16[2,1,192,1536]{3,2,1,0:T(8,128)(2,1)S(1)}, bf16[2,1,192,1536]{3,2,1,0:T(8,128)(2,1)}, u32[]{:S(2)}) copy-start(bf16[2,1,192,1536]{3,2,1,0:T(8,128)(2,1)} %param.9) | copy-start | bytes 3538948
  226.6 376.4 %all-reduce.10.cloned.1.call-start = ((), (), s32[]{:S(2)}) async-start(), calls=%async_computation.2 | async-start | bytes 2359296 | tf_op jit(solution)/shard_map/psum | solution.py:131
Sparse Core Ops, SparseCore 0:
  10.8 66.0 all-reduce.5
  226.7 170.3 all-reduce.7
  400.6 202.4 all-reduce.9
where the time goes:
time: 614 us; the launch traced here: 613 us
  waiting for transfers between devices  488 us (79%)
  starting transfers between devices  56.6 us (9%)
  matrix products  19.3 us (3%)
  other arithmetic  17 us (3%)
  between operations  13.9 us (2%)
  local copies, waits for them, and re-layouts  12.1 us (2%)
    psum x1, waiting for transfers between devices, per_device(): lax.psum(layer_gradient.astype(jnp.bfloat16), 'angle').astype(jnp.float32)  203 us
    psum x1, waiting for transfers between devices, per_device(): lax.psum(tile_gradient.astype(jnp.bfloat16), 'slab').astype(jnp.float32)  170 us
    psum x1, waiting for transfers between devices, per_device(): projection = lax.psum(partial_sum.astype(jnp.bfloat16), 'slab')  66.1 us
    ppermute x2, starting transfers between devices, passed_along(): lax.ppermute(value, axis, [(source, source + steps) for source in range(i...  56.5 us
    ppermute x2, waiting for transfers between devices, passed_along(): lax.ppermute(value, axis, [(source, source + steps) for source in range(i...  49 us
    dot_general x16, matrix products, twodot(): jnp.dot(left_matrix, right_matrix, preferred_element_type=jnp.float32)  19.3 us
  transfers between devices with their start and end apart: 5, of which 5 were waited for; matrix products, arithmetic and copies ran while one was open for 0% of the time, Pallas kernels for 0%

commit v1 on v0

v1 whole, which is shorter than its diff:
```python
import functools

import jax
import jax.numpy as jnp
import ml_dtypes
import numpy as np
from jax import lax
from jax.experimental import pallas as pl
from jax.experimental.pallas import tpu as pltpu
from jax.sharding import PartitionSpec as P

angle_center = 600
shear_divisor = 64
step_size = 0.03
floor_square = 0.25

LANE = 128
HALO = 64
SMEM = pl.BlockSpec(memory_space=pltpu.SMEM)
VMEM = pl.BlockSpec(memory_space=pltpu.VMEM)


def dft_tables(plane_width):
    index_line = np.arange(plane_width, dtype=np.int32)
    product_mod = np.mod(index_line[:, None] * index_line[None, :], plane_width)
    phase_table = product_mod.astype(np.float32) * np.float32(2.0 * 3.141592653589793 / plane_width)
    scale_factor = np.float32(plane_width ** (-0.5))
    table_real = (np.cos(phase_table) * scale_factor).astype(ml_dtypes.bfloat16)
    table_imag = (-np.sin(phase_table) * scale_factor).astype(ml_dtypes.bfloat16)
    return table_real, table_imag


def dot(left, right):
    return jnp.dot(left, right, preferred_element_type=jnp.float32)


def one_hot(rows, columns, down):
    row = lax.broadcasted_iota(jnp.int32, (rows, columns), 0)
    column = lax.broadcasted_iota(jnp.int32, (rows, columns), 1)
    return (row - column == down).astype(jnp.float32).astype(jnp.bfloat16)


def call(body, out_shape, in_specs, scratch=()):
    return pl.pallas_call(
        body,
        out_shape=out_shape,
        in_specs=in_specs,
        out_specs=jax.tree.map(lambda _: VMEM, out_shape),
        scratch_shapes=scratch,
        compiler_params=pltpu.CompilerParams(vmem_limit_bytes=48 * 1024 * 1024),
    )


def cut_body(columns, place_ref, volume_ref, *outs):
    rows, width = outs[0].shape[1:]
    blocks = columns // LANE

    for n, out in enumerate(outs):
        top, left, live = (place_ref[3 * n + i] for i in range(3))

        @pl.when(live > 0)
        def _():
            block, inside = left // LANE, left % LANE
            pick_rows = one_hot(rows, volume_ref.shape[1], -top)
            pick_columns = one_hot(width + LANE, width, inside)
            for part in range(2):
                pieces = []
                for i in range(width // LANE + 1):
                    start = pl.multiple_of(lax.rem(block + i, blocks) * LANE, LANE)
                    pieces.append(volume_ref[part, :, pl.ds(start, LANE)])
                narrow = dot(jnp.concatenate(pieces, axis=1), pick_columns).astype(jnp.bfloat16)
                out[part] = dot(pick_rows, narrow).astype(jnp.bfloat16)

        @pl.when(live == 0)
        def _():
            out[...] = jnp.zeros_like(out)


def cut_windows(place, layer, count, rows, width):
    shape = jax.ShapeDtypeStruct((2, rows, width), jnp.bfloat16)
    return call(
        functools.partial(cut_body, layer.shape[2]), [shape] * count, [SMEM, VMEM]
    )(place, layer)


def patch_body(
    live_ref, upper0, upper1, upper2, upper3, lower, probe, pattern, wr_ref, wi_ref, up_out, low_out
):
    @pl.when(live_ref[0] > 0)
    def _():
        rows = upper0.shape[1]
        f32, bf16 = jnp.float32, jnp.bfloat16

        def window(part):
            above = sum(u[part].astype(f32) for u in (upper0, upper1, upper2, upper3))
            above = above.astype(bf16).astype(f32)
            below = lower[part].astype(f32)
            return jnp.concatenate(
                [above[:HALO], above[HALO:] + below[: rows - HALO], below[rows - HALO :]], axis=0
            )

        phase, absorption = window(0), window(1)
        magnitude = jnp.exp(-absorption)
        trans_real = magnitude * jnp.cos(phase)
        trans_imag = magnitude * jnp.sin(phase)
        probe_real, probe_imag = probe[0], probe[1]
        wr, wi = wr_ref[...], wi_ref[...]
        wave_real = (probe_real * trans_real - probe_imag * trans_imag).astype(bf16)
        wave_imag = (probe_real * trans_imag + probe_imag * trans_real).astype(bf16)
        left_real = (dot(wr, wave_real) - dot(wi, wave_imag)).astype(bf16)
        left_imag = (dot(wr, wave_imag) + dot(wi, wave_real)).astype(bf16)
        far_real = dot(left_real, wr) - dot(left_imag, wi)
        far_imag = dot(left_real, wi) + dot(left_imag, wr)
        power = far_real * far_real + far_imag * far_imag + floor_square
        keeping = 1.0 - pattern[...].astype(f32) * lax.rsqrt(power)
        resid_real = (far_real * keeping).astype(bf16)
        resid_imag = (far_imag * keeping).astype(bf16)
        back_real = (dot(wr, resid_real) + dot(wi, resid_imag)).astype(bf16)
        back_imag = (dot(wr, resid_imag) - dot(wi, resid_real)).astype(bf16)
        exit_real = dot(back_real, wr) + dot(back_imag, wi)
        exit_imag = dot(back_imag, wr) - dot(back_real, wi)
        mixed_real = probe_real * exit_real + probe_imag * exit_imag
        mixed_imag = probe_real * exit_imag - probe_imag * exit_real
        final_real = trans_real * mixed_real + trans_imag * mixed_imag
        final_imag = trans_real * mixed_imag - trans_imag * mixed_real
        for part, value in enumerate((final_imag, -final_real)):
            value = value.astype(bf16)
            up_out[part] = value[:rows]
            low_out[part] = value[HALO:]

    @pl.when(live_ref[0] == 0)
    def _():
        up_out[...] = jnp.zeros_like(up_out)
        low_out[...] = jnp.zeros_like(low_out)


def patch_gradient(live, uppers, lower, probe_wave, pattern, tables):
    shape = jax.ShapeDtypeStruct(lower.shape, jnp.bfloat16)
    return call(patch_body, [shape] * 2, [SMEM] + [VMEM] * 9)(
        live, *uppers, lower, probe_wave, pattern, *tables
    )


def place_body(count, place_ref, *refs):
    windows, (keep_out, send_out, total) = refs[:count], refs[count:]
    rows, width = windows[0].shape[1:]
    blocks = total.shape[2] // LANE
    total[...] = jnp.zeros_like(total)
    for n, window in enumerate(windows):
        top, left, live = (place_ref[3 * n + i] for i in range(3))

        @pl.when(live > 0)
        def _():
            block, inside = left // LANE, left % LANE
            put_rows = one_hot(total.shape[1], rows, top)
            put_columns = one_hot(width, width + LANE, -inside)
            for part in range(2):
                moved = dot(put_rows, window[part]).astype(jnp.bfloat16)
                wide = dot(moved, put_columns)
                for i in range(width // LANE + 1):
                    start = pl.multiple_of(lax.rem(block + i, blocks) * LANE, LANE)
                    total[part, :, pl.ds(start, LANE)] += wide[:, i * LANE : (i + 1) * LANE]

    core = place_ref[3 * count]
    keep_out[...] = total[core]
    send_out[...] = total[1 - core].astype(jnp.bfloat16)


def place_windows(place, windows, tile_rows, columns):
    shapes = [
        jax.ShapeDtypeStruct((tile_rows, columns), jnp.float32),
        jax.ShapeDtypeStruct((tile_rows, columns), jnp.bfloat16),
    ]
    return call(
        functools.partial(place_body, len(windows)),
        shapes,
        [SMEM] + [VMEM] * len(windows),
        [pltpu.VMEM((2, tile_rows, columns), jnp.float32)],
    )(place, *windows)


def step_body(where_ref, volume_ref, *refs):
    out = refs[-1]
    core, group = where_ref[0], where_ref[1]
    blocks = (len(refs) - 1) // 2
    for n, ref in enumerate(refs[:-1]):
        part = core if n < blocks else 1 - core
        rows = ref.shape[0]
        start = pl.multiple_of((group ^ (n % blocks)) * rows, 16)
        old = volume_ref[part, pl.ds(start, rows), :].astype(jnp.float32)
        out[part, pl.ds(start, rows), :] = old - step_size * ref[...].astype(jnp.float32)


def step(where, layer, blocks):
    return call(
        step_body,
        jax.ShapeDtypeStruct(layer.shape, jnp.float32),
        [SMEM] + [VMEM] * (1 + len(blocks)),
    )(where, layer, *blocks)


def to_slab(value, by):
    count = lax.axis_size("slab")
    return lax.ppermute(value, "slab", [(i, (i + by) % count) for i in range(count)])


def to_tile(value, by):
    count = lax.axis_size("tile")
    pairs = [(i, i + by) for i in range(count) if 0 <= i + by < count]
    return lax.ppermute(value, "tile", pairs)


def to_next_tile_and_slab(value, by):
    tiles, slabs = lax.axis_size("tile"), lax.axis_size("slab")
    pairs = [
        (s * tiles + t, (s + by) % slabs * tiles + t + 1) for t in range(tiles - 1) for s in range(slabs)
    ]
    return lax.ppermute(value, ("slab", "tile"), pairs)


def swap_angle(value, mask):
    return lax.ppermute(value, "angle", [(i, i ^ mask) for i in range(lax.axis_size("angle"))])


def per_device(volume, probe_wave, amplitudes, offsets, column_starts, counts, angle_ids):
    layer = volume.reshape(volume.shape[0], *volume.shape[2:])
    tile_rows, columns = layer.shape[1:]
    width = amplitudes.shape[-1]
    capacity = offsets.shape[3]
    slabs = lax.axis_size("slab")
    slab = lax.axis_index("slab")
    angle = lax.axis_index("angle")
    core, group, far = angle & 1, (angle >> 1) & 3, angle >> 3
    f32, bf16 = jnp.float32, jnp.bfloat16
    tables = dft_tables(width)
    window_rows = width - HALO
    patterns = amplitudes.reshape(capacity, width, width)

    sheared = jnp.floor_divide((angle_ids[0] - angle_center) * (slab - slabs // 2), shear_divisor)
    shift = jnp.mod(sheared, columns)
    live = (jnp.arange(capacity) < counts.reshape(1)).astype(jnp.int32)
    meta = jnp.stack([offsets.reshape(capacity), column_starts.reshape(capacity), live], axis=1)
    own_meta = [meta] + [to_slab(meta, -k) for k in range(1, slabs)]
    before_meta = [to_next_tile_and_slab(meta, -k) for k in range(slabs)]

    def place(metas, down):
        table = jnp.stack(metas)
        top = table[..., 0] + down
        left = jnp.mod(table[..., 1] + shift, columns)
        return jnp.stack([top, left, table[..., 2]], axis=-1)

    below = HALO - tile_rows
    lower_cuts = cut_windows(
        place(before_meta, below).transpose(1, 0, 2).reshape(-1), layer, capacity * slabs, window_rows, width
    )
    upper_cuts = cut_windows(
        place(own_meta, 0).transpose(1, 0, 2).reshape(-1), layer, capacity * slabs, window_rows, width
    )

    def exchanged(cuts):
        return [cuts[0]] + [to_slab(cuts[k], k) for k in range(1, slabs)]

    lowers = []
    for slot in range(capacity):
        partials = exchanged(lower_cuts[slot * slabs : (slot + 1) * slabs])
        summed = sum(p.astype(f32) for p in partials).astype(bf16)
        lowers.append(to_tile(summed, -1))
    uppers = [exchanged(upper_cuts[slot * slabs : (slot + 1) * slabs]) for slot in range(capacity)]

    own_grads, before_grads = [], []
    for slot in range(capacity):
        up, low = patch_gradient(
            live[slot : slot + 1], uppers[slot], lowers[slot], probe_wave, patterns[slot], tables
        )
        own_grads.append([up] + [to_slab(up, k) for k in range(1, slabs)])
        low = to_tile(low, 1)
        before_grads.append([low] + [to_slab(low, k) for k in range(1, slabs)])

    order = [(slabs - k) % slabs for k in range(slabs)]
    places = [
        place([own_meta[k] for k in order], 0).transpose(1, 0, 2).reshape(-1),
        place([before_meta[k] for k in order], below).transpose(1, 0, 2).reshape(-1),
        core.reshape(1),
    ]
    kept, sent = place_windows(
        jnp.concatenate(places).astype(jnp.int32),
        [w for slot in own_grads for w in slot] + [w for slot in before_grads for w in slot],
        tile_rows,
        columns,
    )

    kept = kept + swap_angle(sent, 1).astype(f32)
    kept = kept.reshape(4, tile_rows // 4, columns)
    block = lambda k: lax.dynamic_index_in_dim(kept, group ^ k, 0, keepdims=False)
    arrived = [swap_angle(block(k).astype(bf16), k << 1) for k in range(1, 4)]
    mine = sum((a.astype(f32) for a in arrived), block(0))
    mine = mine.reshape(2, tile_rows // 8, columns)
    half = lambda k: lax.dynamic_index_in_dim(mine, far ^ k, 0, keepdims=False)
    done = (half(0) + swap_angle(half(1).astype(bf16), 8).astype(f32)).astype(bf16)

    other = swap_angle(done, 8)
    first = jnp.where(far == 0, done, other)
    second = jnp.where(far == 0, other, done)
    block0 = jnp.concatenate([first, second], axis=0)
    blocks = [block0] + [swap_angle(block0, k << 1) for k in range(1, 4)]
    blocks = blocks + [swap_angle(b, 1) for b in blocks]
    new = step(jnp.stack([core, group]).astype(jnp.int32), layer, blocks)
    return new.reshape(volume.shape)


def solution(mesh):
    in_specs = (
        P(None, "slab", "tile", None),
        P(),
        P("angle", "tile", "slab", None, None, None),
        P("angle", "tile", "slab", None),
        P("angle", "tile", "slab", None),
        P("angle", "tile", "slab"),
        P("angle"),
    )
    out_specs = P(None, "slab", "tile", None)
    return jax.shard_map(
        per_device, mesh=mesh, in_specs=in_specs, out_specs=out_specs, check_vma=False
    )
```

time: 614 us -> 312 us (0.51)
  the two profiles are of different devices: /device:TPU:1 before, /device:TPU:11 now
where the time goes in v1:
time: 312 us; the launch traced here: 310 us
  starting transfers between devices  233 us (75%)
  waiting for transfers between devices  29.3 us (9%)
  local copies, waits for them, and re-layouts  20.7 us (7%)
  Pallas kernels  19 us (6%)
  other arithmetic  5.72 us (2%)
    ppermute x27, starting transfers between devices, to_slab(): lax.ppermute(value, 'slab', [(i, (i + by) % count) for i in range(count)])  89.3 us
    ppermute x13, starting transfers between devices, swap_angle(): lax.ppermute(value, 'angle', [(i, i ^ mask) for i in range(lax.axis_size(...  69.5 us
    ppermute x4, starting transfers between devices, to_tile(): return lax.ppermute(value, 'tile', pairs)  38.8 us
    ppermute x4, starting transfers between devices, to_next_tile_and_slab(): return lax.ppermute(value, ('slab', 'tile'), pairs)  35.4 us
    ppermute x13, waiting for transfers between devices, swap_angle(): lax.ppermute(value, 'angle', [(i, i ^ mask) for i in range(lax.axis_size(...  26.1 us
    unnamed x50, local copies, waits for them, and re-layouts  17.3 us
    pallas_call x2, Pallas kernels, cut_windows(): call(functools.partial(cut_body, layer.shape[2]), [shape] * count, [SMEM,...  6.87 us
  transfers between devices with their start and end apart: 48, of which 9 were waited for; matrix products, arithmetic and copies ran while one was open for 2% of the time, Pallas kernels for 3%

profile of v1, /device:TPU:11, one launch (start us, length us, event | category | flops | bytes accessed | tf_op | source)
XLA Modules:
  0.0 309.9 jit_solution(5481889885543953284)
XLA Ops:
  1.3 15.4 %collective-permute-start.3 = (s32[2,3]{0,1:T(4,128)S(1)}, s32[2,3]{0,1:T(4,128)S(1)}, u32[]{:S(2)}, u32[]{:S(2)}) collective-permute-start(s32[2,3]{0,1:T(4,128)S(1)} %pad_add_fusion.8), channel_id=1, source_target_pairs={{0,1},{8,9},{16,17},{24,25},{1,2},{9,10},{17,18},{25,26},{2,3},{10... | collective-permute-start | bytes 80 | tf_op jit(solution)/shard_map/ppermute | solution.py:218
  19.6 13.6 %collective-permute-start.5 = (s32[2,3]{0,1:T(4,128)S(1)}, s32[2,3]{0,1:T(4,128)S(1)}, u32[]{:S(2)}, u32[]{:S(2)}) collective-permute-start(s32[2,3]{0,1:T(4,128)S(1)} %pad_add_fusion.8), channel_id=1, source_target_pairs={{0,17},{8,25},{16,1},{24,9},{1,18},{9,26},{17,2},{25,10},{2,19},{1... | collective-permute-start | bytes 80 | tf_op jit(solution)/shard_map/ppermute | solution.py:218
  33.3 3.5 %collective-permute-start.6 = (s32[2,3]{0,1:T(4,128)S(1)}, s32[2,3]{0,1:T(4,128)S(1)}, u32[]{:S(2)}, u32[]{:S(2)}) collective-permute-start(s32[2,3]{0,1:T(4,128)S(1)} %pad_add_fusion.8), channel_id=1, source_target_pairs={{0,25},{8,1},{16,9},{24,17},{1,26},{9,2},{17,10},{25,18},{2,27},{1... | collective-permute-start | bytes 80 | tf_op jit(solution)/shard_map/ppermute | solution.py:218
  41.2 4.8 %collective-permute-start.1 = (s32[2,3]{0,1:T(4,128)S(1)}, s32[2,3]{0,1:T(4,128)S(1)}, u32[]{:S(2)}, u32[]{:S(2)}) collective-permute-start(s32[2,3]{0,1:T(4,128)S(1)} %pad_add_fusion.8), channel_id=1, source_target_pairs={{0,16},{8,24},{16,0},{24,8},{1,17},{9,25},{17,1},{25,9},{2,18},{10... | collective-permute-start | bytes 80 | tf_op jit(solution)/shard_map/ppermute | solution.py:204
  49.9 3.4 %shard_map.92 = (bf16[2,192,256]{2,1,0:T(8,128)(2,1)S(1)}, bf16[2,192,256]{2,1,0:T(8,128)(2,1)S(1)}, bf16[2,192,256]{2,1,0:T(8,128)(2,1)S(1)}, bf16[2,192,256]{2...) custom-call(s32[24]{0:T(128)S(1)} %reshape.52.place_ref, ...), custom_call_target="tpu_custom_call" | custom-call | tf_op jit(solution)/shard_map/pallas_call | solution.py:81
  53.3 3.4 %collective-permute-start.20 = (bf16[2,192,256]{2,1,0:T(8,128)(2,1)S(1)}, bf16[2,192,256]{2,1,0:T(8,128)(2,1)S(1)}, u32[]{:S(2)}, u32[]{:S(2)}) collective-permute-start(bf16[2,192,256]{2,1,0:T(8,128)(2,1)S(1)} %get-tuple-element.41), channel_id=1, source_target_pairs={{0,8},{8,16},{16,24},{24,0},{1,9},{9,17},{17,25},{25,1},{2,10},{10... | collective-permute-start | bytes 589832 | tf_op jit(solution)/shard_map/ppermute | solution.py:204
  56.7 4.0 %collective-permute-start.21 = (bf16[2,192,256]{2,1,0:T(8,128)(2,1)S(1)}, bf16[2,192,256]{2,1,0:T(8,128)(2,1)S(1)}, u32[]{:S(2)}, u32[]{:S(2)}) collective-permute-start(bf16[2,192,256]{2,1,0:T(8,128)(2,1)S(1)} %get-tuple-element.42), channel_id=1, source_target_pairs={{0,16},{8,24},{16,0},{24,8},{1,17},{9,25},{17,1},{25,9},{2,18},{10... | collective-permute-start | bytes 589832 | tf_op jit(solution)/shard_map/ppermute | solution.py:204
  60.7 3.7 %collective-permute-start.22 = (bf16[2,192,256]{2,1,0:T(8,128)(2,1)S(1)}, bf16[2,192,256]{2,1,0:T(8,128)(2,1)}, u32[]{:S(2)}, u32[]{:S(2)}) collective-permute-start(bf16[2,192,256]{2,1,0:T(8,128)(2,1)S(1)} %get-tuple-element.43), channel_id=1, source_target_pairs={{0,24},{8,0},{16,8},{24,16},{1,25},{9,1},{17,9},{25,17},{2,26},{10... | collective-permute-start | bytes 589832 | tf_op jit(solution)/shard_map/ppermute | solution.py:204
  65.5 3.4 %shard_map.91 = (bf16[2,192,256]{2,1,0:T(8,128)(2,1)S(1)}, bf16[2,192,256]{2,1,0:T(8,128)(2,1)S(1)}, bf16[2,192,256]{2,1,0:T(8,128)(2,1)S(1)}, bf16[2,192,256]{2...) custom-call(s32[24]{0:T(128)S(1)} %reshape.51.place_ref, ...), custom_call_target="tpu_custom_call" | custom-call | tf_op jit(solution)/shard_map/pallas_call | solution.py:81
  71.1 3.7 %collective-permute-start.18 = (bf16[2,192,256]{2,1,0:T(8,128)(2,1)S(1)}, bf16[2,192,256]{2,1,0:T(8,128)(2,1)S(1)}, u32[]{:S(2)}, u32[]{:S(2)}) collective-permute-start(bf16[2,192,256]{2,1,0:T(8,128)(2,1)S(1)} %get-tuple-element.38), channel_id=1, source_target_pairs={{0,16},{8,24},{16,0},{24,8},{1,17},{9,25},{17,1},{25,9},{2,18},{10... | collective-permute-start | bytes 589832 | tf_op jit(solution)/shard_map/ppermute | solution.py:204
  80.1 3.7 %collective-permute-start.12 = (bf16[2,192,256]{2,1,0:T(8,128)(2,1)S(1)}, bf16[2,192,256]{2,1,0:T(8,128)(2,1)S(1)}, u32[]{:S(2)}, u32[]{:S(2)}) collective-permute-start(bf16[2,192,256]{2,1,0:T(8,128)(2,1)S(1)} %get-tuple-element.34), channel_id=1, source_target_pairs={{0,24},{8,0},{16,8},{24,16},{1,25},{9,1},{17,9},{25,17},{2,26},{10... | collective-permute-start | bytes 589832 | tf_op jit(solution)/shard_map/ppermute | solution.py:204
  84.9 3.4 %collective-permute-start.19 = (bf16[2,192,256]{2,1,0:T(8,128)(2,1)S(1)}, bf16[2,192,256]{2,1,0:T(8,128)(2,1)S(1)}, u32[]{:S(2)}, u32[]{:S(2)}) collective-permute-start(bf16[2,192,256]{2,1,0:T(8,128)(2,1)S(1)} %get-tuple-element.39), channel_id=1, source_target_pairs={{0,24},{8,0},{16,8},{24,16},{1,25},{9,1},{17,9},{25,17},{2,26},{10... | collective-permute-start | bytes 589832 | tf_op jit(solution)/shard_map/ppermute | solution.py:204
  90.2 3.7 %collective-permute-start.8 = (bf16[2,192,256]{2,1,0:T(8,128)(2,1)S(1)}, bf16[2,192,256]{2,1,0:T(8,128)(2,1)S(1)}, u32[]{:S(2)}, u32[]{:S(2)}) collective-permute-start(bf16[2,192,256]{2,1,0:T(8,128)(2,1)S(1)} %get-tuple-element.29), channel_id=1, source_target_pairs={{0,16},{8,24},{16,0},{24,8},{1,17},{9,25},{17,1},{25,9},{2,18},{10... | collective-permute-start | bytes 589832 | tf_op jit(solution)/shard_map/ppermute | solution.py:204
  95.9 13.0 %collective-permute-start.23 = (bf16[2,192,256]{2,1,0:T(8,128)(2,1)S(1)}, bf16[2,192,256]{2,1,0:T(8,128)(2,1)S(1)}, u32[]{:S(2)}, u32[]{:S(2)}) collective-permute-start(bf16[2,192,256]{2,1,0:T(8,128)(2,1)S(1)} %add_convert_fusion), channel_id=1, source_target_pairs={{1,0},{2,1},{3,2},{4,3},{5,4},{6,5},{7,6},{9,8},{10,9},{11,10},{12... | collective-permute-start | bytes 589832 | tf_op jit(solution)/shard_map/ppermute | solution.py:210
  112.7 17.0 %collective-permute-start.31 = (bf16[2,192,256]{2,1,0:T(8,128)(2,1)S(1)}, bf16[2,192,256]{2,1,0:T(8,128)(2,1)S(1)}, u32[]{:S(2)}, u32[]{:S(2)}) collective-permute-start(bf16[2,192,256]{2,1,0:T(8,128)(2,1)S(1)} %get-tuple-element.46), channel_id=1, source_target_pairs={{0,1},{1,2},{2,3},{3,4},{4,5},{5,6},{6,7},{8,9},{9,10},{10,11},{11... | collective-permute-start | bytes 589832 | tf_op jit(solution)/shard_map/ppermute | solution.py:210
  129.7 7.9 %collective-permute-start.24 = (bf16[2,192,256]{2,1,0:T(8,128)(2,1)S(1)}, bf16[2,192,256]{2,1,0:T(8,128)(2,1)S(1)}, u32[]{:S(2)}, u32[]{:S(2)}) collective-permute-start(bf16[2,192,256]{2,1,0:T(8,128)(2,1)S(1)} %get-tuple-element.44.refs_4_), channel_id=1, source_target_pairs={{0,8},{8,16},{16,24},{24,0},{1,9},{9,17},{17,25},{25,1},{2,10},{10... | collective-permute-start | bytes 589832 | tf_op jit(solution)/shard_map/ppermute | solution.py:204
  139.6 3.7 %collective-permute-start.26 = (bf16[2,192,256]{2,1,0:T(8,128)(2,1)S(1)}, bf16[2,192,256]{2,1,0:T(8,128)(2,1)S(1)}, u32[]{:S(2)}, u32[]{:S(2)}) collective-permute-start(bf16[2,192,256]{2,1,0:T(8,128)(2,1)S(1)} %get-tuple-element.44.refs_4_), channel_id=1, source_target_pairs={{0,24},{8,0},{16,8},{24,16},{1,25},{9,1},{17,9},{25,17},{2,26},{10... | collective-permute-start | bytes 589832 | tf_op jit(solution)/shard_map/ppermute | solution.py:204
  146.4 6.9 %collective-permute-start.27 = (bf16[2,192,256]{2,1,0:T(8,128)(2,1)S(1)}, bf16[2,192,256]{2,1,0:T(8,128)(2,1)S(1)}, u32[]{:S(2)}, u32[]{:S(2)}) collective-permute-start(bf16[2,192,256]{2,1,0:T(8,128)(2,1)S(1)} %get-tuple-element.45), channel_id=1, source_target_pairs={{0,1},{1,2},{2,3},{3,4},{4,5},{5,6},{6,7},{8,9},{9,10},{10,11},{11... | collective-permute-start | bytes 589832 | tf_op jit(solution)/shard_map/ppermute | solution.py:210
  153.3 6.2 %collective-permute-start.14 = (bf16[2,192,256]{2,1,0:T(8,128)(2,1)S(1)}, bf16[2,192,256]{2,1,0:T(8,128)(2,1)S(1)}, u32[]{:S(2)}, u32[]{:S(2)}) collective-permute-start(bf16[2,192,256]{2,1,0:T(8,128)(2,1)S(1)} %get-tuple-element.35.refs_0_), channel_id=1, source_target_pairs={{0,8},{8,16},{16,24},{24,0},{1,9},{9,17},{17,25},{25,1},{2,10},{10... | collective-permute-start | bytes 589832 | tf_op jit(solution)/shard_map/ppermute | solution.py:204
  161.4 3.7 %collective-permute-start.16 = (bf16[2,192,256]{2,1,0:T(8,128)(2,1)S(1)}, bf16[2,192,256]{2,1,0:T(8,128)(2,1)S(1)}, u32[]{:S(2)}, u32[]{:S(2)}) collective-permute-start(bf16[2,192,256]{2,1,0:T(8,128)(2,1)S(1)} %get-tuple-element.35.refs_0_), channel_id=1, source_target_pairs={{0,24},{8,0},{16,8},{24,16},{1,25},{9,1},{17,9},{25,17},{2,26},{10... | collective-permute-start | bytes 589832 | tf_op jit(solution)/shard_map/ppermute | solution.py:204
  169.0 5.4 %collective-permute-start.33 = (bf16[2,192,256]{2,1,0:T(8,128)(2,1)S(1)}, bf16[2,192,256]{2,1,0:T(8,128)(2,1)S(1)}, u32[]{:S(2)}, u32[]{:S(2)}) collective-permute-start(bf16[2,192,256]{2,1,0:T(8,128)(2,1)S(1)} %collective-permute-done.31.refs_12_), channel_id=1, source_target_pairs={{0,16},{8,24},{16,0},{24,8},{1,17},{9,25},{17,1},{25,9},{2,18},{10... | collective-permute-start | bytes 589832 | tf_op jit(solution)/shard_map/ppermute | solution.py:204
  204.3 6.1 %shard_map.95 = (f32[192,1536]{1,0:T(8,128)S(1)}, bf16[192,1536]{1,0:T(8,128)(2,1)}) custom-call(s32[49]{0:T(128)S(1)} %pad_add_fusion.10.place_ref, bf16[2,192,256]{2,1,0:T(8,128)(2,1)S(1)} %get-tuple-element.35.refs_0_, bf16[2,192,256]{2,1,0:T(8,128)(2,1)S(1)} %copy-done.8, bf16[2,192,256]{2,1,0:T(8,128)(2,1)S(1)} %copy-done.10, ...), custom_call_target="tpu_custom_call" | custom-call | tf_op jit(solution)/shard_map/pallas_call | solution.py:174
  210.4 22.3 %collective-permute-start.35 = (bf16[192,1536]{1,0:T(8,128)(2,1)}, bf16[192,1536]{1,0:T(8,128)(2,1)}, u32[]{:S(2)}, u32[]{:S(2)}) collective-permute-start(bf16[192,1536]{1,0:T(8,128)(2,1)} %get-tuple-element.48), channel_id=1, source_target_pairs={{0,32},{32,0},{64,96},{96,64},{128,160},{160,128},{192,224},{224,1... | collective-permute-start | bytes 1769480 | tf_op jit(solution)/shard_map/ppermute | solution.py:222
  235.9 10.1 %collective-permute-start.36 = (bf16[48,1536]{1,0:T(8,128)(2,1)S(1)}, bf16[48,1536]{1,0:T(8,128)(2,1)S(1)}, u32[]{:S(2)}, u32[]{:S(2)}) collective-permute-start(bf16[48,1536]{1,0:T(8,128)(2,1)S(1)} %get-tuple-element.49), channel_id=1, source_target_pairs={{0,64},{32,96},{64,0},{96,32},{128,192},{160,224},{192,128},{224,1... | collective-permute-start | bytes 442376 | tf_op jit(solution)/shard_map/ppermute | solution.py:222
  248.0 4.0 %collective-permute-start.38 = (bf16[48,1536]{1,0:T(8,128)(2,1)S(1)}, bf16[48,1536]{1,0:T(8,128)(2,1)S(1)}, u32[]{:S(2)}, u32[]{:S(2)}) collective-permute-start(bf16[48,1536]{1,0:T(8,128)(2,1)S(1)} %get-tuple-element.50), channel_id=1, source_target_pairs={{0,192},{32,224},{64,128},{96,160},{128,64},{160,96},{192,0},{224,... | collective-permute-start | bytes 442376 | tf_op jit(solution)/shard_map/ppermute | solution.py:222
  252.0 8.7 %collective-permute-done.37 = bf16[48,1536]{1,0:T(8,128)(2,1)S(1)} collective-permute-done((bf16[48,1536]{1,0:T(8,128)(2,1)S(1)}, bf16[48,1536]{1,0:T(8,128)(2,1)S(1)}, u32[]{:S(2)}, u32[]{:S(2)}) %collective-permute-start.37) | collective-permute-done | bytes 147488 | tf_op jit(solution)/shard_map/ppermute | solution.py:222
  262.7 7.2 %collective-permute-done.39 = bf16[24,1536]{1,0:T(8,128)(2,1)S(1)} collective-permute-done((bf16[24,1536]{1,0:T(8,128)(2,1)S(1)}, bf16[24,1536]{1,0:T(8,128)(2,1)S(1)}, u32[]{:S(2)}, u32[]{:S(2)}) %collective-permute-start.39) | collective-permute-done | bytes 73760 | tf_op jit(solution)/shard_map/ppermute | solution.py:222
  272.1 6.9 %collective-permute-done.40 = bf16[24,1536]{1,0:T(8,128)(2,1)S(1)} collective-permute-done((bf16[24,1536]{1,0:T(8,128)(2,1)S(1)}, bf16[24,1536]{1,0:T(8,128)(2,1)S(1)}, u32[]{:S(2)}, u32[]{:S(2)}) %collective-permute-start.40) | collective-permute-done | bytes 73760 | tf_op jit(solution)/shard_map/ppermute | solution.py:222
  279.0 7.5 %collective-permute-start.41 = (bf16[48,1536]{1,0:T(8,128)(2,1)S(1)}, bf16[48,1536]{1,0:T(8,128)(2,1)S(1)}, u32[]{:S(2)}, u32[]{:S(2)}) collective-permute-start(bf16[48,1536]{1,0:T(8,128)(2,1)S(1)} %pad_maximum_fusion.refs_0_), channel_id=1, source_target_pairs={{0,64},{32,96},{64,0},{96,32},{128,192},{160,224},{192,128},{224,1... | collective-permute-start | bytes 442376 | tf_op jit(solution)/shard_map/ppermute | solution.py:222
  288.4 4.0 %collective-permute-start.43 = (bf16[48,1536]{1,0:T(8,128)(2,1)S(1)}, bf16[48,1536]{1,0:T(8,128)(2,1)S(1)}, u32[]{:S(2)}, u32[]{:S(2)}) collective-permute-start(bf16[48,1536]{1,0:T(8,128)(2,1)S(1)} %pad_maximum_fusion.refs_0_), channel_id=1, source_target_pairs={{0,192},{32,224},{64,128},{96,160},{128,64},{160,96},{192,0},{224,... | collective-permute-start | bytes 442376 | tf_op jit(solution)/shard_map/ppermute | solution.py:222
  292.4 5.8 %collective-permute-start.44 = (bf16[48,1536]{1,0:T(8,128)(2,1)S(1)}, bf16[48,1536]{1,0:T(8,128)(2,1)S(1)}, u32[]{:S(2)}, u32[]{:S(2)}) collective-permute-start(bf16[48,1536]{1,0:T(8,128)(2,1)S(1)} %pad_maximum_fusion.refs_0_), channel_id=1, source_target_pairs={{0,32},{32,0},{64,96},{96,64},{128,160},{160,128},{192,224},{224,1... | collective-permute-start | bytes 442376 | tf_op jit(solution)/shard_map/ppermute | solution.py:222
  300.4 4.0 %collective-permute-start.46 = (bf16[48,1536]{1,0:T(8,128)(2,1)S(1)}, bf16[48,1536]{1,0:T(8,128)(2,1)S(1)}, u32[]{:S(2)}, u32[]{:S(2)}) collective-permute-start(bf16[48,1536]{1,0:T(8,128)(2,1)S(1)} %collective-permute-done.42.refs_2_), channel_id=1, source_target_pairs={{0,32},{32,0},{64,96},{96,64},{128,160},{160,128},{192,224},{224,1... | collective-permute-start | bytes 442376 | tf_op jit(solution)/shard_map/ppermute | solution.py:222
  (160 shorter events, 87.6 us)
Async XLA Ops:
  1.3 39.8 %collective-permute-start.3 = (s32[2,3]{0,1:T(4,128)S(1)}, s32[2,3]{0,1:T(4,128)S(1)}, u32[]{:S(2)}, u32[]{:S(2)}) collective-permute-start(s32[2,3]{0,1:T(4,128)S(1)} %pad_add_fusion.8), channel_id=1, source_target_pairs={{0,1},{8,9},{16,17},{24,25},{1,2},{9,10},{17,18},{25,26},{2,3},{10... | collective-permute-start | bytes 80 | tf_op jit(solution)/shard_map/ppermute | solution.py:218
  16.8 29.3 %collective-permute-start.4 = (s32[2,3]{0,1:T(4,128)S(1)}, s32[2,3]{0,1:T(4,128)S(1)}, u32[]{:S(2)}, u32[]{:S(2)}) collective-permute-start(s32[2,3]{0,1:T(4,128)S(1)} %pad_add_fusion.8), channel_id=1, source_target_pairs={{0,9},{8,17},{16,25},{24,1},{1,10},{9,18},{17,26},{25,2},{2,11},{1... | collective-permute-start | bytes 80 | tf_op jit(solution)/shard_map/ppermute | solution.py:218
  19.6 28.5 %collective-permute-start.5 = (s32[2,3]{0,1:T(4,128)S(1)}, s32[2,3]{0,1:T(4,128)S(1)}, u32[]{:S(2)}, u32[]{:S(2)}) collective-permute-start(s32[2,3]{0,1:T(4,128)S(1)} %pad_add_fusion.8), channel_id=1, source_target_pairs={{0,17},{8,25},{16,1},{24,9},{1,18},{9,26},{17,2},{25,10},{2,19},{1... | collective-permute-start | bytes 80 | tf_op jit(solution)/shard_map/ppermute | solution.py:218
  36.8 23.9 %collective-permute-start = (s32[2,3]{0,1:T(4,128)S(1)}, s32[2,3]{0,1:T(4,128)S(1)}, u32[]{:S(2)}, u32[]{:S(2)}) collective-permute-start(s32[2,3]{0,1:T(4,128)S(1)} %pad_add_fusion.8), channel_id=1, source_target_pairs={{0,8},{8,16},{16,24},{24,0},{1,9},{9,17},{17,25},{25,1},{2,10},{10... | collective-permute-start | bytes 80 | tf_op jit(solution)/shard_map/ppermute | solution.py:204
  41.2 23.3 %collective-permute-start.1 = (s32[2,3]{0,1:T(4,128)S(1)}, s32[2,3]{0,1:T(4,128)S(1)}, u32[]{:S(2)}, u32[]{:S(2)}) collective-permute-start(s32[2,3]{0,1:T(4,128)S(1)} %pad_add_fusion.8), channel_id=1, source_target_pairs={{0,16},{8,24},{16,0},{24,8},{1,17},{9,25},{17,1},{25,9},{2,18},{10... | collective-permute-start | bytes 80 | tf_op jit(solution)/shard_map/ppermute | solution.py:204
  46.1 18.5 %collective-permute-start.2 = (s32[2,3]{0,1:T(4,128)S(1)}, s32[2,3]{0,1:T(4,128)S(1)}, u32[]{:S(2)}, u32[]{:S(2)}) collective-permute-start(s32[2,3]{0,1:T(4,128)S(1)} %pad_add_fusion.8), channel_id=1, source_target_pairs={{0,24},{8,0},{16,8},{24,16},{1,25},{9,1},{17,9},{25,17},{2,26},{10... | collective-permute-start | bytes 80 | tf_op jit(solution)/shard_map/ppermute | solution.py:204
  53.3 21.5 %collective-permute-start.20 = (bf16[2,192,256]{2,1,0:T(8,128)(2,1)S(1)}, bf16[2,192,256]{2,1,0:T(8,128)(2,1)S(1)}, u32[]{:S(2)}, u32[]{:S(2)}) collective-permute-start(bf16[2,192,256]{2,1,0:T(8,128)(2,1)S(1)} %get-tuple-element.41), channel_id=1, source_target_pairs={{0,8},{8,16},{16,24},{24,0},{1,9},{9,17},{17,25},{25,1},{2,10},{10... | collective-permute-start | bytes 589832 | tf_op jit(solution)/shard_map/ppermute | solution.py:204
  56.7 20.9 %collective-permute-start.21 = (bf16[2,192,256]{2,1,0:T(8,128)(2,1)S(1)}, bf16[2,192,256]{2,1,0:T(8,128)(2,1)S(1)}, u32[]{:S(2)}, u32[]{:S(2)}) collective-permute-start(bf16[2,192,256]{2,1,0:T(8,128)(2,1)S(1)} %get-tuple-element.42), channel_id=1, source_target_pairs={{0,16},{8,24},{16,0},{24,8},{1,17},{9,25},{17,1},{25,9},{2,18},{10... | collective-permute-start | bytes 589832 | tf_op jit(solution)/shard_map/ppermute | solution.py:204
  60.7 19.4 %collective-permute-start.22 = (bf16[2,192,256]{2,1,0:T(8,128)(2,1)S(1)}, bf16[2,192,256]{2,1,0:T(8,128)(2,1)}, u32[]{:S(2)}, u32[]{:S(2)}) collective-permute-start(bf16[2,192,256]{2,1,0:T(8,128)(2,1)S(1)} %get-tuple-element.43), channel_id=1, source_target_pairs={{0,24},{8,0},{16,8},{24,16},{1,25},{9,1},{17,9},{25,17},{2,26},{10... | collective-permute-start | bytes 589832 | tf_op jit(solution)/shard_map/ppermute | solution.py:204
  69.0 15.8 %collective-permute-start.17 = (bf16[2,192,256]{2,1,0:T(8,128)(2,1)S(1)}, bf16[2,192,256]{2,1,0:T(8,128)(2,1)S(1)}, u32[]{:S(2)}, u32[]{:S(2)}) collective-permute-start(bf16[2,192,256]{2,1,0:T(8,128)(2,1)S(1)} %get-tuple-element.37), channel_id=1, source_target_pairs={{0,8},{8,16},{16,24},{24,0},{1,9},{9,17},{17,25},{25,1},{2,10},{10... | collective-permute-start | bytes 589832 | tf_op jit(solution)/shard_map/ppermute | solution.py:204
  71.1 17.2 %collective-permute-start.18 = (bf16[2,192,256]{2,1,0:T(8,128)(2,1)S(1)}, bf16[2,192,256]{2,1,0:T(8,128)(2,1)S(1)}, u32[]{:S(2)}, u32[]{:S(2)}) collective-permute-start(bf16[2,192,256]{2,1,0:T(8,128)(2,1)S(1)} %get-tuple-element.38), channel_id=1, source_target_pairs={{0,16},{8,24},{16,0},{24,8},{1,17},{9,25},{17,1},{25,9},{2,18},{10... | collective-permute-start | bytes 589832 | tf_op jit(solution)/shard_map/ppermute | solution.py:204
  77.6 16.3 %collective-permute-start.11 = (bf16[2,192,256]{2,1,0:T(8,128)(2,1)S(1)}, bf16[2,192,256]{2,1,0:T(8,128)(2,1)S(1)}, u32[]{:S(2)}, u32[]{:S(2)}) collective-permute-start(bf16[2,192,256]{2,1,0:T(8,128)(2,1)S(1)} %get-tuple-element.33), channel_id=1, source_target_pairs={{0,16},{8,24},{16,0},{24,8},{1,17},{9,25},{17,1},{25,9},{2,18},{10... | collective-permute-start | bytes 589832 | tf_op jit(solution)/shard_map/ppermute | solution.py:204
  84.9 24.1 %collective-permute-start.19 = (bf16[2,192,256]{2,1,0:T(8,128)(2,1)S(1)}, bf16[2,192,256]{2,1,0:T(8,128)(2,1)S(1)}, u32[]{:S(2)}, u32[]{:S(2)}) collective-permute-start(bf16[2,192,256]{2,1,0:T(8,128)(2,1)S(1)} %get-tuple-element.39), channel_id=1, source_target_pairs={{0,24},{8,0},{16,8},{24,16},{1,25},{9,1},{17,9},{25,17},{2,26},{10... | collective-permute-start | bytes 589832 | tf_op jit(solution)/shard_map/ppermute | solution.py:204
  88.3 41.4 %collective-permute-start.7 = (bf16[2,192,256]{2,1,0:T(8,128)(2,1)S(1)}, bf16[2,192,256]{2,1,0:T(8,128)(2,1)S(1)}, u32[]{:S(2)}, u32[]{:S(2)}) collective-permute-start(bf16[2,192,256]{2,1,0:T(8,128)(2,1)S(1)} %get-tuple-element.28), channel_id=1, source_target_pairs={{0,8},{8,16},{16,24},{24,0},{1,9},{9,17},{17,25},{25,1},{2,10},{10... | collective-permute-start | bytes 589832 | tf_op jit(solution)/shard_map/ppermute | solution.py:204
  90.2 47.4 %collective-permute-start.8 = (bf16[2,192,256]{2,1,0:T(8,128)(2,1)S(1)}, bf16[2,192,256]{2,1,0:T(8,128)(2,1)S(1)}, u32[]{:S(2)}, u32[]{:S(2)}) collective-permute-start(bf16[2,192,256]{2,1,0:T(8,128)(2,1)S(1)} %get-tuple-element.29), channel_id=1, source_target_pairs={{0,16},{8,24},{16,0},{24,8},{1,17},{9,25},{17,1},{25,9},{2,18},{10... | collective-permute-start | bytes 589832 | tf_op jit(solution)/shard_map/ppermute | solution.py:204
  93.9 45.6 %collective-permute-start.9 = (bf16[2,192,256]{2,1,0:T(8,128)(2,1)S(1)}, bf16[2,192,256]{2,1,0:T(8,128)(2,1)S(1)}, u32[]{:S(2)}, u32[]{:S(2)}) collective-permute-start(bf16[2,192,256]{2,1,0:T(8,128)(2,1)S(1)} %get-tuple-element.30), channel_id=1, source_target_pairs={{0,24},{8,0},{16,8},{24,16},{1,25},{9,1},{17,9},{25,17},{2,26},{10... | collective-permute-start | bytes 589832 | tf_op jit(solution)/shard_map/ppermute | solution.py:204
  95.9 16.1 %collective-permute-start.23 = (bf16[2,192,256]{2,1,0:T(8,128)(2,1)S(1)}, bf16[2,192,256]{2,1,0:T(8,128)(2,1)S(1)}, u32[]{:S(2)}, u32[]{:S(2)}) collective-permute-start(bf16[2,192,256]{2,1,0:T(8,128)(2,1)S(1)} %add_convert_fusion), channel_id=1, source_target_pairs={{1,0},{2,1},{3,2},{4,3},{5,4},{6,5},{7,6},{9,8},{10,9},{11,10},{12... | collective-permute-start | bytes 589832 | tf_op jit(solution)/shard_map/ppermute | solution.py:210
  108.9 34.3 %collective-permute-start.13 = (bf16[2,192,256]{2,1,0:T(8,128)(2,1)S(1)}, bf16[2,192,256]{2,1,0:T(8,128)(2,1)S(1)}, u32[]{:S(2)}, u32[]{:S(2)}) collective-permute-start(bf16[2,192,256]{2,1,0:T(8,128)(2,1)S(1)} %add_convert_fusion.1), channel_id=1, source_target_pairs={{1,0},{2,1},{3,2},{4,3},{5,4},{6,5},{7,6},{9,8},{10,9},{11,10},{12... | collective-permute-start | bytes 589832 | tf_op jit(solution)/shard_map/ppermute | solution.py:210
  112.7 40.6 %collective-permute-start.31 = (bf16[2,192,256]{2,1,0:T(8,128)(2,1)S(1)}, bf16[2,192,256]{2,1,0:T(8,128)(2,1)S(1)}, u32[]{:S(2)}, u32[]{:S(2)}) collective-permute-start(bf16[2,192,256]{2,1,0:T(8,128)(2,1)S(1)} %get-tuple-element.46), channel_id=1, source_target_pairs={{0,1},{1,2},{2,3},{3,4},{4,5},{5,6},{6,7},{8,9},{9,10},{10,11},{11... | collective-permute-start | bytes 589832 | tf_op jit(solution)/shard_map/ppermute | solution.py:210
  129.7 29.7 %collective-permute-start.24 = (bf16[2,192,256]{2,1,0:T(8,128)(2,1)S(1)}, bf16[2,192,256]{2,1,0:T(8,128)(2,1)S(1)}, u32[]{:S(2)}, u32[]{:S(2)}) collective-permute-start(bf16[2,192,256]{2,1,0:T(8,128)(2,1)S(1)} %get-tuple-element.44.refs_4_), channel_id=1, source_target_pairs={{0,8},{8,16},{16,24},{24,0},{1,9},{9,17},{17,25},{25,1},{2,10},{10... | collective-permute-start | bytes 589832 | tf_op jit(solution)/shard_map/ppermute | solution.py:204
  137.6 23.8 %collective-permute-start.25 = (bf16[2,192,256]{2,1,0:T(8,128)(2,1)S(1)}, bf16[2,192,256]{2,1,0:T(8,128)(2,1)S(1)}, u32[]{:S(2)}, u32[]{:S(2)}) collective-permute-start(bf16[2,192,256]{2,1,0:T(8,128)(2,1)S(1)} %get-tuple-element.44.refs_4_), channel_id=1, source_target_pairs={{0,16},{8,24},{16,0},{24,8},{1,17},{9,25},{17,1},{25,9},{2,18},{10... | collective-permute-start | bytes 589832 | tf_op jit(solution)/shard_map/ppermute | solution.py:204
  139.6 25.5 %collective-permute-start.26 = (bf16[2,192,256]{2,1,0:T(8,128)(2,1)S(1)}, bf16[2,192,256]{2,1,0:T(8,128)(2,1)S(1)}, u32[]{:S(2)}, u32[]{:S(2)}) collective-permute-start(bf16[2,192,256]{2,1,0:T(8,128)(2,1)S(1)} %get-tuple-element.44.refs_4_), channel_id=1, source_target_pairs={{0,24},{8,0},{16,8},{24,16},{1,25},{9,1},{17,9},{25,17},{2,26},{10... | collective-permute-start | bytes 589832 | tf_op jit(solution)/shard_map/ppermute | solution.py:204
  146.4 22.6 %collective-permute-start.27 = (bf16[2,192,256]{2,1,0:T(8,128)(2,1)S(1)}, bf16[2,192,256]{2,1,0:T(8,128)(2,1)S(1)}, u32[]{:S(2)}, u32[]{:S(2)}) collective-permute-start(bf16[2,192,256]{2,1,0:T(8,128)(2,1)S(1)} %get-tuple-element.45), channel_id=1, source_target_pairs={{0,1},{1,2},{2,3},{3,4},{4,5},{5,6},{6,7},{8,9},{9,10},{10,11},{11... | collective-permute-start | bytes 589832 | tf_op jit(solution)/shard_map/ppermute | solution.py:210
  153.3 21.2 %collective-permute-start.14 = (bf16[2,192,256]{2,1,0:T(8,128)(2,1)S(1)}, bf16[2,192,256]{2,1,0:T(8,128)(2,1)S(1)}, u32[]{:S(2)}, u32[]{:S(2)}) collective-permute-start(bf16[2,192,256]{2,1,0:T(8,128)(2,1)S(1)} %get-tuple-element.35.refs_0_), channel_id=1, source_target_pairs={{0,8},{8,16},{16,24},{24,0},{1,9},{9,17},{17,25},{25,1},{2,10},{10... | collective-permute-start | bytes 589832 | tf_op jit(solution)/shard_map/ppermute | solution.py:204
  159.5 17.6 %collective-permute-start.15 = (bf16[2,192,256]{2,1,0:T(8,128)(2,1)S(1)}, bf16[2,192,256]{2,1,0:T(8,128)(2,1)S(1)}, u32[]{:S(2)}, u32[]{:S(2)}) collective-permute-start(bf16[2,192,256]{2,1,0:T(8,128)(2,1)S(1)} %get-tuple-element.35.refs_0_), channel_id=1, source_target_pairs={{0,16},{8,24},{16,0},{24,8},{1,17},{9,25},{17,1},{25,9},{2,18},{10... | collective-permute-start | bytes 589832 | tf_op jit(solution)/shard_map/ppermute | solution.py:204
  161.4 19.7 %collective-permute-start.16 = (bf16[2,192,256]{2,1,0:T(8,128)(2,1)S(1)}, bf16[2,192,256]{2,1,0:T(8,128)(2,1)S(1)}, u32[]{:S(2)}, u32[]{:S(2)}) collective-permute-start(bf16[2,192,256]{2,1,0:T(8,128)(2,1)S(1)} %get-tuple-element.35.refs_0_), channel_id=1, source_target_pairs={{0,24},{8,0},{16,8},{24,16},{1,25},{9,1},{17,9},{25,17},{2,26},{10... | collective-permute-start | bytes 589832 | tf_op jit(solution)/shard_map/ppermute | solution.py:204
  165.1 19.8 %collective-permute-start.32 = (bf16[2,192,256]{2,1,0:T(8,128)(2,1)S(1)}, bf16[2,192,256]{2,1,0:T(8,128)(2,1)S(1)}, u32[]{:S(2)}, u32[]{:S(2)}) collective-permute-start(bf16[2,192,256]{2,1,0:T(8,128)(2,1)S(1)} %collective-permute-done.31.refs_12_), channel_id=1, source_target_pairs={{0,8},{8,16},{16,24},{24,0},{1,9},{9,17},{17,25},{25,1},{2,10},{10... | collective-permute-start | bytes 589832 | tf_op jit(solution)/shard_map/ppermute | solution.py:204
  169.0 21.1 %collective-permute-start.33 = (bf16[2,192,256]{2,1,0:T(8,128)(2,1)S(1)}, bf16[2,192,256]{2,1,0:T(8,128)(2,1)S(1)}, u32[]{:S(2)}, u32[]{:S(2)}) collective-permute-start(bf16[2,192,256]{2,1,0:T(8,128)(2,1)S(1)} %collective-permute-done.31.refs_12_), channel_id=1, source_target_pairs={{0,16},{8,24},{16,0},{24,8},{1,17},{9,25},{17,1},{25,9},{2,18},{10... | collective-permute-start | bytes 589832 | tf_op jit(solution)/shard_map/ppermute | solution.py:204
  210.4 24.3 %collective-permute-start.35 = (bf16[192,1536]{1,0:T(8,128)(2,1)}, bf16[192,1536]{1,0:T(8,128)(2,1)}, u32[]{:S(2)}, u32[]{:S(2)}) collective-permute-start(bf16[192,1536]{1,0:T(8,128)(2,1)} %get-tuple-element.48), channel_id=1, source_target_pairs={{0,32},{32,0},{64,96},{96,64},{128,160},{160,128},{192,224},{224,1... | collective-permute-start | bytes 1769480 | tf_op jit(solution)/shard_map/ppermute | solution.py:222
  235.9 16.0 %collective-permute-start.36 = (bf16[48,1536]{1,0:T(8,128)(2,1)S(1)}, bf16[48,1536]{1,0:T(8,128)(2,1)S(1)}, u32[]{:S(2)}, u32[]{:S(2)}) collective-permute-start(bf16[48,1536]{1,0:T(8,128)(2,1)S(1)} %get-tuple-element.49), channel_id=1, source_target_pairs={{0,64},{32,96},{64,0},{96,32},{128,192},{160,224},{192,128},{224,1... | collective-permute-start | bytes 442376 | tf_op jit(solution)/shard_map/ppermute | solution.py:222
  279.0 19.3 %collective-permute-start.41 = (bf16[48,1536]{1,0:T(8,128)(2,1)S(1)}, bf16[48,1536]{1,0:T(8,128)(2,1)S(1)}, u32[]{:S(2)}, u32[]{:S(2)}) collective-permute-start(bf16[48,1536]{1,0:T(8,128)(2,1)S(1)} %pad_maximum_fusion.refs_0_), channel_id=1, source_target_pairs={{0,64},{32,96},{64,0},{96,32},{128,192},{160,224},{192,128},{224,1... | collective-permute-start | bytes 442376 | tf_op jit(solution)/shard_map/ppermute | solution.py:222
  288.4 15.9 %collective-permute-start.43 = (bf16[48,1536]{1,0:T(8,128)(2,1)S(1)}, bf16[48,1536]{1,0:T(8,128)(2,1)S(1)}, u32[]{:S(2)}, u32[]{:S(2)}) collective-permute-start(bf16[48,1536]{1,0:T(8,128)(2,1)S(1)} %pad_maximum_fusion.refs_0_), channel_id=1, source_target_pairs={{0,192},{32,224},{64,128},{96,160},{128,64},{160,96},{192,0},{224,... | collective-permute-start | bytes 442376 | tf_op jit(solution)/shard_map/ppermute | solution.py:222
  (41 other events, 347.2 us)

commit v2 on v0

v2 whole, which is shorter than its diff:
```python
import functools

import jax
import jax.numpy as jnp
import ml_dtypes
import numpy as np
from jax import lax
from jax.experimental import pallas as pl
from jax.experimental.pallas import tpu as pltpu
from jax.sharding import PartitionSpec as P

angle_center = 600
shear_divisor = 64
step_size = 0.03
floor_square = 0.25

LANE = 128
HALO = 64


def dft_tables(plane_width):
    index_line = np.arange(plane_width, dtype=np.int32)
    product_mod = np.mod(index_line[:, None] * index_line[None, :], plane_width)
    phase_table = product_mod.astype(np.float32) * np.float32(2.0 * 3.141592653589793 / plane_width)
    scale_factor = np.float32(plane_width ** (-0.5))
    table_real = (np.cos(phase_table) * scale_factor).astype(ml_dtypes.bfloat16)
    table_imag = (-np.sin(phase_table) * scale_factor).astype(ml_dtypes.bfloat16)
    return table_real, table_imag


def dot(left, right):
    return jnp.dot(left, right, preferred_element_type=jnp.float32)


def one_hot(rows, columns, down):
    row = lax.broadcasted_iota(jnp.int32, (rows, columns), 0)
    column = lax.broadcasted_iota(jnp.int32, (rows, columns), 1)
    return (row - column == down).astype(jnp.float32).astype(jnp.bfloat16)


def call(body, out_shape, scratch, *args):
    def spec(x):
        if x.dtype == jnp.int32:
            return pl.BlockSpec(memory_space=pltpu.SMEM)
        return pl.BlockSpec(x.shape, functools.partial(lambda rank, i: (0,) * rank, len(x.shape)))

    return pl.pallas_call(
        body,
        grid=(1,),
        out_shape=out_shape,
        in_specs=[spec(x) for x in args],
        out_specs=[spec(x) for x in out_shape],
        scratch_shapes=scratch,
        compiler_params=pltpu.CompilerParams(vmem_limit_bytes=56 * 1024 * 1024),
    )(*args)


def column_blocks(left, width, columns):
    blocks = columns // LANE
    return [
        pl.multiple_of(lax.rem(left // LANE + i, blocks) * LANE, LANE) for i in range(width // LANE + 1)
    ]


def cut_body(slabs, slots, place_ref, first_ref, second_ref, *outs):
    rows, width = outs[0].shape[2:]
    tile_rows, columns = first_ref.shape
    first_part = place_ref[3 * slabs * slots]
    for slab in range(slabs):
        for slot in range(slots):
            top, left, live = (place_ref[3 * (slab * slots + slot) + i] for i in range(3))
            out = outs[slot]

            @pl.when(live > 0)
            def _():
                pick_rows = one_hot(rows, tile_rows, -top)
                pick_columns = one_hot(width + LANE, width, lax.rem(left, LANE))
                starts = column_blocks(left, width, columns)
                for turn, ref in enumerate((first_ref, second_ref)):
                    pieces = [ref[:, pl.ds(start, LANE)] for start in starts]
                    narrow = dot(jnp.concatenate(pieces, axis=1), pick_columns).astype(jnp.bfloat16)
                    out[slab, first_part ^ turn] = dot(pick_rows, narrow).astype(jnp.bfloat16)

            @pl.when(live == 0)
            def _():
                out[slab] = jnp.zeros(out.shape[1:], out.dtype)


def cut_windows(place, first_part, first, second, rows, width):
    slabs, slots = place.shape[:2]
    shape = jax.ShapeDtypeStruct((slabs, 2, rows, width), jnp.bfloat16)
    scalars = jnp.concatenate([place.reshape(-1), first_part.reshape(1)]).astype(jnp.int32)
    return call(
        functools.partial(cut_body, slabs, slots), [shape] * slots, [], scalars, first, second
    )


def patch_body(slots, live_ref, *refs):
    uppers, lowers = refs[:slots], refs[slots : 2 * slots]
    probe, patterns, wr_ref, wi_ref = refs[2 * slots : 2 * slots + 4]
    outs = refs[2 * slots + 4 :]
    rows = uppers[0].shape[2]
    f32, bf16 = jnp.float32, jnp.bfloat16

    def window(slot, part):
        def projected(ref):
            return sum(ref[slab, part].astype(f32) for slab in range(ref.shape[0])).astype(bf16).astype(f32)

        above, below = projected(uppers[slot]), projected(lowers[slot])
        return jnp.concatenate(
            [above[:HALO], above[HALO:] + below[: rows - HALO], below[rows - HALO :]], axis=0
        )

    for slot in range(slots):

        @pl.when(live_ref[slot] > 0)
        def _():
            phase, absorption = window(slot, 0), window(slot, 1)
            magnitude = jnp.exp(-absorption)
            trans_real = magnitude * jnp.cos(phase)
            trans_imag = magnitude * jnp.sin(phase)
            probe_real, probe_imag = probe[0], probe[1]
            wr, wi = wr_ref[...], wi_ref[...]
            wave_real = (probe_real * trans_real - probe_imag * trans_imag).astype(bf16)
            wave_imag = (probe_real * trans_imag + probe_imag * trans_real).astype(bf16)
            left_real = (dot(wr, wave_real) - dot(wi, wave_imag)).astype(bf16)
            left_imag = (dot(wr, wave_imag) + dot(wi, wave_real)).astype(bf16)
            far_real = dot(left_real, wr) - dot(left_imag, wi)
            far_imag = dot(left_real, wi) + dot(left_imag, wr)
            power = far_real * far_real + far_imag * far_imag + floor_square
            keeping = 1.0 - patterns[slot].astype(f32) * lax.rsqrt(power)
            resid_real = (far_real * keeping).astype(bf16)
            resid_imag = (far_imag * keeping).astype(bf16)
            back_real = (dot(wr, resid_real) + dot(wi, resid_imag)).astype(bf16)
            back_imag = (dot(wr, resid_imag) - dot(wi, resid_real)).astype(bf16)
            exit_real = dot(back_real, wr) + dot(back_imag, wi)
            exit_imag = dot(back_imag, wr) - dot(back_real, wi)
            mixed_real = probe_real * exit_real + probe_imag * exit_imag
            mixed_imag = probe_real * exit_imag - probe_imag * exit_real
            final_real = trans_real * mixed_real + trans_imag * mixed_imag
            final_imag = trans_real * mixed_imag - trans_imag * mixed_real
            for part, value in enumerate((final_imag, -final_real)):
                value = value.astype(bf16)
                for slab in range(outs[slot].shape[0]):
                    outs[slot][slab, part] = value

        @pl.when(live_ref[slot] == 0)
        def _():
            outs[slot][...] = jnp.zeros(outs[slot].shape, bf16)


def patch_gradients(live, uppers, lowers, probe_wave, patterns, tables):
    slots, width = patterns.shape[:2]
    shape = jax.ShapeDtypeStruct((uppers[0].shape[0], 2, width, width), jnp.bfloat16)
    return call(
        functools.partial(patch_body, slots),
        [shape] * slots,
        [],
        live,
        *uppers,
        *lowers,
        probe_wave,
        patterns,
        *tables,
    )


def place_body(slots, pieces, place_ref, *refs):
    windows, (keep_out, send_out, total) = refs[:slots], refs[slots:]
    slabs, _, width, _ = windows[0].shape
    tile_rows, columns = keep_out.shape[1:]
    total[...] = jnp.zeros_like(total)

    stored = lax.broadcasted_iota(jnp.int32, (2 * tile_rows, width), 0)
    size = tile_rows // pieces
    piece = sum((stored >= tile_rows + k * size).astype(jnp.int32) for k in range(1, pieces))
    true_row = jnp.where(stored < tile_rows, stored, stored + (pieces - 1 - 2 * piece) * size)
    patch_row = true_row - lax.broadcasted_iota(jnp.int32, (2 * tile_rows, width), 1)

    for slab in range(slabs):
        for slot in range(slots):
            top, left, live = (place_ref[3 * (slab * slots + slot) + i] for i in range(3))

            @pl.when(live > 0)
            def _():
                put_rows = (patch_row == top).astype(jnp.float32).astype(jnp.bfloat16)
                put_columns = one_hot(width, width + LANE, -lax.rem(left, LANE))
                starts = column_blocks(left, width, columns)
                for part in range(2):
                    moved = dot(put_rows, windows[slot][slab, part]).astype(jnp.bfloat16)
                    wide = dot(moved, put_columns)
                    for i, start in enumerate(starts):
                        total[part, :, pl.ds(start, LANE)] += wide[:, i * LANE : (i + 1) * LANE]

    core = place_ref[3 * slabs * slots]
    for which in range(2):
        rows = slice(which * tile_rows, (which + 1) * tile_rows)
        keep_out[which] = total[core, rows]
        send_out[which] = total[1 - core, rows].astype(jnp.bfloat16)


def place_windows(place, core, windows, pieces, tile_rows, columns):
    shape = (2, tile_rows, columns)
    scalars = jnp.concatenate([place.reshape(-1), core.reshape(1)]).astype(jnp.int32)
    return call(
        functools.partial(place_body, len(windows), pieces),
        [jax.ShapeDtypeStruct(shape, jnp.float32), jax.ShapeDtypeStruct(shape, jnp.bfloat16)],
        [pltpu.VMEM((2, 2 * tile_rows, columns), jnp.float32)],
        scalars,
        *windows,
    )


def step_body(core_ref, layer_ref, mine_ref, other_ref, out):
    core = core_ref[0]
    for turn, ref in enumerate((mine_ref, other_ref)):
        part = core ^ turn
        out[part] = layer_ref[part].astype(jnp.float32) - step_size * ref[...].astype(jnp.float32)


def step(core, layer, mine, other):
    shape = jax.ShapeDtypeStruct(layer.shape, jnp.float32)
    return call(step_body, [shape], [], core.reshape(1).astype(jnp.int32), layer, mine, other)[0]


def per_device(volume, probe_wave, amplitudes, offsets, column_starts, counts, angle_ids):
    layer = volume.reshape(volume.shape[0], *volume.shape[2:])
    tile_rows, columns = layer.shape[1:]
    width = amplitudes.shape[-1]
    slots = offsets.shape[3]
    angles, slabs, tiles = (lax.axis_size(axis) for axis in ("angle", "slab", "tile"))
    slab, angle = lax.axis_index("slab"), lax.axis_index("angle")
    f32, bf16 = jnp.float32, jnp.bfloat16
    tables = dft_tables(width)
    window_rows = width - HALO
    patterns = amplitudes.reshape(slots, width, width)

    fours = angles // 8
    core, far = angle % 2, angle // 8
    four_groups = [[8 * f + 2 * q + c for q in range(4)] for f in range(fours) for c in range(2)]
    pieces = 4 * fours
    piece_rows = tile_rows // pieces

    def swap(value, by):
        return lax.ppermute(value, "angle", [(i, i ^ by) for i in range(angles)])

    def mirrored(value, by):
        pairs = [
            (a * tiles + t, (angles - 2 - (a - a % 2) + a % 2) * tiles + t + by)
            for a in range(angles)
            for t in range(tiles)
            if 0 <= t + by < tiles
        ]
        return lax.ppermute(value, ("angle", "tile"), pairs)

    def to_slabs(value):
        return lax.all_to_all(value, "slab", 0, 0, tiled=True)

    def to_four(value):
        return lax.all_to_all(value, "angle", 0, 0, axis_index_groups=four_groups, tiled=True)

    def spread(piece):
        other = swap(piece, 8)
        pair = jnp.concatenate([jnp.where(far == 0, piece, other), jnp.where(far == 0, other, piece)])
        return to_four(jnp.broadcast_to(pair, (4, *pair.shape))).reshape(tile_rows, columns)

    def summed(blocks):
        total = jnp.sum(to_four(blocks).astype(f32), axis=0).reshape(fours, piece_rows, columns)
        here = lax.dynamic_index_in_dim(total, far, 0, keepdims=False)
        there = lax.dynamic_index_in_dim(total, 1 - far, 0, keepdims=False).astype(bf16)
        return here + swap(there, 8).astype(f32)

    place_z = angles // 2 - 1 - angle // 2
    first_row = (place_z % 4) * (piece_rows * fours) + place_z // 4 * piece_rows
    own_part = lax.dynamic_index_in_dim(layer, core, 0, keepdims=False)
    after = mirrored(lax.dynamic_slice(own_part, (first_row, 0), (piece_rows, columns)), -1)

    live = (jnp.arange(slots) < counts.reshape(1)).astype(jnp.int32)
    meta = jnp.stack([offsets.reshape(slots), column_starts.reshape(slots), live], axis=1)
    group = to_slabs(jnp.broadcast_to(meta, (slabs, *meta.shape)))
    more = jnp.max(group[:, 1:, 2]) > 0
    sheared = jnp.floor_divide((angle_ids[0] - angle_center) * (slab - slabs // 2), shear_divisor)
    lefts = jnp.mod(group[..., 1] + jnp.mod(sheared, columns), columns)

    def place(down):
        return jnp.stack([group[..., 0] + down, lefts, group[..., 2]], axis=-1)

    def exchanged(first, *others):
        return lax.cond(
            more,
            lambda values: tuple(to_slabs(v) for v in values),
            lambda values: (to_slabs(values[0]), *values[1:]),
            (first, *others),
        )

    zero = jnp.zeros((), jnp.int32)
    uppers = cut_windows(place(0), zero, layer[0], layer[1], window_rows, width)
    uppers = [to_slabs(u) for u in uppers]
    after = spread(after)
    lowers = cut_windows(
        place(HALO - tile_rows), core, after, swap(after, 1), window_rows, width
    )
    lowers = exchanged(*lowers)

    gradients = patch_gradients(live, uppers, lowers, probe_wave, patterns, tables)
    gradients = exchanged(*gradients)
    kept, sent = place_windows(place(0), core, gradients, pieces, tile_rows, columns)

    kept = (kept + swap(sent, 1).astype(f32)).astype(bf16).reshape(2, 4, tile_rows // 4, columns)
    spilled = mirrored(summed(kept[1]).astype(bf16), 1)
    total = (summed(kept[0]) + spilled.astype(f32)).astype(bf16)

    total = spread(total)
    return step(core, layer, total, swap(total, 1)).reshape(volume.shape)


def solution(mesh):
    in_specs = (
        P(None, "slab", "tile", None),
        P(),
        P("angle", "tile", "slab", None, None, None),
        P("angle", "tile", "slab", None),
        P("angle", "tile", "slab", None),
        P("angle", "tile", "slab"),
        P("angle"),
    )
    out_specs = P(None, "slab", "tile", None)
    return jax.shard_map(
        per_device, mesh=mesh, in_specs=in_specs, out_specs=out_specs, check_vma=False
    )
```

time: 614 us -> 272 us (0.44)
  waiting for transfers between devices: 488 us -> 82.8 us
  blocking collectives: 0 us -> 75.6 us
  Pallas kernels: 0 us -> 23.1 us
  matrix products: 19.3 us -> 0 us
  starting transfers between devices: 56.6 us -> 74.8 us
  other arithmetic: 17 us -> 5.12 us
  between operations: 13.9 us -> 2.29 us
    psum x3 -> x0, waiting for transfers between devices: 439 us -> none  [the longest x1 203 us: per_device(): lax.psum(layer_gradient.astype(jnp.bfloat16), 'angle').astype(jnp.float32)]
    all_to_all x0 -> x5, blocking collectives: none -> 75.6 us  [the longest x3 43.7 us: to_slabs(): return lax.all_to_all(value, 'slab', 0, 0, tiled=True)]
    all_to_all x0 -> x4, waiting for transfers between devices: none -> 36.1 us  [the longest x2 27.7 us: to_four(): lax.all_to_all(value, 'angle', 0, 0, axis_index_groups=four_groups, tiled...]
    pallas_call x0 -> x5, Pallas kernels: none -> 23.1 us  [call(): pl.pallas_call(body, grid=(1,), out_shape=out_shape, in_specs=[spec(x) fo...]
    dot_general x16 -> x0, matrix products: 19.3 us -> none  [twodot(): jnp.dot(left_matrix, right_matrix, preferred_element_type=jnp.float32)]
    all_to_all x0 -> x4, starting transfers between devices: none -> 14.5 us  [the longest x2 7.51 us: to_slabs(): return lax.all_to_all(value, 'slab', 0, 0, tiled=True)]
    dynamic_update_slice x1 -> x0, local copies, waits for them, and re-layouts: 6.29 us -> none  [slot_update(): return lax.dynamic_update_slice(buffer, previous + gradient, corner)]
    ppermute x2 -> x9, starting transfers between devices: 56.5 us -> 60.3 us  [the longest x7 57.7 us: swap(): return lax.ppermute(value, 'angle', [(i, i ^ by) for i in range(angles)])]
  transfers between devices with their start and end apart: 5 -> 13, of which waited for: 5 -> 10; matrix products, arithmetic and copies ran while one was open for 0% -> 2% of each run, Pallas kernels for 0% -> 2%
where the time goes in v2:
time: 272 us; the launch traced here: 271 us
  waiting for transfers between devices  82.8 us (30%)
  blocking collectives  75.6 us (28%)
  starting transfers between devices  74.8 us (28%)
  Pallas kernels  23.1 us (8%)
  local copies, waits for them, and re-layouts  7.28 us (3%)
  other arithmetic  5.12 us (2%)
    ppermute x7, starting transfers between devices, swap(): return lax.ppermute(value, 'angle', [(i, i ^ by) for i in range(angles)])  57.7 us
    all_to_all x3, blocking collectives, to_slabs(): return lax.all_to_all(value, 'slab', 0, 0, tiled=True)  43.7 us
    all_to_all x2, blocking collectives, to_four(): lax.all_to_all(value, 'angle', 0, 0, axis_index_groups=four_groups, tiled...  31.9 us
    ppermute x7, waiting for transfers between devices, swap(): return lax.ppermute(value, 'angle', [(i, i ^ by) for i in range(angles)])  29 us
    all_to_all x2, waiting for transfers between devices, to_four(): lax.all_to_all(value, 'angle', 0, 0, axis_index_groups=four_groups, tiled...  27.7 us
    pallas_call x5, Pallas kernels, call(): pl.pallas_call(body, grid=(1,), out_shape=out_shape, in_specs=[spec(x) fo...  23.1 us
    ppermute x2, waiting for transfers between devices, mirrored(): return lax.ppermute(value, ('angle', 'tile'), pairs)  17.7 us
    all_to_all x2, waiting for transfers between devices, to_slabs(): return lax.all_to_all(value, 'slab', 0, 0, tiled=True)  8.35 us
  transfers between devices with their start and end apart: 13, of which 10 were waited for; matrix products, arithmetic and copies ran while one was open for 2% of the time, Pallas kernels for 2%

profile of v2, /device:TPU:1, one launch (start us, length us, event | category | flops | bytes accessed | tf_op | source)
XLA Modules:
  0.0 271.0 jit_solution(8854859551042865339)
XLA Ops:
  2.2 17.7 %collective-permute-done = bf16[24,1536]{1,0:T(8,128)(2,1)S(1)} collective-permute-done((bf16[24,1536]{1,0:T(8,128)(2,1)S(1)}, bf16[24,1536]{1,0:T(8,128)(2,1)S(1)}, u32[]{:S(2)}, u32[]{:S(2)}) %collective-permute-start) | collective-permute-done | bytes 73760 | tf_op jit(solution)/shard_map/ppermute | solution.py:254
  19.9 2.9 %collective-permute-start.1 = (bf16[24,1536]{1,0:T(8,128)(2,1)S(1)}, bf16[24,1536]{1,0:T(8,128)(2,1)S(1)}, u32[]{:S(2)}, u32[]{:S(2)}) collective-permute-start(bf16[24,1536]{1,0:T(8,128)(2,1)S(1)} %collective-permute-done), channel_id=1, source_target_pairs={{0,256},{32,288},{64,320},{96,352},{128,384},{160,416},{192,448},{... | collective-permute-start | bytes 221192 | tf_op jit(solution)/shard_map/ppermute | solution.py:245
  22.8 11.0 %collective-permute-done.1 = bf16[24,1536]{1,0:T(8,128)(2,1)S(1)} collective-permute-done((bf16[24,1536]{1,0:T(8,128)(2,1)S(1)}, bf16[24,1536]{1,0:T(8,128)(2,1)S(1)}, u32[]{:S(2)}, u32[]{:S(2)}) %collective-permute-start.1) | collective-permute-done | bytes 73760 | tf_op jit(solution)/shard_map/ppermute | solution.py:245
  34.8 3.5 %all-to-all-start.9 = ((bf16[4,48,1536]{2,1,0:T(8,128)(2,1)}), bf16[4,48,1536]{2,1,0:T(8,128)(2,1)S(1)}, u32[]{:S(2)}, u32[]{:S(2)}) async-start(bf16[4,48,1536]{2,1,0:T(8,128)(2,1)} %broadcast_in_dim.10), calls=%async_computation.9 | async-start | bytes 1179648 | tf_op jit(solution)/shard_map/all_to_all | solution.py:260
  40.8 12.9 %all-to-all-done.9 = bf16[4,48,1536]{2,1,0:T(8,128)(2,1)S(1)} async-done(((bf16[4,48,1536]{2,1,0:T(8,128)(2,1)}), bf16[4,48,1536]{2,1,0:T(8,128)(2,1)S(1)}, u32[]{:S(2)}, u32[]{:S(2)}) %all-to-all-start.9) | async-done | bytes 589856 | tf_op jit(solution)/shard_map/all_to_all | solution.py:260
  54.4 4.0 %all-to-all-start.6 = ((s32[4,2,3]{2,1,0:T(2,128)}), s32[4,2,3]{2,1,0:T(2,128)S(1)}, u32[]{:S(2)}, u32[]{:S(2)}) async-start(s32[4,2,3]{2,1,0:T(2,128)} %broadcast_in_dim.9), calls=%async_computation.6 | async-start | bytes 8192 | tf_op jit(solution)/shard_map/all_to_all | solution.py:257
  58.4 3.5 %collective-permute-start.2 = (bf16[192,1536]{1,0:T(8,128)(2,1)S(1)}, bf16[192,1536]{1,0:T(8,128)(2,1)S(1)}, u32[]{:S(2)}, u32[]{:S(2)}) collective-permute-start(bf16[192,1536]{1,0:T(8,128)(2,1)S(1)} %bitcast.41), channel_id=1, source_target_pairs={{0,32},{32,0},{64,96},{96,64},{128,160},{160,128},{192,224},{224,1... | collective-permute-start | bytes 1769480 | tf_op jit(solution)/shard_map/ppermute | solution.py:245
  64.9 5.3 %shard_map.91 = (bf16[4,2,192,256]{3,2,1,0:T(8,128)(2,1)}, bf16[4,2,192,256]{3,2,1,0:T(8,128)(2,1)}) custom-call(s32[25]{0:T(128)} %get-tuple-element.59.place_ref, bf16[192,1536]{1,0:T(8,128)(2,1)} %get-tuple-element.48.first_ref, bf16[192,1536]{1,0:T(8,128)(2,1)} %get-tuple-element.47.second_ref), custom_call_target="tpu_custom_call" | custom-call | tf_op jit(solution)/shard_map/pallas_call | solution.py:47
  71.7 4.1 %shard_map.92 = (bf16[4,2,192,256]{3,2,1,0:T(8,128)(2,1)S(1)}, bf16[4,2,192,256]{3,2,1,0:T(8,128)(2,1)S(1)}) custom-call(s32[25]{0:T(128)} %pad_add_fusion.2.place_ref, bf16[192,1536]{1,0:T(8,128)(2,1)} %bitcast.42, bf16[192,1536]{1,0:T(8,128)(2,1)} %copy-done.5), custom_call_target="tpu_custom_call" | custom-call | tf_op jit(solution)/shard_map/pallas_call | solution.py:47
  75.8 12.9 %conditional.2 = (bf16[4,2,192,256]{3,2,1,0:T(8,128)(2,1)S(1)}, bf16[4,2,192,256]{3,2,1,0:T(8,128)(2,1)S(1)}) conditional(s32[]{:T(128)} %convert_element_type.49, (bf16[4,2,192,256]{3,2,1,0:T(8,128)(2,1)S(1)}, bf16[4,2,192,256]{3,2,1,0:T(8,128)(2,1)S(1)}) %shard_map.92, (bf16[4,2,192,256]{3,2,1,0:T(8,128)(2,1)S(1)}, ...), branch_computations={%region_1.2_spmd, %region_2.3_spmd} | conditional | bytes 4718608 | solution.py:289
  75.8 12.9 %all_to_all.59 = bf16[4,2,192,256]{3,2,1,0:T(8,128)(2,1)S(1)} all-to-all(bf16[4,2,192,256]{3,2,1,0:T(8,128)(2,1)S(1)} %get-tuple-element.21), channel_id=1, replica_groups=mesh['angle'=16,'slab'=4,'tile'=8] {'slab'}, dimensions={0} | all-to-all | bytes 1572864 | tf_op jit(solution)/shard_map/cond/branch_0_fun/all_to_all | solution.py:257
  88.8 14.2 %all_to_all.63.refs_0_ = bf16[4,2,192,256]{3,2,1,0:T(8,128)(2,1)} all-to-all(bf16[4,2,192,256]{3,2,1,0:T(8,128)(2,1)} %get-tuple-element.37), channel_id=1, replica_groups=mesh['angle'=16,'slab'=4,'tile'=8] {'slab'}, dimensions={0} | all-to-all | bytes 1572864 | tf_op jit(solution)/shard_map/all_to_all | solution.py:257
  102.9 3.5 %all-to-all-start.8 = ((bf16[4,2,192,256]{3,2,1,0:T(8,128)(2,1)}), bf16[4,2,192,256]{3,2,1,0:T(8,128)(2,1)S(1)}, u32[]{:S(2)}, u32[]{:S(2)}) async-start(bf16[4,2,192,256]{3,2,1,0:T(8,128)(2,1)} %get-tuple-element.38), calls=%async_computation.8 | async-start | bytes 1572864 | tf_op jit(solution)/shard_map/all_to_all | solution.py:257
  107.0 7.7 %all-to-all-done.8.refs_1_ = bf16[4,2,192,256]{3,2,1,0:T(8,128)(2,1)S(1)} async-done(((bf16[4,2,192,256]{3,2,1,0:T(8,128)(2,1)}), bf16[4,2,192,256]{3,2,1,0:T(8,128)(2,1)S(1)}, u32[]{:S(2)}, u32[]{:S(2)}) %all-to-all-start.8) | async-done | bytes 786464 | tf_op jit(solution)/shard_map/all_to_all | solution.py:257
  115.6 4.4 %shard_map.93 = (bf16[4,2,256,256]{3,2,1,0:T(8,128)(2,1)S(1)}, bf16[4,2,256,256]{3,2,1,0:T(8,128)(2,1)S(1)}) custom-call(s32[2]{0:T(128)} %compare_convert_fusion.live_ref, bf16[4,2,192,256]{3,2,1,0:T(8,128)(2,1)} %all_to_all.63.refs_0_, bf16[4,2,192,256]{3,2,1,0:T(8,128)(2,1)} %copy-done.1, bf16[4,2,192,256]{3,2,1,0:T(8,128)(2,1)S(1)} %get-tuple-element.39.refs_2_, ...), custom_call_target="tpu_custom_call" | custom-call | tf_op jit(solution)/shard_map/pallas_call | solution.py:47
  120.0 16.7 %conditional.3 = (bf16[4,2,256,256]{3,2,1,0:T(8,128)(2,1)S(1)}, bf16[4,2,256,256]{3,2,1,0:T(8,128)(2,1)S(1)}) conditional(s32[]{:T(128)} %convert_element_type.49, (bf16[4,2,256,256]{3,2,1,0:T(8,128)(2,1)S(1)}, bf16[4,2,256,256]{3,2,1,0:T(8,128)(2,1)S(1)}) %shard_map.93, (bf16[4,2,256,256]{3,2,1,0:T(8,128)(2,1)S(1)}, ...), branch_computations={%region_3.4_spmd, %region_4.5_spmd} | conditional | bytes 6291472 | solution.py:289
  120.0 16.6 %all_to_all.61 = bf16[4,2,256,256]{3,2,1,0:T(8,128)(2,1)S(1)} all-to-all(bf16[4,2,256,256]{3,2,1,0:T(8,128)(2,1)S(1)} %get-tuple-element.25), channel_id=1, replica_groups=mesh['angle'=16,'slab'=4,'tile'=8] {'slab'}, dimensions={0} | all-to-all | bytes 2097152 | tf_op jit(solution)/shard_map/cond/branch_0_fun/all_to_all | solution.py:257
  136.7 6.0 %shard_map.94 = (f32[2,192,1536]{2,1,0:T(8,128)}, bf16[2,192,1536]{2,1,0:T(8,128)(2,1)}) custom-call(s32[25]{0:T(128)} %get-tuple-element.60.place_ref, bf16[4,2,256,256]{3,2,1,0:T(8,128)(2,1)S(1)} %get-tuple-element.41.refs_0_, bf16[4,2,256,256]{3,2,1,0:T(8,128)(2,1)S(1)} %get-tuple-element.42.refs_1_), custom_call_target="tpu_custom_call" | custom-call | tf_op jit(solution)/shard_map/pallas_call | solution.py:47
  142.7 37.4 %collective-permute-start.3 = (bf16[2,192,1536]{2,1,0:T(8,128)(2,1)}, bf16[2,192,1536]{2,1,0:T(8,128)(2,1)S(1)}, u32[]{:S(2)}, u32[]{:S(2)}) collective-permute-start(bf16[2,192,1536]{2,1,0:T(8,128)(2,1)} %get-tuple-element.44), channel_id=1, source_target_pairs={{0,32},{32,0},{64,96},{96,64},{128,160},{160,128},{192,224},{224,1... | collective-permute-start | bytes 3538952 | tf_op jit(solution)/shard_map/ppermute | solution.py:245
  180.1 2.7 collective-permute-done.3
  182.8 2.0 add_convert_fusion
  185.7 17.7 %all_to_all.64 = bf16[4,48,1536]{2,1,0:T(8,128)(2,1)S(1)} all-to-all(bf16[4,48,1536]{2,1,0:T(8,128)(2,1)S(1)} %bitcast.43), channel_id=1, replica_groups={{0,64,128,192},{32,96,160,224},{256,320,384,448},{288,352,416,480},{1,6..., dimensions={0} | all-to-all | bytes 1179648 | tf_op jit(solution)/shard_map/all_to_all | solution.py:260
  203.4 3.5 %all-to-all-start.10 = ((bf16[4,48,1536]{2,1,0:T(8,128)(2,1)}), bf16[4,48,1536]{2,1,0:T(8,128)(2,1)S(1)}, u32[]{:S(2)}, u32[]{:S(2)}) async-start(bf16[4,48,1536]{2,1,0:T(8,128)(2,1)} %bitcast.11), calls=%async_computation.10 | async-start | bytes 1179648 | tf_op jit(solution)/shard_map/all_to_all | solution.py:260
  207.0 1.9 collective-permute-start.5
  209.0 14.8 %all-to-all-done.10 = bf16[4,48,1536]{2,1,0:T(8,128)(2,1)S(1)} async-done(((bf16[4,48,1536]{2,1,0:T(8,128)(2,1)}), bf16[4,48,1536]{2,1,0:T(8,128)(2,1)S(1)}, u32[]{:S(2)}, u32[]{:S(2)}) %all-to-all-start.10) | async-done | bytes 589856 | tf_op jit(solution)/shard_map/all_to_all | solution.py:260
  223.9 1.9 collective-permute-start.4
  227.2 7.1 %collective-permute-done.4 = bf16[24,1536]{1,0:T(8,128)(2,1)S(1)} collective-permute-done((bf16[24,1536]{1,0:T(8,128)(2,1)S(1)}, bf16[24,1536]{1,0:T(8,128)(2,1)S(1)}, u32[]{:S(2)}, u32[]{:S(2)}) %collective-permute-start.4) | collective-permute-done | bytes 73760 | tf_op jit(solution)/shard_map/ppermute | solution.py:245
  234.3 3.1 %collective-permute-start.7 = (bf16[24,1536]{1,0:T(8,128)(2,1)S(1)}, bf16[24,1536]{1,0:T(8,128)(2,1)S(1)}, u32[]{:S(2)}, u32[]{:S(2)}) collective-permute-start(bf16[24,1536]{1,0:T(8,128)(2,1)S(1)} %fusion.2), channel_id=1, source_target_pairs={{0,256},{32,288},{64,320},{96,352},{128,384},{160,416},{192,448},{... | collective-permute-start | bytes 221192 | tf_op jit(solution)/shard_map/ppermute | solution.py:245
  237.4 6.6 %collective-permute-done.7 = bf16[24,1536]{1,0:T(8,128)(2,1)S(1)} collective-permute-done((bf16[24,1536]{1,0:T(8,128)(2,1)S(1)}, bf16[24,1536]{1,0:T(8,128)(2,1)S(1)}, u32[]{:S(2)}, u32[]{:S(2)}) %collective-permute-start.7) | collective-permute-done | bytes 73760 | tf_op jit(solution)/shard_map/ppermute | solution.py:245
  244.2 14.2 %all_to_all.65 = bf16[4,48,1536]{2,1,0:T(8,128)(2,1)S(1)} all-to-all(bf16[4,48,1536]{2,1,0:T(8,128)(2,1)S(1)} %broadcast_in_dim.11), channel_id=1, replica_groups={{0,64,128,192},{32,96,160,224},{256,320,384,448},{288,352,416,480},{1,6..., dimensions={0} | all-to-all | bytes 1179648 | tf_op jit(solution)/shard_map/all_to_all | solution.py:260
  258.3 6.9 %collective-permute-start.8 = (bf16[192,1536]{1,0:T(8,128)(2,1)S(1)}, bf16[192,1536]{1,0:T(8,128)(2,1)S(1)}, u32[]{:S(2)}, u32[]{:S(2)}) collective-permute-start(bf16[192,1536]{1,0:T(8,128)(2,1)S(1)} %bitcast.39), channel_id=1, source_target_pairs={{0,32},{32,0},{64,96},{96,64},{128,160},{160,128},{192,224},{224,1... | collective-permute-start | bytes 1769480 | tf_op jit(solution)/shard_map/ppermute | solution.py:245
  267.7 3.3 %shard_map.95 = f32[2,192,1536]{2,1,0:T(8,128)} custom-call(s32[1]{0:T(128)} %bitcast.core_ref, bf16[2,192,1536]{2,1,0:T(8,128)(2,1)} %bitcast.38, bf16[192,1536]{1,0:T(8,128)(2,1)} %bitcast.40, bf16[192,1536]{1,0:T(8,128)(2,1)} %copy-done.4), custom_call_target="tpu_custom_call" | custom-call | tf_op jit(solution)/shard_map/pallas_call | solution.py:47
  (50 shorter events, 15.2 us)
Async XLA Ops:
  0.9 19.0 %collective-permute-start = (bf16[24,1536]{1,0:T(8,128)(2,1)S(1)}, bf16[24,1536]{1,0:T(8,128)(2,1)S(1)}, u32[]{:S(2)}, u32[]{:S(2)}) collective-permute-start(bf16[24,1536]{1,0:T(8,128)(2,1)S(1)} %dynamic-slice_bitcast_fusion), channel_id=1, source_target_pairs={{1,448},{2,449},{3,450},{4,451},{5,452},{6,453},{7,454},{33,480},{... | collective-permute-start | bytes 221192 | tf_op jit(solution)/shard_map/ppermute | solution.py:254
  19.9 13.9 %collective-permute-start.1 = (bf16[24,1536]{1,0:T(8,128)(2,1)S(1)}, bf16[24,1536]{1,0:T(8,128)(2,1)S(1)}, u32[]{:S(2)}, u32[]{:S(2)}) collective-permute-start(bf16[24,1536]{1,0:T(8,128)(2,1)S(1)} %collective-permute-done), channel_id=1, source_target_pairs={{0,256},{32,288},{64,320},{96,352},{128,384},{160,416},{192,448},{... | collective-permute-start | bytes 221192 | tf_op jit(solution)/shard_map/ppermute | solution.py:245
  33.8 5.8 %copy-start.6 = (s32[1,1,1,2]{3,2,1,0:T(1,128)S(1)}, s32[1,1,1,2]{3,2,1,0:T(1,128)}, u32[]{:S(2)}) copy-start(s32[1,1,1,2]{3,2,1,0:T(1,128)} %param.17) | copy-start | bytes 28
  33.9 5.7 %copy-start.7 = (s32[1,1,1,2]{3,2,1,0:T(1,128)S(1)}, s32[1,1,1,2]{3,2,1,0:T(1,128)}, u32[]{:S(2)}) copy-start(s32[1,1,1,2]{3,2,1,0:T(1,128)} %param.16) | copy-start | bytes 28
  33.9 5.9 %copy-start = (bf16[2,1,192,1536]{3,2,1,0:T(8,128)(2,1)S(1)}, bf16[2,1,192,1536]{3,2,1,0:T(8,128)(2,1)}, u32[]{:S(2)}) copy-start(bf16[2,1,192,1536]{3,2,1,0:T(8,128)(2,1)} %param.13) | copy-start | bytes 3538948
  34.8 19.0 %all-to-all-start.9 = ((bf16[4,48,1536]{2,1,0:T(8,128)(2,1)}), bf16[4,48,1536]{2,1,0:T(8,128)(2,1)S(1)}, u32[]{:S(2)}, u32[]{:S(2)}) async-start(bf16[4,48,1536]{2,1,0:T(8,128)(2,1)} %broadcast_in_dim.10), calls=%async_computation.9 | async-start | bytes 1179648 | tf_op jit(solution)/shard_map/all_to_all | solution.py:260
  53.7 17.1 %copy-start.3 = (bf16[4,48,1536]{2,1,0:T(8,128)(2,1)}, bf16[4,48,1536]{2,1,0:T(8,128)(2,1)S(1)}, u32[]{:S(2)}) copy-start(bf16[4,48,1536]{2,1,0:T(8,128)(2,1)S(1)} %all-to-all-done.9) | copy-start | bytes 1769476
  54.4 8.2 %all-to-all-start.6 = ((s32[4,2,3]{2,1,0:T(2,128)}), s32[4,2,3]{2,1,0:T(2,128)S(1)}, u32[]{:S(2)}, u32[]{:S(2)}) async-start(s32[4,2,3]{2,1,0:T(2,128)} %broadcast_in_dim.9), calls=%async_computation.6 | async-start | bytes 8192 | tf_op jit(solution)/shard_map/all_to_all | solution.py:257
  58.4 12.5 %collective-permute-start.2 = (bf16[192,1536]{1,0:T(8,128)(2,1)S(1)}, bf16[192,1536]{1,0:T(8,128)(2,1)S(1)}, u32[]{:S(2)}, u32[]{:S(2)}) collective-permute-start(bf16[192,1536]{1,0:T(8,128)(2,1)S(1)} %bitcast.41), channel_id=1, source_target_pairs={{0,32},{32,0},{64,96},{96,64},{128,160},{160,128},{192,224},{224,1... | collective-permute-start | bytes 1769480 | tf_op jit(solution)/shard_map/ppermute | solution.py:245
  70.8 0.8 copy-start.5
  102.9 11.8 %all-to-all-start.8 = ((bf16[4,2,192,256]{3,2,1,0:T(8,128)(2,1)}), bf16[4,2,192,256]{3,2,1,0:T(8,128)(2,1)S(1)}, u32[]{:S(2)}, u32[]{:S(2)}) async-start(bf16[4,2,192,256]{3,2,1,0:T(8,128)(2,1)} %get-tuple-element.38), calls=%async_computation.8 | async-start | bytes 1572864 | tf_op jit(solution)/shard_map/all_to_all | solution.py:257
  114.7 0.9 copy-start.1
  142.7 40.1 %collective-permute-start.3 = (bf16[2,192,1536]{2,1,0:T(8,128)(2,1)}, bf16[2,192,1536]{2,1,0:T(8,128)(2,1)S(1)}, u32[]{:S(2)}, u32[]{:S(2)}) collective-permute-start(bf16[2,192,1536]{2,1,0:T(8,128)(2,1)} %get-tuple-element.44), channel_id=1, source_target_pairs={{0,32},{32,0},{64,96},{96,64},{128,160},{160,128},{192,224},{224,1... | collective-permute-start | bytes 3538952 | tf_op jit(solution)/shard_map/ppermute | solution.py:245
  203.4 20.4 %all-to-all-start.10 = ((bf16[4,48,1536]{2,1,0:T(8,128)(2,1)}), bf16[4,48,1536]{2,1,0:T(8,128)(2,1)S(1)}, u32[]{:S(2)}, u32[]{:S(2)}) async-start(bf16[4,48,1536]{2,1,0:T(8,128)(2,1)} %bitcast.11), calls=%async_computation.10 | async-start | bytes 1179648 | tf_op jit(solution)/shard_map/all_to_all | solution.py:260
  207.0 18.8 %collective-permute-start.5 = (bf16[24,1536]{1,0:T(8,128)(2,1)S(1)}, bf16[24,1536]{1,0:T(8,128)(2,1)S(1)}, u32[]{:S(2)}, u32[]{:S(2)}) collective-permute-start(bf16[24,1536]{1,0:T(8,128)(2,1)S(1)} %fusion.4), channel_id=1, source_target_pairs={{0,256},{32,288},{64,320},{96,352},{128,384},{160,416},{192,448},{... | collective-permute-start | bytes 221192 | tf_op jit(solution)/shard_map/ppermute | solution.py:245
  223.9 10.4 %collective-permute-start.4 = (bf16[24,1536]{1,0:T(8,128)(2,1)S(1)}, bf16[24,1536]{1,0:T(8,128)(2,1)S(1)}, u32[]{:S(2)}, u32[]{:S(2)}) collective-permute-start(bf16[24,1536]{1,0:T(8,128)(2,1)S(1)} %fusion.3), channel_id=1, source_target_pairs={{0,256},{32,288},{64,320},{96,352},{128,384},{160,416},{192,448},{... | collective-permute-start | bytes 221192 | tf_op jit(solution)/shard_map/ppermute | solution.py:245
  225.9 8.4 %collective-permute-start.6 = (bf16[24,1536]{1,0:T(8,128)(2,1)S(1)}, bf16[24,1536]{1,0:T(8,128)(2,1)S(1)}, u32[]{:S(2)}, u32[]{:S(2)}) collective-permute-start(bf16[24,1536]{1,0:T(8,128)(2,1)S(1)} %fusion), channel_id=1, source_target_pairs={{0,449},{1,450},{2,451},{3,452},{4,453},{5,454},{6,455},{32,481},{... | collective-permute-start | bytes 221192 | tf_op jit(solution)/shard_map/ppermute | solution.py:254
  234.3 9.7 %collective-permute-start.7 = (bf16[24,1536]{1,0:T(8,128)(2,1)S(1)}, bf16[24,1536]{1,0:T(8,128)(2,1)S(1)}, u32[]{:S(2)}, u32[]{:S(2)}) collective-permute-start(bf16[24,1536]{1,0:T(8,128)(2,1)S(1)} %fusion.2), channel_id=1, source_target_pairs={{0,256},{32,288},{64,320},{96,352},{128,384},{160,416},{192,448},{... | collective-permute-start | bytes 221192 | tf_op jit(solution)/shard_map/ppermute | solution.py:245
  258.3 8.6 %copy-start.2 = (bf16[4,48,1536]{2,1,0:T(8,128)(2,1)}, bf16[4,48,1536]{2,1,0:T(8,128)(2,1)S(1)}, u32[]{:S(2)}) copy-start(bf16[4,48,1536]{2,1,0:T(8,128)(2,1)S(1)} %all_to_all.65) | copy-start | bytes 1769476
  258.3 8.6 %collective-permute-start.8 = (bf16[192,1536]{1,0:T(8,128)(2,1)S(1)}, bf16[192,1536]{1,0:T(8,128)(2,1)S(1)}, u32[]{:S(2)}, u32[]{:S(2)}) collective-permute-start(bf16[192,1536]{1,0:T(8,128)(2,1)S(1)} %bitcast.39), channel_id=1, source_target_pairs={{0,32},{32,0},{64,96},{96,64},{128,160},{160,128},{192,224},{224,1... | collective-permute-start | bytes 1769480 | tf_op jit(solution)/shard_map/ppermute | solution.py:245
  266.9 0.8 copy-start.4

commit v3 on v2

--- a/solution.py
+++ b/solution.py
@@ -62,14 +62,14 @@
     ]
 
 
-def cut_body(slabs, slots, place_ref, first_ref, second_ref, *outs):
-    rows, width = outs[0].shape[2:]
+def cut_body(place_ref, first_ref, second_ref, out):
+    rows, width = out.shape[3:]
+    slabs, slots = out.shape[:2]
     tile_rows, columns = first_ref.shape
     first_part = place_ref[3 * slabs * slots]
     for slab in range(slabs):
         for slot in range(slots):
             top, left, live = (place_ref[3 * (slab * slots + slot) + i] for i in range(3))
-            out = outs[slot]
 
             @pl.when(live > 0)
             def _():
@@ -79,34 +79,28 @@
                 for turn, ref in enumerate((first_ref, second_ref)):
                     pieces = [ref[:, pl.ds(start, LANE)] for start in starts]
                     narrow = dot(jnp.concatenate(pieces, axis=1), pick_columns).astype(jnp.bfloat16)
-                    out[slab, first_part ^ turn] = dot(pick_rows, narrow).astype(jnp.bfloat16)
+                    out[slab, slot, first_part ^ turn] = dot(pick_rows, narrow).astype(jnp.bfloat16)
 
             @pl.when(live == 0)
             def _():
-                out[slab] = jnp.zeros(out.shape[1:], out.dtype)
+                out[slab, slot] = jnp.zeros(out.shape[2:], out.dtype)
 
 
 def cut_windows(place, first_part, first, second, rows, width):
-    slabs, slots = place.shape[:2]
-    shape = jax.ShapeDtypeStruct((slabs, 2, rows, width), jnp.bfloat16)
+    shape = jax.ShapeDtypeStruct((*place.shape[:2], 2, rows, width), jnp.bfloat16)
     scalars = jnp.concatenate([place.reshape(-1), first_part.reshape(1)]).astype(jnp.int32)
-    return call(
-        functools.partial(cut_body, slabs, slots), [shape] * slots, [], scalars, first, second
-    )
-
-
-def patch_body(slots, live_ref, *refs):
-    uppers, lowers = refs[:slots], refs[slots : 2 * slots]
-    probe, patterns, wr_ref, wi_ref = refs[2 * slots : 2 * slots + 4]
-    outs = refs[2 * slots + 4 :]
-    rows = uppers[0].shape[2]
+    return call(cut_body, [shape], [], scalars, first, second)[0]
+
+
+def patch_body(live_ref, uppers, lowers, probe, patterns, wr_ref, wi_ref, out):
+    slabs, slots, _, rows, _ = uppers.shape
     f32, bf16 = jnp.float32, jnp.bfloat16
 
     def window(slot, part):
         def projected(ref):
-            return sum(ref[slab, part].astype(f32) for slab in range(ref.shape[0])).astype(bf16).astype(f32)
-
-        above, below = projected(uppers[slot]), projected(lowers[slot])
+            return sum(ref[slab, slot, part].astype(f32) for slab in range(slabs)).astype(bf16).astype(f32)
+
+        above, below = projected(uppers), projected(lowers)
         return jnp.concatenate(
             [above[:HALO], above[HALO:] + below[: rows - HALO], below[rows - HALO :]], axis=0
         )
@@ -141,33 +135,23 @@
             final_imag = trans_real * mixed_imag - trans_imag * mixed_real
             for part, value in enumerate((final_imag, -final_real)):
                 value = value.astype(bf16)
-                for slab in range(outs[slot].shape[0]):
-                    outs[slot][slab, part] = value
+                for slab in range(slabs):
+                    out[slab, slot, part] = value
 
         @pl.when(live_ref[slot] == 0)
         def _():
-            outs[slot][...] = jnp.zeros(outs[slot].shape, bf16)
+            for slab in range(slabs):
+                out[slab, slot] = jnp.zeros(out.shape[2:], bf16)
 
 
 def patch_gradients(live, uppers, lowers, probe_wave, patterns, tables):
     slots, width = patterns.shape[:2]
-    shape = jax.ShapeDtypeStruct((uppers[0].shape[0], 2, width, width), jnp.bfloat16)
-    return call(
-        functools.partial(patch_body, slots),
-        [shape] * slots,
-        [],
-        live,
-        *uppers,
-        *lowers,
-        probe_wave,
-        patterns,
-        *tables,
-    )
-
-
-def place_body(slots, pieces, place_ref, *refs):
-    windows, (keep_out, send_out, total) = refs[:slots], refs[slots:]
-    slabs, _, width, _ = windows[0].shape
+    shape = jax.ShapeDtypeStruct((uppers.shape[0], slots, 2, width, width), jnp.bfloat16)
+    return call(patch_body, [shape], [], live, uppers, lowers, probe_wave, patterns, *tables)[0]
+
+
+def place_body(pieces, place_ref, windows, keep_out, send_out, total):
+    slabs, slots, _, width, _ = windows.shape
     tile_rows, columns = keep_out.shape[1:]
     total[...] = jnp.zeros_like(total)
 
@@ -187,7 +171,7 @@
                 put_columns = one_hot(width, width + LANE, -lax.rem(left, LANE))
                 starts = column_blocks(left, width, columns)
                 for part in range(2):
-                    moved = dot(put_rows, windows[slot][slab, part]).astype(jnp.bfloat16)
+                    moved = dot(put_rows, windows[slab, slot, part]).astype(jnp.bfloat16)
                     wide = dot(moved, put_columns)
                     for i, start in enumerate(starts):
                         total[part, :, pl.ds(start, LANE)] += wide[:, i * LANE : (i + 1) * LANE]
@@ -203,11 +187,11 @@
     shape = (2, tile_rows, columns)
     scalars = jnp.concatenate([place.reshape(-1), core.reshape(1)]).astype(jnp.int32)
     return call(
-        functools.partial(place_body, len(windows), pieces),
+        functools.partial(place_body, pieces),
         [jax.ShapeDtypeStruct(shape, jnp.float32), jax.ShapeDtypeStruct(shape, jnp.bfloat16)],
         [pltpu.VMEM((2, 2 * tile_rows, columns), jnp.float32)],
         scalars,
-        *windows,
+        windows,
     )
 
 
@@ -259,13 +243,14 @@
     def to_four(value):
         return lax.all_to_all(value, "angle", 0, 0, axis_index_groups=four_groups, tiled=True)
 
-    def spread(piece):
-        other = swap(piece, 8)
-        pair = jnp.concatenate([jnp.where(far == 0, piece, other), jnp.where(far == 0, other, piece)])
+    def paired(piece, other):
+        return jnp.concatenate([jnp.where(far == 0, piece, other), jnp.where(far == 0, other, piece)])
+
+    def spread(pair):
         return to_four(jnp.broadcast_to(pair, (4, *pair.shape))).reshape(tile_rows, columns)
 
     def summed(blocks):
-        total = jnp.sum(to_four(blocks).astype(f32), axis=0).reshape(fours, piece_rows, columns)
+        total = jnp.sum(blocks.astype(f32), axis=0).reshape(fours, piece_rows, columns)
         here = lax.dynamic_index_in_dim(total, far, 0, keepdims=False)
         there = lax.dynamic_index_in_dim(total, 1 - far, 0, keepdims=False).astype(bf16)
         return here + swap(there, 8).astype(f32)
@@ -278,6 +263,7 @@
     live = (jnp.arange(slots) < counts.reshape(1)).astype(jnp.int32)
     meta = jnp.stack([offsets.reshape(slots), column_starts.reshape(slots), live], axis=1)
     group = to_slabs(jnp.broadcast_to(meta, (slabs, *meta.shape)))
+    after, group = lax.optimization_barrier((after, group))
     more = jnp.max(group[:, 1:, 2]) > 0
     sheared = jnp.floor_divide((angle_ids[0] - angle_center) * (slab - slabs // 2), shear_divisor)
     lefts = jnp.mod(group[..., 1] + jnp.mod(sheared, columns), columns)
@@ -285,32 +271,32 @@
     def place(down):
         return jnp.stack([group[..., 0] + down, lefts, group[..., 2]], axis=-1)
 
-    def exchanged(first, *others):
+    def exchanged(values):
         return lax.cond(
             more,
-            lambda values: tuple(to_slabs(v) for v in values),
-            lambda values: (to_slabs(values[0]), *values[1:]),
-            (first, *others),
+            to_slabs,
+            lambda v: jnp.concatenate([to_slabs(v[:, :1]), v[:, 1:]], axis=1),
+            values,
         )
 
     zero = jnp.zeros((), jnp.int32)
     uppers = cut_windows(place(0), zero, layer[0], layer[1], window_rows, width)
-    uppers = [to_slabs(u) for u in uppers]
-    after = spread(after)
-    lowers = cut_windows(
-        place(HALO - tile_rows), core, after, swap(after, 1), window_rows, width
-    )
-    lowers = exchanged(*lowers)
-
-    gradients = patch_gradients(live, uppers, lowers, probe_wave, patterns, tables)
-    gradients = exchanged(*gradients)
+    after, uppers = lax.optimization_barrier((paired(after, swap(after, 8)), uppers))
+    uppers, after = to_slabs(uppers), spread(after)
+    after, after_too, uppers = lax.optimization_barrier((after, swap(after, 1), uppers))
+    lowers = cut_windows(place(HALO - tile_rows), core, after, after_too, window_rows, width)
+    lowers = exchanged(lowers)
+
+    gradients = exchanged(patch_gradients(live, uppers, lowers, probe_wave, patterns, tables))
     kept, sent = place_windows(place(0), core, gradients, pieces, tile_rows, columns)
 
     kept = (kept + swap(sent, 1).astype(f32)).astype(bf16).reshape(2, 4, tile_rows // 4, columns)
-    spilled = mirrored(summed(kept[1]).astype(bf16), 1)
-    total = (summed(kept[0]) + spilled.astype(f32)).astype(bf16)
-
-    total = spread(total)
+    spill, own = to_four(kept[1]), to_four(kept[0])
+    spill, own = lax.optimization_barrier((summed(spill).astype(bf16), own))
+    spill = mirrored(spill, 1)
+    total = (summed(own) + spill.astype(f32)).astype(bf16)
+
+    total = spread(paired(total, swap(total, 8)))
     return step(core, layer, total, swap(total, 1)).reshape(volume.shape)
 
 

time: 272 us -> 229 us (0.84)
  waiting for transfers between devices: 82.8 us -> 61.1 us
  starting transfers between devices: 74.8 us -> 56.3 us
  blocking collectives: 75.6 us -> 70.9 us
    all_to_all x2 -> x1, waiting for transfers between devices: 27.7 us -> 6.85 us  [to_four(): lax.all_to_all(value, 'angle', 0, 0, axis_index_groups=four_groups, tiled...]
    all_to_all x3 -> x2, blocking collectives: 43.7 us -> 23.3 us  [to_slabs(): return lax.all_to_all(value, 'slab', 0, 0, tiled=True)]
    ppermute x7, starting transfers between devices: 57.7 us -> 41.4 us  [swap(): return lax.ppermute(value, 'angle', [(i, i ^ by) for i in range(angles)])]
    all_to_all x2 -> x3, blocking collectives: 31.9 us -> 47.6 us  [to_four(): lax.all_to_all(value, 'angle', 0, 0, axis_index_groups=four_groups, tiled...]
    ppermute x2, waiting for transfers between devices: 17.7 us -> 7.94 us  [mirrored(): return lax.ppermute(value, ('angle', 'tile'), pairs)]
    all_to_all x2, waiting for transfers between devices: 8.35 us -> 14.2 us  [to_slabs(): return lax.all_to_all(value, 'slab', 0, 0, tiled=True)]
    all_to_all x2 -> x1, starting transfers between devices: 6.96 us -> 3.48 us  [to_four(): lax.all_to_all(value, 'angle', 0, 0, axis_index_groups=four_groups, tiled...]
    ppermute x7, waiting for transfers between devices: 29 us -> 32.1 us  [swap(): return lax.ppermute(value, 'angle', [(i, i ^ by) for i in range(angles)])]
  transfers between devices with their start and end apart: 13 -> 12, of which waited for: 10 -> 11; matrix products, arithmetic and copies ran while one was open for 2% -> 3% of each run, Pallas kernels for 2% -> 2%
where the time goes in v3:
time: 229 us; the launch traced here: 228 us
  blocking collectives  70.9 us (31%)
  waiting for transfers between devices  61.1 us (27%)
  starting transfers between devices  56.3 us (25%)
  Pallas kernels  23.9 us (10%)
  local copies, waits for them, and re-layouts  7.12 us (3%)
  other arithmetic  6.8 us (3%)
    all_to_all x3, blocking collectives, to_four(): lax.all_to_all(value, 'angle', 0, 0, axis_index_groups=four_groups, tiled...  47.6 us
    ppermute x7, starting transfers between devices, swap(): return lax.ppermute(value, 'angle', [(i, i ^ by) for i in range(angles)])  41.4 us
    ppermute x7, waiting for transfers between devices, swap(): return lax.ppermute(value, 'angle', [(i, i ^ by) for i in range(angles)])  32.1 us
    pallas_call x5, Pallas kernels, call(): pl.pallas_call(body, grid=(1,), out_shape=out_shape, in_specs=[spec(x) fo...  23.9 us
    all_to_all x2, blocking collectives, to_slabs(): return lax.all_to_all(value, 'slab', 0, 0, tiled=True)  23.3 us
    all_to_all x2, waiting for transfers between devices, to_slabs(): return lax.all_to_all(value, 'slab', 0, 0, tiled=True)  14.2 us
    all_to_all x2, starting transfers between devices, to_slabs(): return lax.all_to_all(value, 'slab', 0, 0, tiled=True)  8.86 us
    ppermute x2, waiting for transfers between devices, mirrored(): return lax.ppermute(value, ('angle', 'tile'), pairs)  7.94 us
  transfers between devices with their start and end apart: 12, of which 11 were waited for; matrix products, arithmetic and copies ran while one was open for 3% of the time, Pallas kernels for 2%

profile of v3, /device:TPU:1, one launch (start us, length us, event | category | flops | bytes accessed | tf_op | source)
XLA Modules:
  0.0 228.4 jit_solution(13807978869537549598)
XLA Ops:
  4.2 4.8 %all-to-all-start.4 = ((s32[4,2,3]{2,1,0:T(2,128)}), s32[4,2,3]{2,1,0:T(2,128)S(1)}, u32[]{:S(2)}, u32[]{:S(2)}) async-start(s32[4,2,3]{2,1,0:T(2,128)} %broadcast_in_dim.9), calls=%async_computation.4 | async-start | bytes 8192 | tf_op jit(solution)/shard_map/all_to_all | solution.py:241
  9.1 2.3 %slice_bitcast_fusion = (bf16[192,1536]{1,0:T(8,128)(2,1)}, bf16[192,1536]{1,0:T(8,128)(2,1)}) fusion(bf16[2,1,192,1536]{3,2,1,0:T(8,128)(2,1)} %param.13), kind=kLoop, calls=%fused_computation.5 | loop fusion | bytes 2359296 | tf_op jit(solution)/shard_map/squeeze | solution.py:283
  13.2 6.7 %collective-permute-done = bf16[24,1536]{1,0:T(8,128)(2,1)S(1)} collective-permute-done((bf16[24,1536]{1,0:T(8,128)(2,1)S(1)}, bf16[24,1536]{1,0:T(8,128)(2,1)S(1)}, u32[]{:S(2)}, u32[]{:S(2)}) %collective-permute-start) | collective-permute-done | bytes 73760 | tf_op jit(solution)/shard_map/ppermute | solution.py:238
  20.2 2.9 %collective-permute-start.1 = (bf16[24,1536]{1,0:T(8,128)(2,1)S(1)}, bf16[24,1536]{1,0:T(8,128)(2,1)S(1)}, u32[]{:S(2)}, u32[]{:S(2)}) collective-permute-start(bf16[24,1536]{1,0:T(8,128)(2,1)S(1)} %collective-permute-done), channel_id=1, source_target_pairs={{0,256},{32,288},{64,320},{96,352},{128,384},{160,416},{192,448},{... | collective-permute-start | bytes 221192 | tf_op jit(solution)/shard_map/ppermute | solution.py:229
  23.9 5.3 %shard_map.91 = bf16[4,2,2,192,256]{4,3,2,1,0:T(8,128)(2,1)} custom-call(s32[25]{0:T(128)} %get-tuple-element.55.place_ref, bf16[192,1536]{1,0:T(8,128)(2,1)} %get-tuple-element.44.first_ref, bf16[192,1536]{1,0:T(8,128)(2,1)} %get-tuple-element.43.second_ref), custom_call_target="tpu_custom_call" | custom-call | tf_op jit(solution)/shard_map/pallas_call | solution.py:47
  29.1 5.0 %collective-permute-done.1 = bf16[24,1536]{1,0:T(8,128)(2,1)S(1)} collective-permute-done((bf16[24,1536]{1,0:T(8,128)(2,1)S(1)}, bf16[24,1536]{1,0:T(8,128)(2,1)S(1)}, u32[]{:S(2)}, u32[]{:S(2)}) %collective-permute-start.1) | collective-permute-done | bytes 73760 | tf_op jit(solution)/shard_map/ppermute | solution.py:229
  34.3 17.7 %all_to_all.50 = bf16[4,48,1536]{2,1,0:T(8,128)(2,1)S(1)} all-to-all(bf16[4,48,1536]{2,1,0:T(8,128)(2,1)S(1)} %broadcast_in_dim.10), channel_id=1, replica_groups={{0,64,128,192},{32,96,160,224},{256,320,384,448},{288,352,416,480},{1,6..., dimensions={0} | all-to-all | bytes 1179648 | tf_op jit(solution)/shard_map/all_to_all | solution.py:244
  51.9 4.0 %all-to-all-start.6 = ((bf16[4,2,2,192,256]{4,3,2,1,0:T(8,128)(2,1)}), bf16[4,2,2,192,256]{4,3,2,1,0:T(8,128)(2,1)S(1)}, u32[]{:S(2)}, u32[]{:S(2)}) async-start(bf16[4,2,2,192,256]{4,3,2,1,0:T(8,128)(2,1)} %shard_map.91), calls=%async_computation.6 | async-start | bytes 3145728 | tf_op jit(solution)/shard_map/all_to_all | solution.py:241
  55.9 3.8 %collective-permute-start.2 = (bf16[192,1536]{1,0:T(8,128)(2,1)S(1)}, bf16[192,1536]{1,0:T(8,128)(2,1)S(1)}, u32[]{:S(2)}, u32[]{:S(2)}) collective-permute-start(bf16[192,1536]{1,0:T(8,128)(2,1)S(1)} %bitcast.41), channel_id=1, source_target_pairs={{0,32},{32,0},{64,96},{96,64},{128,160},{160,128},{192,224},{224,1... | collective-permute-start | bytes 1769480 | tf_op jit(solution)/shard_map/ppermute | solution.py:229
  61.7 13.1 %all-to-all-done.6.uppers = bf16[4,2,2,192,256]{4,3,2,1,0:T(8,128)(2,1)S(1)} async-done(((bf16[4,2,2,192,256]{4,3,2,1,0:T(8,128)(2,1)}), bf16[4,2,2,192,256]{4,3,2,1,0:T(8,128)(2,1)S(1)}, u32[]{:S(2)}, u32[]{:S(2)}) %all-to-all-start.6) | async-done | bytes 1572896 | tf_op jit(solution)/shard_map/all_to_all | solution.py:241
  75.7 4.1 %shard_map.92 = bf16[4,2,2,192,256]{4,3,2,1,0:T(8,128)(2,1)S(1)} custom-call(s32[25]{0:T(128)} %get-tuple-element.57.place_ref, bf16[192,1536]{1,0:T(8,128)(2,1)} %bitcast.42, bf16[192,1536]{1,0:T(8,128)(2,1)} %copy-done.4), custom_call_target="tpu_custom_call" | custom-call | tf_op jit(solution)/shard_map/pallas_call | solution.py:47
  79.9 11.4 %conditional.2 = (bf16[4,2,2,192,256]{4,3,2,1,0:T(8,128)(2,1)S(1)}) conditional(s32[]{:T(128)} %convert_element_type.49, bf16[4,2,2,192,256]{4,3,2,1,0:T(8,128)(2,1)S(1)} %shard_map.92, bf16[4,2,2,192,256]{4,3,2,1,0:T(8,128)(2,1)S(1)} %shard_map.92), branch_computations={%region_1.2_spmd, %region_2.3_spmd} | conditional | flops 786432 | bytes 7864328 | solution.py:275
  80.0 11.1 %all_to_all.46 = bf16[4,1,2,192,256]{4,3,2,1,0:T(8,128)(2,1)S(1)} all-to-all(bf16[4,1,2,192,256]{4,3,2,1,0:T(8,128)(2,1)S(1)} %get-tuple-element.37), channel_id=1, replica_groups=mesh['angle'=16,'slab'=4,'tile'=8] {'slab'}, dimensions={0} | all-to-all | bytes 1572864 | tf_op jit(solution)/shard_map/cond/branch_0_fun/all_to_all | solution.py:241
  91.3 4.2 %shard_map.93 = bf16[4,2,2,256,256]{4,3,2,1,0:T(8,128)(2,1)S(1)} custom-call(s32[2]{0:T(128)} %compare_convert_fusion.live_ref, bf16[4,2,2,192,256]{4,3,2,1,0:T(8,128)(2,1)} %copy-done, bf16[4,2,2,192,256]{4,3,2,1,0:T(8,128)(2,1)S(1)} %get-tuple-element.58.lowers, f32[2,256,256]{2,1,0:T(8,128)} %probe.1, bf16[2,256,256]{2,1,0:T(8,128)(2,1)} %bitcast.48, ...), custom_call_target="tpu_custom_call" | custom-call | tf_op jit(solution)/shard_map/pallas_call | solution.py:47
  95.5 13.8 %conditional.3 = (bf16[4,2,2,256,256]{4,3,2,1,0:T(8,128)(2,1)}) conditional(s32[]{:T(128)} %convert_element_type.49, bf16[4,2,2,256,256]{4,3,2,1,0:T(8,128)(2,1)S(1)} %shard_map.93, bf16[4,2,2,256,256]{4,3,2,1,0:T(8,128)(2,1)S(1)} %shard_map.93), branch_computations={%region_3.4_spmd, %region_4.5_spmd} | conditional | flops 1048576 | bytes 10485768 | solution.py:275
  95.6 12.2 %all_to_all.48 = bf16[4,1,2,256,256]{4,3,2,1,0:T(8,128)(2,1)S(1)} all-to-all(bf16[4,1,2,256,256]{4,3,2,1,0:T(8,128)(2,1)S(1)} %get-tuple-element.39), channel_id=1, replica_groups=mesh['angle'=16,'slab'=4,'tile'=8] {'slab'}, dimensions={0} | all-to-all | bytes 2097152 | tf_op jit(solution)/shard_map/cond/branch_0_fun/all_to_all | solution.py:241
  109.3 6.9 %shard_map.94 = (f32[2,192,1536]{2,1,0:T(8,128)}, bf16[2,192,1536]{2,1,0:T(8,128)(2,1)}) custom-call(s32[25]{0:T(128)} %get-tuple-element.56.place_ref, bf16[4,2,2,256,256]{4,3,2,1,0:T(8,128)(2,1)} %get-tuple-element.59.windows), custom_call_target="tpu_custom_call" | custom-call | tf_op jit(solution)/shard_map/pallas_call | solution.py:47
  116.3 19.7 %collective-permute-start.3 = (bf16[2,192,1536]{2,1,0:T(8,128)(2,1)}, bf16[2,192,1536]{2,1,0:T(8,128)(2,1)S(1)}, u32[]{:S(2)}, u32[]{:S(2)}) collective-permute-start(bf16[2,192,1536]{2,1,0:T(8,128)(2,1)} %get-tuple-element.34), channel_id=1, source_target_pairs={{0,32},{32,0},{64,96},{96,64},{128,160},{160,128},{192,224},{224,1... | collective-permute-start | bytes 3538952 | tf_op jit(solution)/shard_map/ppermute | solution.py:229
  136.0 2.7 %collective-permute-done.3 = bf16[2,192,1536]{2,1,0:T(8,128)(2,1)S(1)} collective-permute-done((bf16[2,192,1536]{2,1,0:T(8,128)(2,1)}, bf16[2,192,1536]{2,1,0:T(8,128)(2,1)S(1)}, u32[]{:S(2)}, u32[]{:S(2)}) %collective-permute-start.3) | collective-permute-done | bytes 1179680 | tf_op jit(solution)/shard_map/ppermute | solution.py:229
  138.7 2.0 add_convert_fusion
  141.6 17.7 %all_to_all.51 = bf16[4,48,1536]{2,1,0:T(8,128)(2,1)S(1)} all-to-all(bf16[4,48,1536]{2,1,0:T(8,128)(2,1)S(1)} %bitcast.43), channel_id=1, replica_groups={{0,64,128,192},{32,96,160,224},{256,320,384,448},{288,352,416,480},{1,6..., dimensions={0} | all-to-all | bytes 1179648 | tf_op jit(solution)/shard_map/all_to_all | solution.py:244
  159.3 3.5 %all-to-all-start.8 = ((bf16[4,48,1536]{2,1,0:T(8,128)(2,1)}), bf16[4,48,1536]{2,1,0:T(8,128)(2,1)S(1)}, u32[]{:S(2)}, u32[]{:S(2)}) async-start(bf16[4,48,1536]{2,1,0:T(8,128)(2,1)} %bitcast.15), calls=%async_computation.8 | async-start | bytes 1179648 | tf_op jit(solution)/shard_map/all_to_all | solution.py:244
  163.0 1.9 collective-permute-start.4
  164.9 7.9 %collective-permute-done.4 = bf16[24,1536]{1,0:T(8,128)(2,1)S(1)} collective-permute-done((bf16[24,1536]{1,0:T(8,128)(2,1)S(1)}, bf16[24,1536]{1,0:T(8,128)(2,1)S(1)}, u32[]{:S(2)}, u32[]{:S(2)}) %collective-permute-start.4) | collective-permute-done | bytes 73760 | tf_op jit(solution)/shard_map/ppermute | solution.py:229
  172.9 6.8 %all-to-all-done.8 = bf16[4,48,1536]{2,1,0:T(8,128)(2,1)S(1)} async-done(((bf16[4,48,1536]{2,1,0:T(8,128)(2,1)}), bf16[4,48,1536]{2,1,0:T(8,128)(2,1)S(1)}, u32[]{:S(2)}, u32[]{:S(2)}) %all-to-all-start.8) | async-done | bytes 589856 | tf_op jit(solution)/shard_map/all_to_all | solution.py:244
  181.1 1.9 collective-permute-start.5
  184.3 7.5 %collective-permute-done.5 = bf16[24,1536]{1,0:T(8,128)(2,1)S(1)} collective-permute-done((bf16[24,1536]{1,0:T(8,128)(2,1)S(1)}, bf16[24,1536]{1,0:T(8,128)(2,1)S(1)}, u32[]{:S(2)}, u32[]{:S(2)}) %collective-permute-start.5) | collective-permute-done | bytes 73760 | tf_op jit(solution)/shard_map/ppermute | solution.py:229
  191.8 1.9 collective-permute-start.7
  193.8 7.3 %collective-permute-done.7 = bf16[24,1536]{1,0:T(8,128)(2,1)S(1)} collective-permute-done((bf16[24,1536]{1,0:T(8,128)(2,1)S(1)}, bf16[24,1536]{1,0:T(8,128)(2,1)S(1)}, u32[]{:S(2)}, u32[]{:S(2)}) %collective-permute-start.7) | collective-permute-done | bytes 73760 | tf_op jit(solution)/shard_map/ppermute | solution.py:229
  201.1 12.2 %all_to_all.52 = bf16[4,48,1536]{2,1,0:T(8,128)(2,1)S(1)} all-to-all(bf16[4,48,1536]{2,1,0:T(8,128)(2,1)S(1)} %broadcast_in_dim.11), channel_id=1, replica_groups={{0,64,128,192},{32,96,160,224},{256,320,384,448},{288,352,416,480},{1,6..., dimensions={0} | all-to-all | bytes 1179648 | tf_op jit(solution)/shard_map/all_to_all | solution.py:244
  213.4 9.2 %collective-permute-start.8 = (bf16[192,1536]{1,0:T(8,128)(2,1)S(1)}, bf16[192,1536]{1,0:T(8,128)(2,1)S(1)}, u32[]{:S(2)}, u32[]{:S(2)}) collective-permute-start(bf16[192,1536]{1,0:T(8,128)(2,1)S(1)} %bitcast.39), channel_id=1, source_target_pairs={{0,32},{32,0},{64,96},{96,64},{128,160},{160,128},{192,224},{224,1... | collective-permute-start | bytes 1769480 | tf_op jit(solution)/shard_map/ppermute | solution.py:229
  225.1 3.3 %shard_map.95 = f32[2,192,1536]{2,1,0:T(8,128)} custom-call(s32[1]{0:T(128)} %bitcast.core_ref, bf16[2,192,1536]{2,1,0:T(8,128)(2,1)} %bitcast.38, bf16[192,1536]{1,0:T(8,128)(2,1)} %bitcast.40, bf16[192,1536]{1,0:T(8,128)(2,1)} %copy-done.3), custom_call_target="tpu_custom_call" | custom-call | tf_op jit(solution)/shard_map/pallas_call | solution.py:47
  (45 shorter events, 16.1 us)
Async XLA Ops:
  0.9 19.0 %collective-permute-start = (bf16[24,1536]{1,0:T(8,128)(2,1)S(1)}, bf16[24,1536]{1,0:T(8,128)(2,1)S(1)}, u32[]{:S(2)}, u32[]{:S(2)}) collective-permute-start(bf16[24,1536]{1,0:T(8,128)(2,1)S(1)} %dynamic-slice_bitcast_fusion), channel_id=1, source_target_pairs={{1,448},{2,449},{3,450},{4,451},{5,452},{6,453},{7,454},{33,480},{... | collective-permute-start | bytes 221192 | tf_op jit(solution)/shard_map/ppermute | solution.py:238
  4.2 9.0 %all-to-all-start.4 = ((s32[4,2,3]{2,1,0:T(2,128)}), s32[4,2,3]{2,1,0:T(2,128)S(1)}, u32[]{:S(2)}, u32[]{:S(2)}) async-start(s32[4,2,3]{2,1,0:T(2,128)} %broadcast_in_dim.9), calls=%async_computation.4 | async-start | bytes 8192 | tf_op jit(solution)/shard_map/all_to_all | solution.py:241
  20.2 13.9 %collective-permute-start.1 = (bf16[24,1536]{1,0:T(8,128)(2,1)S(1)}, bf16[24,1536]{1,0:T(8,128)(2,1)S(1)}, u32[]{:S(2)}, u32[]{:S(2)}) collective-permute-start(bf16[24,1536]{1,0:T(8,128)(2,1)S(1)} %collective-permute-done), channel_id=1, source_target_pairs={{0,256},{32,288},{64,320},{96,352},{128,384},{160,416},{192,448},{... | collective-permute-start | bytes 221192 | tf_op jit(solution)/shard_map/ppermute | solution.py:229
  51.9 4.0 %copy-start.2 = (bf16[4,48,1536]{2,1,0:T(8,128)(2,1)}, bf16[4,48,1536]{2,1,0:T(8,128)(2,1)S(1)}, u32[]{:S(2)}) copy-start(bf16[4,48,1536]{2,1,0:T(8,128)(2,1)S(1)} %all_to_all.50) | copy-start | bytes 1769476
  51.9 22.9 %all-to-all-start.6 = ((bf16[4,2,2,192,256]{4,3,2,1,0:T(8,128)(2,1)}), bf16[4,2,2,192,256]{4,3,2,1,0:T(8,128)(2,1)S(1)}, u32[]{:S(2)}, u32[]{:S(2)}) async-start(bf16[4,2,2,192,256]{4,3,2,1,0:T(8,128)(2,1)} %shard_map.91), calls=%async_computation.6 | async-start | bytes 3145728 | tf_op jit(solution)/shard_map/all_to_all | solution.py:241
  55.9 18.9 %collective-permute-start.2 = (bf16[192,1536]{1,0:T(8,128)(2,1)S(1)}, bf16[192,1536]{1,0:T(8,128)(2,1)S(1)}, u32[]{:S(2)}, u32[]{:S(2)}) collective-permute-start(bf16[192,1536]{1,0:T(8,128)(2,1)S(1)} %bitcast.41), channel_id=1, source_target_pairs={{0,32},{32,0},{64,96},{96,64},{128,160},{160,128},{192,224},{224,1... | collective-permute-start | bytes 1769480 | tf_op jit(solution)/shard_map/ppermute | solution.py:229
  74.8 5.0 %copy-start = (bf16[4,2,2,192,256]{4,3,2,1,0:T(8,128)(2,1)}, bf16[4,2,2,192,256]{4,3,2,1,0:T(8,128)(2,1)S(1)}, u32[]{:S(2)}) copy-start(bf16[4,2,2,192,256]{4,3,2,1,0:T(8,128)(2,1)S(1)} %all-to-all-done.6.uppers) | copy-start | bytes 4718596
  74.8 0.9 copy-start.4
  116.3 22.4 %collective-permute-start.3 = (bf16[2,192,1536]{2,1,0:T(8,128)(2,1)}, bf16[2,192,1536]{2,1,0:T(8,128)(2,1)S(1)}, u32[]{:S(2)}, u32[]{:S(2)}) collective-permute-start(bf16[2,192,1536]{2,1,0:T(8,128)(2,1)} %get-tuple-element.34), channel_id=1, source_target_pairs={{0,32},{32,0},{64,96},{96,64},{128,160},{160,128},{192,224},{224,1... | collective-permute-start | bytes 3538952 | tf_op jit(solution)/shard_map/ppermute | solution.py:229
  159.3 20.4 %all-to-all-start.8 = ((bf16[4,48,1536]{2,1,0:T(8,128)(2,1)}), bf16[4,48,1536]{2,1,0:T(8,128)(2,1)S(1)}, u32[]{:S(2)}, u32[]{:S(2)}) async-start(bf16[4,48,1536]{2,1,0:T(8,128)(2,1)} %bitcast.15), calls=%async_computation.8 | async-start | bytes 1179648 | tf_op jit(solution)/shard_map/all_to_all | solution.py:244
  163.0 9.9 %collective-permute-start.4 = (bf16[24,1536]{1,0:T(8,128)(2,1)S(1)}, bf16[24,1536]{1,0:T(8,128)(2,1)S(1)}, u32[]{:S(2)}, u32[]{:S(2)}) collective-permute-start(bf16[24,1536]{1,0:T(8,128)(2,1)S(1)} %fusion.3), channel_id=1, source_target_pairs={{0,256},{32,288},{64,320},{96,352},{128,384},{160,416},{192,448},{... | collective-permute-start | bytes 221192 | tf_op jit(solution)/shard_map/ppermute | solution.py:229
  179.7 4.6 %collective-permute-start.6 = (bf16[24,1536]{1,0:T(8,128)(2,1)S(1)}, bf16[24,1536]{1,0:T(8,128)(2,1)S(1)}, u32[]{:S(2)}, u32[]{:S(2)}) collective-permute-start(bf16[24,1536]{1,0:T(8,128)(2,1)S(1)} %fusion.2), channel_id=1, source_target_pairs={{0,449},{1,450},{2,451},{3,452},{4,453},{5,454},{6,455},{32,481},{... | collective-permute-start | bytes 221192 | tf_op jit(solution)/shard_map/ppermute | solution.py:238
  181.1 10.7 %collective-permute-start.5 = (bf16[24,1536]{1,0:T(8,128)(2,1)S(1)}, bf16[24,1536]{1,0:T(8,128)(2,1)S(1)}, u32[]{:S(2)}, u32[]{:S(2)}) collective-permute-start(bf16[24,1536]{1,0:T(8,128)(2,1)S(1)} %fusion.4), channel_id=1, source_target_pairs={{0,256},{32,288},{64,320},{96,352},{128,384},{160,416},{192,448},{... | collective-permute-start | bytes 221192 | tf_op jit(solution)/shard_map/ppermute | solution.py:229
  191.8 9.2 %collective-permute-start.7 = (bf16[24,1536]{1,0:T(8,128)(2,1)S(1)}, bf16[24,1536]{1,0:T(8,128)(2,1)S(1)}, u32[]{:S(2)}, u32[]{:S(2)}) collective-permute-start(bf16[24,1536]{1,0:T(8,128)(2,1)S(1)} %fusion.1), channel_id=1, source_target_pairs={{0,256},{32,288},{64,320},{96,352},{128,384},{160,416},{192,448},{... | collective-permute-start | bytes 221192 | tf_op jit(solution)/shard_map/ppermute | solution.py:229
  213.4 10.9 %copy-start.1 = (bf16[4,48,1536]{2,1,0:T(8,128)(2,1)}, bf16[4,48,1536]{2,1,0:T(8,128)(2,1)S(1)}, u32[]{:S(2)}) copy-start(bf16[4,48,1536]{2,1,0:T(8,128)(2,1)S(1)} %all_to_all.52) | copy-start | bytes 1769476
  213.4 10.9 %collective-permute-start.8 = (bf16[192,1536]{1,0:T(8,128)(2,1)S(1)}, bf16[192,1536]{1,0:T(8,128)(2,1)S(1)}, u32[]{:S(2)}, u32[]{:S(2)}) collective-permute-start(bf16[192,1536]{1,0:T(8,128)(2,1)S(1)} %bitcast.39), channel_id=1, source_target_pairs={{0,32},{32,0},{64,96},{96,64},{128,160},{160,128},{192,224},{224,1... | collective-permute-start | bytes 1769480 | tf_op jit(solution)/shard_map/ppermute | solution.py:229
  224.2 0.8 copy-start.3

commit v4 on v3

--- a/solution.py
+++ b/solution.py
@@ -62,11 +62,17 @@
     ]
 
 
-def cut_body(place_ref, first_ref, second_ref, out):
-    rows, width = out.shape[3:]
-    slabs, slots = out.shape[:2]
-    tile_rows, columns = first_ref.shape
-    first_part = place_ref[3 * slabs * slots]
+def cut_body(place_ref, *refs):
+    blocks, (out, rows_held) = refs[:-2], refs[-2:]
+    slabs, slots, _, rows, width = out.shape
+    tile_rows, columns = rows_held.shape[1:]
+    first_part, first_block = (place_ref[3 * slabs * slots + i] for i in range(2))
+    each = len(blocks) // 2
+    for n, block in enumerate(blocks):
+        size = tile_rows // each
+        start = pl.multiple_of((first_block ^ (n % each)) * size, size)
+        rows_held[first_part ^ (n // each), pl.ds(start, size), :] = block[...]
+
     for slab in range(slabs):
         for slot in range(slots):
             top, left, live = (place_ref[3 * (slab * slots + slot) + i] for i in range(3))
@@ -76,20 +82,22 @@
                 pick_rows = one_hot(rows, tile_rows, -top)
                 pick_columns = one_hot(width + LANE, width, lax.rem(left, LANE))
                 starts = column_blocks(left, width, columns)
-                for turn, ref in enumerate((first_ref, second_ref)):
-                    pieces = [ref[:, pl.ds(start, LANE)] for start in starts]
+                for part in range(2):
+                    pieces = [rows_held[part, :, pl.ds(start, LANE)] for start in starts]
                     narrow = dot(jnp.concatenate(pieces, axis=1), pick_columns).astype(jnp.bfloat16)
-                    out[slab, slot, first_part ^ turn] = dot(pick_rows, narrow).astype(jnp.bfloat16)
+                    out[slab, slot, part] = dot(pick_rows, narrow).astype(jnp.bfloat16)
 
             @pl.when(live == 0)
             def _():
                 out[slab, slot] = jnp.zeros(out.shape[2:], out.dtype)
 
 
-def cut_windows(place, first_part, first, second, rows, width):
+def cut_windows(place, firsts, blocks, rows, width):
     shape = jax.ShapeDtypeStruct((*place.shape[:2], 2, rows, width), jnp.bfloat16)
-    scalars = jnp.concatenate([place.reshape(-1), first_part.reshape(1)]).astype(jnp.int32)
-    return call(cut_body, [shape], [], scalars, first, second)[0]
+    scalars = jnp.concatenate([place.reshape(-1), jnp.stack(firsts)]).astype(jnp.int32)
+    each = len(blocks) // 2
+    held = pltpu.VMEM((2, each * blocks[0].shape[0], blocks[0].shape[1]), jnp.bfloat16)
+    return call(cut_body, [shape], [held], scalars, *blocks)[0]
 
 
 def patch_body(live_ref, uppers, lowers, probe, patterns, wr_ref, wi_ref, out):
@@ -150,24 +158,17 @@
     return call(patch_body, [shape], [], live, uppers, lowers, probe_wave, patterns, *tables)[0]
 
 
-def place_body(pieces, place_ref, windows, keep_out, send_out, total):
+def place_body(blocks, place_ref, windows, own_out, next_out, send_out, total):
     slabs, slots, _, width, _ = windows.shape
-    tile_rows, columns = keep_out.shape[1:]
+    tile_rows, columns = own_out.shape
     total[...] = jnp.zeros_like(total)
-
-    stored = lax.broadcasted_iota(jnp.int32, (2 * tile_rows, width), 0)
-    size = tile_rows // pieces
-    piece = sum((stored >= tile_rows + k * size).astype(jnp.int32) for k in range(1, pieces))
-    true_row = jnp.where(stored < tile_rows, stored, stored + (pieces - 1 - 2 * piece) * size)
-    patch_row = true_row - lax.broadcasted_iota(jnp.int32, (2 * tile_rows, width), 1)
-
     for slab in range(slabs):
         for slot in range(slots):
             top, left, live = (place_ref[3 * (slab * slots + slot) + i] for i in range(3))
 
             @pl.when(live > 0)
             def _():
-                put_rows = (patch_row == top).astype(jnp.float32).astype(jnp.bfloat16)
+                put_rows = one_hot(2 * tile_rows, width, top)
                 put_columns = one_hot(width, width + LANE, -lax.rem(left, LANE))
                 starts = column_blocks(left, width, columns)
                 for part in range(2):
@@ -177,18 +178,22 @@
                         total[part, :, pl.ds(start, LANE)] += wide[:, i * LANE : (i + 1) * LANE]
 
     core = place_ref[3 * slabs * slots]
-    for which in range(2):
-        rows = slice(which * tile_rows, (which + 1) * tile_rows)
-        keep_out[which] = total[core, rows]
-        send_out[which] = total[1 - core, rows].astype(jnp.bfloat16)
-
-
-def place_windows(place, core, windows, pieces, tile_rows, columns):
-    shape = (2, tile_rows, columns)
+    own_out[...] = total[core, :tile_rows]
+    send_out[1] = total[1 - core, :tile_rows].astype(jnp.bfloat16)
+    size = tile_rows // blocks
+    for block in range(blocks):
+        to = slice(block * size, (block + 1) * size)
+        rows = slice(2 * tile_rows - (block + 1) * size, 2 * tile_rows - block * size)
+        next_out[to] = total[core, rows]
+        send_out[0, to] = total[1 - core, rows].astype(jnp.bfloat16)
+
+
+def place_windows(place, core, windows, blocks, tile_rows, columns):
+    kept = jax.ShapeDtypeStruct((tile_rows, columns), jnp.float32)
     scalars = jnp.concatenate([place.reshape(-1), core.reshape(1)]).astype(jnp.int32)
     return call(
-        functools.partial(place_body, pieces),
-        [jax.ShapeDtypeStruct(shape, jnp.float32), jax.ShapeDtypeStruct(shape, jnp.bfloat16)],
+        functools.partial(place_body, blocks),
+        [kept, kept, jax.ShapeDtypeStruct((2, tile_rows, columns), jnp.bfloat16)],
         [pltpu.VMEM((2, 2 * tile_rows, columns), jnp.float32)],
         scalars,
         windows,
@@ -219,11 +224,9 @@
     window_rows = width - HALO
     patterns = amplitudes.reshape(slots, width, width)
 
-    fours = angles // 8
-    core, far = angle % 2, angle // 8
-    four_groups = [[8 * f + 2 * q + c for q in range(4)] for f in range(fours) for c in range(2)]
-    pieces = 4 * fours
-    piece_rows = tile_rows // pieces
+    core, place_z = angle % 2, angle // 2 % 4
+    four_groups = [[8 * f + 2 * q + c for q in range(4)] for f in range(angles // 8) for c in range(2)]
+    block_rows = tile_rows // 4
 
     def swap(value, by):
         return lax.ppermute(value, "angle", [(i, i ^ by) for i in range(angles)])
@@ -243,22 +246,13 @@
     def to_four(value):
         return lax.all_to_all(value, "angle", 0, 0, axis_index_groups=four_groups, tiled=True)
 
-    def paired(piece, other):
-        return jnp.concatenate([jnp.where(far == 0, piece, other), jnp.where(far == 0, other, piece)])
-
-    def spread(pair):
-        return to_four(jnp.broadcast_to(pair, (4, *pair.shape))).reshape(tile_rows, columns)
-
-    def summed(blocks):
-        total = jnp.sum(blocks.astype(f32), axis=0).reshape(fours, piece_rows, columns)
-        here = lax.dynamic_index_in_dim(total, far, 0, keepdims=False)
-        there = lax.dynamic_index_in_dim(total, 1 - far, 0, keepdims=False).astype(bf16)
-        return here + swap(there, 8).astype(f32)
-
-    place_z = angles // 2 - 1 - angle // 2
-    first_row = (place_z % 4) * (piece_rows * fours) + place_z // 4 * piece_rows
+    def added(blocks):
+        return jnp.sum(to_four(blocks).astype(f32), axis=0)
+
     own_part = lax.dynamic_index_in_dim(layer, core, 0, keepdims=False)
-    after = mirrored(lax.dynamic_slice(own_part, (first_row, 0), (piece_rows, columns)), -1)
+    after = mirrored(
+        lax.dynamic_slice(own_part, ((3 - place_z) * block_rows, 0), (block_rows, columns)), -1
+    )
 
     live = (jnp.arange(slots) < counts.reshape(1)).astype(jnp.int32)
     meta = jnp.stack([offsets.reshape(slots), column_starts.reshape(slots), live], axis=1)
@@ -280,23 +274,27 @@
         )
 
     zero = jnp.zeros((), jnp.int32)
-    uppers = cut_windows(place(0), zero, layer[0], layer[1], window_rows, width)
-    after, uppers = lax.optimization_barrier((paired(after, swap(after, 8)), uppers))
-    uppers, after = to_slabs(uppers), spread(after)
-    after, after_too, uppers = lax.optimization_barrier((after, swap(after, 1), uppers))
-    lowers = cut_windows(place(HALO - tile_rows), core, after, after_too, window_rows, width)
+    uppers = cut_windows(place(0), [zero, zero], [layer[0], layer[1]], window_rows, width)
+    after, uppers = lax.optimization_barrier((after, uppers))
+    uppers = to_slabs(uppers)
+    mine = [after] + [swap(after, k << 1) for k in range(1, 4)]
+    afters = mine + [swap(block, 1) for block in mine]
+    afters, uppers = lax.optimization_barrier((afters, uppers))
+    lowers = cut_windows(place(HALO - tile_rows), [core, place_z], afters, window_rows, width)
     lowers = exchanged(lowers)
 
     gradients = exchanged(patch_gradients(live, uppers, lowers, probe_wave, patterns, tables))
-    kept, sent = place_windows(place(0), core, gradients, pieces, tile_rows, columns)
-
-    kept = (kept + swap(sent, 1).astype(f32)).astype(bf16).reshape(2, 4, tile_rows // 4, columns)
-    spill, own = to_four(kept[1]), to_four(kept[0])
-    spill, own = lax.optimization_barrier((summed(spill).astype(bf16), own))
+    own, spill, sent = place_windows(place(0), core, gradients, 4, tile_rows, columns)
+
+    sent = swap(sent, 1).astype(f32)
+    spill = (spill + sent[0]).astype(bf16).reshape(4, block_rows, columns)
+    own = (own + sent[1]).astype(bf16).reshape(4, block_rows, columns)
+    spill, own = lax.optimization_barrier((added(spill).astype(bf16), own))
     spill = mirrored(spill, 1)
-    total = (summed(own) + spill.astype(f32)).astype(bf16)
-
-    total = spread(paired(total, swap(total, 8)))
+    total = lax.optimization_barrier((added(own) + spill.astype(f32)).astype(bf16))
+    total = (total.astype(f32) + swap(total, 8).astype(f32)).astype(bf16)
+
+    total = to_four(jnp.broadcast_to(total, (4, *total.shape))).reshape(tile_rows, columns)
     return step(core, layer, total, swap(total, 1)).reshape(volume.shape)
 
 

time: 229 us -> 216 us (0.943)
  waiting for transfers between devices: 61.1 us -> 49.5 us
  blocking collectives: 70.9 us -> 60.5 us
  starting transfers between devices: 56.3 us -> 64.7 us
    ppermute x7 -> x10, waiting for transfers between devices: 32.1 us -> 12.2 us  [swap(): return lax.ppermute(value, 'angle', [(i, i ^ by) for i in range(angles)])]
    all_to_all x3 -> x2, blocking collectives: 47.6 us -> 33.3 us  [to_four(): lax.all_to_all(value, 'angle', 0, 0, axis_index_groups=four_groups, tiled...]
    all_to_all x2, waiting for transfers between devices: 14.2 us -> 0.01 us  [to_slabs(): return lax.all_to_all(value, 'slab', 0, 0, tiled=True)]
    ppermute x2, waiting for transfers between devices: 7.94 us -> 20.1 us  [mirrored(): return lax.ppermute(value, ('angle', 'tile'), pairs)]
    all_to_all x1, waiting for transfers between devices: 6.85 us -> 17.2 us  [to_four(): lax.all_to_all(value, 'angle', 0, 0, axis_index_groups=four_groups, tiled...]
    ppermute x7 -> x10, starting transfers between devices: 41.4 us -> 49.6 us  [swap(): return lax.ppermute(value, 'angle', [(i, i ^ by) for i in range(angles)])]
    all_to_all x2, blocking collectives: 23.3 us -> 27.2 us  [to_slabs(): return lax.all_to_all(value, 'slab', 0, 0, tiled=True)]
  transfers between devices with their start and end apart: 12 -> 15, of which waited for: 11 -> 5; matrix products, arithmetic and copies ran while one was open for 3% -> 3% of each run, Pallas kernels for 2% -> 0%
where the time goes in v4:
time: 216 us; the launch traced here: 215 us
  starting transfers between devices  64.7 us (30%)
  blocking collectives  60.5 us (28%)
  waiting for transfers between devices  49.5 us (23%)
  Pallas kernels  24.9 us (12%)
  other arithmetic  6.68 us (3%)
  local copies, waits for them, and re-layouts  6.64 us (3%)
  between operations  2.3 us (1%)
    ppermute x10, starting transfers between devices, swap(): return lax.ppermute(value, 'angle', [(i, i ^ by) for i in range(angles)])  49.6 us
    all_to_all x2, blocking collectives, to_four(): lax.all_to_all(value, 'angle', 0, 0, axis_index_groups=four_groups, tiled...  33.3 us
    all_to_all x2, blocking collectives, to_slabs(): return lax.all_to_all(value, 'slab', 0, 0, tiled=True)  27.2 us
    pallas_call x5, Pallas kernels, call(): pl.pallas_call(body, grid=(1,), out_shape=out_shape, in_specs=[spec(x) fo...  24.9 us
    ppermute x2, waiting for transfers between devices, mirrored(): return lax.ppermute(value, ('angle', 'tile'), pairs)  20.1 us
    all_to_all x1, waiting for transfers between devices, to_four(): lax.all_to_all(value, 'angle', 0, 0, axis_index_groups=four_groups, tiled...  17.2 us
    ppermute x10, waiting for transfers between devices, swap(): return lax.ppermute(value, 'angle', [(i, i ^ by) for i in range(angles)])  12.2 us
    all_to_all x2, starting transfers between devices, to_slabs(): return lax.all_to_all(value, 'slab', 0, 0, tiled=True)  9.04 us
  transfers between devices with their start and end apart: 15, of which 5 were waited for; matrix products, arithmetic and copies ran while one was open for 3% of the time, Pallas kernels for 0%

profile of v4, /device:TPU:1, one launch (start us, length us, event | category | flops | bytes accessed | tf_op | source)
XLA Modules:
  0.0 215.2 jit_solution(13488420541216737033)
XLA Ops:
  2.0 4.8 %all-to-all-start.4 = ((s32[4,2,3]{2,1,0:T(2,128)}), s32[4,2,3]{2,1,0:T(2,128)S(1)}, u32[]{:S(2)}, u32[]{:S(2)}) async-start(s32[4,2,3]{2,1,0:T(2,128)} %broadcast_in_dim.6), calls=%async_computation.4 | async-start | bytes 8192 | tf_op jit(solution)/shard_map/all_to_all | solution.py:244
  9.1 2.3 %slice_bitcast_fusion.2 = (bf16[192,1536]{1,0:T(8,128)(2,1)}, bf16[192,1536]{1,0:T(8,128)(2,1)}) fusion(bf16[2,1,192,1536]{3,2,1,0:T(8,128)(2,1)} %param.13), kind=kLoop, calls=%fused_computation.9 | loop fusion | bytes 2359296 | tf_op jit(solution)/shard_map/squeeze | solution.py:277
  12.2 20.1 %collective-permute-done.refs_0_ = bf16[48,1536]{1,0:T(8,128)(2,1)S(1)} collective-permute-done((bf16[48,1536]{1,0:T(8,128)(2,1)S(1)}, bf16[48,1536]{1,0:T(8,128)(2,1)S(1)}, u32[]{:S(2)}, u32[]{:S(2)}) %collective-permute-start) | collective-permute-done | bytes 147488 | tf_op jit(solution)/shard_map/ppermute | solution.py:241
  33.1 5.4 %shard_map.91 = bf16[4,2,2,192,256]{4,3,2,1,0:T(8,128)(2,1)} custom-call(s32[26]{0:T(128)} %concatenate.16.place_ref, bf16[192,1536]{1,0:T(8,128)(2,1)} %get-tuple-element.58.refs_0_, bf16[192,1536]{1,0:T(8,128)(2,1)} %get-tuple-element.57.refs_1_), custom_call_target="tpu_custom_call" | custom-call | tf_op jit(solution)/shard_map/pallas_call | solution.py:47
  38.5 4.2 %all-to-all-start.5 = ((bf16[4,2,2,192,256]{4,3,2,1,0:T(8,128)(2,1)}), bf16[4,2,2,192,256]{4,3,2,1,0:T(8,128)(2,1)S(1)}, u32[]{:S(2)}, u32[]{:S(2)}) async-start(bf16[4,2,2,192,256]{4,3,2,1,0:T(8,128)(2,1)} %shard_map.91), calls=%async_computation.5 | async-start | bytes 3145728 | tf_op jit(solution)/shard_map/all_to_all | solution.py:244
  42.7 1.9 collective-permute-start.3
  44.6 1.9 collective-permute-start.2
  46.5 5.4 %collective-permute-start.1 = (bf16[48,1536]{1,0:T(8,128)(2,1)S(1)}, bf16[48,1536]{1,0:T(8,128)(2,1)S(1)}, u32[]{:S(2)}, u32[]{:S(2)}) collective-permute-start(bf16[48,1536]{1,0:T(8,128)(2,1)S(1)} %collective-permute-done.refs_0_), channel_id=1, source_target_pairs={{0,64},{32,96},{64,0},{96,32},{128,192},{160,224},{192,128},{224,1... | collective-permute-start | bytes 442376 | tf_op jit(solution)/shard_map/ppermute | solution.py:232
  52.5 4.7 %collective-permute-start.4 = (bf16[48,1536]{1,0:T(8,128)(2,1)S(1)}, bf16[48,1536]{1,0:T(8,128)(2,1)S(1)}, u32[]{:S(2)}, u32[]{:S(2)}) collective-permute-start(bf16[48,1536]{1,0:T(8,128)(2,1)S(1)} %collective-permute-done.refs_0_), channel_id=1, source_target_pairs={{0,32},{32,0},{64,96},{96,64},{128,160},{160,128},{192,224},{224,1... | collective-permute-start | bytes 442376 | tf_op jit(solution)/shard_map/ppermute | solution.py:232
  57.9 1.9 collective-permute-start.7
  59.8 2.4 %collective-permute-start.6 = (bf16[48,1536]{1,0:T(8,128)(2,1)S(1)}, bf16[48,1536]{1,0:T(8,128)(2,1)S(1)}, u32[]{:S(2)}, u32[]{:S(2)}) collective-permute-start(bf16[48,1536]{1,0:T(8,128)(2,1)S(1)} %collective-permute-done.2.refs_2_), channel_id=1, source_target_pairs={{0,32},{32,0},{64,96},{96,64},{128,160},{160,128},{192,224},{224,1... | collective-permute-start | bytes 442376 | tf_op jit(solution)/shard_map/ppermute | solution.py:232
  62.3 1.9 collective-permute-start.5
  67.0 4.9 %shard_map.92 = bf16[4,2,2,192,256]{4,3,2,1,0:T(8,128)(2,1)S(1)} custom-call(s32[26]{0:T(128)} %pad_add_fusion.2.place_ref, bf16[48,1536]{1,0:T(8,128)(2,1)} %copy-done.5, bf16[48,1536]{1,0:T(8,128)(2,1)} %copy-done.8, bf16[48,1536]{1,0:T(8,128)(2,1)} %copy-done.7, bf16[48,1536]{1,0:T(8,128)(2,1)} %copy-done.6, bf16[48,1536]{1,0:T(8,128)(2,1)} %copy-done.9, ...), custom_call_target="tpu_custom_call" | custom-call | tf_op jit(solution)/shard_map/pallas_call | solution.py:47
  71.9 15.3 %conditional.2 = (bf16[4,2,2,192,256]{4,3,2,1,0:T(8,128)(2,1)S(1)}) conditional(s32[]{:T(128)} %convert_element_type.39, bf16[4,2,2,192,256]{4,3,2,1,0:T(8,128)(2,1)S(1)} %shard_map.92, bf16[4,2,2,192,256]{4,3,2,1,0:T(8,128)(2,1)S(1)} %shard_map.92), branch_computations={%region_1.2_spmd, %region_2.3_spmd} | conditional | flops 786432 | bytes 7864328 | solution.py:269
  72.1 15.0 %all_to_all.41 = bf16[4,1,2,192,256]{4,3,2,1,0:T(8,128)(2,1)S(1)} all-to-all(bf16[4,1,2,192,256]{4,3,2,1,0:T(8,128)(2,1)S(1)} %get-tuple-element.51), channel_id=1, replica_groups=mesh['angle'=16,'slab'=4,'tile'=8] {'slab'}, dimensions={0} | all-to-all | bytes 1572864 | tf_op jit(solution)/shard_map/cond/branch_0_fun/all_to_all | solution.py:244
  87.2 4.4 %shard_map.93 = bf16[4,2,2,256,256]{4,3,2,1,0:T(8,128)(2,1)S(1)} custom-call(s32[2]{0:T(128)} %compare_convert_fusion.live_ref, bf16[4,2,2,192,256]{4,3,2,1,0:T(8,128)(2,1)} %copy-done, bf16[4,2,2,192,256]{4,3,2,1,0:T(8,128)(2,1)S(1)} %get-tuple-element.65.lowers, f32[2,256,256]{2,1,0:T(8,128)} %probe.1, bf16[2,256,256]{2,1,0:T(8,128)(2,1)} %bitcast.38, ...), custom_call_target="tpu_custom_call" | custom-call | tf_op jit(solution)/shard_map/pallas_call | solution.py:47
  91.6 13.9 %conditional.3 = (bf16[4,2,2,256,256]{4,3,2,1,0:T(8,128)(2,1)}) conditional(s32[]{:T(128)} %convert_element_type.39, bf16[4,2,2,256,256]{4,3,2,1,0:T(8,128)(2,1)S(1)} %shard_map.93, bf16[4,2,2,256,256]{4,3,2,1,0:T(8,128)(2,1)S(1)} %shard_map.93), branch_computations={%region_3.4_spmd, %region_4.5_spmd} | conditional | flops 1048576 | bytes 10485768 | solution.py:269
  91.8 12.2 %all_to_all.43 = bf16[4,1,2,256,256]{4,3,2,1,0:T(8,128)(2,1)S(1)} all-to-all(bf16[4,1,2,256,256]{4,3,2,1,0:T(8,128)(2,1)S(1)} %get-tuple-element.53), channel_id=1, replica_groups=mesh['angle'=16,'slab'=4,'tile'=8] {'slab'}, dimensions={0} | all-to-all | bytes 2097152 | tf_op jit(solution)/shard_map/cond/branch_0_fun/all_to_all | solution.py:244
  104.0 1.5 pad_maximum_fusion.1
  105.5 6.9 %shard_map.94 = (f32[192,1536]{1,0:T(8,128)}, f32[192,1536]{1,0:T(8,128)}, bf16[2,192,1536]{2,1,0:T(8,128)(2,1)}) custom-call(s32[25]{0:T(128)} %pad_add_fusion.1.place_ref, bf16[4,2,2,256,256]{4,3,2,1,0:T(8,128)(2,1)} %get-tuple-element.66.windows), custom_call_target="tpu_custom_call" | custom-call | tf_op jit(solution)/shard_map/pallas_call | solution.py:47
  112.4 17.7 %collective-permute-start.8 = (bf16[2,192,1536]{2,1,0:T(8,128)(2,1)}, bf16[2,192,1536]{2,1,0:T(8,128)(2,1)S(1)}, u32[]{:S(2)}, u32[]{:S(2)}) collective-permute-start(bf16[2,192,1536]{2,1,0:T(8,128)(2,1)} %get-tuple-element.47), channel_id=1, source_target_pairs={{0,32},{32,0},{64,96},{96,64},{128,160},{160,128},{192,224},{224,1... | collective-permute-start | bytes 3538952 | tf_op jit(solution)/shard_map/ppermute | solution.py:232
  130.1 2.7 %collective-permute-done.8 = bf16[2,192,1536]{2,1,0:T(8,128)(2,1)S(1)} collective-permute-done((bf16[2,192,1536]{2,1,0:T(8,128)(2,1)}, bf16[2,192,1536]{2,1,0:T(8,128)(2,1)S(1)}, u32[]{:S(2)}, u32[]{:S(2)}) %collective-permute-start.8) | collective-permute-done | bytes 1179680 | tf_op jit(solution)/shard_map/ppermute | solution.py:232
  134.2 17.7 %all_to_all.45 = bf16[4,48,1536]{2,1,0:T(8,128)(2,1)S(1)} all-to-all(bf16[4,48,1536]{2,1,0:T(8,128)(2,1)S(1)} %bitcast.37), channel_id=1, replica_groups={{0,64,128,192},{32,96,160,224},{256,320,384,448},{288,352,416,480},{1,6..., dimensions={0} | all-to-all | bytes 1179648 | tf_op jit(solution)/shard_map/all_to_all | solution.py:247
  152.0 3.5 %all-to-all-start.7 = ((bf16[4,48,1536]{2,1,0:T(8,128)(2,1)}), bf16[4,48,1536]{2,1,0:T(8,128)(2,1)S(1)}, u32[]{:S(2)}, u32[]{:S(2)}) async-start(bf16[4,48,1536]{2,1,0:T(8,128)(2,1)} %bitcast.14), calls=%async_computation.7 | async-start | bytes 1179648 | tf_op jit(solution)/shard_map/all_to_all | solution.py:247
  155.5 1.3 collective-permute-start.9
  156.8 17.2 %all-to-all-done.7 = bf16[4,48,1536]{2,1,0:T(8,128)(2,1)S(1)} async-done(((bf16[4,48,1536]{2,1,0:T(8,128)(2,1)}), bf16[4,48,1536]{2,1,0:T(8,128)(2,1)S(1)}, u32[]{:S(2)}, u32[]{:S(2)}) %all-to-all-start.7) | async-done | bytes 589856 | tf_op jit(solution)/shard_map/all_to_all | solution.py:247
  174.2 1.9 collective-permute-start.10
  176.1 7.9 %collective-permute-done.10 = bf16[48,1536]{1,0:T(8,128)(2,1)S(1)} collective-permute-done((bf16[48,1536]{1,0:T(8,128)(2,1)S(1)}, bf16[48,1536]{1,0:T(8,128)(2,1)S(1)}, u32[]{:S(2)}, u32[]{:S(2)}) %collective-permute-start.10) | collective-permute-done | bytes 147488 | tf_op jit(solution)/shard_map/ppermute | solution.py:232
  184.1 15.6 %all_to_all.46 = bf16[4,48,1536]{2,1,0:T(8,128)(2,1)S(1)} all-to-all(bf16[4,48,1536]{2,1,0:T(8,128)(2,1)S(1)} %broadcast_in_dim.7), channel_id=1, replica_groups={{0,64,128,192},{32,96,160,224},{256,320,384,448},{288,352,416,480},{1,6..., dimensions={0} | all-to-all | bytes 1179648 | tf_op jit(solution)/shard_map/all_to_all | solution.py:247
  199.6 9.8 %collective-permute-start.11 = (bf16[192,1536]{1,0:T(8,128)(2,1)S(1)}, bf16[192,1536]{1,0:T(8,128)(2,1)S(1)}, u32[]{:S(2)}, u32[]{:S(2)}) collective-permute-start(bf16[192,1536]{1,0:T(8,128)(2,1)S(1)} %bitcast.35), channel_id=1, source_target_pairs={{0,32},{32,0},{64,96},{96,64},{128,160},{160,128},{192,224},{224,1... | collective-permute-start | bytes 1769480 | tf_op jit(solution)/shard_map/ppermute | solution.py:232
  209.4 1.6 collective-permute-done.11.other_ref
  211.9 3.3 %shard_map.95 = f32[2,192,1536]{2,1,0:T(8,128)} custom-call(s32[1]{0:T(128)} %bitcast.core_ref, bf16[2,192,1536]{2,1,0:T(8,128)(2,1)} %bitcast.34, bf16[192,1536]{1,0:T(8,128)(2,1)} %bitcast.36, bf16[192,1536]{1,0:T(8,128)(2,1)} %copy-done.4), custom_call_target="tpu_custom_call" | custom-call | tf_op jit(solution)/shard_map/pallas_call | solution.py:47
  (61 shorter events, 10.8 us)
Async XLA Ops:
  2.0 10.1 %all-to-all-start.4 = ((s32[4,2,3]{2,1,0:T(2,128)}), s32[4,2,3]{2,1,0:T(2,128)S(1)}, u32[]{:S(2)}, u32[]{:S(2)}) async-start(s32[4,2,3]{2,1,0:T(2,128)} %broadcast_in_dim.6), calls=%async_computation.4 | async-start | bytes 8192 | tf_op jit(solution)/shard_map/all_to_all | solution.py:244
  7.8 24.5 %collective-permute-start = (bf16[48,1536]{1,0:T(8,128)(2,1)S(1)}, bf16[48,1536]{1,0:T(8,128)(2,1)S(1)}, u32[]{:S(2)}, u32[]{:S(2)}) collective-permute-start(bf16[48,1536]{1,0:T(8,128)(2,1)S(1)} %dynamic-slice_bitcast_fusion), channel_id=1, source_target_pairs={{1,448},{2,449},{3,450},{4,451},{5,452},{6,453},{7,454},{33,480},{... | collective-permute-start | bytes 442376 | tf_op jit(solution)/shard_map/ppermute | solution.py:241
  32.3 20.2 %copy-start.5 = (bf16[48,1536]{1,0:T(8,128)(2,1)}, bf16[48,1536]{1,0:T(8,128)(2,1)S(1)}, u32[]{:S(2)}) copy-start(bf16[48,1536]{1,0:T(8,128)(2,1)S(1)} %collective-permute-done.refs_0_) | copy-start | bytes 442372
  38.5 27.8 %all-to-all-start.5 = ((bf16[4,2,2,192,256]{4,3,2,1,0:T(8,128)(2,1)}), bf16[4,2,2,192,256]{4,3,2,1,0:T(8,128)(2,1)S(1)}, u32[]{:S(2)}, u32[]{:S(2)}) async-start(bf16[4,2,2,192,256]{4,3,2,1,0:T(8,128)(2,1)} %shard_map.91), calls=%async_computation.5 | async-start | bytes 3145728 | tf_op jit(solution)/shard_map/all_to_all | solution.py:244
  42.7 15.2 %collective-permute-start.3 = (bf16[48,1536]{1,0:T(8,128)(2,1)S(1)}, bf16[48,1536]{1,0:T(8,128)(2,1)S(1)}, u32[]{:S(2)}, u32[]{:S(2)}) collective-permute-start(bf16[48,1536]{1,0:T(8,128)(2,1)S(1)} %collective-permute-done.refs_0_), channel_id=1, source_target_pairs={{0,192},{32,224},{64,128},{96,160},{128,64},{160,96},{192,0},{224,... | collective-permute-start | bytes 442376 | tf_op jit(solution)/shard_map/ppermute | solution.py:232
  44.6 15.2 %collective-permute-start.2 = (bf16[48,1536]{1,0:T(8,128)(2,1)S(1)}, bf16[48,1536]{1,0:T(8,128)(2,1)S(1)}, u32[]{:S(2)}, u32[]{:S(2)}) collective-permute-start(bf16[48,1536]{1,0:T(8,128)(2,1)S(1)} %collective-permute-done.refs_0_), channel_id=1, source_target_pairs={{0,128},{32,160},{64,192},{96,224},{128,0},{160,32},{192,64},{224,... | collective-permute-start | bytes 442376 | tf_op jit(solution)/shard_map/ppermute | solution.py:232
  46.5 15.7 %collective-permute-start.1 = (bf16[48,1536]{1,0:T(8,128)(2,1)S(1)}, bf16[48,1536]{1,0:T(8,128)(2,1)S(1)}, u32[]{:S(2)}, u32[]{:S(2)}) collective-permute-start(bf16[48,1536]{1,0:T(8,128)(2,1)S(1)} %collective-permute-done.refs_0_), channel_id=1, source_target_pairs={{0,64},{32,96},{64,0},{96,32},{128,192},{160,224},{192,128},{224,1... | collective-permute-start | bytes 442376 | tf_op jit(solution)/shard_map/ppermute | solution.py:232
  52.5 13.7 %collective-permute-start.4 = (bf16[48,1536]{1,0:T(8,128)(2,1)S(1)}, bf16[48,1536]{1,0:T(8,128)(2,1)S(1)}, u32[]{:S(2)}, u32[]{:S(2)}) collective-permute-start(bf16[48,1536]{1,0:T(8,128)(2,1)S(1)} %collective-permute-done.refs_0_), channel_id=1, source_target_pairs={{0,32},{32,0},{64,96},{96,64},{128,160},{160,128},{192,224},{224,1... | collective-permute-start | bytes 442376 | tf_op jit(solution)/shard_map/ppermute | solution.py:232
  57.9 8.3 %copy-start.6 = (bf16[48,1536]{1,0:T(8,128)(2,1)}, bf16[48,1536]{1,0:T(8,128)(2,1)S(1)}, u32[]{:S(2)}) copy-start(bf16[48,1536]{1,0:T(8,128)(2,1)S(1)} %collective-permute-done.3.refs_3_) | copy-start | bytes 442372
  57.9 8.3 %collective-permute-start.7 = (bf16[48,1536]{1,0:T(8,128)(2,1)S(1)}, bf16[48,1536]{1,0:T(8,128)(2,1)S(1)}, u32[]{:S(2)}, u32[]{:S(2)}) collective-permute-start(bf16[48,1536]{1,0:T(8,128)(2,1)S(1)} %collective-permute-done.3.refs_3_), channel_id=1, source_target_pairs={{0,32},{32,0},{64,96},{96,64},{128,160},{160,128},{192,224},{224,1... | collective-permute-start | bytes 442376 | tf_op jit(solution)/shard_map/ppermute | solution.py:232
  59.8 6.4 %copy-start.7 = (bf16[48,1536]{1,0:T(8,128)(2,1)}, bf16[48,1536]{1,0:T(8,128)(2,1)S(1)}, u32[]{:S(2)}) copy-start(bf16[48,1536]{1,0:T(8,128)(2,1)S(1)} %collective-permute-done.2.refs_2_) | copy-start | bytes 442372
  59.8 6.3 %collective-permute-start.6 = (bf16[48,1536]{1,0:T(8,128)(2,1)S(1)}, bf16[48,1536]{1,0:T(8,128)(2,1)S(1)}, u32[]{:S(2)}, u32[]{:S(2)}) collective-permute-start(bf16[48,1536]{1,0:T(8,128)(2,1)S(1)} %collective-permute-done.2.refs_2_), channel_id=1, source_target_pairs={{0,32},{32,0},{64,96},{96,64},{128,160},{160,128},{192,224},{224,1... | collective-permute-start | bytes 442376 | tf_op jit(solution)/shard_map/ppermute | solution.py:232
  62.3 4.0 %copy-start.8 = (bf16[48,1536]{1,0:T(8,128)(2,1)}, bf16[48,1536]{1,0:T(8,128)(2,1)S(1)}, u32[]{:S(2)}) copy-start(bf16[48,1536]{1,0:T(8,128)(2,1)S(1)} %collective-permute-done.1.refs_1_) | copy-start | bytes 442372
  62.3 3.9 %collective-permute-start.5 = (bf16[48,1536]{1,0:T(8,128)(2,1)S(1)}, bf16[48,1536]{1,0:T(8,128)(2,1)S(1)}, u32[]{:S(2)}, u32[]{:S(2)}) collective-permute-start(bf16[48,1536]{1,0:T(8,128)(2,1)S(1)} %collective-permute-done.1.refs_1_), channel_id=1, source_target_pairs={{0,32},{32,0},{64,96},{96,64},{128,160},{160,128},{192,224},{224,1... | collective-permute-start | bytes 442376 | tf_op jit(solution)/shard_map/ppermute | solution.py:232
  66.2 0.7 copy-start.9
  66.2 0.7 copy-start.10
  66.2 0.8 copy-start.11
  66.2 0.8 copy-start.12
  67.0 4.9 %copy-start = (bf16[4,2,2,192,256]{4,3,2,1,0:T(8,128)(2,1)}, bf16[4,2,2,192,256]{4,3,2,1,0:T(8,128)(2,1)S(1)}, u32[]{:S(2)}) copy-start(bf16[4,2,2,192,256]{4,3,2,1,0:T(8,128)(2,1)S(1)} %all-to-all-done.5.uppers) | copy-start | bytes 4718596
  112.4 20.6 %copy-start.2 = (f32[192,1536]{1,0:T(8,128)S(1)}, f32[192,1536]{1,0:T(8,128)}, u32[]{:S(2)}) copy-start(f32[192,1536]{1,0:T(8,128)} %get-tuple-element.48) | copy-start | bytes 3538948
  112.4 20.6 %copy-start.3 = (f32[192,1536]{1,0:T(8,128)S(1)}, f32[192,1536]{1,0:T(8,128)}, u32[]{:S(2)}) copy-start(f32[192,1536]{1,0:T(8,128)} %get-tuple-element.46) | copy-start | bytes 3538948
  112.4 20.3 %collective-permute-start.8 = (bf16[2,192,1536]{2,1,0:T(8,128)(2,1)}, bf16[2,192,1536]{2,1,0:T(8,128)(2,1)S(1)}, u32[]{:S(2)}, u32[]{:S(2)}) collective-permute-start(bf16[2,192,1536]{2,1,0:T(8,128)(2,1)} %get-tuple-element.47), channel_id=1, source_target_pairs={{0,32},{32,0},{64,96},{96,64},{128,160},{160,128},{192,224},{224,1... | collective-permute-start | bytes 3538952 | tf_op jit(solution)/shard_map/ppermute | solution.py:232
  152.0 22.0 %all-to-all-start.7 = ((bf16[4,48,1536]{2,1,0:T(8,128)(2,1)}), bf16[4,48,1536]{2,1,0:T(8,128)(2,1)S(1)}, u32[]{:S(2)}, u32[]{:S(2)}) async-start(bf16[4,48,1536]{2,1,0:T(8,128)(2,1)} %bitcast.14), calls=%async_computation.7 | async-start | bytes 1179648 | tf_op jit(solution)/shard_map/all_to_all | solution.py:247
  155.5 18.6 %collective-permute-start.9 = (bf16[48,1536]{1,0:T(8,128)(2,1)S(1)}, bf16[48,1536]{1,0:T(8,128)(2,1)S(1)}, u32[]{:S(2)}, u32[]{:S(2)}) collective-permute-start(bf16[48,1536]{1,0:T(8,128)(2,1)S(1)} %reduce_sum.21), channel_id=1, source_target_pairs={{0,449},{1,450},{2,451},{3,452},{4,453},{5,454},{6,455},{32,481},{... | collective-permute-start | bytes 442376 | tf_op jit(solution)/shard_map/ppermute | solution.py:241
  174.2 9.8 %collective-permute-start.10 = (bf16[48,1536]{1,0:T(8,128)(2,1)S(1)}, bf16[48,1536]{1,0:T(8,128)(2,1)S(1)}, u32[]{:S(2)}, u32[]{:S(2)}) collective-permute-start(bf16[48,1536]{1,0:T(8,128)(2,1)S(1)} %add_convert_fusion.1), channel_id=1, source_target_pairs={{0,256},{32,288},{64,320},{96,352},{128,384},{160,416},{192,448},{... | collective-permute-start | bytes 442376 | tf_op jit(solution)/shard_map/ppermute | solution.py:232
  199.6 11.5 %copy-start.1 = (bf16[4,48,1536]{2,1,0:T(8,128)(2,1)}, bf16[4,48,1536]{2,1,0:T(8,128)(2,1)S(1)}, u32[]{:S(2)}) copy-start(bf16[4,48,1536]{2,1,0:T(8,128)(2,1)S(1)} %all_to_all.46) | copy-start | bytes 1769476
  199.6 11.5 %collective-permute-start.11 = (bf16[192,1536]{1,0:T(8,128)(2,1)S(1)}, bf16[192,1536]{1,0:T(8,128)(2,1)S(1)}, u32[]{:S(2)}, u32[]{:S(2)}) collective-permute-start(bf16[192,1536]{1,0:T(8,128)(2,1)S(1)} %bitcast.35), channel_id=1, source_target_pairs={{0,32},{32,0},{64,96},{96,64},{128,160},{160,128},{192,224},{224,1... | collective-permute-start | bytes 1769480 | tf_op jit(solution)/shard_map/ppermute | solution.py:232
  211.1 0.8 copy-start.4

commit v5 on v4

v5 whole, which is shorter than its diff:
```python
import functools

import jax
import jax.numpy as jnp
import ml_dtypes
import numpy as np
from jax import lax
from jax.experimental import pallas as pl
from jax.experimental.pallas import tpu as pltpu
from jax.sharding import PartitionSpec as P

angle_center = 600
shear_divisor = 64
step_size = 0.03
floor_square = 0.25

LANE = 128
HALO = 64


def dft_tables(plane_width):
    index_line = np.arange(plane_width, dtype=np.int32)
    product_mod = np.mod(index_line[:, None] * index_line[None, :], plane_width)
    phase_table = product_mod.astype(np.float32) * np.float32(2.0 * 3.141592653589793 / plane_width)
    scale_factor = np.float32(plane_width ** (-0.5))
    table_real = (np.cos(phase_table) * scale_factor).astype(ml_dtypes.bfloat16)
    table_imag = (-np.sin(phase_table) * scale_factor).astype(ml_dtypes.bfloat16)
    return table_real, table_imag


def dot(left, right):
    return jnp.dot(left, right, preferred_element_type=jnp.float32)


def one_hot(rows, columns, down):
    row = lax.broadcasted_iota(jnp.int32, (rows, columns), 0)
    column = lax.broadcasted_iota(jnp.int32, (rows, columns), 1)
    return (row - column == down).astype(jnp.float32).astype(jnp.bfloat16)


HBM = pl.BlockSpec(memory_space=pltpu.HBM)


def call(body, out_shape, scratch, facts, *args):
    return pl.pallas_call(
        body,
        out_shape=out_shape,
        in_specs=[pl.BlockSpec(memory_space=pltpu.SMEM)] + [HBM] * len(args),
        out_specs=[HBM] * len(out_shape),
        scratch_shapes=scratch,
        compiler_params=pltpu.CompilerParams(vmem_limit_bytes=56 * 1024 * 1024),
    )(facts, *args)


class Facts:
    def __init__(self, ref, slabs, slots):
        self.ref, self.slots = ref, slots
        self.shift, self.core, self.place_z = (ref[3 * slabs * slots + i] for i in range(3))

    def slot(self, slab, slot):
        return tuple(self.ref[3 * (slab * self.slots + slot) + i] for i in range(3))


def column_blocks(left, width, columns):
    blocks = columns // LANE
    return [
        pl.multiple_of(lax.rem(left // LANE + i, blocks) * LANE, LANE) for i in range(width // LANE + 1)
    ]


def cut_body(down, facts_ref, *refs):
    blocks, (out, held, made, in_sems, out_sems) = refs[:-5], refs[-5:]
    slabs, slots, _, rows, width = out.shape
    tile_rows, columns = held.shape[1:]
    facts = Facts(facts_ref, slabs, slots)
    if len(blocks) == 1:
        copies = [pltpu.make_async_copy(blocks[0], held, in_sems.at[0])]
    else:
        *mine, other = blocks
        size = tile_rows // len(mine)
        copies = []
        for k, block in enumerate(mine):
            at = pl.ds(pl.multiple_of((facts.place_z ^ k) * size, size), size)
            copies.append(pltpu.make_async_copy(block, held.at[facts.core, at], in_sems.at[2 * k]))
            copies.append(
                pltpu.make_async_copy(other.at[k], held.at[1 - facts.core, at], in_sems.at[2 * k + 1])
            )
    for copy in copies:
        copy.start()
    for copy in copies:
        copy.wait()

    def written(slab, slot):
        return pltpu.make_async_copy(
            made.at[slab, slot], out.at[slab, slot], out_sems.at[slab, slot]
        )

    each = [(slab, slot) for slot in range(slots) for slab in range(slabs)]
    for slab, slot in each:
        row, column, live = facts.slot(slab, slot)

        @pl.when(live > 0)
        def _():
            left = lax.rem(column + facts.shift, columns)
            pick_rows = one_hot(rows, tile_rows, -(row + down))
            pick_columns = one_hot(width + LANE, width, lax.rem(left, LANE))
            wide = jnp.concatenate(
                [held[:, :, pl.ds(start, LANE)] for start in column_blocks(left, width, columns)], axis=2
            )
            narrow = dot(wide.reshape(2 * tile_rows, width + LANE), pick_columns).astype(jnp.bfloat16)
            for part in range(2):
                picked = dot(pick_rows, narrow[part * tile_rows : (part + 1) * tile_rows])
                made[slab, slot, part] = picked.astype(jnp.bfloat16)
            written(slab, slot).start()

    for slab, slot in each:

        @pl.when(facts.slot(slab, slot)[2] > 0)
        def _():
            written(slab, slot).wait()


def cut_windows(facts, slabs, slots, down, blocks, rows, width):
    shape = (slabs, slots, 2, rows, width)
    columns = blocks[0].shape[-1]
    tile_rows = blocks[0].shape[1] if len(blocks) == 1 else blocks[0].shape[0] * (len(blocks) - 1)
    scratch = [
        pltpu.VMEM((2, tile_rows, columns), jnp.bfloat16),
        pltpu.VMEM(shape, jnp.bfloat16),
        pltpu.SemaphoreType.DMA((2 * len(blocks),)),
        pltpu.SemaphoreType.DMA((slabs, slots)),
    ]
    out = jax.ShapeDtypeStruct(shape, jnp.bfloat16)
    return call(functools.partial(cut_body, down), [out], scratch, facts, *blocks)[0]


def cos_sin(angle):
    turns = jnp.round(angle * 0.6366197723675814)
    rest = angle - turns * 1.5703125
    rest = rest - turns * 4.837512969970703e-4
    rest = rest - turns * 7.549789948768648e-8
    square = rest * rest
    sine = (-1.9515295891e-4 * square + 8.3321608736e-3) * square - 1.6666654611e-1
    sine = sine * square * rest + rest
    cosine = (2.443315711809948e-5 * square - 1.388731625493765e-3) * square + 4.166664568298827e-2
    cosine = cosine * square * square - 0.5 * square + 1.0
    quarter = turns.astype(jnp.int32)
    odd = (quarter & 1) == 1
    first, second = jnp.where(odd, sine, cosine), jnp.where(odd, cosine, sine)
    return (
        jnp.where(((quarter + 1) & 2) == 2, -first, first),
        jnp.where((quarter & 2) == 2, -second, second),
    )


def patch_body(
    live_ref, uppers, lowers, probe_in, patterns_in, wr_in, wi_in,
    out, upper, lower, probe, patterns, wr_ref, wi_ref, made, in_sems, slot_sems, out_sems,
):
    slabs, slots, _, rows, _ = uppers.shape
    f32, bf16 = jnp.float32, jnp.bfloat16

    def arrive(slot):
        return [
            pltpu.make_async_copy(ref.at[:, slot], to.at[slot], slot_sems.at[slot, n])
            for n, (ref, to) in enumerate(((uppers, upper), (lowers, lower)))
        ] + [pltpu.make_async_copy(patterns_in.at[slot], patterns.at[slot], slot_sems.at[slot, 2])]

    def leave(slot):
        return [
            pltpu.make_async_copy(made.at[slot], out.at[slab, slot], out_sems.at[slab, slot])
            for slab in range(slabs)
        ]

    common = [
        pltpu.make_async_copy(ref, to, in_sems.at[n])
        for n, (ref, to) in enumerate(((probe_in, probe), (wr_in, wr_ref), (wi_in, wi_ref)))
    ]
    for slot in range(slots):

        @pl.when(live_ref[slot] > 0)
        def _():
            for copy in arrive(slot):
                copy.start()

        if slot == 0:
            for copy in common:
                copy.start()
    for copy in common:
        copy.wait()

    def window(slot, part):
        def projected(ref):
            return sum(ref[slot, slab, part].astype(f32) for slab in range(slabs)).astype(bf16).astype(f32)

        above, below = projected(upper), projected(lower)
        return jnp.concatenate(
            [above[:HALO], above[HALO:] + below[: rows - HALO], below[rows - HALO :]], axis=0
        )

    for slot in range(slots):

        @pl.when(live_ref[slot] > 0)
        def _():
            for copy in arrive(slot):
                copy.wait()
            phase, absorption = window(slot, 0), window(slot, 1)
            magnitude = jnp.exp(-absorption)
            cosine, sine = cos_sin(phase)
            trans_real = magnitude * cosine
            trans_imag = magnitude * sine
            probe_real, probe_imag = probe[0], probe[1]
            wr, wi = wr_ref[...], wi_ref[...]
            wave_real = (probe_real * trans_real - probe_imag * trans_imag).astype(bf16)
            wave_imag = (probe_real * trans_imag + probe_imag * trans_real).astype(bf16)
            left_real = (dot(wr, wave_real) - dot(wi, wave_imag)).astype(bf16)
            left_imag = (dot(wr, wave_imag) + dot(wi, wave_real)).astype(bf16)
            far_real = dot(left_real, wr) - dot(left_imag, wi)
            far_imag = dot(left_real, wi) + dot(left_imag, wr)
            power = far_real * far_real + far_imag * far_imag + floor_square
            keeping = 1.0 - patterns[slot].astype(f32) * lax.rsqrt(power)
            resid_real = (far_real * keeping).astype(bf16)
            resid_imag = (far_imag * keeping).astype(bf16)
            back_real = (dot(wr, resid_real) + dot(wi, resid_imag)).astype(bf16)
            back_imag = (dot(wr, resid_imag) - dot(wi, resid_real)).astype(bf16)
            exit_real = dot(back_real, wr) + dot(back_imag, wi)
            exit_imag = dot(back_imag, wr) - dot(back_real, wi)
            mixed_real = probe_real * exit_real + probe_imag * exit_imag
            mixed_imag = probe_real * exit_imag - probe_imag * exit_real
            made[slot, 0] = (trans_real * mixed_imag - trans_imag * mixed_real).astype(bf16)
            made[slot, 1] = (-(trans_real * mixed_real + trans_imag * mixed_imag)).astype(bf16)
            for copy in leave(slot):
                copy.start()

    for slot in range(slots):

        @pl.when(live_ref[slot] > 0)
        def _():
            for copy in leave(slot):
                copy.wait()


def patch_gradients(live, uppers, lowers, probe_wave, patterns, tables):
    slabs, slots, _, rows, width = uppers.shape
    bf16 = jnp.bfloat16
    scratch = [
        pltpu.VMEM((slots, slabs, 2, rows, width), bf16),
        pltpu.VMEM((slots, slabs, 2, rows, width), bf16),
        pltpu.VMEM(probe_wave.shape, jnp.float32),
        pltpu.VMEM(patterns.shape, bf16),
        pltpu.VMEM((width, width), bf16),
        pltpu.VMEM((width, width), bf16),
        pltpu.VMEM((slots, 2, width, width), bf16),
        pltpu.SemaphoreType.DMA((3,)),
        pltpu.SemaphoreType.DMA((slots, 3)),
        pltpu.SemaphoreType.DMA((slabs, slots)),
    ]
    out = jax.ShapeDtypeStruct((slabs, slots, 2, width, width), bf16)
    return call(patch_body, [out], scratch, live, uppers, lowers, probe_wave, patterns, *tables)[0]


def place_body(
    first_row, reverse, facts_ref, windows, keep_out, send_out, total, patches, send, in_sems, out_sems
):
    slabs, slots, _, width, _ = windows.shape
    rows = patches.shape[3]
    tile_rows, columns = keep_out.shape
    facts = Facts(facts_ref, slabs, slots)
    down = first_row - (tile_rows if first_row else 0)
    each = [(slab, slot) for slot in range(slots) for slab in range(slabs)]

    def arrive(slab, slot):
        return pltpu.make_async_copy(
            windows.at[slab, slot, :, pl.ds(first_row, rows)], patches.at[slab, slot], in_sems.at[slab, slot]
        )

    for slab, slot in each:

        @pl.when(facts.slot(slab, slot)[2] > 0)
        def _():
            arrive(slab, slot).start()

    total[...] = jnp.zeros_like(total)
    for slab, slot in each:
        row, column, live = facts.slot(slab, slot)

        @pl.when(live > 0)
        def _():
            arrive(slab, slot).wait()
            left = lax.rem(column + facts.shift, columns)
            put_rows = one_hot(tile_rows, rows, row + down)
            put_columns = one_hot(width, width + LANE, -lax.rem(left, LANE))
            moved = [dot(put_rows, patches[slab, slot, part]).astype(jnp.bfloat16) for part in range(2)]
            wide = dot(jnp.concatenate(moved, axis=0), put_columns)
            wide = wide.reshape(2, tile_rows, width + LANE)
            for i, start in enumerate(column_blocks(left, width, columns)):
                total[:, :, pl.ds(start, LANE)] += wide[:, :, i * LANE : (i + 1) * LANE]

    send[...] = total[1 - facts.core].astype(jnp.bfloat16)
    blocks = 4 if reverse else 1
    size = tile_rows // blocks
    copies = []
    for block in range(blocks):
        here, there = pl.ds(block * size, size), pl.ds((blocks - 1 - block) * size, size)
        copies.append(pltpu.make_async_copy(send.at[here], send_out.at[there], out_sems.at[0, block]))
        copies.append(
            pltpu.make_async_copy(total.at[facts.core, here], keep_out.at[there], out_sems.at[1, block])
        )
    for copy in copies:
        copy.start()
    for copy in copies:
        copy.wait()


def place_windows(facts, windows, first_row, reverse, rows, tile_rows, columns):
    slabs, slots, _, width, _ = windows.shape
    scratch = [
        pltpu.VMEM((2, tile_rows, columns), jnp.float32),
        pltpu.VMEM((slabs, slots, 2, rows, width), jnp.bfloat16),
        pltpu.VMEM((tile_rows, columns), jnp.bfloat16),
        pltpu.SemaphoreType.DMA((slabs, slots)),
        pltpu.SemaphoreType.DMA((2, 4)),
    ]
    shapes = [jax.ShapeDtypeStruct((tile_rows, columns), t) for t in (jnp.float32, jnp.bfloat16)]
    return call(functools.partial(place_body, first_row, reverse), shapes, scratch, facts, windows)


def step_body(part_ref, layer_ref, gradient_ref, *refs):
    refs[-1][...] = layer_ref[...].astype(jnp.float32) - step_size * gradient_ref[...].astype(jnp.float32)


def step(part, layer, gradient, *stepped):
    block = gradient.shape[0] // 4
    columns = gradient.shape[1]
    of_part = pl.BlockSpec((None, block, columns), lambda i, part_ref: (part_ref[0], i, 0))
    return pl.pallas_call(
        step_body,
        grid_spec=pltpu.PrefetchScalarGridSpec(
            num_scalar_prefetch=1,
            grid=(4,),
            in_specs=[of_part, pl.BlockSpec((block, columns), lambda i, part_ref: (i, 0))]
            + [pl.BlockSpec(memory_space=pl.ANY)] * len(stepped),
            out_specs=of_part,
        ),
        out_shape=jax.ShapeDtypeStruct(layer.shape, jnp.float32),
        input_output_aliases={3: 0} if stepped else {},
    )(part.reshape(1).astype(jnp.int32), layer, gradient, *stepped)


def per_device(volume, probe_wave, amplitudes, offsets, column_starts, counts, angle_ids):
    layer = volume.reshape(volume.shape[0], *volume.shape[2:])
    tile_rows, columns = layer.shape[1:]
    width = amplitudes.shape[-1]
    slots = offsets.shape[3]
    angles, slabs, tiles = (lax.axis_size(axis) for axis in ("angle", "slab", "tile"))
    slab, angle = lax.axis_index("slab"), lax.axis_index("angle")
    f32, bf16 = jnp.float32, jnp.bfloat16
    tables = dft_tables(width)
    window_rows = width - HALO
    patterns = amplitudes.reshape(slots, width, width)

    core, place_z = angle % 2, angle // 2 % 4
    four_groups = [[8 * f + 2 * q + c for q in range(4)] for f in range(angles // 8) for c in range(2)]
    block_rows = tile_rows // 4

    def swap(value, by):
        return lax.ppermute(value, "angle", [(i, i ^ by) for i in range(angles)])

    def mirrored(value, by):
        pairs = [
            (a * tiles + t, (angles - 2 - (a - a % 2) + a % 2) * tiles + t + by)
            for a in range(angles)
            for t in range(tiles)
            if 0 <= t + by < tiles
        ]
        return lax.ppermute(value, ("angle", "tile"), pairs)

    def to_slabs(value):
        return lax.all_to_all(value, "slab", 0, 0, tiled=True)

    def to_four(value):
        return lax.all_to_all(value, "angle", 0, 0, axis_index_groups=four_groups, tiled=True)

    def added(blocks):
        return jnp.sum(to_four(blocks).astype(f32), axis=0)

    own_part = lax.dynamic_index_in_dim(layer, core, 0, keepdims=False)
    after = lax.dynamic_slice(own_part, ((3 - place_z) * block_rows, 0), (block_rows, columns))
    live = (jnp.arange(slots) < counts.reshape(1)).astype(jnp.int32)
    meta = jnp.stack([offsets.reshape(slots), column_starts.reshape(slots), live], axis=1)
    after, meta = lax.optimization_barrier((after, jnp.broadcast_to(meta, (slabs, *meta.shape))))
    after = mirrored(after, -1)
    group = to_slabs(meta)
    more = jnp.max(group[:, 1:, 2]) > 0
    sheared = jnp.floor_divide((angle_ids[0] - angle_center) * (slab - slabs // 2), shear_divisor)
    others = jnp.stack([jnp.mod(sheared, columns), core, place_z])
    facts = jnp.concatenate([group.reshape(-1), others]).astype(jnp.int32)

    def exchanged(values):
        return lax.cond(
            more,
            to_slabs,
            lambda v: jnp.concatenate([to_slabs(v[:, :1]), v[:, 1:]], axis=1),
            values,
        )

    uppers = cut_windows(facts, slabs, slots, 0, [layer], window_rows, width)
    after, uppers = lax.optimization_barrier((after, uppers))
    uppers = to_slabs(uppers)
    mine = [after] + [swap(after, k << 1) for k in range(1, 4)]
    afters = mine + [swap(jnp.stack(mine), 1)]
    afters, uppers = lax.optimization_barrier((afters, uppers))
    lowers = cut_windows(facts, slabs, slots, HALO - tile_rows, afters, window_rows, width)
    lowers = exchanged(lowers)

    gradients = exchanged(patch_gradients(live, uppers, lowers, probe_wave, patterns, tables))

    def placed(first_row, reverse):
        keep, send = place_windows(facts, gradients, first_row, reverse, window_rows, tile_rows, columns)
        return (keep + swap(send, 1).astype(f32)).astype(bf16).reshape(4, block_rows, columns)

    spill, own = placed(HALO, True), placed(0, False)
    spill, own = lax.optimization_barrier((added(spill).astype(bf16), own))
    spill = mirrored(spill, 1)
    total = lax.optimization_barrier((added(own) + spill.astype(f32)).astype(bf16))
    total = (total.astype(f32) + swap(total, 8).astype(f32)).astype(bf16)

    total = to_four(jnp.broadcast_to(total, (4, *total.shape))).reshape(tile_rows, columns)
    new = step(core, layer, total)
    return step(1 - core, layer, swap(total, 1), new).reshape(volume.shape)


def solution(mesh):
    in_specs = (
        P(None, "slab", "tile", None),
        P(),
        P("angle", "tile", "slab", None, None, None),
        P("angle", "tile", "slab", None),
        P("angle", "tile", "slab", None),
        P("angle", "tile", "slab"),
        P("angle"),
    )
    out_specs = P(None, "slab", "tile", None)
    return jax.shard_map(
        per_device, mesh=mesh, in_specs=in_specs, out_specs=out_specs, check_vma=False
    )
```

time: 216 us -> 207 us (0.958)
  blocking collectives: 60.5 us -> 43.1 us
  Pallas kernels: 24.9 us -> 31.2 us
  local copies, waits for them, and re-layouts: 6.64 us -> 3.67 us
  waiting for transfers between devices: 49.5 us -> 52 us
  other arithmetic: 6.68 us -> 9.08 us
    all_to_all x2 -> x1, blocking collectives: 33.3 us -> 15.5 us  [to_four(): lax.all_to_all(value, 'angle', 0, 0, axis_index_groups=four_groups, tiled...]
    ppermute x2, waiting for transfers between devices: 20.1 us -> 9.4 us  [mirrored(): return lax.ppermute(value, ('angle', 'tile'), pairs)]
    pallas_call x5 -> x7, Pallas kernels: 24.9 us -> 31.2 us  [the longest x5 24.2 us: call(): pl.pallas_call(body, out_shape=out_shape, in_specs=[pl.BlockSpec(memory_s...]
    ppermute x10 -> x8, waiting for transfers between devices: 12.2 us -> 17.9 us  [swap(): return lax.ppermute(value, 'angle', [(i, i ^ by) for i in range(angles)])]
    ppermute x10 -> x8, starting transfers between devices: 49.6 us -> 44.7 us  [swap(): return lax.ppermute(value, 'angle', [(i, i ^ by) for i in range(angles)])]
    all_to_all x1 -> x2, waiting for transfers between devices: 17.2 us -> 21.3 us  [to_four(): lax.all_to_all(value, 'angle', 0, 0, axis_index_groups=four_groups, tiled...]
    all_to_all x1 -> x2, starting transfers between devices: 3.49 us -> 6.96 us  [to_four(): lax.all_to_all(value, 'angle', 0, 0, axis_index_groups=four_groups, tiled...]
    all_to_all x2, waiting for transfers between devices: 0.01 us -> 3.46 us  [to_slabs(): return lax.all_to_all(value, 'slab', 0, 0, tiled=True)]
  transfers between devices with their start and end apart: 15 -> 14, of which waited for: 5 -> 8; matrix products, arithmetic and copies ran while one was open for 3% -> 2% of each run, Pallas kernels for 0% -> 6%
where the time goes in v5:
time: 207 us; the launch traced here: 205 us
  starting transfers between devices  63.1 us (30%)
  waiting for transfers between devices  52 us (25%)
  blocking collectives  43.1 us (21%)
  Pallas kernels  31.2 us (15%)
  other arithmetic  9.08 us (4%)
  local copies, waits for them, and re-layouts  3.67 us (2%)
  between operations  2.26 us (1%)
    ppermute x8, starting transfers between devices, swap(): return lax.ppermute(value, 'angle', [(i, i ^ by) for i in range(angles)])  44.7 us
    all_to_all x2, blocking collectives, to_slabs(): return lax.all_to_all(value, 'slab', 0, 0, tiled=True)  27.6 us
    pallas_call x5, Pallas kernels, call(): pl.pallas_call(body, out_shape=out_shape, in_specs=[pl.BlockSpec(memory_s...  24.2 us
    all_to_all x2, waiting for transfers between devices, to_four(): lax.all_to_all(value, 'angle', 0, 0, axis_index_groups=four_groups, tiled...  21.3 us
    ppermute x8, waiting for transfers between devices, swap(): return lax.ppermute(value, 'angle', [(i, i ^ by) for i in range(angles)])  17.9 us
    all_to_all x1, blocking collectives, to_four(): lax.all_to_all(value, 'angle', 0, 0, axis_index_groups=four_groups, tiled...  15.5 us
    ppermute x2, waiting for transfers between devices, mirrored(): return lax.ppermute(value, ('angle', 'tile'), pairs)  9.4 us
    all_to_all x2, starting transfers between devices, to_slabs(): return lax.all_to_all(value, 'slab', 0, 0, tiled=True)  8.87 us
  transfers between devices with their start and end apart: 14, of which 8 were waited for; matrix products, arithmetic and copies ran while one was open for 2% of the time, Pallas kernels for 6%

profile of v5, /device:TPU:1, one launch (start us, length us, event | category | flops | bytes accessed | tf_op | source)
XLA Modules:
  0.0 204.5 jit_solution(4810669797949733594)
XLA Ops:
  4.3 4.9 %all-to-all-start.4 = ((s32[4,2,3]{2,1,0:T(2,128)}), s32[4,2,3]{2,1,0:T(2,128)S(1)}, u32[]{:S(2)}, u32[]{:S(2)}) async-start(s32[4,2,3]{2,1,0:T(2,128)} %broadcast_in_dim.6), calls=%async_computation.4 | async-start | bytes 8192 | tf_op jit(solution)/shard_map/all_to_all | solution.py:379
  9.8 3.5 %all-to-all-done.4 = s32[4,2,3]{2,1,0:T(2,128)S(1)} async-done(((s32[4,2,3]{2,1,0:T(2,128)}), s32[4,2,3]{2,1,0:T(2,128)S(1)}, u32[]{:S(2)}, u32[]{:S(2)}) %all-to-all-start.4) | async-done | bytes 128 | tf_op jit(solution)/shard_map/all_to_all | solution.py:379
  14.0 4.9 %shard_map.91 = bf16[4,2,2,192,256]{4,3,2,1,0:T(8,128)(2,1)} custom-call(s32[27]{0:T(128)} %pad_add_fusion.1.facts_ref, bf16[2,192,1536]{2,1,0:T(8,128)(2,1)} %bitcast.24), custom_call_target="tpu_custom_call" | custom-call | tf_op jit(solution)/shard_map/pallas_call | solution.py:45
  18.9 9.4 %collective-permute-done.refs_0_ = bf16[48,1536]{1,0:T(8,128)(2,1)S(1)} collective-permute-done((bf16[48,1536]{1,0:T(8,128)(2,1)S(1)}, bf16[48,1536]{1,0:T(8,128)(2,1)S(1)}, u32[]{:S(2)}, u32[]{:S(2)}) %collective-permute-start) | collective-permute-done | bytes 147488 | tf_op jit(solution)/shard_map/ppermute | solution.py:376
  28.3 4.0 %all-to-all-start.5 = ((bf16[4,2,2,192,256]{4,3,2,1,0:T(8,128)(2,1)}), bf16[4,2,2,192,256]{4,3,2,1,0:T(8,128)(2,1)S(1)}, u32[]{:S(2)}, u32[]{:S(2)}) async-start(bf16[4,2,2,192,256]{4,3,2,1,0:T(8,128)(2,1)} %shard_map.91), calls=%async_computation.5 | async-start | bytes 3145728 | tf_op jit(solution)/shard_map/all_to_all | solution.py:379
  32.3 1.9 collective-permute-start.1
  34.2 1.9 collective-permute-start.2
  36.2 5.4 %collective-permute-start.3 = (bf16[48,1536]{1,0:T(8,128)(2,1)S(1)}, bf16[48,1536]{1,0:T(8,128)(2,1)S(1)}, u32[]{:S(2)}, u32[]{:S(2)}) collective-permute-start(bf16[48,1536]{1,0:T(8,128)(2,1)S(1)} %collective-permute-done.refs_0_), channel_id=1, source_target_pairs={{0,192},{32,224},{64,128},{96,160},{128,64},{160,96},{192,0},{224,... | collective-permute-start | bytes 442376 | tf_op jit(solution)/shard_map/ppermute | solution.py:367
  41.6 6.3 %collective-permute-done.2.refs_2_ = bf16[48,1536]{1,0:T(8,128)(2,1)S(1)} collective-permute-done((bf16[48,1536]{1,0:T(8,128)(2,1)S(1)}, bf16[48,1536]{1,0:T(8,128)(2,1)S(1)}, u32[]{:S(2)}, u32[]{:S(2)}) %collective-permute-start.2) | collective-permute-done | bytes 147488 | tf_op jit(solution)/shard_map/ppermute | solution.py:367
  48.1 4.9 %collective-permute-start.4 = (bf16[4,48,1536]{2,1,0:T(8,128)(2,1)S(1)}, bf16[4,48,1536]{2,1,0:T(8,128)(2,1)S(1)}, u32[]{:S(2)}, u32[]{:S(2)}) collective-permute-start(bf16[4,48,1536]{2,1,0:T(8,128)(2,1)S(1)} %pad_maximum_fusion.2), channel_id=1, source_target_pairs={{0,32},{32,0},{64,96},{96,64},{128,160},{160,128},{192,224},{224,1... | collective-permute-start | bytes 1769480 | tf_op jit(solution)/shard_map/ppermute | solution.py:367
  55.7 5.4 %shard_map.92 = bf16[4,2,2,192,256]{4,3,2,1,0:T(8,128)(2,1)S(1)} custom-call(s32[27]{0:T(128)} %pad_add_fusion.1.facts_ref, bf16[48,1536]{1,0:T(8,128)(2,1)} %copy-done.3, bf16[48,1536]{1,0:T(8,128)(2,1)} %copy-done.4, bf16[48,1536]{1,0:T(8,128)(2,1)} %copy-done.5, bf16[48,1536]{1,0:T(8,128)(2,1)} %copy-done.6, bf16[4,48,1536]{2,1,0:T(8,128)(2,1)} %copy-done.7), custom_call_target="tpu_custom_call" | custom-call | tf_op jit(solution)/shard_map/pallas_call | solution.py:45
  61.2 15.7 %conditional.2 = (bf16[4,2,2,192,256]{4,3,2,1,0:T(8,128)(2,1)S(1)}) conditional(s32[]{:T(128)} %convert_element_type.42, bf16[4,2,2,192,256]{4,3,2,1,0:T(8,128)(2,1)S(1)} %shard_map.92, bf16[4,2,2,192,256]{4,3,2,1,0:T(8,128)(2,1)S(1)} %shard_map.92), branch_computations={%region_1.2_spmd, %region_2.3_spmd} | conditional | flops 786432 | bytes 7864328 | solution.py:400
  61.3 15.4 %all_to_all.41 = bf16[4,1,2,192,256]{4,3,2,1,0:T(8,128)(2,1)S(1)} all-to-all(bf16[4,1,2,192,256]{4,3,2,1,0:T(8,128)(2,1)S(1)} %get-tuple-element.47), channel_id=1, replica_groups=mesh['angle'=16,'slab'=4,'tile'=8] {'slab'}, dimensions={0} | all-to-all | bytes 1572864 | tf_op jit(solution)/shard_map/cond/branch_0_fun/all_to_all | solution.py:379
  76.9 4.2 %shard_map.93 = bf16[4,2,2,256,256]{4,3,2,1,0:T(8,128)(2,1)S(1)} custom-call(s32[2]{0:T(128)} %compare_convert_fusion.live_ref, bf16[4,2,2,192,256]{4,3,2,1,0:T(8,128)(2,1)} %copy-done, bf16[4,2,2,192,256]{4,3,2,1,0:T(8,128)(2,1)S(1)} %get-tuple-element.51.lowers, f32[2,256,256]{2,1,0:T(8,128)} %probe_in.1, bf16[2,256,256]{2,1,0:T(8,128)(2,1)} %bitcast.33, ...), custom_call_target="tpu_custom_call" | custom-call | tf_op jit(solution)/shard_map/pallas_call | solution.py:45
  81.0 13.8 %conditional.3 = (bf16[4,2,2,256,256]{4,3,2,1,0:T(8,128)(2,1)}) conditional(s32[]{:T(128)} %convert_element_type.42, bf16[4,2,2,256,256]{4,3,2,1,0:T(8,128)(2,1)S(1)} %shard_map.93, bf16[4,2,2,256,256]{4,3,2,1,0:T(8,128)(2,1)S(1)} %shard_map.93), branch_computations={%region_3.4_spmd, %region_4.5_spmd} | conditional | flops 1048576 | bytes 10485768 | solution.py:400
  81.2 12.2 %all_to_all.43 = bf16[4,1,2,256,256]{4,3,2,1,0:T(8,128)(2,1)S(1)} all-to-all(bf16[4,1,2,256,256]{4,3,2,1,0:T(8,128)(2,1)S(1)} %get-tuple-element.49), channel_id=1, replica_groups=mesh['angle'=16,'slab'=4,'tile'=8] {'slab'}, dimensions={0} | all-to-all | bytes 2097152 | tf_op jit(solution)/shard_map/cond/branch_0_fun/all_to_all | solution.py:379
  94.9 5.0 %shard_map.94 = (f32[192,1536]{1,0:T(8,128)}, bf16[192,1536]{1,0:T(8,128)(2,1)}) custom-call(s32[27]{0:T(128)} %pad_add_fusion.1.facts_ref, bf16[4,2,2,256,256]{4,3,2,1,0:T(8,128)(2,1)} %get-tuple-element.52.windows), custom_call_target="tpu_custom_call" | custom-call | tf_op jit(solution)/shard_map/pallas_call | solution.py:45
  99.9 16.1 %collective-permute-start.5 = (bf16[192,1536]{1,0:T(8,128)(2,1)}, bf16[192,1536]{1,0:T(8,128)(2,1)S(1)}, u32[]{:S(2)}, u32[]{:S(2)}) collective-permute-start(bf16[192,1536]{1,0:T(8,128)(2,1)} %get-tuple-element.42), channel_id=1, source_target_pairs={{0,32},{32,0},{64,96},{96,64},{128,160},{160,128},{192,224},{224,1... | collective-permute-start | bytes 1769480 | tf_op jit(solution)/shard_map/ppermute | solution.py:367
  117.8 2.2 %add_convert_fusion.1 = bf16[192,1536]{1,0:T(8,128)(2,1)} fusion(f32[192,1536]{1,0:T(8,128)} %get-tuple-element.41, bf16[192,1536]{1,0:T(8,128)(2,1)S(1)} %collective-permute-done.5), kind=kLoop, calls=%fused_computation.4 | loop fusion | flops 884736 | bytes 2359296 | tf_op jit(solution)/shard_map/convert_element_type | solution.py:420
  120.0 3.5 %all-to-all-start.6 = ((bf16[4,48,1536]{2,1,0:T(8,128)(2,1)}), bf16[4,48,1536]{2,1,0:T(8,128)(2,1)S(1)}, u32[]{:S(2)}, u32[]{:S(2)}) async-start(bf16[4,48,1536]{2,1,0:T(8,128)(2,1)} %bitcast.15), calls=%async_computation.6 | async-start | bytes 1179648 | tf_op jit(solution)/shard_map/all_to_all | solution.py:382
  123.5 4.8 %shard_map.95 = (f32[192,1536]{1,0:T(8,128)}, bf16[192,1536]{1,0:T(8,128)(2,1)}) custom-call(s32[27]{0:T(128)} %pad_add_fusion.1.facts_ref, bf16[4,2,2,256,256]{4,3,2,1,0:T(8,128)(2,1)} %get-tuple-element.52.windows), custom_call_target="tpu_custom_call" | custom-call | tf_op jit(solution)/shard_map/pallas_call | solution.py:45
  128.3 2.7 %collective-permute-start.6 = (bf16[192,1536]{1,0:T(8,128)(2,1)}, bf16[192,1536]{1,0:T(8,128)(2,1)S(1)}, u32[]{:S(2)}, u32[]{:S(2)}) collective-permute-start(bf16[192,1536]{1,0:T(8,128)(2,1)} %get-tuple-element.44), channel_id=1, source_target_pairs={{0,32},{32,0},{64,96},{96,64},{128,160},{160,128},{192,224},{224,1... | collective-permute-start | bytes 1769480 | tf_op jit(solution)/shard_map/ppermute | solution.py:367
  132.8 2.2 %add_convert_fusion = bf16[192,1536]{1,0:T(8,128)(2,1)} fusion(f32[192,1536]{1,0:T(8,128)} %get-tuple-element.43, bf16[192,1536]{1,0:T(8,128)(2,1)S(1)} %collective-permute-done.6), kind=kLoop, calls=%fused_computation.3 | loop fusion | flops 884736 | bytes 2359296 | tf_op jit(solution)/shard_map/convert_element_type | solution.py:420
  135.1 4.1 %all-to-all-done.6 = bf16[4,48,1536]{2,1,0:T(8,128)(2,1)S(1)} async-done(((bf16[4,48,1536]{2,1,0:T(8,128)(2,1)}), bf16[4,48,1536]{2,1,0:T(8,128)(2,1)S(1)}, u32[]{:S(2)}, u32[]{:S(2)}) %all-to-all-start.6) | async-done | bytes 589856 | tf_op jit(solution)/shard_map/all_to_all | solution.py:382
  139.2 3.5 %all-to-all-start.7 = ((bf16[4,48,1536]{2,1,0:T(8,128)(2,1)}), bf16[4,48,1536]{2,1,0:T(8,128)(2,1)S(1)}, u32[]{:S(2)}, u32[]{:S(2)}) async-start(bf16[4,48,1536]{2,1,0:T(8,128)(2,1)} %bitcast.16), calls=%async_computation.7 | async-start | bytes 1179648 | tf_op jit(solution)/shard_map/all_to_all | solution.py:382
  144.0 17.2 %all-to-all-done.7 = bf16[4,48,1536]{2,1,0:T(8,128)(2,1)S(1)} async-done(((bf16[4,48,1536]{2,1,0:T(8,128)(2,1)}), bf16[4,48,1536]{2,1,0:T(8,128)(2,1)S(1)}, u32[]{:S(2)}, u32[]{:S(2)}) %all-to-all-start.7) | async-done | bytes 589856 | tf_op jit(solution)/shard_map/all_to_all | solution.py:382
  161.4 1.9 collective-permute-start.8
  163.3 7.9 %collective-permute-done.8 = bf16[48,1536]{1,0:T(8,128)(2,1)S(1)} collective-permute-done((bf16[48,1536]{1,0:T(8,128)(2,1)S(1)}, bf16[48,1536]{1,0:T(8,128)(2,1)S(1)}, u32[]{:S(2)}, u32[]{:S(2)}) %collective-permute-start.8) | collective-permute-done | bytes 147488 | tf_op jit(solution)/shard_map/ppermute | solution.py:367
  171.2 15.5 %all_to_all.45 = bf16[4,48,1536]{2,1,0:T(8,128)(2,1)S(1)} all-to-all(bf16[4,48,1536]{2,1,0:T(8,128)(2,1)S(1)} %broadcast_in_dim.7), channel_id=1, replica_groups={{0,64,128,192},{32,96,160,224},{256,320,384,448},{288,352,416,480},{1,6..., dimensions={0} | all-to-all | bytes 1179648 | tf_op jit(solution)/shard_map/all_to_all | solution.py:382
  186.8 9.9 %collective-permute-start.9 = (bf16[192,1536]{1,0:T(8,128)(2,1)S(1)}, bf16[192,1536]{1,0:T(8,128)(2,1)S(1)}, u32[]{:S(2)}, u32[]{:S(2)}) collective-permute-start(bf16[192,1536]{1,0:T(8,128)(2,1)S(1)} %bitcast.27), channel_id=1, source_target_pairs={{0,32},{32,0},{64,96},{96,64},{128,160},{160,128},{192,224},{224,1... | collective-permute-start | bytes 1769480 | tf_op jit(solution)/shard_map/ppermute | solution.py:367
  196.6 3.5 %shard_map.96.refs_0_ = f32[2,192,1536]{2,1,0:T(8,128)} custom-call(s32[1]{0:T(128)} %bitcast.8.part_ref, bf16[2,192,1536]{2,1,0:T(8,128)(2,1)} %bitcast.25, bf16[192,1536]{1,0:T(8,128)(2,1)} %bitcast.28), custom_call_target="tpu_custom_call" | custom-call | tf_op jit(solution)/shard_map/pallas_call | solution.py:336
  201.0 3.5 %shard_map.97 = f32[2,192,1536]{2,1,0:T(8,128)} custom-call(s32[1]{0:T(128)} %bitcast.part_ref, bf16[2,192,1536]{2,1,0:T(8,128)(2,1)} %bitcast.26, bf16[192,1536]{1,0:T(8,128)(2,1)} %copy-done.2, f32[2,192,1536]{2,1,0:T(8,128)} %shard_map.96.refs_0_), custom_call_target="tpu_custom_call", output_to_operand_aliasing={{}: (3, {})} | custom-call | tf_op jit(solution)/shard_map/pallas_call | solution.py:336
  (45 shorter events, 14.6 us)
Async XLA Ops:
  3.0 25.3 %collective-permute-start = (bf16[48,1536]{1,0:T(8,128)(2,1)S(1)}, bf16[48,1536]{1,0:T(8,128)(2,1)S(1)}, u32[]{:S(2)}, u32[]{:S(2)}) collective-permute-start(bf16[48,1536]{1,0:T(8,128)(2,1)S(1)} %dynamic-slice_bitcast_fusion), channel_id=1, source_target_pairs={{1,448},{2,449},{3,450},{4,451},{5,452},{6,453},{7,454},{33,480},{... | collective-permute-start | bytes 442376 | tf_op jit(solution)/shard_map/ppermute | solution.py:376
  4.3 9.0 %all-to-all-start.4 = ((s32[4,2,3]{2,1,0:T(2,128)}), s32[4,2,3]{2,1,0:T(2,128)S(1)}, u32[]{:S(2)}, u32[]{:S(2)}) async-start(s32[4,2,3]{2,1,0:T(2,128)} %broadcast_in_dim.6), calls=%async_computation.4 | async-start | bytes 8192 | tf_op jit(solution)/shard_map/all_to_all | solution.py:379
  28.3 19.7 %copy-start.3 = (bf16[48,1536]{1,0:T(8,128)(2,1)}, bf16[48,1536]{1,0:T(8,128)(2,1)S(1)}, u32[]{:S(2)}) copy-start(bf16[48,1536]{1,0:T(8,128)(2,1)S(1)} %collective-permute-done.refs_0_) | copy-start | bytes 442372
  28.3 26.6 %all-to-all-start.5 = ((bf16[4,2,2,192,256]{4,3,2,1,0:T(8,128)(2,1)}), bf16[4,2,2,192,256]{4,3,2,1,0:T(8,128)(2,1)S(1)}, u32[]{:S(2)}, u32[]{:S(2)}) async-start(bf16[4,2,2,192,256]{4,3,2,1,0:T(8,128)(2,1)} %shard_map.91), calls=%async_computation.5 | async-start | bytes 3145728 | tf_op jit(solution)/shard_map/all_to_all | solution.py:379
  32.3 9.3 %collective-permute-start.1 = (bf16[48,1536]{1,0:T(8,128)(2,1)S(1)}, bf16[48,1536]{1,0:T(8,128)(2,1)S(1)}, u32[]{:S(2)}, u32[]{:S(2)}) collective-permute-start(bf16[48,1536]{1,0:T(8,128)(2,1)S(1)} %collective-permute-done.refs_0_), channel_id=1, source_target_pairs={{0,64},{32,96},{64,0},{96,32},{128,192},{160,224},{192,128},{224,1... | collective-permute-start | bytes 442376 | tf_op jit(solution)/shard_map/ppermute | solution.py:367
  34.2 13.7 %collective-permute-start.2 = (bf16[48,1536]{1,0:T(8,128)(2,1)S(1)}, bf16[48,1536]{1,0:T(8,128)(2,1)S(1)}, u32[]{:S(2)}, u32[]{:S(2)}) collective-permute-start(bf16[48,1536]{1,0:T(8,128)(2,1)S(1)} %collective-permute-done.refs_0_), channel_id=1, source_target_pairs={{0,128},{32,160},{64,192},{96,224},{128,0},{160,32},{192,64},{224,... | collective-permute-start | bytes 442376 | tf_op jit(solution)/shard_map/ppermute | solution.py:367
  36.2 11.8 %collective-permute-start.3 = (bf16[48,1536]{1,0:T(8,128)(2,1)S(1)}, bf16[48,1536]{1,0:T(8,128)(2,1)S(1)}, u32[]{:S(2)}, u32[]{:S(2)}) collective-permute-start(bf16[48,1536]{1,0:T(8,128)(2,1)S(1)} %collective-permute-done.refs_0_), channel_id=1, source_target_pairs={{0,192},{32,224},{64,128},{96,160},{128,64},{160,96},{192,0},{224,... | collective-permute-start | bytes 442376 | tf_op jit(solution)/shard_map/ppermute | solution.py:367
  41.6 13.3 %copy-start.4 = (bf16[48,1536]{1,0:T(8,128)(2,1)}, bf16[48,1536]{1,0:T(8,128)(2,1)S(1)}, u32[]{:S(2)}) copy-start(bf16[48,1536]{1,0:T(8,128)(2,1)S(1)} %collective-permute-done.1.refs_1_) | copy-start | bytes 442372
  48.0 7.0 %copy-start.5 = (bf16[48,1536]{1,0:T(8,128)(2,1)}, bf16[48,1536]{1,0:T(8,128)(2,1)S(1)}, u32[]{:S(2)}) copy-start(bf16[48,1536]{1,0:T(8,128)(2,1)S(1)} %collective-permute-done.2.refs_2_) | copy-start | bytes 442372
  48.0 7.0 %copy-start.6 = (bf16[48,1536]{1,0:T(8,128)(2,1)}, bf16[48,1536]{1,0:T(8,128)(2,1)S(1)}, u32[]{:S(2)}) copy-start(bf16[48,1536]{1,0:T(8,128)(2,1)S(1)} %collective-permute-done.3.refs_3_) | copy-start | bytes 442372
  48.1 6.8 %collective-permute-start.4 = (bf16[4,48,1536]{2,1,0:T(8,128)(2,1)S(1)}, bf16[4,48,1536]{2,1,0:T(8,128)(2,1)S(1)}, u32[]{:S(2)}, u32[]{:S(2)}) collective-permute-start(bf16[4,48,1536]{2,1,0:T(8,128)(2,1)S(1)} %pad_maximum_fusion.2), channel_id=1, source_target_pairs={{0,32},{32,0},{64,96},{96,64},{128,160},{160,128},{192,224},{224,1... | collective-permute-start | bytes 1769480 | tf_op jit(solution)/shard_map/ppermute | solution.py:367
  54.9 0.8 copy-start.7
  55.7 5.4 %copy-start = (bf16[4,2,2,192,256]{4,3,2,1,0:T(8,128)(2,1)}, bf16[4,2,2,192,256]{4,3,2,1,0:T(8,128)(2,1)S(1)}, u32[]{:S(2)}) copy-start(bf16[4,2,2,192,256]{4,3,2,1,0:T(8,128)(2,1)S(1)} %all-to-all-done.5.uppers) | copy-start | bytes 4718596
  99.9 17.9 %collective-permute-start.5 = (bf16[192,1536]{1,0:T(8,128)(2,1)}, bf16[192,1536]{1,0:T(8,128)(2,1)S(1)}, u32[]{:S(2)}, u32[]{:S(2)}) collective-permute-start(bf16[192,1536]{1,0:T(8,128)(2,1)} %get-tuple-element.42), channel_id=1, source_target_pairs={{0,32},{32,0},{64,96},{96,64},{128,160},{160,128},{192,224},{224,1... | collective-permute-start | bytes 1769480 | tf_op jit(solution)/shard_map/ppermute | solution.py:367
  120.0 19.1 %all-to-all-start.6 = ((bf16[4,48,1536]{2,1,0:T(8,128)(2,1)}), bf16[4,48,1536]{2,1,0:T(8,128)(2,1)S(1)}, u32[]{:S(2)}, u32[]{:S(2)}) async-start(bf16[4,48,1536]{2,1,0:T(8,128)(2,1)} %bitcast.15), calls=%async_computation.6 | async-start | bytes 1179648 | tf_op jit(solution)/shard_map/all_to_all | solution.py:382
  128.3 4.5 %collective-permute-start.6 = (bf16[192,1536]{1,0:T(8,128)(2,1)}, bf16[192,1536]{1,0:T(8,128)(2,1)S(1)}, u32[]{:S(2)}, u32[]{:S(2)}) collective-permute-start(bf16[192,1536]{1,0:T(8,128)(2,1)} %get-tuple-element.44), channel_id=1, source_target_pairs={{0,32},{32,0},{64,96},{96,64},{128,160},{160,128},{192,224},{224,1... | collective-permute-start | bytes 1769480 | tf_op jit(solution)/shard_map/ppermute | solution.py:367
  139.2 22.0 %all-to-all-start.7 = ((bf16[4,48,1536]{2,1,0:T(8,128)(2,1)}), bf16[4,48,1536]{2,1,0:T(8,128)(2,1)S(1)}, u32[]{:S(2)}, u32[]{:S(2)}) async-start(bf16[4,48,1536]{2,1,0:T(8,128)(2,1)} %bitcast.16), calls=%async_computation.7 | async-start | bytes 1179648 | tf_op jit(solution)/shard_map/all_to_all | solution.py:382
  142.7 18.6 %collective-permute-start.7 = (bf16[48,1536]{1,0:T(8,128)(2,1)S(1)}, bf16[48,1536]{1,0:T(8,128)(2,1)S(1)}, u32[]{:S(2)}, u32[]{:S(2)}) collective-permute-start(bf16[48,1536]{1,0:T(8,128)(2,1)S(1)} %reduce_sum.21), channel_id=1, source_target_pairs={{0,449},{1,450},{2,451},{3,452},{4,453},{5,454},{6,455},{32,481},{... | collective-permute-start | bytes 442376 | tf_op jit(solution)/shard_map/ppermute | solution.py:376
  161.4 9.8 %collective-permute-start.8 = (bf16[48,1536]{1,0:T(8,128)(2,1)S(1)}, bf16[48,1536]{1,0:T(8,128)(2,1)S(1)}, u32[]{:S(2)}, u32[]{:S(2)}) collective-permute-start(bf16[48,1536]{1,0:T(8,128)(2,1)S(1)} %add_convert_fusion.3), channel_id=1, source_target_pairs={{0,256},{32,288},{64,320},{96,352},{128,384},{160,416},{192,448},{... | collective-permute-start | bytes 442376 | tf_op jit(solution)/shard_map/ppermute | solution.py:367
  186.8 9.9 %copy-start.1 = (bf16[4,48,1536]{2,1,0:T(8,128)(2,1)}, bf16[4,48,1536]{2,1,0:T(8,128)(2,1)S(1)}, u32[]{:S(2)}) copy-start(bf16[4,48,1536]{2,1,0:T(8,128)(2,1)S(1)} %all_to_all.45) | copy-start | bytes 1769476
  186.8 13.4 %collective-permute-start.9 = (bf16[192,1536]{1,0:T(8,128)(2,1)S(1)}, bf16[192,1536]{1,0:T(8,128)(2,1)S(1)}, u32[]{:S(2)}, u32[]{:S(2)}) collective-permute-start(bf16[192,1536]{1,0:T(8,128)(2,1)S(1)} %bitcast.27), channel_id=1, source_target_pairs={{0,32},{32,0},{64,96},{96,64},{128,160},{160,128},{192,224},{224,1... | collective-permute-start | bytes 1769480 | tf_op jit(solution)/shard_map/ppermute | solution.py:367
  200.2 0.8 copy-start.2

commit v6 on v4

v6 whole, which is shorter than its diff:
```python
import functools

import jax
import jax.numpy as jnp
import ml_dtypes
import numpy as np
from jax import lax
from jax.experimental import pallas as pl
from jax.experimental.pallas import tpu as pltpu
from jax.sharding import PartitionSpec as P

angle_center = 600
shear_divisor = 64
step_size = 0.03
floor_square = 0.25

LANE = 128
HALO = 64


def dft_tables(plane_width):
    index_line = np.arange(plane_width, dtype=np.int32)
    product_mod = np.mod(index_line[:, None] * index_line[None, :], plane_width)
    phase_table = product_mod.astype(np.float32) * np.float32(2.0 * 3.141592653589793 / plane_width)
    scale_factor = np.float32(plane_width ** (-0.5))
    table_real = (np.cos(phase_table) * scale_factor).astype(ml_dtypes.bfloat16)
    table_imag = (-np.sin(phase_table) * scale_factor).astype(ml_dtypes.bfloat16)
    return table_real, table_imag


def dot(left, right):
    return jnp.dot(left, right, preferred_element_type=jnp.float32)


def one_hot(rows, columns, down):
    row = lax.broadcasted_iota(jnp.int32, (rows, columns), 0)
    column = lax.broadcasted_iota(jnp.int32, (rows, columns), 1)
    return (row - column == down).astype(jnp.float32).astype(jnp.bfloat16)


VMEM = pl.BlockSpec(memory_space=pltpu.VMEM)


def call(body, out_shape, scratch, facts, *args):
    return pl.pallas_call(
        body,
        out_shape=out_shape,
        in_specs=[pl.BlockSpec(memory_space=pltpu.SMEM)] + [VMEM] * len(args),
        out_specs=[VMEM] * len(out_shape),
        scratch_shapes=scratch,
        compiler_params=pltpu.CompilerParams(vmem_limit_bytes=24 * 1024 * 1024),
    )(facts, *args)


class Facts:
    def __init__(self, ref, slabs, slots):
        self.ref, self.slots = ref, slots
        self.shift, self.core, self.place_z = (ref[3 * slabs * slots + i] for i in range(3))

    def slot(self, slab, slot):
        return tuple(self.ref[3 * (slab * self.slots + slot) + i] for i in range(3))


def column_blocks(left, width, columns):
    blocks = columns // LANE
    return [
        pl.multiple_of(lax.rem(left // LANE + i, blocks) * LANE, LANE) for i in range(width // LANE + 1)
    ]


def cut_body(down, facts_ref, *refs):
    blocks, (out, held) = refs[:-2], refs[-2:]
    slabs, slots, _, rows, width = out.shape
    facts = Facts(facts_ref, slabs, slots)
    if len(blocks) == 1:
        held = blocks[0]
    else:
        *mine, other = blocks
        size = mine[0].shape[0]
        for k, block in enumerate(mine):
            at = pl.ds(pl.multiple_of((facts.place_z ^ k) * size, size), size)
            held[facts.core, at] = block[...]
            held[1 - facts.core, at] = other[k]
    tile_rows, columns = held.shape[1:]

    for slot in range(slots):
        for slab in range(slabs):
            row, column, live = facts.slot(slab, slot)

            @pl.when(live > 0)
            def _():
                left = lax.rem(column + facts.shift, columns)
                pick_rows = one_hot(rows, tile_rows, -(row + down))
                pick_columns = one_hot(width + LANE, width, lax.rem(left, LANE))
                wide = jnp.concatenate(
                    [held[:, :, pl.ds(start, LANE)] for start in column_blocks(left, width, columns)], axis=2
                )
                narrow = dot(wide.reshape(2 * tile_rows, width + LANE), pick_columns).astype(jnp.bfloat16)
                for part in range(2):
                    picked = dot(pick_rows, narrow[part * tile_rows : (part + 1) * tile_rows])
                    out[slab, slot, part] = picked.astype(jnp.bfloat16)


def cut_windows(facts, slabs, slots, down, blocks, rows, width):
    out = jax.ShapeDtypeStruct((slabs, slots, 2, rows, width), jnp.bfloat16)
    size, columns = blocks[0].shape[-2:]
    held = pltpu.VMEM((2, size * max(1, len(blocks) - 1), columns), jnp.bfloat16)
    return call(functools.partial(cut_body, down), [out], [held], facts, *blocks)[0]


def cos_sin(angle):
    turns = jnp.round(angle * 0.6366197723675814)
    rest = angle - turns * 1.5703125
    rest = rest - turns * 4.837512969970703e-4
    rest = rest - turns * 7.549789948768648e-8
    square = rest * rest
    sine = (-1.9515295891e-4 * square + 8.3321608736e-3) * square - 1.6666654611e-1
    sine = sine * square * rest + rest
    cosine = (2.443315711809948e-5 * square - 1.388731625493765e-3) * square + 4.166664568298827e-2
    cosine = cosine * square * square - 0.5 * square + 1.0
    quarter = turns.astype(jnp.int32)
    odd = (quarter & 1) == 1
    first, second = jnp.where(odd, sine, cosine), jnp.where(odd, cosine, sine)
    return (
        jnp.where(((quarter + 1) & 2) == 2, -first, first),
        jnp.where((quarter & 2) == 2, -second, second),
    )


def patch_body(live_ref, uppers, lowers, probe, patterns, wr_ref, wi_ref, out):
    slabs, slots, _, rows, _ = uppers.shape
    f32, bf16 = jnp.float32, jnp.bfloat16

    def window(slot, part):
        def projected(ref):
            return sum(ref[slab, slot, part].astype(f32) for slab in range(slabs)).astype(bf16).astype(f32)

        above, below = projected(uppers), projected(lowers)
        return jnp.concatenate(
            [above[:HALO], above[HALO:] + below[: rows - HALO], below[rows - HALO :]], axis=0
        )

    for slot in range(slots):

        @pl.when(live_ref[slot] > 0)
        def _():
            phase, absorption = window(slot, 0), window(slot, 1)
            magnitude = jnp.exp(-absorption)
            cosine, sine = cos_sin(phase)
            trans_real = magnitude * cosine
            trans_imag = magnitude * sine
            probe_real, probe_imag = probe[0], probe[1]
            wr, wi = wr_ref[...], wi_ref[...]
            wave_real = (probe_real * trans_real - probe_imag * trans_imag).astype(bf16)
            wave_imag = (probe_real * trans_imag + probe_imag * trans_real).astype(bf16)
            left_real = (dot(wr, wave_real) - dot(wi, wave_imag)).astype(bf16)
            left_imag = (dot(wr, wave_imag) + dot(wi, wave_real)).astype(bf16)
            far_real = dot(left_real, wr) - dot(left_imag, wi)
            far_imag = dot(left_real, wi) + dot(left_imag, wr)
            power = far_real * far_real + far_imag * far_imag + floor_square
            keeping = 1.0 - patterns[slot].astype(f32) * lax.rsqrt(power)
            resid_real = (far_real * keeping).astype(bf16)
            resid_imag = (far_imag * keeping).astype(bf16)
            back_real = (dot(wr, resid_real) + dot(wi, resid_imag)).astype(bf16)
            back_imag = (dot(wr, resid_imag) - dot(wi, resid_real)).astype(bf16)
            exit_real = dot(back_real, wr) + dot(back_imag, wi)
            exit_imag = dot(back_imag, wr) - dot(back_real, wi)
            mixed_real = probe_real * exit_real + probe_imag * exit_imag
            mixed_imag = probe_real * exit_imag - probe_imag * exit_real
            phase_out = (trans_real * mixed_imag - trans_imag * mixed_real).astype(bf16)
            absorption_out = (-(trans_real * mixed_real + trans_imag * mixed_imag)).astype(bf16)
            for slab in range(slabs):
                out[slab, slot, 0] = phase_out
                out[slab, slot, 1] = absorption_out


def patch_gradients(live, uppers, lowers, probe_wave, patterns, tables):
    slabs, slots, _, _, width = uppers.shape
    out = jax.ShapeDtypeStruct((slabs, slots, 2, width, width), jnp.bfloat16)
    return call(patch_body, [out], [], live, uppers, lowers, probe_wave, patterns, *tables)[0]


def place_body(first_row, rows, reverse, facts_ref, windows, keep_out, send_out, total):
    slabs, slots, _, width, _ = windows.shape
    tile_rows, columns = keep_out.shape
    facts = Facts(facts_ref, slabs, slots)
    down = first_row - (tile_rows if first_row else 0)
    total[...] = jnp.zeros_like(total)
    for slot in range(slots):
        for slab in range(slabs):
            row, column, live = facts.slot(slab, slot)

            @pl.when(live > 0)
            def _():
                left = lax.rem(column + facts.shift, columns)
                put_rows = one_hot(tile_rows, rows, row + down)
                put_columns = one_hot(width, width + LANE, -lax.rem(left, LANE))
                moved = [
                    dot(put_rows, windows[slab, slot, part, first_row : first_row + rows]) for part in range(2)
                ]
                wide = dot(jnp.concatenate(moved, axis=0).astype(jnp.bfloat16), put_columns)
                wide = wide.reshape(2, tile_rows, width + LANE)
                for i, start in enumerate(column_blocks(left, width, columns)):
                    total[:, :, pl.ds(start, LANE)] += wide[:, :, i * LANE : (i + 1) * LANE]

    blocks = 4 if reverse else 1
    size = tile_rows // blocks
    for block in range(blocks):
        here = slice(block * size, (block + 1) * size)
        there = slice((blocks - 1 - block) * size, (blocks - block) * size)
        keep_out[there] = total[facts.core, here]
        send_out[there] = total[1 - facts.core, here].astype(jnp.bfloat16)


def place_windows(facts, windows, first_row, reverse, rows, tile_rows, columns):
    shapes = [jax.ShapeDtypeStruct((tile_rows, columns), t) for t in (jnp.float32, jnp.bfloat16)]
    total = pltpu.VMEM((2, tile_rows, columns), jnp.float32)
    return call(functools.partial(place_body, first_row, rows, reverse), shapes, [total], facts, windows)


def step_body(part_ref, layer, gradient, *refs):
    out, made, sems = refs[-3:]
    part = part_ref[0]
    size = gradient.shape[0] // 4
    copies = []
    for n in range(4):
        rows = slice(n * size, (n + 1) * size)
        made[rows] = layer[part, rows].astype(jnp.float32) - step_size * gradient[rows].astype(jnp.float32)
        copies.append(
            pltpu.make_async_copy(made.at[pl.ds(n * size, size)], out.at[part, pl.ds(n * size, size)], sems.at[n])
        )
        copies[-1].start()
    for copy in copies:
        copy.wait()


def step(part, layer, gradient, *stepped):
    return pl.pallas_call(
        step_body,
        out_shape=jax.ShapeDtypeStruct(layer.shape, jnp.float32),
        in_specs=[pl.BlockSpec(memory_space=pltpu.SMEM), VMEM, VMEM]
        + [pl.BlockSpec(memory_space=pltpu.HBM)] * len(stepped),
        out_specs=pl.BlockSpec(memory_space=pltpu.HBM),
        scratch_shapes=[pltpu.VMEM(gradient.shape, jnp.float32), pltpu.SemaphoreType.DMA((4,))],
        input_output_aliases={3: 0} if stepped else {},
        compiler_params=pltpu.CompilerParams(vmem_limit_bytes=24 * 1024 * 1024),
    )(part.reshape(1).astype(jnp.int32), layer, gradient, *stepped)


def per_device(volume, probe_wave, amplitudes, offsets, column_starts, counts, angle_ids):
    layer = volume.reshape(volume.shape[0], *volume.shape[2:])
    tile_rows, columns = layer.shape[1:]
    width = amplitudes.shape[-1]
    slots = offsets.shape[3]
    angles, slabs, tiles = (lax.axis_size(axis) for axis in ("angle", "slab", "tile"))
    slab, angle = lax.axis_index("slab"), lax.axis_index("angle")
    f32, bf16 = jnp.float32, jnp.bfloat16
    tables = dft_tables(width)
    window_rows = width - HALO
    patterns = amplitudes.reshape(slots, width, width)

    core, place_z = angle % 2, angle // 2 % 4
    four_groups = [[8 * f + 2 * q + c for q in range(4)] for f in range(angles // 8) for c in range(2)]
    block_rows = tile_rows // 4

    def swap(value, by):
        return lax.ppermute(value, "angle", [(i, i ^ by) for i in range(angles)])

    def mirrored(value, by):
        pairs = [
            (a * tiles + t, (angles - 2 - (a - a % 2) + a % 2) * tiles + t + by)
            for a in range(angles)
            for t in range(tiles)
            if 0 <= t + by < tiles
        ]
        return lax.ppermute(value, ("angle", "tile"), pairs)

    def to_slabs(value):
        return lax.all_to_all(value, "slab", 0, 0, tiled=True)

    def to_four(value):
        return lax.all_to_all(value, "angle", 0, 0, axis_index_groups=four_groups, tiled=True)

    def added(blocks):
        return jnp.sum(to_four(blocks).astype(f32), axis=0)

    own_part = lax.dynamic_index_in_dim(layer, core, 0, keepdims=False)
    after = lax.dynamic_slice(own_part, ((3 - place_z) * block_rows, 0), (block_rows, columns))
    after, counts = lax.optimization_barrier((after, counts))
    after = mirrored(after, -1)
    live = (jnp.arange(slots) < counts.reshape(1)).astype(jnp.int32)
    meta = jnp.stack([offsets.reshape(slots), column_starts.reshape(slots), live], axis=1)
    group = to_slabs(jnp.broadcast_to(meta, (slabs, *meta.shape)))
    more = jnp.max(group[:, 1:, 2]) > 0
    sheared = jnp.floor_divide((angle_ids[0] - angle_center) * (slab - slabs // 2), shear_divisor)
    others = jnp.stack([jnp.mod(sheared, columns), core, place_z])
    facts = jnp.concatenate([group.reshape(-1), others]).astype(jnp.int32)

    def exchanged(values):
        return lax.cond(
            more,
            to_slabs,
            lambda v: jnp.concatenate([to_slabs(v[:, :1]), v[:, 1:]], axis=1),
            values,
        )

    uppers = cut_windows(facts, slabs, slots, 0, [layer], window_rows, width)
    after, uppers = lax.optimization_barrier((after, uppers))
    uppers = to_slabs(uppers)
    mine = [after] + [swap(after, k << 1) for k in range(1, 4)]
    afters = mine + [swap(jnp.stack(mine), 1)]
    afters, uppers = lax.optimization_barrier((afters, uppers))
    lowers = cut_windows(facts, slabs, slots, HALO - tile_rows, afters, window_rows, width)
    lowers = exchanged(lowers)

    gradients = exchanged(patch_gradients(live, uppers, lowers, probe_wave, patterns, tables))

    def placed(first_row, reverse):
        keep, send = place_windows(facts, gradients, first_row, reverse, window_rows, tile_rows, columns)
        return (keep + swap(send, 1).astype(f32)).astype(bf16).reshape(4, block_rows, columns)

    spill, own = placed(HALO, True), placed(0, False)
    spill, own = lax.optimization_barrier((added(spill).astype(bf16), own))
    spill = mirrored(spill, 1)
    total = lax.optimization_barrier((added(own) + spill.astype(f32)).astype(bf16))
    total = (total.astype(f32) + swap(total, 8).astype(f32)).astype(bf16)

    total = to_four(jnp.broadcast_to(total, (4, *total.shape))).reshape(tile_rows, columns)
    new = step(core, layer, total)
    return step(1 - core, layer, swap(total, 1), new).reshape(volume.shape)


def solution(mesh):
    in_specs = (
        P(None, "slab", "tile", None),
        P(),
        P("angle", "tile", "slab", None, None, None),
        P("angle", "tile", "slab", None),
        P("angle", "tile", "slab", None),
        P("angle", "tile", "slab"),
        P("angle"),
    )
    out_specs = P(None, "slab", "tile", None)
    return jax.shard_map(
        per_device, mesh=mesh, in_specs=in_specs, out_specs=out_specs, check_vma=False
    )
```

time: 216 us -> 192 us (0.89); the launches traced: 215 us -> 189 us
  blocking collectives: 60.5 us -> 43.2 us
  Pallas kernels: 24.9 us -> 17.6 us
  waiting for transfers between devices: 49.5 us -> 54.3 us
  local copies, waits for them, and re-layouts: 6.64 us -> 3.33 us
    all_to_all x2 -> x1, blocking collectives: 33.3 us -> 15.5 us  [to_four(): lax.all_to_all(value, 'angle', 0, 0, axis_index_groups=four_groups, tiled...]
    ppermute x2, waiting for transfers between devices: 20.1 us -> 7.69 us  [mirrored(): return lax.ppermute(value, ('angle', 'tile'), pairs)]
    all_to_all x1 -> x2, waiting for transfers between devices: 17.2 us -> 24.9 us  [to_four(): lax.all_to_all(value, 'angle', 0, 0, axis_index_groups=four_groups, tiled...]
    pallas_call x5 -> x7, Pallas kernels: 24.9 us -> 17.6 us  [the longest x5 15.5 us: call(): pl.pallas_call(body, out_shape=out_shape, in_specs=[pl.BlockSpec(memory_s...]
    ppermute x10 -> x8, waiting for transfers between devices: 12.2 us -> 18.2 us  [swap(): return lax.ppermute(value, 'angle', [(i, i ^ by) for i in range(angles)])]
    ppermute x10 -> x8, starting transfers between devices: 49.6 us -> 44.4 us  [swap(): return lax.ppermute(value, 'angle', [(i, i ^ by) for i in range(angles)])]
    all_to_all x1 -> x2, starting transfers between devices: 3.49 us -> 6.96 us  [to_four(): lax.all_to_all(value, 'angle', 0, 0, axis_index_groups=four_groups, tiled...]
    all_to_all x2, waiting for transfers between devices: 0.01 us -> 3.46 us  [to_slabs(): return lax.all_to_all(value, 'slab', 0, 0, tiled=True)]
  transfers between devices with their start and end apart: 15 -> 14, of which waited for: 5 -> 10; matrix products, arithmetic and copies ran while one was open for 3% -> 2% of each run, Pallas kernels for 0% -> 4%
where the time goes in v6:
time: 192 us; the launch traced here: 189 us
  starting transfers between devices  62.8 us (33%)
  waiting for transfers between devices  54.3 us (28%)
  blocking collectives  43.2 us (22%)
  Pallas kernels  17.6 us (9%)
  other arithmetic  5.19 us (3%)
  local copies, waits for them, and re-layouts  3.33 us (2%)
  between operations  2.41 us (1%)
    ppermute x8, starting transfers between devices, swap(): return lax.ppermute(value, 'angle', [(i, i ^ by) for i in range(angles)])  44.4 us
    all_to_all x2, blocking collectives, to_slabs(): return lax.all_to_all(value, 'slab', 0, 0, tiled=True)  27.7 us
    all_to_all x2, waiting for transfers between devices, to_four(): lax.all_to_all(value, 'angle', 0, 0, axis_index_groups=four_groups, tiled...  24.9 us
    ppermute x8, waiting for transfers between devices, swap(): return lax.ppermute(value, 'angle', [(i, i ^ by) for i in range(angles)])  18.2 us
    all_to_all x1, blocking collectives, to_four(): lax.all_to_all(value, 'angle', 0, 0, axis_index_groups=four_groups, tiled...  15.5 us
    pallas_call x5, Pallas kernels, call(): pl.pallas_call(body, out_shape=out_shape, in_specs=[pl.BlockSpec(memory_s...  15.5 us
    all_to_all x2, starting transfers between devices, to_slabs(): return lax.all_to_all(value, 'slab', 0, 0, tiled=True)  8.86 us
    ppermute x2, waiting for transfers between devices, mirrored(): return lax.ppermute(value, ('angle', 'tile'), pairs)  7.69 us
  transfers between devices with their start and end apart: 14, of which 10 were waited for; matrix products, arithmetic and copies ran while one was open for 2% of the time, Pallas kernels for 4%

profile of v6, /device:TPU:1, one launch (start us, length us, event | category | flops | bytes accessed | tf_op | source)
XLA Modules:
  0.0 188.9 jit_solution(9644463967940711730)
XLA Ops:
  4.3 4.8 %all-to-all-start.4 = ((s32[4,2,3]{2,1,0:T(2,128)}), s32[4,2,3]{2,1,0:T(2,128)S(1)}, u32[]{:S(2)}, u32[]{:S(2)}) async-start(s32[4,2,3]{2,1,0:T(2,128)} %broadcast_in_dim.6), calls=%async_computation.4 | async-start | bytes 8192 | tf_op jit(solution)/shard_map/all_to_all | solution.py:279
  9.8 3.5 %all-to-all-done.4 = s32[4,2,3]{2,1,0:T(2,128)S(1)} async-done(((s32[4,2,3]{2,1,0:T(2,128)}), s32[4,2,3]{2,1,0:T(2,128)S(1)}, u32[]{:S(2)}, u32[]{:S(2)}) %all-to-all-start.4) | async-done | bytes 128 | tf_op jit(solution)/shard_map/all_to_all | solution.py:279
  14.7 3.9 %shard_map.91 = bf16[4,2,2,192,256]{4,3,2,1,0:T(8,128)(2,1)} custom-call(s32[27]{0:T(128)S(1)} %pad_add_fusion.1.facts_ref, bf16[2,192,1536]{2,1,0:T(8,128)(2,1)S(1)} %bitcast.24), custom_call_target="tpu_custom_call" | custom-call | tf_op jit(solution)/shard_map/pallas_call | solution.py:45
  18.6 7.7 %collective-permute-done.refs_0_ = bf16[48,1536]{1,0:T(8,128)(2,1)S(1)} collective-permute-done((bf16[48,1536]{1,0:T(8,128)(2,1)S(1)}, bf16[48,1536]{1,0:T(8,128)(2,1)S(1)}, u32[]{:S(2)}, u32[]{:S(2)}) %collective-permute-start) | collective-permute-done | bytes 147488 | tf_op jit(solution)/shard_map/ppermute | solution.py:276
  26.3 4.0 %all-to-all-start.5 = ((bf16[4,2,2,192,256]{4,3,2,1,0:T(8,128)(2,1)}), bf16[4,2,2,192,256]{4,3,2,1,0:T(8,128)(2,1)S(1)}, u32[]{:S(2)}, u32[]{:S(2)}) async-start(bf16[4,2,2,192,256]{4,3,2,1,0:T(8,128)(2,1)} %shard_map.91), calls=%async_computation.5 | async-start | bytes 3145728 | tf_op jit(solution)/shard_map/all_to_all | solution.py:279
  30.3 1.9 %collective-permute-start.1 = (bf16[48,1536]{1,0:T(8,128)(2,1)S(1)}, bf16[48,1536]{1,0:T(8,128)(2,1)S(1)}, u32[]{:S(2)}, u32[]{:S(2)}) collective-permute-start(bf16[48,1536]{1,0:T(8,128)(2,1)S(1)} %collective-permute-done.refs_0_), channel_id=1, source_target_pairs={{0,64},{32,96},{64,0},{96,32},{128,192},{160,224},{192,128},{224,1... | collective-permute-start | bytes 442376 | tf_op jit(solution)/shard_map/ppermute | solution.py:267
  32.2 1.9 %collective-permute-start.2 = (bf16[48,1536]{1,0:T(8,128)(2,1)S(1)}, bf16[48,1536]{1,0:T(8,128)(2,1)S(1)}, u32[]{:S(2)}, u32[]{:S(2)}) collective-permute-start(bf16[48,1536]{1,0:T(8,128)(2,1)S(1)} %collective-permute-done.refs_0_), channel_id=1, source_target_pairs={{0,128},{32,160},{64,192},{96,224},{128,0},{160,32},{192,64},{224,... | collective-permute-start | bytes 442376 | tf_op jit(solution)/shard_map/ppermute | solution.py:267
  34.1 5.4 %collective-permute-start.3 = (bf16[48,1536]{1,0:T(8,128)(2,1)S(1)}, bf16[48,1536]{1,0:T(8,128)(2,1)S(1)}, u32[]{:S(2)}, u32[]{:S(2)}) collective-permute-start(bf16[48,1536]{1,0:T(8,128)(2,1)S(1)} %collective-permute-done.refs_0_), channel_id=1, source_target_pairs={{0,192},{32,224},{64,128},{96,160},{128,64},{160,96},{192,0},{224,... | collective-permute-start | bytes 442376 | tf_op jit(solution)/shard_map/ppermute | solution.py:267
  39.6 6.4 %collective-permute-done.2.refs_2_ = bf16[48,1536]{1,0:T(8,128)(2,1)S(1)} collective-permute-done((bf16[48,1536]{1,0:T(8,128)(2,1)S(1)}, bf16[48,1536]{1,0:T(8,128)(2,1)S(1)}, u32[]{:S(2)}, u32[]{:S(2)}) %collective-permute-start.2) | collective-permute-done | bytes 147488 | tf_op jit(solution)/shard_map/ppermute | solution.py:267
  46.0 4.9 %collective-permute-start.4 = (bf16[4,48,1536]{2,1,0:T(8,128)(2,1)S(1)}, bf16[4,48,1536]{2,1,0:T(8,128)(2,1)S(1)}, u32[]{:S(2)}, u32[]{:S(2)}) collective-permute-start(bf16[4,48,1536]{2,1,0:T(8,128)(2,1)S(1)} %pad_maximum_fusion.2), channel_id=1, source_target_pairs={{0,32},{32,0},{64,96},{96,64},{128,160},{160,128},{192,224},{224,1... | collective-permute-start | bytes 1769480 | tf_op jit(solution)/shard_map/ppermute | solution.py:267
  52.5 2.8 %shard_map.92 = bf16[4,2,2,192,256]{4,3,2,1,0:T(8,128)(2,1)S(1)} custom-call(s32[27]{0:T(128)S(1)} %pad_add_fusion.1.facts_ref, bf16[48,1536]{1,0:T(8,128)(2,1)S(1)} %collective-permute-done.refs_0_, bf16[48,1536]{1,0:T(8,128)(2,1)S(1)} %collective-permute-done.1.refs_1_, bf16[48,1536]{1,0:T(8,128)(2,1)S(1)} %collective-permute-done.2.refs_2_, ...), custom_call_target="tpu_custom_call" | custom-call | tf_op jit(solution)/shard_map/pallas_call | solution.py:45
  55.4 17.0 %conditional.2 = (bf16[4,2,2,192,256]{4,3,2,1,0:T(8,128)(2,1)}) conditional(s32[]{:T(128)} %convert_element_type.42, bf16[4,2,2,192,256]{4,3,2,1,0:T(8,128)(2,1)S(1)} %shard_map.92, bf16[4,2,2,192,256]{4,3,2,1,0:T(8,128)(2,1)S(1)} %shard_map.92), branch_computations={%region_1.2_spmd, %region_2.3_spmd} | conditional | flops 786432 | bytes 7864328 | solution.py:300
  55.5 15.5 %all_to_all.41 = bf16[4,1,2,192,256]{4,3,2,1,0:T(8,128)(2,1)S(1)} all-to-all(bf16[4,1,2,192,256]{4,3,2,1,0:T(8,128)(2,1)S(1)} %get-tuple-element.47), channel_id=1, replica_groups=mesh['angle'=16,'slab'=4,'tile'=8] {'slab'}, dimensions={0} | all-to-all | bytes 1572864 | tf_op jit(solution)/shard_map/cond/branch_0_fun/all_to_all | solution.py:279
  71.0 1.3 pad_maximum_fusion
  72.4 3.3 %shard_map.93 = bf16[4,2,2,256,256]{4,3,2,1,0:T(8,128)(2,1)S(1)} custom-call(s32[2]{0:T(128)S(1)} %compare_convert_fusion.live_ref, bf16[4,2,2,192,256]{4,3,2,1,0:T(8,128)(2,1)S(1)} %all-to-all-done.5.uppers, bf16[4,2,2,192,256]{4,3,2,1,0:T(8,128)(2,1)} %get-tuple-element.51.lowers, f32[2,256,256]{2,1,0:T(8,128)S(1)} %copy-done.2, ...), custom_call_target="tpu_custom_call" | custom-call | tf_op jit(solution)/shard_map/pallas_call | solution.py:45
  75.7 12.5 %conditional.3 = (bf16[4,2,2,256,256]{4,3,2,1,0:T(8,128)(2,1)S(1)}) conditional(s32[]{:T(128)} %convert_element_type.42, bf16[4,2,2,256,256]{4,3,2,1,0:T(8,128)(2,1)S(1)} %shard_map.93, bf16[4,2,2,256,256]{4,3,2,1,0:T(8,128)(2,1)S(1)} %shard_map.93), branch_computations={%region_3.4_spmd, %region_4.5_spmd} | conditional | flops 1048576 | bytes 10485768 | solution.py:300
  75.9 12.2 %all_to_all.43 = bf16[4,1,2,256,256]{4,3,2,1,0:T(8,128)(2,1)S(1)} all-to-all(bf16[4,1,2,256,256]{4,3,2,1,0:T(8,128)(2,1)S(1)} %get-tuple-element.49), channel_id=1, replica_groups=mesh['angle'=16,'slab'=4,'tile'=8] {'slab'}, dimensions={0} | all-to-all | bytes 2097152 | tf_op jit(solution)/shard_map/cond/branch_0_fun/all_to_all | solution.py:279
  88.2 2.8 %shard_map.94 = (f32[192,1536]{1,0:T(8,128)S(1)}, bf16[192,1536]{1,0:T(8,128)(2,1)S(1)}) custom-call(s32[27]{0:T(128)S(1)} %pad_add_fusion.1.facts_ref, bf16[4,2,2,256,256]{4,3,2,1,0:T(8,128)(2,1)S(1)} %get-tuple-element.52.windows), custom_call_target="tpu_custom_call" | custom-call | tf_op jit(solution)/shard_map/pallas_call | solution.py:45
  91.1 15.6 %collective-permute-start.5 = (bf16[192,1536]{1,0:T(8,128)(2,1)S(1)}, bf16[192,1536]{1,0:T(8,128)(2,1)S(1)}, u32[]{:S(2)}, u32[]{:S(2)}) collective-permute-start(bf16[192,1536]{1,0:T(8,128)(2,1)S(1)} %get-tuple-element.42), channel_id=1, source_target_pairs={{0,32},{32,0},{64,96},{96,64},{128,160},{160,128},{192,224},{224,1... | collective-permute-start | bytes 1769480 | tf_op jit(solution)/shard_map/ppermute | solution.py:267
  106.7 1.6 collective-permute-done.5
  109.2 3.5 %all-to-all-start.6 = ((bf16[4,48,1536]{2,1,0:T(8,128)(2,1)}), bf16[4,48,1536]{2,1,0:T(8,128)(2,1)S(1)}, u32[]{:S(2)}, u32[]{:S(2)}) async-start(bf16[4,48,1536]{2,1,0:T(8,128)(2,1)} %bitcast.15), calls=%async_computation.6 | async-start | bytes 1179648 | tf_op jit(solution)/shard_map/all_to_all | solution.py:282
  112.7 2.6 %shard_map.95 = (f32[192,1536]{1,0:T(8,128)S(1)}, bf16[192,1536]{1,0:T(8,128)(2,1)S(1)}) custom-call(s32[27]{0:T(128)S(1)} %pad_add_fusion.1.facts_ref, bf16[4,2,2,256,256]{4,3,2,1,0:T(8,128)(2,1)S(1)} %get-tuple-element.52.windows), custom_call_target="tpu_custom_call" | custom-call | tf_op jit(solution)/shard_map/pallas_call | solution.py:45
  115.4 2.7 %collective-permute-start.6 = (bf16[192,1536]{1,0:T(8,128)(2,1)S(1)}, bf16[192,1536]{1,0:T(8,128)(2,1)S(1)}, u32[]{:S(2)}, u32[]{:S(2)}) collective-permute-start(bf16[192,1536]{1,0:T(8,128)(2,1)S(1)} %get-tuple-element.44), channel_id=1, source_target_pairs={{0,32},{32,0},{64,96},{96,64},{128,160},{160,128},{192,224},{224,1... | collective-permute-start | bytes 1769480 | tf_op jit(solution)/shard_map/ppermute | solution.py:267
  118.1 1.6 collective-permute-done.6
  120.6 7.7 %all-to-all-done.6 = bf16[4,48,1536]{2,1,0:T(8,128)(2,1)S(1)} async-done(((bf16[4,48,1536]{2,1,0:T(8,128)(2,1)}), bf16[4,48,1536]{2,1,0:T(8,128)(2,1)S(1)}, u32[]{:S(2)}, u32[]{:S(2)}) %all-to-all-start.6) | async-done | bytes 589856 | tf_op jit(solution)/shard_map/all_to_all | solution.py:282
  128.4 3.5 %all-to-all-start.7 = ((bf16[4,48,1536]{2,1,0:T(8,128)(2,1)}), bf16[4,48,1536]{2,1,0:T(8,128)(2,1)S(1)}, u32[]{:S(2)}, u32[]{:S(2)}) async-start(bf16[4,48,1536]{2,1,0:T(8,128)(2,1)} %bitcast.16), calls=%async_computation.7 | async-start | bytes 1179648 | tf_op jit(solution)/shard_map/all_to_all | solution.py:282
  131.9 1.3 collective-permute-start.7
  133.2 17.2 %all-to-all-done.7 = bf16[4,48,1536]{2,1,0:T(8,128)(2,1)S(1)} async-done(((bf16[4,48,1536]{2,1,0:T(8,128)(2,1)}), bf16[4,48,1536]{2,1,0:T(8,128)(2,1)S(1)}, u32[]{:S(2)}, u32[]{:S(2)}) %all-to-all-start.7) | async-done | bytes 589856 | tf_op jit(solution)/shard_map/all_to_all | solution.py:282
  150.6 2.1 %collective-permute-start.8 = (bf16[48,1536]{1,0:T(8,128)(2,1)S(1)}, bf16[48,1536]{1,0:T(8,128)(2,1)S(1)}, u32[]{:S(2)}, u32[]{:S(2)}) collective-permute-start(bf16[48,1536]{1,0:T(8,128)(2,1)S(1)} %add_convert_fusion.3), channel_id=1, source_target_pairs={{0,256},{32,288},{64,320},{96,352},{128,384},{160,416},{192,448},{... | collective-permute-start | bytes 442376 | tf_op jit(solution)/shard_map/ppermute | solution.py:267
  152.7 7.9 %collective-permute-done.8 = bf16[48,1536]{1,0:T(8,128)(2,1)S(1)} collective-permute-done((bf16[48,1536]{1,0:T(8,128)(2,1)S(1)}, bf16[48,1536]{1,0:T(8,128)(2,1)S(1)}, u32[]{:S(2)}, u32[]{:S(2)}) %collective-permute-start.8) | collective-permute-done | bytes 147488 | tf_op jit(solution)/shard_map/ppermute | solution.py:267
  160.6 15.5 %all_to_all.45 = bf16[4,48,1536]{2,1,0:T(8,128)(2,1)S(1)} all-to-all(bf16[4,48,1536]{2,1,0:T(8,128)(2,1)S(1)} %broadcast_in_dim.7), channel_id=1, replica_groups={{0,64,128,192},{32,96,160,224},{256,320,384,448},{288,352,416,480},{1,6..., dimensions={0} | all-to-all | bytes 1179648 | tf_op jit(solution)/shard_map/all_to_all | solution.py:282
  176.2 9.9 %collective-permute-start.9 = (bf16[192,1536]{1,0:T(8,128)(2,1)S(1)}, bf16[192,1536]{1,0:T(8,128)(2,1)S(1)}, u32[]{:S(2)}, u32[]{:S(2)}) collective-permute-start(bf16[192,1536]{1,0:T(8,128)(2,1)S(1)} %bitcast.27), channel_id=1, source_target_pairs={{0,32},{32,0},{64,96},{96,64},{128,160},{160,128},{192,224},{224,1... | collective-permute-start | bytes 1769480 | tf_op jit(solution)/shard_map/ppermute | solution.py:267
  (41 shorter events, 11.4 us)
Async XLA Ops:
  1.0 25.3 %collective-permute-start = (bf16[48,1536]{1,0:T(8,128)(2,1)S(1)}, bf16[48,1536]{1,0:T(8,128)(2,1)S(1)}, u32[]{:S(2)}, u32[]{:S(2)}) collective-permute-start(bf16[48,1536]{1,0:T(8,128)(2,1)S(1)} %dynamic-slice_bitcast_fusion), channel_id=1, source_target_pairs={{1,448},{2,449},{3,450},{4,451},{5,452},{6,453},{7,454},{33,480},{... | collective-permute-start | bytes 442376 | tf_op jit(solution)/shard_map/ppermute | solution.py:276
  4.3 9.0 %all-to-all-start.4 = ((s32[4,2,3]{2,1,0:T(2,128)}), s32[4,2,3]{2,1,0:T(2,128)S(1)}, u32[]{:S(2)}, u32[]{:S(2)}) async-start(s32[4,2,3]{2,1,0:T(2,128)} %broadcast_in_dim.6), calls=%async_computation.4 | async-start | bytes 8192 | tf_op jit(solution)/shard_map/all_to_all | solution.py:279
  13.4 1.3 copy-start
  26.3 26.2 %all-to-all-start.5 = ((bf16[4,2,2,192,256]{4,3,2,1,0:T(8,128)(2,1)}), bf16[4,2,2,192,256]{4,3,2,1,0:T(8,128)(2,1)S(1)}, u32[]{:S(2)}, u32[]{:S(2)}) async-start(bf16[4,2,2,192,256]{4,3,2,1,0:T(8,128)(2,1)} %shard_map.91), calls=%async_computation.5 | async-start | bytes 3145728 | tf_op jit(solution)/shard_map/all_to_all | solution.py:279
  30.3 9.3 %collective-permute-start.1 = (bf16[48,1536]{1,0:T(8,128)(2,1)S(1)}, bf16[48,1536]{1,0:T(8,128)(2,1)S(1)}, u32[]{:S(2)}, u32[]{:S(2)}) collective-permute-start(bf16[48,1536]{1,0:T(8,128)(2,1)S(1)} %collective-permute-done.refs_0_), channel_id=1, source_target_pairs={{0,64},{32,96},{64,0},{96,32},{128,192},{160,224},{192,128},{224,1... | collective-permute-start | bytes 442376 | tf_op jit(solution)/shard_map/ppermute | solution.py:267
  32.2 13.7 %collective-permute-start.2 = (bf16[48,1536]{1,0:T(8,128)(2,1)S(1)}, bf16[48,1536]{1,0:T(8,128)(2,1)S(1)}, u32[]{:S(2)}, u32[]{:S(2)}) collective-permute-start(bf16[48,1536]{1,0:T(8,128)(2,1)S(1)} %collective-permute-done.refs_0_), channel_id=1, source_target_pairs={{0,128},{32,160},{64,192},{96,224},{128,0},{160,32},{192,64},{224,... | collective-permute-start | bytes 442376 | tf_op jit(solution)/shard_map/ppermute | solution.py:267
  34.1 11.8 %collective-permute-start.3 = (bf16[48,1536]{1,0:T(8,128)(2,1)S(1)}, bf16[48,1536]{1,0:T(8,128)(2,1)S(1)}, u32[]{:S(2)}, u32[]{:S(2)}) collective-permute-start(bf16[48,1536]{1,0:T(8,128)(2,1)S(1)} %collective-permute-done.refs_0_), channel_id=1, source_target_pairs={{0,192},{32,224},{64,128},{96,160},{128,64},{160,96},{192,0},{224,... | collective-permute-start | bytes 442376 | tf_op jit(solution)/shard_map/ppermute | solution.py:267
  46.0 6.5 %collective-permute-start.4 = (bf16[4,48,1536]{2,1,0:T(8,128)(2,1)S(1)}, bf16[4,48,1536]{2,1,0:T(8,128)(2,1)S(1)}, u32[]{:S(2)}, u32[]{:S(2)}) collective-permute-start(bf16[4,48,1536]{2,1,0:T(8,128)(2,1)S(1)} %pad_maximum_fusion.2), channel_id=1, source_target_pairs={{0,32},{32,0},{64,96},{96,64},{128,160},{160,128},{192,224},{224,1... | collective-permute-start | bytes 1769480 | tf_op jit(solution)/shard_map/ppermute | solution.py:267
  55.3 17.0 %copy-start.2 = (f32[2,256,256]{2,1,0:T(8,128)S(1)}, f32[2,256,256]{2,1,0:T(8,128)}, u32[]{:S(2)}) copy-start(f32[2,256,256]{2,1,0:T(8,128)} %probe.1) | copy-start | bytes 1572868
  55.4 17.0 %copy-start.3 = (bf16[1,1,1,2,256,256]{5,4,3,2,1,0:T(8,128)(2,1)S(1)}, bf16[1,1,1,2,256,256]{5,4,3,2,1,0:T(8,128)(2,1)}, u32[]{:S(2)}) copy-start(bf16[1,1,1,2,256,256]{5,4,3,2,1,0:T(8,128)(2,1)} %param.15) | copy-start | bytes 786436
  55.4 17.0 %copy-start.4 = (bf16[256,256]{1,0:T(8,128)(2,1)S(1)}, bf16[256,256]{1,0:T(8,128)(2,1)}, u32[]{:S(2)}) copy-start(bf16[256,256]{1,0:T(8,128)(2,1)} %constant.112.clone.wr_ref) | copy-start | bytes 393220
  55.4 17.0 %copy-start.5 = (bf16[256,256]{1,0:T(8,128)(2,1)S(1)}, bf16[256,256]{1,0:T(8,128)(2,1)}, u32[]{:S(2)}) copy-start(bf16[256,256]{1,0:T(8,128)(2,1)} %constant.113.clone.wi_ref) | copy-start | bytes 393220
  91.1 17.2 %collective-permute-start.5 = (bf16[192,1536]{1,0:T(8,128)(2,1)S(1)}, bf16[192,1536]{1,0:T(8,128)(2,1)S(1)}, u32[]{:S(2)}, u32[]{:S(2)}) collective-permute-start(bf16[192,1536]{1,0:T(8,128)(2,1)S(1)} %get-tuple-element.42), channel_id=1, source_target_pairs={{0,32},{32,0},{64,96},{96,64},{128,160},{160,128},{192,224},{224,1... | collective-permute-start | bytes 1769480 | tf_op jit(solution)/shard_map/ppermute | solution.py:267
  109.2 19.1 %all-to-all-start.6 = ((bf16[4,48,1536]{2,1,0:T(8,128)(2,1)}), bf16[4,48,1536]{2,1,0:T(8,128)(2,1)S(1)}, u32[]{:S(2)}, u32[]{:S(2)}) async-start(bf16[4,48,1536]{2,1,0:T(8,128)(2,1)} %bitcast.15), calls=%async_computation.6 | async-start | bytes 1179648 | tf_op jit(solution)/shard_map/all_to_all | solution.py:282
  115.4 4.3 %collective-permute-start.6 = (bf16[192,1536]{1,0:T(8,128)(2,1)S(1)}, bf16[192,1536]{1,0:T(8,128)(2,1)S(1)}, u32[]{:S(2)}, u32[]{:S(2)}) collective-permute-start(bf16[192,1536]{1,0:T(8,128)(2,1)S(1)} %get-tuple-element.44), channel_id=1, source_target_pairs={{0,32},{32,0},{64,96},{96,64},{128,160},{160,128},{192,224},{224,1... | collective-permute-start | bytes 1769480 | tf_op jit(solution)/shard_map/ppermute | solution.py:267
  128.4 22.0 %all-to-all-start.7 = ((bf16[4,48,1536]{2,1,0:T(8,128)(2,1)}), bf16[4,48,1536]{2,1,0:T(8,128)(2,1)S(1)}, u32[]{:S(2)}, u32[]{:S(2)}) async-start(bf16[4,48,1536]{2,1,0:T(8,128)(2,1)} %bitcast.16), calls=%async_computation.7 | async-start | bytes 1179648 | tf_op jit(solution)/shard_map/all_to_all | solution.py:282
  131.9 18.6 %collective-permute-start.7 = (bf16[48,1536]{1,0:T(8,128)(2,1)S(1)}, bf16[48,1536]{1,0:T(8,128)(2,1)S(1)}, u32[]{:S(2)}, u32[]{:S(2)}) collective-permute-start(bf16[48,1536]{1,0:T(8,128)(2,1)S(1)} %reduce_sum.21), channel_id=1, source_target_pairs={{0,449},{1,450},{2,451},{3,452},{4,453},{5,454},{6,455},{32,481},{... | collective-permute-start | bytes 442376 | tf_op jit(solution)/shard_map/ppermute | solution.py:276
  150.5 35.5 %copy-start.1 = (bf16[2,1,192,1536]{3,2,1,0:T(8,128)(2,1)S(1)}, bf16[2,1,192,1536]{3,2,1,0:T(8,128)(2,1)}, u32[]{:S(2)}) copy-start(bf16[2,1,192,1536]{3,2,1,0:T(8,128)(2,1)} %param.13) | copy-start | bytes 3538948
  150.6 9.9 %collective-permute-start.8 = (bf16[48,1536]{1,0:T(8,128)(2,1)S(1)}, bf16[48,1536]{1,0:T(8,128)(2,1)S(1)}, u32[]{:S(2)}, u32[]{:S(2)}) collective-permute-start(bf16[48,1536]{1,0:T(8,128)(2,1)S(1)} %add_convert_fusion.3), channel_id=1, source_target_pairs={{0,256},{32,288},{64,320},{96,352},{128,384},{160,416},{192,448},{... | collective-permute-start | bytes 442376 | tf_op jit(solution)/shard_map/ppermute | solution.py:267
  176.2 11.5 %collective-permute-start.9 = (bf16[192,1536]{1,0:T(8,128)(2,1)S(1)}, bf16[192,1536]{1,0:T(8,128)(2,1)S(1)}, u32[]{:S(2)}, u32[]{:S(2)}) collective-permute-start(bf16[192,1536]{1,0:T(8,128)(2,1)S(1)} %bitcast.27), channel_id=1, source_target_pairs={{0,32},{32,0},{64,96},{96,64},{128,160},{160,128},{192,224},{224,1... | collective-permute-start | bytes 1769480 | tf_op jit(solution)/shard_map/ppermute | solution.py:267

commit v7 on v6

v7 whole, which is shorter than its diff:
```python
import functools

import jax
import jax.numpy as jnp
import ml_dtypes
import numpy as np
from jax import lax
from jax.experimental import pallas as pl
from jax.experimental.pallas import tpu as pltpu
from jax.sharding import PartitionSpec as P

angle_center = 600
shear_divisor = 64
step_size = 0.03
floor_square = 0.25

LANE = 128


def dft_tables(plane_width):
    index_line = np.arange(plane_width, dtype=np.int32)
    product_mod = np.mod(index_line[:, None] * index_line[None, :], plane_width)
    phase_table = product_mod.astype(np.float32) * np.float32(2.0 * 3.141592653589793 / plane_width)
    scale_factor = np.float32(plane_width ** (-0.5))
    table_real = (np.cos(phase_table) * scale_factor).astype(ml_dtypes.bfloat16)
    table_imag = (-np.sin(phase_table) * scale_factor).astype(ml_dtypes.bfloat16)
    return table_real, table_imag


def dot(left, right):
    return jnp.dot(left, right, preferred_element_type=jnp.float32)


def one_hot(rows, columns, down):
    row = lax.broadcasted_iota(jnp.int32, (rows, columns), 0)
    column = lax.broadcasted_iota(jnp.int32, (rows, columns), 1)
    return (row - column == down).astype(jnp.float32).astype(jnp.bfloat16)


VMEM = pl.BlockSpec(memory_space=pltpu.VMEM)


def call(body, out_shape, scratch, facts, *args):
    return pl.pallas_call(
        body,
        out_shape=out_shape,
        in_specs=[pl.BlockSpec(memory_space=pltpu.SMEM)] + [VMEM] * len(args),
        out_specs=[VMEM] * len(out_shape),
        scratch_shapes=scratch,
        compiler_params=pltpu.CompilerParams(vmem_limit_bytes=24 * 1024 * 1024),
    )(facts, *args)


class Facts:
    def __init__(self, ref, slots, slabs, columns):
        self.ref, self.slots, self.slabs, self.columns = ref, slots, slabs, columns
        self.stride = 3 * slots + 1

    def slot(self, angle, slot):
        return tuple(self.ref[self.stride * angle + 3 * slot + i] for i in range(3))

    def columns_of(self, angle, slot, step):
        layer = lax.rem(self.ref[8 * self.stride] + self.slabs + step, self.slabs)
        index = self.ref[self.stride * angle + self.stride - 1]
        shift = ((index - angle_center) * (layer - self.slabs // 2)) >> (shear_divisor.bit_length() - 1)
        shift = lax.rem(lax.rem(shift, self.columns) + self.columns, self.columns)
        left = lax.rem(self.slot(angle, slot)[1] + shift, self.columns)
        blocks = self.columns // LANE
        starts = [pl.multiple_of(lax.rem(left // LANE + i, blocks) * LANE, LANE) for i in range(3)]
        return starts, lax.rem(left, LANE)


def cut_body(slabs, facts_ref, *refs):
    blocks, out = refs[:-1], refs[-1]
    angles, slots, rows, width = out.shape
    facts = Facts(facts_ref, slots, slabs, blocks[0].shape[1])
    lane = lax.broadcasted_iota(jnp.int32, (rows, LANE), 1)
    for slot in range(slots):
        for angle in range(angles):

            @pl.when(facts.slot(angle, slot)[2] > 0)
            def _():
                total = [jnp.zeros((rows, LANE), jnp.float32)] * 2
                for k, block in enumerate(blocks):
                    starts, inside = facts.columns_of(angle, slot, -k)
                    turned = [
                        pltpu.roll(block[:, pl.ds(start, LANE)].astype(jnp.float32), (LANE - inside) % LANE, 1)
                        for start in starts
                    ]
                    here = lane < LANE - inside
                    total = [t + jnp.where(here, turned[i], turned[i + 1]) for i, t in enumerate(total)]
                out[angle, slot] = jnp.concatenate(total, axis=1).astype(jnp.bfloat16)


def cut_windows(facts, blocks, angles, slots, width):
    out = jax.ShapeDtypeStruct((angles, slots, blocks[0].shape[0], width), jnp.bfloat16)
    return call(functools.partial(cut_body, len(blocks)), [out], [], facts, *blocks)[0]


def cos_sin(angle):
    turns = jnp.round(angle * 0.6366197723675814)
    rest = angle - turns * 1.5703125
    rest = rest - turns * 4.837512969970703e-4
    rest = rest - turns * 7.549789948768648e-8
    square = rest * rest
    sine = (-1.9515295891e-4 * square + 8.3321608736e-3) * square - 1.6666654611e-1
    sine = sine * square * rest + rest
    cosine = (2.443315711809948e-5 * square - 1.388731625493765e-3) * square + 4.166664568298827e-2
    cosine = cosine * square * square - 0.5 * square + 1.0
    quarter = turns.astype(jnp.int32)
    odd = (quarter & 1) == 1
    first, second = jnp.where(odd, sine, cosine), jnp.where(odd, cosine, sine)
    return (
        jnp.where(((quarter + 1) & 2) == 2, -first, first),
        jnp.where((quarter & 2) == 2, -second, second),
    )


def patch_body(slot_ref, own_in, next_in, probe, patterns, wr_ref, wi_ref, own_out, next_out):
    angles, slots, rows, width = own_in.shape
    f32, bf16 = jnp.float32, jnp.bfloat16
    blocks = angles // 2
    tall = 2 * blocks * rows
    for slot in range(slots):
        row, live = slot_ref[2 * slot], slot_ref[2 * slot + 1]

        @pl.when(live > 0)
        def _():
            pick = one_hot(width, tall, -row)
            window = []
            for part in range(2):
                held = [ref[2 * k + part, slot] for ref in (own_in, next_in) for k in range(blocks)]
                window.append(dot(pick, jnp.concatenate(held, axis=0)))
            phase, absorption = window
            magnitude = jnp.exp(-absorption)
            cosine, sine = cos_sin(phase)
            trans_real = magnitude * cosine
            trans_imag = magnitude * sine
            probe_real, probe_imag = probe[0], probe[1]
            wr, wi = wr_ref[...], wi_ref[...]
            wave_real = (probe_real * trans_real - probe_imag * trans_imag).astype(bf16)
            wave_imag = (probe_real * trans_imag + probe_imag * trans_real).astype(bf16)
            left_real = (dot(wr, wave_real) - dot(wi, wave_imag)).astype(bf16)
            left_imag = (dot(wr, wave_imag) + dot(wi, wave_real)).astype(bf16)
            far_real = dot(left_real, wr) - dot(left_imag, wi)
            far_imag = dot(left_real, wi) + dot(left_imag, wr)
            power = far_real * far_real + far_imag * far_imag + floor_square
            keeping = 1.0 - patterns[slot].astype(f32) * lax.rsqrt(power)
            resid_real = (far_real * keeping).astype(bf16)
            resid_imag = (far_imag * keeping).astype(bf16)
            back_real = (dot(wr, resid_real) + dot(wi, resid_imag)).astype(bf16)
            back_imag = (dot(wr, resid_imag) - dot(wi, resid_real)).astype(bf16)
            exit_real = dot(back_real, wr) + dot(back_imag, wi)
            exit_imag = dot(back_imag, wr) - dot(back_real, wi)
            mixed_real = probe_real * exit_real + probe_imag * exit_imag
            mixed_imag = probe_real * exit_imag - probe_imag * exit_real
            final_real = trans_real * mixed_real + trans_imag * mixed_imag
            final_imag = trans_real * mixed_imag - trans_imag * mixed_real
            put = one_hot(tall, width, row)
            for part, value in enumerate((final_imag, -final_real)):
                placed = dot(put, value.astype(bf16)).astype(bf16)
                for k in range(blocks):
                    own_out[2 * k + part, slot] = placed[k * rows : (k + 1) * rows]
                    below = placed[(blocks + k) * rows : (blocks + k + 1) * rows]
                    next_out[2 * (blocks - 1 - k) + part, slot] = below


def patch_gradients(slot_facts, own, after, probe_wave, patterns, tables):
    out = jax.ShapeDtypeStruct(own.shape, jnp.bfloat16)
    return call(patch_body, [out, out], [], slot_facts, own, after, probe_wave, patterns, *tables)


def place_body(facts_ref, windows, *refs):
    outs, total = refs[:-1], refs[-1]
    angles, slots, rows, width = windows.shape
    facts = Facts(facts_ref, slots, len(outs), total.shape[2])
    lane = lax.broadcasted_iota(jnp.int32, (rows, LANE), 1)
    total[...] = jnp.zeros_like(total)
    for slot in range(slots):
        for angle in range(angles):

            @pl.when(facts.slot(angle, slot)[2] > 0)
            def _():
                window = windows[angle, slot].astype(jnp.float32)
                for k in range(len(outs)):
                    starts, inside = facts.columns_of(angle, slot, k)
                    first, second = (pltpu.roll(window[:, i * LANE : (i + 1) * LANE], inside, 1) for i in range(2))
                    there = lane < inside
                    total[k, :, pl.ds(starts[0], LANE)] += jnp.where(there, 0.0, first)
                    total[k, :, pl.ds(starts[1], LANE)] += jnp.where(there, first, second)
                    total[k, :, pl.ds(starts[2], LANE)] += jnp.where(there, second, 0.0)
    for k, out in enumerate(outs):
        out[...] = total[k].astype(out.dtype)


def place_windows(facts, windows, slabs, columns):
    shape = (windows.shape[2], columns)
    outs = [jax.ShapeDtypeStruct(shape, jnp.bfloat16 if k else jnp.float32) for k in range(slabs)]
    return call(place_body, outs, [pltpu.VMEM((slabs, *shape), jnp.float32)], facts, windows)


def step_body(part_ref, layer, gradient, *refs):
    out, made, sems = refs[-3:]
    part = part_ref[0]
    size = gradient.shape[0] // 4
    copies = []
    for n in range(4):
        rows = slice(n * size, (n + 1) * size)
        made[rows] = layer[part, rows].astype(jnp.float32) - step_size * gradient[rows].astype(jnp.float32)
        copies.append(
            pltpu.make_async_copy(made.at[pl.ds(n * size, size)], out.at[part, pl.ds(n * size, size)], sems.at[n])
        )
        copies[-1].start()
    for copy in copies:
        copy.wait()


def step(part, layer, gradient, *stepped):
    return pl.pallas_call(
        step_body,
        out_shape=jax.ShapeDtypeStruct(layer.shape, jnp.float32),
        in_specs=[pl.BlockSpec(memory_space=pltpu.SMEM), VMEM, VMEM]
        + [pl.BlockSpec(memory_space=pltpu.HBM)] * len(stepped),
        out_specs=pl.BlockSpec(memory_space=pltpu.HBM),
        scratch_shapes=[pltpu.VMEM(gradient.shape, jnp.float32), pltpu.SemaphoreType.DMA((4,))],
        input_output_aliases={3: 0} if stepped else {},
        compiler_params=pltpu.CompilerParams(vmem_limit_bytes=24 * 1024 * 1024),
    )(part.reshape(1).astype(jnp.int32), layer, gradient, *stepped)


def per_device(volume, probe_wave, amplitudes, offsets, column_starts, counts, angle_ids):
    layer = volume.reshape(volume.shape[0], *volume.shape[2:])
    tile_rows, columns = layer.shape[1:]
    width = amplitudes.shape[-1]
    slots = offsets.shape[3]
    angles, slabs, tiles = (lax.axis_size(axis) for axis in ("angle", "slab", "tile"))
    slab, angle = lax.axis_index("slab"), lax.axis_index("angle")
    f32, bf16 = jnp.float32, jnp.bfloat16
    tables = dft_tables(width)
    patterns = amplitudes.reshape(slots, width, width)

    core, place_z = angle % 2, angle // 2 % 4
    eight_groups = [[8 * f + i for i in range(8)] for f in range(angles // 8)]
    four_groups = [[8 * f + 2 * q + c for q in range(4)] for f in range(angles // 8) for c in range(2)]
    block_rows = tile_rows // 4

    def swap(value, by):
        return lax.ppermute(value, "angle", [(i, i ^ by) for i in range(angles)])

    def mirrored(value, by):
        pairs = [
            (a * tiles + t, (angles - 2 - (a - a % 2) + a % 2) * tiles + t + by)
            for a in range(angles)
            for t in range(tiles)
            if 0 <= t + by < tiles
        ]
        return lax.ppermute(value, ("angle", "tile"), pairs)

    def to_slab(value, by):
        return lax.ppermute(value, "slab", [(i, (i + by) % slabs) for i in range(slabs)])

    def to_eight(value):
        return lax.all_to_all(value, "angle", 0, 0, axis_index_groups=eight_groups, tiled=True)

    def to_four(value):
        return lax.all_to_all(value, "angle", 0, 0, axis_index_groups=four_groups, tiled=True)

    def of_slabs(block):
        return [block] + [to_slab(block, k) for k in range(1, slabs)]

    def over_slabs(kept, *sent):
        return sum((to_slab(block, k + 1).astype(f32) for k, block in enumerate(sent)), kept)

    own_part = lax.dynamic_index_in_dim(layer, core, 0, keepdims=False)

    def rows_of(block):
        return lax.dynamic_slice(own_part, (block * block_rows, 0), (block_rows, columns))

    after, own, counts = lax.optimization_barrier((rows_of(3 - place_z), rows_of(place_z), counts))
    after, own = mirrored(after, -1), of_slabs(own)

    live = (jnp.arange(slots) < counts.reshape(1)).astype(jnp.int32)
    meta = jnp.stack([offsets.reshape(slots), column_starts.reshape(slots), live], axis=1)
    eight = to_eight(jnp.broadcast_to(jnp.concatenate([meta.reshape(-1), angle_ids]), (8, 3 * slots + 1)))
    facts = jnp.concatenate([eight.reshape(-1), slab.reshape(1)]).astype(jnp.int32)
    slot_facts = jnp.stack([offsets.reshape(slots), live], axis=1).reshape(-1)

    own = cut_windows(facts, own, 8, slots, width)
    after, own = lax.optimization_barrier((after, own))
    after, own = lax.optimization_barrier((of_slabs(after), to_eight(own)))
    after = to_eight(cut_windows(facts, after, 8, slots, width))

    own, after = patch_gradients(slot_facts, own, after, probe_wave, patterns, tables)
    after = place_windows(facts, to_eight(after), slabs, columns)
    after, own = lax.optimization_barrier((after, own))
    spill = mirrored(over_slabs(*after).astype(bf16), 1)
    own = over_slabs(*place_windows(facts, to_eight(own), slabs, columns))

    total = lax.optimization_barrier((own + spill.astype(f32)).astype(bf16))
    total = (total.astype(f32) + swap(total, 8).astype(f32)).astype(bf16)

    total = to_four(jnp.broadcast_to(total, (4, *total.shape))).reshape(tile_rows, columns)
    new = step(core, layer, total)
    return step(1 - core, layer, swap(total, 1), new).reshape(volume.shape)


def solution(mesh):
    in_specs = (
        P(None, "slab", "tile", None),
        P(),
        P("angle", "tile", "slab", None, None, None),
        P("angle", "tile", "slab", None),
        P("angle", "tile", "slab", None),
        P("angle", "tile", "slab"),
        P("angle"),
    )
    out_specs = P(None, "slab", "tile", None)
    return jax.shard_map(
        per_device, mesh=mesh, in_specs=in_specs, out_specs=out_specs, check_vma=False
    )
```

time: 192 us -> 186 us (0.969); the launches traced: 189 us -> 185 us
  starting transfers between devices: 62.8 us -> 76.1 us
  blocking collectives: 43.2 us -> 34.8 us
  waiting for transfers between devices: 54.3 us -> 49.5 us
  other arithmetic: 5.19 us -> 1.72 us
    ppermute x0 -> x12, starting transfers between devices: none -> 37.3 us  [to_slab(): lax.ppermute(value, 'slab', [(i, (i + by) % slabs) for i in range(slabs)])]
    ppermute x8 -> x2, starting transfers between devices: 44.4 us -> 11.2 us  [swap(): return lax.ppermute(value, 'angle', [(i, i ^ by) for i in range(angles)])]
    ppermute x0 -> x12, waiting for transfers between devices: none -> 16.5 us  [to_slab(): lax.ppermute(value, 'slab', [(i, (i + by) % slabs) for i in range(slabs)])]
    all_to_all x4, waiting for transfers between devices: 28.4 us -> 16.3 us  [to_eight(): lax.all_to_all(value, 'angle', 0, 0, axis_index_groups=eight_groups, tile...]
    all_to_all x2 -> x1, blocking collectives: 27.7 us -> 17 us  [to_eight(): lax.all_to_all(value, 'angle', 0, 0, axis_index_groups=eight_groups, tile...]
    all_to_all x4, starting transfers between devices: 15.8 us -> 22.2 us  [to_eight(): lax.all_to_all(value, 'angle', 0, 0, axis_index_groups=eight_groups, tile...]
    ppermute x2, waiting for transfers between devices: 7.69 us -> 2.89 us  [mirrored(): return lax.ppermute(value, ('angle', 'tile'), pairs)]
    ppermute x8 -> x2, waiting for transfers between devices: 18.2 us -> 13.8 us  [swap(): return lax.ppermute(value, 'angle', [(i, i ^ by) for i in range(angles)])]
  transfers between devices with their start and end apart: 14 -> 20, of which waited for: 10 -> 11; matrix products, arithmetic and copies ran while one was open for 2% -> 2% of each run, Pallas kernels for 4% -> 4%
where the time goes in v7:
time: 186 us; the launch traced here: 185 us
  starting transfers between devices  76.1 us (41%)
  waiting for transfers between devices  49.5 us (27%)
  blocking collectives  34.8 us (19%)
  Pallas kernels  18.2 us (10%)
  local copies, waits for them, and re-layouts  2.8 us (2%)
    ppermute x12, starting transfers between devices, to_slab(): lax.ppermute(value, 'slab', [(i, (i + by) % slabs) for i in range(slabs)])  37.3 us
    all_to_all x4, starting transfers between devices, to_eight(): lax.all_to_all(value, 'angle', 0, 0, axis_index_groups=eight_groups, tile...  22.2 us
    all_to_all x1, blocking collectives, to_four(): lax.all_to_all(value, 'angle', 0, 0, axis_index_groups=four_groups, tiled...  17.7 us
    all_to_all x1, blocking collectives, to_eight(): lax.all_to_all(value, 'angle', 0, 0, axis_index_groups=eight_groups, tile...  17 us
    ppermute x12, waiting for transfers between devices, to_slab(): lax.ppermute(value, 'slab', [(i, (i + by) % slabs) for i in range(slabs)])  16.5 us
    all_to_all x4, waiting for transfers between devices, to_eight(): lax.all_to_all(value, 'angle', 0, 0, axis_index_groups=eight_groups, tile...  16.3 us
    pallas_call x5, Pallas kernels, call(): pl.pallas_call(body, out_shape=out_shape, in_specs=[pl.BlockSpec(memory_s...  16 us
    ppermute x2, waiting for transfers between devices, swap(): return lax.ppermute(value, 'angle', [(i, i ^ by) for i in range(angles)])  13.8 us
  transfers between devices with their start and end apart: 20, of which 11 were waited for; matrix products, arithmetic and copies ran while one was open for 2% of the time, Pallas kernels for 4%

profile of v7, /device:TPU:1, one launch (start us, length us, event | category | flops | bytes accessed | tf_op | source)
XLA Modules:
  0.0 184.8 jit_solution(4781576517712869952)
XLA Ops:
  1.3 5.2 %collective-permute-start.3 = (bf16[48,1536]{1,0:T(8,128)(2,1)S(1)}, bf16[48,1536]{1,0:T(8,128)(2,1)S(1)}, u32[]{:S(2)}, u32[]{:S(2)}) collective-permute-start(bf16[48,1536]{1,0:T(8,128)(2,1)S(1)} %get-tuple-element.32.refs_0_), channel_id=1, source_target_pairs={{0,24},{8,0},{16,8},{24,16},{1,25},{9,1},{17,9},{25,17},{2,26},{10... | collective-permute-start | bytes 442376 | tf_op jit(solution)/shard_map/ppermute | solution.py:260
  6.5 2.4 %collective-permute-start.2 = (bf16[48,1536]{1,0:T(8,128)(2,1)S(1)}, bf16[48,1536]{1,0:T(8,128)(2,1)S(1)}, u32[]{:S(2)}, u32[]{:S(2)}) collective-permute-start(bf16[48,1536]{1,0:T(8,128)(2,1)S(1)} %get-tuple-element.32.refs_0_), channel_id=1, source_target_pairs={{0,16},{8,24},{16,0},{24,8},{1,17},{9,25},{17,1},{25,9},{2,18},{10... | collective-permute-start | bytes 442376 | tf_op jit(solution)/shard_map/ppermute | solution.py:260
  8.9 2.5 %collective-permute-start.1 = (bf16[48,1536]{1,0:T(8,128)(2,1)S(1)}, bf16[48,1536]{1,0:T(8,128)(2,1)S(1)}, u32[]{:S(2)}, u32[]{:S(2)}) collective-permute-start(bf16[48,1536]{1,0:T(8,128)(2,1)S(1)} %get-tuple-element.32.refs_0_), channel_id=1, source_target_pairs={{0,8},{8,16},{16,24},{24,0},{1,9},{9,17},{17,25},{25,1},{2,10},{10... | collective-permute-start | bytes 442376 | tf_op jit(solution)/shard_map/ppermute | solution.py:260
  15.6 7.7 %all-to-all-start = ((s32[8,1,7]{2,1,0:T(1,128)}), s32[8,1,7]{2,1,0:T(1,128)S(1)}, u32[]{:S(2)}, u32[]{:S(2)}) async-start(s32[8,1,7]{2,1,0:T(1,128)} %broadcast_in_dim.6), calls=%async_computation | async-start | bytes 8192 | tf_op jit(solution)/shard_map/all_to_all | solution.py:263
  23.3 4.8 %all-to-all-done = s32[8,1,7]{2,1,0:T(1,128)S(1)} async-done(((s32[8,1,7]{2,1,0:T(1,128)}), s32[8,1,7]{2,1,0:T(1,128)S(1)}, u32[]{:S(2)}, u32[]{:S(2)}) %all-to-all-start) | async-done | bytes 256 | tf_op jit(solution)/shard_map/all_to_all | solution.py:263
  29.5 3.5 %shard_map.91 = bf16[8,2,48,256]{3,2,1,0:T(8,128)(2,1)} custom-call(s32[57]{0:T(128)S(1)} %pad_add_fusion.3.facts_ref, bf16[48,1536]{1,0:T(8,128)(2,1)S(1)} %get-tuple-element.32.refs_0_, bf16[48,1536]{1,0:T(8,128)(2,1)S(1)} %collective-permute-done.1.refs_1_, bf16[48,1536]{1,0:T(8,128)(2,1)S(1)} %collective-permute-done.2.refs_2_, ...), custom_call_target="tpu_custom_call" | custom-call | tf_op jit(solution)/shard_map/pallas_call | solution.py:44
  32.9 2.9 %collective-permute-done.refs_0_ = bf16[48,1536]{1,0:T(8,128)(2,1)S(1)} collective-permute-done((bf16[48,1536]{1,0:T(8,128)(2,1)S(1)}, bf16[48,1536]{1,0:T(8,128)(2,1)S(1)}, u32[]{:S(2)}, u32[]{:S(2)}) %collective-permute-start) | collective-permute-done | bytes 147488 | tf_op jit(solution)/shard_map/ppermute | solution.py:257
  35.8 4.4 %all-to-all-start.1 = ((bf16[8,2,48,256]{3,2,1,0:T(8,128)(2,1)}), bf16[8,2,48,256]{3,2,1,0:T(8,128)(2,1)S(1)}, u32[]{:S(2)}, u32[]{:S(2)}) async-start(bf16[8,2,48,256]{3,2,1,0:T(8,128)(2,1)} %shard_map.91), calls=%async_computation.1 | async-start | bytes 786432 | tf_op jit(solution)/shard_map/all_to_all | solution.py:263
  40.2 4.0 %collective-permute-start.6 = (bf16[48,1536]{1,0:T(8,128)(2,1)S(1)}, bf16[48,1536]{1,0:T(8,128)(2,1)S(1)}, u32[]{:S(2)}, u32[]{:S(2)}) collective-permute-start(bf16[48,1536]{1,0:T(8,128)(2,1)S(1)} %collective-permute-done.refs_0_), channel_id=1, source_target_pairs={{0,24},{8,0},{16,8},{24,16},{1,25},{9,1},{17,9},{25,17},{2,26},{10... | collective-permute-start | bytes 442376 | tf_op jit(solution)/shard_map/ppermute | solution.py:260
  44.2 3.1 %collective-permute-start.5 = (bf16[48,1536]{1,0:T(8,128)(2,1)S(1)}, bf16[48,1536]{1,0:T(8,128)(2,1)S(1)}, u32[]{:S(2)}, u32[]{:S(2)}) collective-permute-start(bf16[48,1536]{1,0:T(8,128)(2,1)S(1)} %collective-permute-done.refs_0_), channel_id=1, source_target_pairs={{0,16},{8,24},{16,0},{24,8},{1,17},{9,25},{17,1},{25,9},{2,18},{10... | collective-permute-start | bytes 442376 | tf_op jit(solution)/shard_map/ppermute | solution.py:260
  49.3 3.3 %collective-permute-done.5.refs_2_ = bf16[48,1536]{1,0:T(8,128)(2,1)S(1)} collective-permute-done((bf16[48,1536]{1,0:T(8,128)(2,1)S(1)}, bf16[48,1536]{1,0:T(8,128)(2,1)S(1)}, u32[]{:S(2)}, u32[]{:S(2)}) %collective-permute-start.5) | collective-permute-done | bytes 147488 | tf_op jit(solution)/shard_map/ppermute | solution.py:260
  52.6 3.7 %collective-permute-done.4.refs_1_ = bf16[48,1536]{1,0:T(8,128)(2,1)S(1)} collective-permute-done((bf16[48,1536]{1,0:T(8,128)(2,1)S(1)}, bf16[48,1536]{1,0:T(8,128)(2,1)S(1)}, u32[]{:S(2)}, u32[]{:S(2)}) %collective-permute-start.4) | collective-permute-done | bytes 147488 | tf_op jit(solution)/shard_map/ppermute | solution.py:260
  56.3 3.5 %shard_map.92 = bf16[8,2,48,256]{3,2,1,0:T(8,128)(2,1)} custom-call(s32[57]{0:T(128)S(1)} %pad_add_fusion.3.facts_ref, bf16[48,1536]{1,0:T(8,128)(2,1)S(1)} %collective-permute-done.refs_0_, bf16[48,1536]{1,0:T(8,128)(2,1)S(1)} %collective-permute-done.4.refs_1_, bf16[48,1536]{1,0:T(8,128)(2,1)S(1)} %collective-permute-done.5.refs_2_, ...), custom_call_target="tpu_custom_call" | custom-call | tf_op jit(solution)/shard_map/pallas_call | solution.py:44
  59.8 5.9 %all-to-all-start.2 = ((bf16[8,2,48,256]{3,2,1,0:T(8,128)(2,1)}), bf16[8,2,48,256]{3,2,1,0:T(8,128)(2,1)S(1)}, u32[]{:S(2)}, u32[]{:S(2)}) async-start(bf16[8,2,48,256]{3,2,1,0:T(8,128)(2,1)} %shard_map.92), calls=%async_computation.2 | async-start | bytes 786432 | tf_op jit(solution)/shard_map/all_to_all | solution.py:263
  65.9 11.5 %all-to-all-done.2.next_in = bf16[8,2,48,256]{3,2,1,0:T(8,128)(2,1)S(1)} async-done(((bf16[8,2,48,256]{3,2,1,0:T(8,128)(2,1)}), bf16[8,2,48,256]{3,2,1,0:T(8,128)(2,1)S(1)}, u32[]{:S(2)}, u32[]{:S(2)}) %all-to-all-start.2) | async-done | bytes 393248 | tf_op jit(solution)/shard_map/all_to_all | solution.py:263
  77.4 3.4 %shard_map.93 = (bf16[8,2,48,256]{3,2,1,0:T(8,128)(2,1)}, bf16[8,2,48,256]{3,2,1,0:T(8,128)(2,1)S(1)}) custom-call(s32[4]{0:T(128)S(1)} %reshape.56.slot_ref, bf16[8,2,48,256]{3,2,1,0:T(8,128)(2,1)S(1)} %all-to-all-done.1.own_in, bf16[8,2,48,256]{3,2,1,0:T(8,128)(2,1)S(1)} %all-to-all-done.2.next_in, f32[2,256,256]{2,1,0:T(8,128)S(1)} %copy-done.1, ...), custom_call_target="tpu_custom_call" | custom-call | tf_op jit(solution)/shard_map/pallas_call | solution.py:44
  80.8 17.0 %all_to_all.31.windows = bf16[8,2,48,256]{3,2,1,0:T(8,128)(2,1)S(1)} all-to-all(bf16[8,2,48,256]{3,2,1,0:T(8,128)(2,1)S(1)} %get-tuple-element.40), channel_id=1, replica_groups={{0,32,64,96,128,160,192,224},{256,288,320,352,384,416,448,480},{1,33,65..., dimensions={0} | all-to-all | bytes 786432 | tf_op jit(solution)/shard_map/all_to_all | solution.py:263
  97.8 2.9 %shard_map.94 = (f32[48,1536]{1,0:T(8,128)S(1)}, bf16[48,1536]{1,0:T(8,128)(2,1)S(1)}, bf16[48,1536]{1,0:T(8,128)(2,1)S(1)}, bf16[48,1536]{1,0:T(8,128)(2,1)S(1)}) custom-call(s32[57]{0:T(128)S(1)} %pad_add_fusion.3.facts_ref, bf16[8,2,48,256]{3,2,1,0:T(8,128)(2,1)S(1)} %all_to_all.31.windows), custom_call_target="tpu_custom_call" | custom-call | tf_op jit(solution)/shard_map/pallas_call | solution.py:44
  100.7 4.2 %all-to-all-start.4 = ((bf16[8,2,48,256]{3,2,1,0:T(8,128)(2,1)}), bf16[8,2,48,256]{3,2,1,0:T(8,128)(2,1)S(1)}, u32[]{:S(2)}, u32[]{:S(2)}) async-start(bf16[8,2,48,256]{3,2,1,0:T(8,128)(2,1)} %get-tuple-element.46), calls=%async_computation.4 | async-start | bytes 786432 | tf_op jit(solution)/shard_map/all_to_all | solution.py:263
  105.0 2.0 %collective-permute-start.10 = (bf16[48,1536]{1,0:T(8,128)(2,1)S(1)}, bf16[48,1536]{1,0:T(8,128)(2,1)S(1)}, u32[]{:S(2)}, u32[]{:S(2)}) collective-permute-start(bf16[48,1536]{1,0:T(8,128)(2,1)S(1)} %get-tuple-element.52), channel_id=1, source_target_pairs={{0,8},{8,16},{16,24},{24,0},{1,9},{9,17},{17,25},{25,1},{2,10},{10... | collective-permute-start | bytes 442376 | tf_op jit(solution)/shard_map/ppermute | solution.py:260
  108.9 4.6 %collective-permute-start.12 = (bf16[48,1536]{1,0:T(8,128)(2,1)S(1)}, bf16[48,1536]{1,0:T(8,128)(2,1)S(1)}, u32[]{:S(2)}, u32[]{:S(2)}) collective-permute-start(bf16[48,1536]{1,0:T(8,128)(2,1)S(1)} %get-tuple-element.54), channel_id=1, source_target_pairs={{0,24},{8,0},{16,8},{24,16},{1,25},{9,1},{17,9},{25,17},{2,26},{10... | collective-permute-start | bytes 442376 | tf_op jit(solution)/shard_map/ppermute | solution.py:260
  113.5 3.1 %collective-permute-done.10 = bf16[48,1536]{1,0:T(8,128)(2,1)S(1)} collective-permute-done((bf16[48,1536]{1,0:T(8,128)(2,1)S(1)}, bf16[48,1536]{1,0:T(8,128)(2,1)S(1)}, u32[]{:S(2)}, u32[]{:S(2)}) %collective-permute-start.10) | collective-permute-done | bytes 147488 | tf_op jit(solution)/shard_map/ppermute | solution.py:260
  116.7 2.2 %collective-permute-done.12 = bf16[48,1536]{1,0:T(8,128)(2,1)S(1)} collective-permute-done((bf16[48,1536]{1,0:T(8,128)(2,1)S(1)}, bf16[48,1536]{1,0:T(8,128)(2,1)S(1)}, u32[]{:S(2)}, u32[]{:S(2)}) %collective-permute-start.12) | collective-permute-done | bytes 147488 | tf_op jit(solution)/shard_map/ppermute | solution.py:260
  118.9 4.2 %collective-permute-start.13 = (bf16[48,1536]{1,0:T(8,128)(2,1)S(1)}, bf16[48,1536]{1,0:T(8,128)(2,1)S(1)}, u32[]{:S(2)}, u32[]{:S(2)}) collective-permute-start(bf16[48,1536]{1,0:T(8,128)(2,1)S(1)} %add_convert_fusion.2), channel_id=1, source_target_pairs={{0,449},{1,450},{2,451},{3,452},{4,453},{5,454},{6,455},{32,481},{... | collective-permute-start | bytes 442376 | tf_op jit(solution)/shard_map/ppermute | solution.py:257
  123.1 2.7 %shard_map.95 = (f32[48,1536]{1,0:T(8,128)S(1)}, bf16[48,1536]{1,0:T(8,128)(2,1)S(1)}, bf16[48,1536]{1,0:T(8,128)(2,1)S(1)}, bf16[48,1536]{1,0:T(8,128)(2,1)S(1)}) custom-call(s32[57]{0:T(128)S(1)} %pad_add_fusion.3.facts_ref, bf16[8,2,48,256]{3,2,1,0:T(8,128)(2,1)S(1)} %all-to-all-done.4.windows), custom_call_target="tpu_custom_call" | custom-call | tf_op jit(solution)/shard_map/pallas_call | solution.py:44
  125.8 2.6 %collective-permute-start.7 = (bf16[48,1536]{1,0:T(8,128)(2,1)S(1)}, bf16[48,1536]{1,0:T(8,128)(2,1)S(1)}, u32[]{:S(2)}, u32[]{:S(2)}) collective-permute-start(bf16[48,1536]{1,0:T(8,128)(2,1)S(1)} %get-tuple-element.48), channel_id=1, source_target_pairs={{0,8},{8,16},{16,24},{24,0},{1,9},{9,17},{17,25},{25,1},{2,10},{10... | collective-permute-start | bytes 442376 | tf_op jit(solution)/shard_map/ppermute | solution.py:260
  128.4 5.0 %collective-permute-start.8 = (bf16[48,1536]{1,0:T(8,128)(2,1)S(1)}, bf16[48,1536]{1,0:T(8,128)(2,1)S(1)}, u32[]{:S(2)}, u32[]{:S(2)}) collective-permute-start(bf16[48,1536]{1,0:T(8,128)(2,1)S(1)} %get-tuple-element.49), channel_id=1, source_target_pairs={{0,16},{8,24},{16,0},{24,8},{1,17},{9,25},{17,1},{25,9},{2,18},{10... | collective-permute-start | bytes 442376 | tf_op jit(solution)/shard_map/ppermute | solution.py:260
  135.4 2.4 %collective-permute-done.8 = bf16[48,1536]{1,0:T(8,128)(2,1)S(1)} collective-permute-done((bf16[48,1536]{1,0:T(8,128)(2,1)S(1)}, bf16[48,1536]{1,0:T(8,128)(2,1)S(1)}, u32[]{:S(2)}, u32[]{:S(2)}) %collective-permute-start.8) | collective-permute-done | bytes 147488 | tf_op jit(solution)/shard_map/ppermute | solution.py:260
  139.7 7.8 %collective-permute-start.14 = (bf16[48,1536]{1,0:T(8,128)(2,1)S(1)}, bf16[48,1536]{1,0:T(8,128)(2,1)S(1)}, u32[]{:S(2)}, u32[]{:S(2)}) collective-permute-start(bf16[48,1536]{1,0:T(8,128)(2,1)S(1)} %add_convert_fusion.1), channel_id=1, source_target_pairs={{0,256},{32,288},{64,320},{96,352},{128,384},{160,416},{192,448},{... | collective-permute-start | bytes 442376 | tf_op jit(solution)/shard_map/ppermute | solution.py:248
  147.4 13.3 %collective-permute-done.14 = bf16[48,1536]{1,0:T(8,128)(2,1)S(1)} collective-permute-done((bf16[48,1536]{1,0:T(8,128)(2,1)S(1)}, bf16[48,1536]{1,0:T(8,128)(2,1)S(1)}, u32[]{:S(2)}, u32[]{:S(2)}) %collective-permute-start.14) | collective-permute-done | bytes 147488 | tf_op jit(solution)/shard_map/ppermute | solution.py:248
  160.8 17.7 %all_to_all.32 = bf16[4,48,1536]{2,1,0:T(8,128)(2,1)S(1)} all-to-all(bf16[4,48,1536]{2,1,0:T(8,128)(2,1)S(1)} %broadcast_in_dim.7), channel_id=1, replica_groups={{0,64,128,192},{32,96,160,224},{256,320,384,448},{288,352,416,480},{1,6..., dimensions={0} | all-to-all | bytes 1179648 | tf_op jit(solution)/shard_map/all_to_all | solution.py:266
  178.6 3.4 %collective-permute-start.15 = (bf16[192,1536]{1,0:T(8,128)(2,1)S(1)}, bf16[192,1536]{1,0:T(8,128)(2,1)S(1)}, u32[]{:S(2)}, u32[]{:S(2)}) collective-permute-start(bf16[192,1536]{1,0:T(8,128)(2,1)S(1)} %bitcast.19), channel_id=1, source_target_pairs={{0,32},{32,0},{64,96},{96,64},{128,160},{160,128},{192,224},{224,1... | collective-permute-start | bytes 1769480 | tf_op jit(solution)/shard_map/ppermute | solution.py:248
  (47 shorter events, 16.0 us)
Async XLA Ops:
  0.0 77.4 %copy-start.3 = (bf16[256,256]{1,0:T(8,128)(2,1)S(1)}, bf16[256,256]{1,0:T(8,128)(2,1)}, u32[]{:S(2)}) copy-start(bf16[256,256]{1,0:T(8,128)(2,1)} %constant.103.clone.wi_ref) | copy-start | bytes 393220
  0.0 77.4 %copy-start.4 = (bf16[256,256]{1,0:T(8,128)(2,1)S(1)}, bf16[256,256]{1,0:T(8,128)(2,1)}, u32[]{:S(2)}) copy-start(bf16[256,256]{1,0:T(8,128)(2,1)} %constant.102.clone.wr_ref) | copy-start | bytes 393220
  0.0 65.7 %copy-start.5 = (s32[1,1,1,2]{3,2,1,0:T(1,128)S(1)}, s32[1,1,1,2]{3,2,1,0:T(1,128)}, u32[]{:S(2)}) copy-start(s32[1,1,1,2]{3,2,1,0:T(1,128)} %param.12) | copy-start | bytes 28
  0.0 77.4 %copy-start.2 = (bf16[1,1,1,2,256,256]{5,4,3,2,1,0:T(8,128)(2,1)S(1)}, bf16[1,1,1,2,256,256]{5,4,3,2,1,0:T(8,128)(2,1)}, u32[]{:S(2)}) copy-start(bf16[1,1,1,2,256,256]{5,4,3,2,1,0:T(8,128)(2,1)} %param.11) | copy-start | bytes 786436
  0.0 77.4 %copy-start.1 = (f32[2,256,256]{2,1,0:T(8,128)S(1)}, f32[2,256,256]{2,1,0:T(8,128)}, u32[]{:S(2)}) copy-start(f32[2,256,256]{2,1,0:T(8,128)} %probe.1) | copy-start | bytes 1572868
  1.3 28.2 %collective-permute-start.3 = (bf16[48,1536]{1,0:T(8,128)(2,1)S(1)}, bf16[48,1536]{1,0:T(8,128)(2,1)S(1)}, u32[]{:S(2)}, u32[]{:S(2)}) collective-permute-start(bf16[48,1536]{1,0:T(8,128)(2,1)S(1)} %get-tuple-element.32.refs_0_), channel_id=1, source_target_pairs={{0,24},{8,0},{16,8},{24,16},{1,25},{9,1},{17,9},{25,17},{2,26},{10... | collective-permute-start | bytes 442376 | tf_op jit(solution)/shard_map/ppermute | solution.py:260
  6.5 22.9 %collective-permute-start.2 = (bf16[48,1536]{1,0:T(8,128)(2,1)S(1)}, bf16[48,1536]{1,0:T(8,128)(2,1)S(1)}, u32[]{:S(2)}, u32[]{:S(2)}) collective-permute-start(bf16[48,1536]{1,0:T(8,128)(2,1)S(1)} %get-tuple-element.32.refs_0_), channel_id=1, source_target_pairs={{0,16},{8,24},{16,0},{24,8},{1,17},{9,25},{17,1},{25,9},{2,18},{10... | collective-permute-start | bytes 442376 | tf_op jit(solution)/shard_map/ppermute | solution.py:260
  8.9 20.5 %collective-permute-start.1 = (bf16[48,1536]{1,0:T(8,128)(2,1)S(1)}, bf16[48,1536]{1,0:T(8,128)(2,1)S(1)}, u32[]{:S(2)}, u32[]{:S(2)}) collective-permute-start(bf16[48,1536]{1,0:T(8,128)(2,1)S(1)} %get-tuple-element.32.refs_0_), channel_id=1, source_target_pairs={{0,8},{8,16},{16,24},{24,0},{1,9},{9,17},{17,25},{25,1},{2,10},{10... | collective-permute-start | bytes 442376 | tf_op jit(solution)/shard_map/ppermute | solution.py:260
  11.5 24.4 %collective-permute-start = (bf16[48,1536]{1,0:T(8,128)(2,1)S(1)}, bf16[48,1536]{1,0:T(8,128)(2,1)S(1)}, u32[]{:S(2)}, u32[]{:S(2)}) collective-permute-start(bf16[48,1536]{1,0:T(8,128)(2,1)S(1)} %get-tuple-element.31), channel_id=1, source_target_pairs={{1,448},{2,449},{3,450},{4,451},{5,452},{6,453},{7,454},{33,480},{... | collective-permute-start | bytes 442376 | tf_op jit(solution)/shard_map/ppermute | solution.py:257
  15.6 12.5 %all-to-all-start = ((s32[8,1,7]{2,1,0:T(1,128)}), s32[8,1,7]{2,1,0:T(1,128)S(1)}, u32[]{:S(2)}, u32[]{:S(2)}) async-start(s32[8,1,7]{2,1,0:T(1,128)} %broadcast_in_dim.6), calls=%async_computation | async-start | bytes 8192 | tf_op jit(solution)/shard_map/all_to_all | solution.py:263
  35.8 20.5 %all-to-all-start.1 = ((bf16[8,2,48,256]{3,2,1,0:T(8,128)(2,1)}), bf16[8,2,48,256]{3,2,1,0:T(8,128)(2,1)S(1)}, u32[]{:S(2)}, u32[]{:S(2)}) async-start(bf16[8,2,48,256]{3,2,1,0:T(8,128)(2,1)} %shard_map.91), calls=%async_computation.1 | async-start | bytes 786432 | tf_op jit(solution)/shard_map/all_to_all | solution.py:263
  40.2 9.1 %collective-permute-start.6 = (bf16[48,1536]{1,0:T(8,128)(2,1)S(1)}, bf16[48,1536]{1,0:T(8,128)(2,1)S(1)}, u32[]{:S(2)}, u32[]{:S(2)}) collective-permute-start(bf16[48,1536]{1,0:T(8,128)(2,1)S(1)} %collective-permute-done.refs_0_), channel_id=1, source_target_pairs={{0,24},{8,0},{16,8},{24,16},{1,25},{9,1},{17,9},{25,17},{2,26},{10... | collective-permute-start | bytes 442376 | tf_op jit(solution)/shard_map/ppermute | solution.py:260
  44.2 8.4 %collective-permute-start.5 = (bf16[48,1536]{1,0:T(8,128)(2,1)S(1)}, bf16[48,1536]{1,0:T(8,128)(2,1)S(1)}, u32[]{:S(2)}, u32[]{:S(2)}) collective-permute-start(bf16[48,1536]{1,0:T(8,128)(2,1)S(1)} %collective-permute-done.refs_0_), channel_id=1, source_target_pairs={{0,16},{8,24},{16,0},{24,8},{1,17},{9,25},{17,1},{25,9},{2,18},{10... | collective-permute-start | bytes 442376 | tf_op jit(solution)/shard_map/ppermute | solution.py:260
  47.3 8.9 %collective-permute-start.4 = (bf16[48,1536]{1,0:T(8,128)(2,1)S(1)}, bf16[48,1536]{1,0:T(8,128)(2,1)S(1)}, u32[]{:S(2)}, u32[]{:S(2)}) collective-permute-start(bf16[48,1536]{1,0:T(8,128)(2,1)S(1)} %collective-permute-done.refs_0_), channel_id=1, source_target_pairs={{0,8},{8,16},{16,24},{24,0},{1,9},{9,17},{17,25},{25,1},{2,10},{10... | collective-permute-start | bytes 442376 | tf_op jit(solution)/shard_map/ppermute | solution.py:260
  59.8 17.6 %all-to-all-start.2 = ((bf16[8,2,48,256]{3,2,1,0:T(8,128)(2,1)}), bf16[8,2,48,256]{3,2,1,0:T(8,128)(2,1)S(1)}, u32[]{:S(2)}, u32[]{:S(2)}) async-start(bf16[8,2,48,256]{3,2,1,0:T(8,128)(2,1)} %shard_map.92), calls=%async_computation.2 | async-start | bytes 786432 | tf_op jit(solution)/shard_map/all_to_all | solution.py:263
  100.7 22.4 %all-to-all-start.4 = ((bf16[8,2,48,256]{3,2,1,0:T(8,128)(2,1)}), bf16[8,2,48,256]{3,2,1,0:T(8,128)(2,1)S(1)}, u32[]{:S(2)}, u32[]{:S(2)}) async-start(bf16[8,2,48,256]{3,2,1,0:T(8,128)(2,1)} %get-tuple-element.46), calls=%async_computation.4 | async-start | bytes 786432 | tf_op jit(solution)/shard_map/all_to_all | solution.py:263
  105.0 77.0 %copy-start = (bf16[2,1,192,1536]{3,2,1,0:T(8,128)(2,1)S(1)}, bf16[2,1,192,1536]{3,2,1,0:T(8,128)(2,1)}, u32[]{:S(2)}) copy-start(bf16[2,1,192,1536]{3,2,1,0:T(8,128)(2,1)} %param.9) | copy-start | bytes 3538948
  105.0 11.7 %collective-permute-start.10 = (bf16[48,1536]{1,0:T(8,128)(2,1)S(1)}, bf16[48,1536]{1,0:T(8,128)(2,1)S(1)}, u32[]{:S(2)}, u32[]{:S(2)}) collective-permute-start(bf16[48,1536]{1,0:T(8,128)(2,1)S(1)} %get-tuple-element.52), channel_id=1, source_target_pairs={{0,8},{8,16},{16,24},{24,0},{1,9},{9,17},{17,25},{25,1},{2,10},{10... | collective-permute-start | bytes 442376 | tf_op jit(solution)/shard_map/ppermute | solution.py:260
  107.0 9.7 %collective-permute-start.11 = (bf16[48,1536]{1,0:T(8,128)(2,1)S(1)}, bf16[48,1536]{1,0:T(8,128)(2,1)S(1)}, u32[]{:S(2)}, u32[]{:S(2)}) collective-permute-start(bf16[48,1536]{1,0:T(8,128)(2,1)S(1)} %get-tuple-element.53), channel_id=1, source_target_pairs={{0,16},{8,24},{16,0},{24,8},{1,17},{9,25},{17,1},{25,9},{2,18},{10... | collective-permute-start | bytes 442376 | tf_op jit(solution)/shard_map/ppermute | solution.py:260
  108.9 9.9 %collective-permute-start.12 = (bf16[48,1536]{1,0:T(8,128)(2,1)S(1)}, bf16[48,1536]{1,0:T(8,128)(2,1)S(1)}, u32[]{:S(2)}, u32[]{:S(2)}) collective-permute-start(bf16[48,1536]{1,0:T(8,128)(2,1)S(1)} %get-tuple-element.54), channel_id=1, source_target_pairs={{0,24},{8,0},{16,8},{24,16},{1,25},{9,1},{17,9},{25,17},{2,26},{10... | collective-permute-start | bytes 442376 | tf_op jit(solution)/shard_map/ppermute | solution.py:260
  118.9 16.5 %collective-permute-start.13 = (bf16[48,1536]{1,0:T(8,128)(2,1)S(1)}, bf16[48,1536]{1,0:T(8,128)(2,1)S(1)}, u32[]{:S(2)}, u32[]{:S(2)}) collective-permute-start(bf16[48,1536]{1,0:T(8,128)(2,1)S(1)} %add_convert_fusion.2), channel_id=1, source_target_pairs={{0,449},{1,450},{2,451},{3,452},{4,453},{5,454},{6,455},{32,481},{... | collective-permute-start | bytes 442376 | tf_op jit(solution)/shard_map/ppermute | solution.py:257
  125.8 9.6 %collective-permute-start.7 = (bf16[48,1536]{1,0:T(8,128)(2,1)S(1)}, bf16[48,1536]{1,0:T(8,128)(2,1)S(1)}, u32[]{:S(2)}, u32[]{:S(2)}) collective-permute-start(bf16[48,1536]{1,0:T(8,128)(2,1)S(1)} %get-tuple-element.48), channel_id=1, source_target_pairs={{0,8},{8,16},{16,24},{24,0},{1,9},{9,17},{17,25},{25,1},{2,10},{10... | collective-permute-start | bytes 442376 | tf_op jit(solution)/shard_map/ppermute | solution.py:260
  128.4 9.4 %collective-permute-start.8 = (bf16[48,1536]{1,0:T(8,128)(2,1)S(1)}, bf16[48,1536]{1,0:T(8,128)(2,1)S(1)}, u32[]{:S(2)}, u32[]{:S(2)}) collective-permute-start(bf16[48,1536]{1,0:T(8,128)(2,1)S(1)} %get-tuple-element.49), channel_id=1, source_target_pairs={{0,16},{8,24},{16,0},{24,8},{1,17},{9,25},{17,1},{25,9},{2,18},{10... | collective-permute-start | bytes 442376 | tf_op jit(solution)/shard_map/ppermute | solution.py:260
  133.5 6.1 %collective-permute-start.9 = (bf16[48,1536]{1,0:T(8,128)(2,1)S(1)}, bf16[48,1536]{1,0:T(8,128)(2,1)S(1)}, u32[]{:S(2)}, u32[]{:S(2)}) collective-permute-start(bf16[48,1536]{1,0:T(8,128)(2,1)S(1)} %get-tuple-element.50), channel_id=1, source_target_pairs={{0,24},{8,0},{16,8},{24,16},{1,25},{9,1},{17,9},{25,17},{2,26},{10... | collective-permute-start | bytes 442376 | tf_op jit(solution)/shard_map/ppermute | solution.py:260
  139.7 21.1 %collective-permute-start.14 = (bf16[48,1536]{1,0:T(8,128)(2,1)S(1)}, bf16[48,1536]{1,0:T(8,128)(2,1)S(1)}, u32[]{:S(2)}, u32[]{:S(2)}) collective-permute-start(bf16[48,1536]{1,0:T(8,128)(2,1)S(1)} %add_convert_fusion.1), channel_id=1, source_target_pairs={{0,256},{32,288},{64,320},{96,352},{128,384},{160,416},{192,448},{... | collective-permute-start | bytes 442376 | tf_op jit(solution)/shard_map/ppermute | solution.py:248
  178.6 5.0 %collective-permute-start.15 = (bf16[192,1536]{1,0:T(8,128)(2,1)S(1)}, bf16[192,1536]{1,0:T(8,128)(2,1)S(1)}, u32[]{:S(2)}, u32[]{:S(2)}) collective-permute-start(bf16[192,1536]{1,0:T(8,128)(2,1)S(1)} %bitcast.19), channel_id=1, source_target_pairs={{0,32},{32,0},{64,96},{96,64},{128,160},{160,128},{192,224},{224,1... | collective-permute-start | bytes 1769480 | tf_op jit(solution)/shard_map/ppermute | solution.py:248

commit v8 on v7

--- a/solution.py
+++ b/solution.py
@@ -40,40 +40,59 @@
 VMEM = pl.BlockSpec(memory_space=pltpu.VMEM)
 
 
-def call(body, out_shape, scratch, facts, *args):
+def call(body, out_shape, scratch, *args):
+    smem = pl.BlockSpec(memory_space=pltpu.SMEM)
     return pl.pallas_call(
         body,
         out_shape=out_shape,
-        in_specs=[pl.BlockSpec(memory_space=pltpu.SMEM)] + [VMEM] * len(args),
+        in_specs=[smem if x.dtype == jnp.int32 else VMEM for x in args],
         out_specs=[VMEM] * len(out_shape),
         scratch_shapes=scratch,
         compiler_params=pltpu.CompilerParams(vmem_limit_bytes=24 * 1024 * 1024),
-    )(facts, *args)
+    )(*args)
+
+
+def facts_body(rows_ref, columns_ref, count_ref, index_ref, out):
+    values = []
+    for slot in range(rows_ref.shape[0]):
+        values += [rows_ref[slot], columns_ref[slot], (slot < count_ref[0]).astype(jnp.int32)]
+    lane = lax.broadcasted_iota(jnp.int32, out.shape, 1)
+    line = jnp.zeros(out.shape, jnp.int32)
+    for n, value in enumerate(values + [index_ref[0]]):
+        line = jnp.where(lane == n, value, line)
+    out[...] = line
 
 
 class Facts:
-    def __init__(self, ref, slots, slabs, columns):
-        self.ref, self.slots, self.slabs, self.columns = ref, slots, slabs, columns
-        self.stride = 3 * slots + 1
+    def __init__(self, ref, slab_ref, slots, slabs, columns):
+        self.ref, self.slab, self.slots, self.slabs, self.columns = ref, slab_ref[0], slots, slabs, columns
 
     def slot(self, angle, slot):
-        return tuple(self.ref[self.stride * angle + 3 * slot + i] for i in range(3))
-
-    def columns_of(self, angle, slot, step):
-        layer = lax.rem(self.ref[8 * self.stride] + self.slabs + step, self.slabs)
-        index = self.ref[self.stride * angle + self.stride - 1]
+        return tuple(self.ref[angle, 3 * slot + i] for i in range(3))
+
+    def layer(self, step):
+        layer = self.slab + step
+        layer = jnp.where(layer < 0, layer + self.slabs, layer)
+        return jnp.where(layer >= self.slabs, layer - self.slabs, layer)
+
+    def columns_of(self, angle, slot, layer):
+        index = self.ref[angle, 3 * self.slots]
         shift = ((index - angle_center) * (layer - self.slabs // 2)) >> (shear_divisor.bit_length() - 1)
-        shift = lax.rem(lax.rem(shift, self.columns) + self.columns, self.columns)
-        left = lax.rem(self.slot(angle, slot)[1] + shift, self.columns)
-        blocks = self.columns // LANE
-        starts = [pl.multiple_of(lax.rem(left // LANE + i, blocks) * LANE, LANE) for i in range(3)]
-        return starts, lax.rem(left, LANE)
-
-
-def cut_body(slabs, facts_ref, *refs):
+        left = self.slot(angle, slot)[1] + shift
+        left = jnp.where(left < 0, left + self.columns, left)
+        left = jnp.where(left >= self.columns, left - self.columns, left)
+        starts = []
+        for i in range(3):
+            start = (left & -LANE) + i * LANE
+            start = jnp.where(start >= self.columns, start - self.columns, start)
+            starts.append(pl.multiple_of(start, LANE))
+        return starts, left & (LANE - 1)
+
+
+def cut_body(absolute, facts_ref, slab_ref, *refs):
     blocks, out = refs[:-1], refs[-1]
     angles, slots, rows, width = out.shape
-    facts = Facts(facts_ref, slots, slabs, blocks[0].shape[1])
+    facts = Facts(facts_ref, slab_ref, slots, len(blocks), blocks[0].shape[1])
     lane = lax.broadcasted_iota(jnp.int32, (rows, LANE), 1)
     for slot in range(slots):
         for angle in range(angles):
@@ -82,9 +101,10 @@
             def _():
                 total = [jnp.zeros((rows, LANE), jnp.float32)] * 2
                 for k, block in enumerate(blocks):
-                    starts, inside = facts.columns_of(angle, slot, -k)
+                    layer = k if absolute else facts.layer(-k)
+                    starts, inside = facts.columns_of(angle, slot, layer)
                     turned = [
-                        pltpu.roll(block[:, pl.ds(start, LANE)].astype(jnp.float32), (LANE - inside) % LANE, 1)
+                        pltpu.roll(block[:, pl.ds(start, LANE)].astype(jnp.float32), (LANE - inside) & (LANE - 1), 1)
                         for start in starts
                     ]
                     here = lane < LANE - inside
@@ -94,7 +114,18 @@
 
 def cut_windows(facts, blocks, angles, slots, width):
     out = jax.ShapeDtypeStruct((angles, slots, blocks[0].shape[0], width), jnp.bfloat16)
-    return call(functools.partial(cut_body, len(blocks)), [out], [], facts, *blocks)[0]
+    return call(functools.partial(cut_body, False), [out], [], *facts, *blocks)[0]
+
+
+def cut_rest(facts, blocks, done, which):
+    angles, slots, rows, width = done.shape
+    out = jax.ShapeDtypeStruct((angles, 2, slots, rows, width), jnp.bfloat16)
+
+    def body(facts_ref, slab_ref, blocks, done, out):
+        out[:, 1 - which] = done[...]
+        cut_body(True, facts_ref, slab_ref, *(blocks.at[k] for k in range(blocks.shape[0])), out.at[:, which])
+
+    return call(body, [out], [], *facts, blocks, done)[0]
 
 
 def cos_sin(angle):
@@ -116,20 +147,20 @@
     )
 
 
-def patch_body(slot_ref, own_in, next_in, probe, patterns, wr_ref, wi_ref, own_out, next_out):
-    angles, slots, rows, width = own_in.shape
+def patch_body(row_ref, count_ref, windows, probe, patterns, wr_ref, wi_ref, own_out, next_out):
+    angles, _, slots, rows, width = windows.shape
     f32, bf16 = jnp.float32, jnp.bfloat16
     blocks = angles // 2
     tall = 2 * blocks * rows
     for slot in range(slots):
-        row, live = slot_ref[2 * slot], slot_ref[2 * slot + 1]
-
-        @pl.when(live > 0)
+        row = row_ref[slot]
+
+        @pl.when(slot < count_ref[0])
         def _():
             pick = one_hot(width, tall, -row)
             window = []
             for part in range(2):
-                held = [ref[2 * k + part, slot] for ref in (own_in, next_in) for k in range(blocks)]
+                held = [windows[2 * k + part, tile, slot] for tile in range(2) for k in range(blocks)]
                 window.append(dot(pick, jnp.concatenate(held, axis=0)))
             phase, absorption = window
             magnitude = jnp.exp(-absorption)
@@ -165,15 +196,17 @@
                     next_out[2 * (blocks - 1 - k) + part, slot] = below
 
 
-def patch_gradients(slot_facts, own, after, probe_wave, patterns, tables):
-    out = jax.ShapeDtypeStruct(own.shape, jnp.bfloat16)
-    return call(patch_body, [out, out], [], slot_facts, own, after, probe_wave, patterns, *tables)
-
-
-def place_body(facts_ref, windows, *refs):
+def patch_gradients(slot_rows, count, windows, probe_wave, patterns, tables):
+    angles, _, slots, rows, width = windows.shape
+    out = jax.ShapeDtypeStruct((angles, slots, rows, width), jnp.bfloat16)
+    return call(patch_body, [out, out], [], slot_rows, count, windows, probe_wave, patterns, *tables)
+
+
+def place_body(facts_ref, slab_ref, windows, *refs):
     outs, total = refs[:-1], refs[-1]
     angles, slots, rows, width = windows.shape
-    facts = Facts(facts_ref, slots, len(outs), total.shape[2])
+    slabs = total.shape[0]
+    facts = Facts(facts_ref, slab_ref, slots, slabs, total.shape[2])
     lane = lax.broadcasted_iota(jnp.int32, (rows, LANE), 1)
     total[...] = jnp.zeros_like(total)
     for slot in range(slots):
@@ -182,21 +215,24 @@
             @pl.when(facts.slot(angle, slot)[2] > 0)
             def _():
                 window = windows[angle, slot].astype(jnp.float32)
-                for k in range(len(outs)):
-                    starts, inside = facts.columns_of(angle, slot, k)
+                for k in range(slabs):
+                    layer = facts.layer(k) if len(outs) > 1 else k
+                    starts, inside = facts.columns_of(angle, slot, layer)
                     first, second = (pltpu.roll(window[:, i * LANE : (i + 1) * LANE], inside, 1) for i in range(2))
                     there = lane < inside
                     total[k, :, pl.ds(starts[0], LANE)] += jnp.where(there, 0.0, first)
                     total[k, :, pl.ds(starts[1], LANE)] += jnp.where(there, first, second)
                     total[k, :, pl.ds(starts[2], LANE)] += jnp.where(there, second, 0.0)
     for k, out in enumerate(outs):
-        out[...] = total[k].astype(out.dtype)
-
-
-def place_windows(facts, windows, slabs, columns):
+        out[...] = (total[k] if len(outs) > 1 else total[...]).astype(out.dtype)
+
+
+def place_windows(facts, windows, slabs, columns, together=False):
     shape = (windows.shape[2], columns)
     outs = [jax.ShapeDtypeStruct(shape, jnp.bfloat16 if k else jnp.float32) for k in range(slabs)]
-    return call(place_body, outs, [pltpu.VMEM((slabs, *shape), jnp.float32)], facts, windows)
+    if together:
+        outs = [jax.ShapeDtypeStruct((slabs, *shape), jnp.bfloat16)]
+    return call(place_body, outs, [pltpu.VMEM((slabs, *shape), jnp.float32)], *facts, windows)
 
 
 def step_body(part_ref, layer, gradient, *refs):
@@ -265,6 +301,9 @@
     def to_four(value):
         return lax.all_to_all(value, "angle", 0, 0, axis_index_groups=four_groups, tiled=True)
 
+    def to_slabs(value):
+        return lax.all_to_all(value, "slab", 0, 0, tiled=True)
+
     def of_slabs(block):
         return [block] + [to_slab(block, k) for k in range(1, slabs)]
 
@@ -277,24 +316,27 @@
         return lax.dynamic_slice(own_part, (block * block_rows, 0), (block_rows, columns))
 
     after, own, counts = lax.optimization_barrier((rows_of(3 - place_z), rows_of(place_z), counts))
-    after, own = mirrored(after, -1), of_slabs(own)
-
-    live = (jnp.arange(slots) < counts.reshape(1)).astype(jnp.int32)
-    meta = jnp.stack([offsets.reshape(slots), column_starts.reshape(slots), live], axis=1)
-    eight = to_eight(jnp.broadcast_to(jnp.concatenate([meta.reshape(-1), angle_ids]), (8, 3 * slots + 1)))
-    facts = jnp.concatenate([eight.reshape(-1), slab.reshape(1)]).astype(jnp.int32)
-    slot_facts = jnp.stack([offsets.reshape(slots), live], axis=1).reshape(-1)
-
+    after = mirrored(after, -1)
+
+    slot_rows, count = offsets.reshape(slots), counts.reshape(1)
+    line = jax.ShapeDtypeStruct((8, LANE), jnp.int32)
+    meta = call(facts_body, [line], [], slot_rows, column_starts.reshape(slots), count, angle_ids)[0]
+    eight = to_eight(meta)
+    eight, own = lax.optimization_barrier((eight, own))
+    facts = (eight, slab.reshape(1).astype(jnp.int32))
+    own = of_slabs(own)
+    after, own = lax.optimization_barrier((after, own))
     own = cut_windows(facts, own, 8, slots, width)
+    after = to_slabs(jnp.broadcast_to(after, (slabs, *after.shape)))
     after, own = lax.optimization_barrier((after, own))
-    after, own = lax.optimization_barrier((of_slabs(after), to_eight(own)))
-    after = to_eight(cut_windows(facts, after, 8, slots, width))
-
-    own, after = patch_gradients(slot_facts, own, after, probe_wave, patterns, tables)
-    after = place_windows(facts, to_eight(after), slabs, columns)
-    after, own = lax.optimization_barrier((after, own))
-    spill = mirrored(over_slabs(*after).astype(bf16), 1)
-    own = over_slabs(*place_windows(facts, to_eight(own), slabs, columns))
+    windows = to_eight(cut_rest(facts, after, own, 1))
+
+    own, after = patch_gradients(slot_rows, count, windows, probe_wave, patterns, tables)
+    after, own = lax.optimization_barrier((to_eight(after), own))
+    own = to_eight(own)
+    spill = mirrored(over_slabs(*place_windows(facts, after, slabs, columns)).astype(bf16), 1)
+    own = to_slabs(place_windows(facts, own, slabs, columns, together=True)[0])
+    own = jnp.sum(own.astype(f32), axis=0)
 
     total = lax.optimization_barrier((own + spill.astype(f32)).astype(bf16))
     total = (total.astype(f32) + swap(total, 8).astype(f32)).astype(bf16)

time: 186 us -> 181 us (0.973); the launches traced: 185 us -> 178 us
  starting transfers between devices: 76.1 us -> 47.6 us
  blocking collectives: 34.8 us -> 59 us
  Pallas kernels: 18.2 us -> 15.3 us
    all_to_all x1 -> x2, blocking collectives: 17 us -> 41.3 us  [to_eight(): lax.all_to_all(value, 'angle', 0, 0, axis_index_groups=eight_groups, tile...]
    ppermute x12 -> x6, starting transfers between devices: 37.3 us -> 15.6 us  [to_slab(): lax.ppermute(value, 'slab', [(i, (i + by) % slabs) for i in range(slabs)])]
    ppermute x12 -> x6, waiting for transfers between devices: 16.5 us -> 0.02 us  [to_slab(): lax.ppermute(value, 'slab', [(i, (i + by) % slabs) for i in range(slabs)])]
    all_to_all x0 -> x2, waiting for transfers between devices: none -> 13.6 us  [to_slabs(): return lax.all_to_all(value, 'slab', 0, 0, tiled=True)]
    ppermute x2, waiting for transfers between devices: 2.89 us -> 16.2 us  [mirrored(): return lax.ppermute(value, ('angle', 'tile'), pairs)]
    all_to_all x4 -> x2, waiting for transfers between devices: 16.3 us -> 3.59 us  [to_eight(): lax.all_to_all(value, 'angle', 0, 0, axis_index_groups=eight_groups, tile...]
    all_to_all x4 -> x2, starting transfers between devices: 22.2 us -> 14.3 us  [to_eight(): lax.all_to_all(value, 'angle', 0, 0, axis_index_groups=eight_groups, tile...]
    all_to_all x0 -> x2, starting transfers between devices: none -> 7.48 us  [to_slabs(): return lax.all_to_all(value, 'slab', 0, 0, tiled=True)]
  transfers between devices with their start and end apart: 20 -> 14, of which waited for: 11 -> 8; matrix products, arithmetic and copies ran while one was open for 2% -> 1% of each run, Pallas kernels for 4% -> 4%
where the time goes in v8:
time: 181 us; the launch traced here: 178 us
  blocking collectives  59 us (33%)
  waiting for transfers between devices  50.7 us (28%)
  starting transfers between devices  47.6 us (26%)
  Pallas kernels  15.3 us (8%)
  local copies, waits for them, and re-layouts  3.31 us (2%)
    all_to_all x2, blocking collectives, to_eight(): lax.all_to_all(value, 'angle', 0, 0, axis_index_groups=eight_groups, tile...  41.3 us
    all_to_all x1, blocking collectives, to_four(): lax.all_to_all(value, 'angle', 0, 0, axis_index_groups=four_groups, tiled...  17.7 us
    ppermute x2, waiting for transfers between devices, swap(): return lax.ppermute(value, 'angle', [(i, i ^ by) for i in range(angles)])  17.3 us
    ppermute x2, waiting for transfers between devices, mirrored(): return lax.ppermute(value, ('angle', 'tile'), pairs)  16.2 us
    ppermute x6, starting transfers between devices, to_slab(): lax.ppermute(value, 'slab', [(i, (i + by) % slabs) for i in range(slabs)])  15.6 us
    all_to_all x2, starting transfers between devices, to_eight(): lax.all_to_all(value, 'angle', 0, 0, axis_index_groups=eight_groups, tile...  14.3 us
    all_to_all x2, waiting for transfers between devices, to_slabs(): return lax.all_to_all(value, 'slab', 0, 0, tiled=True)  13.6 us
    pallas_call x6, Pallas kernels, call(): pl.pallas_call(body, out_shape=out_shape, in_specs=[smem if x.dtype == jn...  13.2 us
  transfers between devices with their start and end apart: 14, of which 8 were waited for; matrix products, arithmetic and copies ran while one was open for 1% of the time, Pallas kernels for 4%

profile of v8, /device:TPU:1, one launch (start us, length us, event | category | flops | bytes accessed | tf_op | source)
XLA Modules:
  0.0 177.7 jit_solution(11358183885492490437)
XLA Ops:
  2.6 1.1 shard_map.91
  3.8 10.1 %all-to-all-start = ((s32[8,1,128]{2,1,0:T(1,128)}), s32[8,1,128]{2,1,0:T(1,128)S(1)}, u32[]{:S(2)}, u32[]{:S(2)}) async-start(s32[8,1,128]{2,1,0:T(1,128)} %bitcast.8), calls=%async_computation | async-start | bytes 8192 | tf_op jit(solution)/shard_map/all_to_all | solution.py:299
  14.9 1.3 collective-permute-start
  16.2 2.4 %all-to-all-done = s32[8,1,128]{2,1,0:T(1,128)S(1)} async-done(((s32[8,1,128]{2,1,0:T(1,128)}), s32[8,1,128]{2,1,0:T(1,128)S(1)}, u32[]{:S(2)}, u32[]{:S(2)}) %all-to-all-start) | async-done | bytes 4128 | tf_op jit(solution)/shard_map/all_to_all | solution.py:299
  18.7 1.9 %collective-permute-start.3 = (bf16[48,1536]{1,0:T(8,128)(2,1)S(1)}, bf16[48,1536]{1,0:T(8,128)(2,1)S(1)}, u32[]{:S(2)}, u32[]{:S(2)}) collective-permute-start(bf16[48,1536]{1,0:T(8,128)(2,1)S(1)} %get-tuple-element.31.refs_0_), channel_id=1, source_target_pairs={{0,24},{8,0},{16,8},{24,16},{1,25},{9,1},{17,9},{25,17},{2,26},{10... | collective-permute-start | bytes 442376 | tf_op jit(solution)/shard_map/ppermute | solution.py:296
  20.6 2.2 %collective-permute-start.2 = (bf16[48,1536]{1,0:T(8,128)(2,1)S(1)}, bf16[48,1536]{1,0:T(8,128)(2,1)S(1)}, u32[]{:S(2)}, u32[]{:S(2)}) collective-permute-start(bf16[48,1536]{1,0:T(8,128)(2,1)S(1)} %get-tuple-element.31.refs_0_), channel_id=1, source_target_pairs={{0,16},{8,24},{16,0},{24,8},{1,17},{9,25},{17,1},{25,9},{2,18},{10... | collective-permute-start | bytes 442376 | tf_op jit(solution)/shard_map/ppermute | solution.py:296
  22.8 3.1 %collective-permute-start.1 = (bf16[48,1536]{1,0:T(8,128)(2,1)S(1)}, bf16[48,1536]{1,0:T(8,128)(2,1)S(1)}, u32[]{:S(2)}, u32[]{:S(2)}) collective-permute-start(bf16[48,1536]{1,0:T(8,128)(2,1)S(1)} %get-tuple-element.31.refs_0_), channel_id=1, source_target_pairs={{0,8},{8,16},{16,24},{24,0},{1,9},{9,17},{17,25},{25,1},{2,10},{10... | collective-permute-start | bytes 442376 | tf_op jit(solution)/shard_map/ppermute | solution.py:296
  25.9 10.2 %collective-permute-done = bf16[48,1536]{1,0:T(8,128)(2,1)S(1)} collective-permute-done((bf16[48,1536]{1,0:T(8,128)(2,1)S(1)}, bf16[48,1536]{1,0:T(8,128)(2,1)S(1)}, u32[]{:S(2)}, u32[]{:S(2)}) %collective-permute-start) | collective-permute-done | bytes 147488 | tf_op jit(solution)/shard_map/ppermute | solution.py:293
  36.9 4.0 %all-to-all-start.1 = ((bf16[4,48,1536]{2,1,0:T(8,128)(2,1)}), bf16[4,48,1536]{2,1,0:T(8,128)(2,1)S(1)}, u32[]{:S(2)}, u32[]{:S(2)}) async-start(bf16[4,48,1536]{2,1,0:T(8,128)(2,1)} %broadcast_in_dim.6), calls=%async_computation.1 | async-start | bytes 1179648 | tf_op jit(solution)/shard_map/all_to_all | solution.py:305
  40.9 1.8 %shard_map.92.done = bf16[8,2,48,256]{3,2,1,0:T(8,128)(2,1)S(1)} custom-call(s32[8,128]{1,0:T(8,128)S(1)} %bitcast.27, s32[1]{0:T(128)} %bitcast.10.slab_ref, bf16[48,1536]{1,0:T(8,128)(2,1)S(1)} %get-tuple-element.31.refs_0_, bf16[48,1536]{1,0:T(8,128)(2,1)S(1)} %collective-permute-done.1.refs_1_, bf16[48,1536]{1,0:T(8,128)(2,1)S(1)} %collective-permute-done.2.refs_2_, ...), custom_call_target="tpu_custom_call" | custom-call | tf_op jit(solution)/shard_map/pallas_call | solution.py:45
  42.7 7.7 %all-to-all-done.1.blocks = bf16[4,48,1536]{2,1,0:T(8,128)(2,1)S(1)} async-done(((bf16[4,48,1536]{2,1,0:T(8,128)(2,1)}), bf16[4,48,1536]{2,1,0:T(8,128)(2,1)S(1)}, u32[]{:S(2)}, u32[]{:S(2)}) %all-to-all-start.1) | async-done | bytes 589856 | tf_op jit(solution)/shard_map/all_to_all | solution.py:305
  50.5 1.8 %shard_map.93 = bf16[8,2,2,48,256]{4,3,2,1,0:T(8,128)(2,1)S(1)} custom-call(s32[8,128]{1,0:T(8,128)S(1)} %bitcast.28, s32[1]{0:T(128)} %bitcast.10.slab_ref, bf16[4,48,1536]{2,1,0:T(8,128)(2,1)S(1)} %all-to-all-done.1.blocks, bf16[8,2,48,256]{3,2,1,0:T(8,128)(2,1)S(1)} %shard_map.92.done), custom_call_target="tpu_custom_call" | custom-call | tf_op jit(solution)/shard_map/pallas_call | solution.py:45
  52.3 24.1 %all_to_all.42.windows = bf16[8,2,2,48,256]{4,3,2,1,0:T(8,128)(2,1)S(1)} all-to-all(bf16[8,2,2,48,256]{4,3,2,1,0:T(8,128)(2,1)S(1)} %shard_map.93), channel_id=1, replica_groups={{0,32,64,96,128,160,192,224},{256,288,320,352,384,416,448,480},{1,33,65..., dimensions={0} | all-to-all | bytes 1572864 | tf_op jit(solution)/shard_map/all_to_all | solution.py:299
  76.5 3.4 %shard_map.94 = (bf16[8,2,48,256]{3,2,1,0:T(8,128)(2,1)}, bf16[8,2,48,256]{3,2,1,0:T(8,128)(2,1)S(1)}) custom-call(s32[2]{0:T(128)S(1)} %bitcast.32, s32[1]{0:T(128)} %bitcast.21.count_ref, bf16[8,2,2,48,256]{4,3,2,1,0:T(8,128)(2,1)S(1)} %all_to_all.42.windows, f32[2,256,256]{2,1,0:T(8,128)S(1)} %copy-done.1, bf16[2,256,256]{2,1,0:T(8,128)(2,1)S(1)} %bitcast.26, ...), custom_call_target="tpu_custom_call" | custom-call | tf_op jit(solution)/shard_map/pallas_call | solution.py:45
  79.9 17.2 %all_to_all.43.windows = bf16[8,2,48,256]{3,2,1,0:T(8,128)(2,1)S(1)} all-to-all(bf16[8,2,48,256]{3,2,1,0:T(8,128)(2,1)S(1)} %get-tuple-element.37), channel_id=1, replica_groups={{0,32,64,96,128,160,192,224},{256,288,320,352,384,416,448,480},{1,33,65..., dimensions={0} | all-to-all | bytes 786432 | tf_op jit(solution)/shard_map/all_to_all | solution.py:299
  97.1 4.2 %all-to-all-start.4 = ((bf16[8,2,48,256]{3,2,1,0:T(8,128)(2,1)}), bf16[8,2,48,256]{3,2,1,0:T(8,128)(2,1)S(1)}, u32[]{:S(2)}, u32[]{:S(2)}) async-start(bf16[8,2,48,256]{3,2,1,0:T(8,128)(2,1)} %get-tuple-element.39), calls=%async_computation.4 | async-start | bytes 786432 | tf_op jit(solution)/shard_map/all_to_all | solution.py:299
  101.4 2.1 %shard_map.96 = (f32[48,1536]{1,0:T(8,128)S(1)}, bf16[48,1536]{1,0:T(8,128)(2,1)S(1)}, bf16[48,1536]{1,0:T(8,128)(2,1)S(1)}, bf16[48,1536]{1,0:T(8,128)(2,1)S(1)}) custom-call(s32[8,128]{1,0:T(8,128)S(1)} %bitcast.29, s32[1]{0:T(128)} %bitcast.10.slab_ref, bf16[8,2,48,256]{3,2,1,0:T(8,128)(2,1)S(1)} %all_to_all.43.windows), custom_call_target="tpu_custom_call" | custom-call | tf_op jit(solution)/shard_map/pallas_call | solution.py:45
  103.5 1.9 %collective-permute-start.4 = (bf16[48,1536]{1,0:T(8,128)(2,1)S(1)}, bf16[48,1536]{1,0:T(8,128)(2,1)S(1)}, u32[]{:S(2)}, u32[]{:S(2)}) collective-permute-start(bf16[48,1536]{1,0:T(8,128)(2,1)S(1)} %get-tuple-element.42), channel_id=1, source_target_pairs={{0,8},{8,16},{16,24},{24,0},{1,9},{9,17},{17,25},{25,1},{2,10},{10... | collective-permute-start | bytes 442376 | tf_op jit(solution)/shard_map/ppermute | solution.py:296
  105.4 1.9 %collective-permute-start.5 = (bf16[48,1536]{1,0:T(8,128)(2,1)S(1)}, bf16[48,1536]{1,0:T(8,128)(2,1)S(1)}, u32[]{:S(2)}, u32[]{:S(2)}) collective-permute-start(bf16[48,1536]{1,0:T(8,128)(2,1)S(1)} %get-tuple-element.43), channel_id=1, source_target_pairs={{0,16},{8,24},{16,0},{24,8},{1,17},{9,25},{17,1},{25,9},{2,18},{10... | collective-permute-start | bytes 442376 | tf_op jit(solution)/shard_map/ppermute | solution.py:296
  107.3 4.6 %collective-permute-start.6 = (bf16[48,1536]{1,0:T(8,128)(2,1)S(1)}, bf16[48,1536]{1,0:T(8,128)(2,1)S(1)}, u32[]{:S(2)}, u32[]{:S(2)}) collective-permute-start(bf16[48,1536]{1,0:T(8,128)(2,1)S(1)} %get-tuple-element.44), channel_id=1, source_target_pairs={{0,24},{8,0},{16,8},{24,16},{1,25},{9,1},{17,9},{25,17},{2,26},{10... | collective-permute-start | bytes 442376 | tf_op jit(solution)/shard_map/ppermute | solution.py:296
  111.9 1.1 all-to-all-done.4.windows
  113.1 2.9 %shard_map.95 = bf16[4,48,1536]{2,1,0:T(8,128)(2,1)} custom-call(s32[8,128]{1,0:T(8,128)S(1)} %bitcast.30, s32[1]{0:T(128)} %bitcast.10.slab_ref, bf16[8,2,48,256]{3,2,1,0:T(8,128)(2,1)S(1)} %all-to-all-done.4.windows), custom_call_target="tpu_custom_call" | custom-call | tf_op jit(solution)/shard_map/pallas_call | solution.py:45
  115.9 3.5 %all-to-all-start.5 = ((bf16[4,48,1536]{2,1,0:T(8,128)(2,1)}), bf16[4,48,1536]{2,1,0:T(8,128)(2,1)S(1)}, u32[]{:S(2)}, u32[]{:S(2)}) async-start(bf16[4,48,1536]{2,1,0:T(8,128)(2,1)} %shard_map.95), calls=%async_computation.5 | async-start | bytes 1179648 | tf_op jit(solution)/shard_map/all_to_all | solution.py:305
  119.5 3.4 %collective-permute-start.7 = (bf16[48,1536]{1,0:T(8,128)(2,1)S(1)}, bf16[48,1536]{1,0:T(8,128)(2,1)S(1)}, u32[]{:S(2)}, u32[]{:S(2)}) collective-permute-start(bf16[48,1536]{1,0:T(8,128)(2,1)S(1)} %add_convert_fusion.2), channel_id=1, source_target_pairs={{0,449},{1,450},{2,451},{3,452},{4,453},{5,454},{6,455},{32,481},{... | collective-permute-start | bytes 442376 | tf_op jit(solution)/shard_map/ppermute | solution.py:293
  122.9 5.9 %all-to-all-done.5 = bf16[4,48,1536]{2,1,0:T(8,128)(2,1)S(1)} async-done(((bf16[4,48,1536]{2,1,0:T(8,128)(2,1)}), bf16[4,48,1536]{2,1,0:T(8,128)(2,1)S(1)}, u32[]{:S(2)}, u32[]{:S(2)}) %all-to-all-start.5) | async-done | bytes 589856 | tf_op jit(solution)/shard_map/all_to_all | solution.py:305
  128.8 6.0 %collective-permute-done.7 = bf16[48,1536]{1,0:T(8,128)(2,1)S(1)} collective-permute-done((bf16[48,1536]{1,0:T(8,128)(2,1)S(1)}, bf16[48,1536]{1,0:T(8,128)(2,1)S(1)}, u32[]{:S(2)}, u32[]{:S(2)}) %collective-permute-start.7) | collective-permute-done | bytes 147488 | tf_op jit(solution)/shard_map/ppermute | solution.py:293
  134.9 2.1 %collective-permute-start.8 = (bf16[48,1536]{1,0:T(8,128)(2,1)S(1)}, bf16[48,1536]{1,0:T(8,128)(2,1)S(1)}, u32[]{:S(2)}, u32[]{:S(2)}) collective-permute-start(bf16[48,1536]{1,0:T(8,128)(2,1)S(1)} %add_convert_fusion.1), channel_id=1, source_target_pairs={{0,256},{32,288},{64,320},{96,352},{128,384},{160,416},{192,448},{... | collective-permute-start | bytes 442376 | tf_op jit(solution)/shard_map/ppermute | solution.py:284
  136.9 16.8 %collective-permute-done.8 = bf16[48,1536]{1,0:T(8,128)(2,1)S(1)} collective-permute-done((bf16[48,1536]{1,0:T(8,128)(2,1)S(1)}, bf16[48,1536]{1,0:T(8,128)(2,1)S(1)}, u32[]{:S(2)}, u32[]{:S(2)}) %collective-permute-start.8) | collective-permute-done | bytes 147488 | tf_op jit(solution)/shard_map/ppermute | solution.py:284
  153.9 17.7 %all_to_all.44 = bf16[4,48,1536]{2,1,0:T(8,128)(2,1)S(1)} all-to-all(bf16[4,48,1536]{2,1,0:T(8,128)(2,1)S(1)} %broadcast_in_dim.7), channel_id=1, replica_groups={{0,64,128,192},{32,96,160,224},{256,320,384,448},{288,352,416,480},{1,6..., dimensions={0} | all-to-all | bytes 1179648 | tf_op jit(solution)/shard_map/all_to_all | solution.py:302
  171.5 3.5 %collective-permute-start.9 = (bf16[192,1536]{1,0:T(8,128)(2,1)S(1)}, bf16[192,1536]{1,0:T(8,128)(2,1)S(1)}, u32[]{:S(2)}, u32[]{:S(2)}) collective-permute-start(bf16[192,1536]{1,0:T(8,128)(2,1)S(1)} %bitcast.24), channel_id=1, source_target_pairs={{0,32},{32,0},{64,96},{96,64},{128,160},{160,128},{192,224},{224,1... | collective-permute-start | bytes 1769480 | tf_op jit(solution)/shard_map/ppermute | solution.py:284
  175.0 1.1 shard_map.97.refs_0_
  176.6 1.1 shard_map.98
  (30 shorter events, 4.1 us)
Async XLA Ops:
  1.3 0.7 copy-start.5
  2.0 0.7 copy-start.7
  3.8 14.9 %all-to-all-start = ((s32[8,1,128]{2,1,0:T(1,128)}), s32[8,1,128]{2,1,0:T(1,128)S(1)}, u32[]{:S(2)}, u32[]{:S(2)}) async-start(s32[8,1,128]{2,1,0:T(1,128)} %bitcast.8), calls=%async_computation | async-start | bytes 8192 | tf_op jit(solution)/shard_map/all_to_all | solution.py:299
  14.9 21.1 %collective-permute-start = (bf16[48,1536]{1,0:T(8,128)(2,1)S(1)}, bf16[48,1536]{1,0:T(8,128)(2,1)S(1)}, u32[]{:S(2)}, u32[]{:S(2)}) collective-permute-start(bf16[48,1536]{1,0:T(8,128)(2,1)S(1)} %get-tuple-element.28), channel_id=1, source_target_pairs={{1,448},{2,449},{3,450},{4,451},{5,452},{6,453},{7,454},{33,480},{... | collective-permute-start | bytes 442376 | tf_op jit(solution)/shard_map/ppermute | solution.py:293
  18.7 17.4 %collective-permute-start.3 = (bf16[48,1536]{1,0:T(8,128)(2,1)S(1)}, bf16[48,1536]{1,0:T(8,128)(2,1)S(1)}, u32[]{:S(2)}, u32[]{:S(2)}) collective-permute-start(bf16[48,1536]{1,0:T(8,128)(2,1)S(1)} %get-tuple-element.31.refs_0_), channel_id=1, source_target_pairs={{0,24},{8,0},{16,8},{24,16},{1,25},{9,1},{17,9},{25,17},{2,26},{10... | collective-permute-start | bytes 442376 | tf_op jit(solution)/shard_map/ppermute | solution.py:296
  20.6 15.5 %collective-permute-start.2 = (bf16[48,1536]{1,0:T(8,128)(2,1)S(1)}, bf16[48,1536]{1,0:T(8,128)(2,1)S(1)}, u32[]{:S(2)}, u32[]{:S(2)}) collective-permute-start(bf16[48,1536]{1,0:T(8,128)(2,1)S(1)} %get-tuple-element.31.refs_0_), channel_id=1, source_target_pairs={{0,16},{8,24},{16,0},{24,8},{1,17},{9,25},{17,1},{25,9},{2,18},{10... | collective-permute-start | bytes 442376 | tf_op jit(solution)/shard_map/ppermute | solution.py:296
  22.8 13.3 %collective-permute-start.1 = (bf16[48,1536]{1,0:T(8,128)(2,1)S(1)}, bf16[48,1536]{1,0:T(8,128)(2,1)S(1)}, u32[]{:S(2)}, u32[]{:S(2)}) collective-permute-start(bf16[48,1536]{1,0:T(8,128)(2,1)S(1)} %get-tuple-element.31.refs_0_), channel_id=1, source_target_pairs={{0,8},{8,16},{16,24},{24,0},{1,9},{9,17},{17,25},{25,1},{2,10},{10... | collective-permute-start | bytes 442376 | tf_op jit(solution)/shard_map/ppermute | solution.py:296
  36.9 13.5 %all-to-all-start.1 = ((bf16[4,48,1536]{2,1,0:T(8,128)(2,1)}), bf16[4,48,1536]{2,1,0:T(8,128)(2,1)S(1)}, u32[]{:S(2)}, u32[]{:S(2)}) async-start(bf16[4,48,1536]{2,1,0:T(8,128)(2,1)} %broadcast_in_dim.6), calls=%async_computation.1 | async-start | bytes 1179648 | tf_op jit(solution)/shard_map/all_to_all | solution.py:305
  52.3 24.1 %copy-start.1 = (f32[2,256,256]{2,1,0:T(8,128)S(1)}, f32[2,256,256]{2,1,0:T(8,128)}, u32[]{:S(2)}) copy-start(f32[2,256,256]{2,1,0:T(8,128)} %probe.1) | copy-start | bytes 1572868
  52.3 24.1 %copy-start.2 = (bf16[1,1,1,2,256,256]{5,4,3,2,1,0:T(8,128)(2,1)S(1)}, bf16[1,1,1,2,256,256]{5,4,3,2,1,0:T(8,128)(2,1)}, u32[]{:S(2)}) copy-start(bf16[1,1,1,2,256,256]{5,4,3,2,1,0:T(8,128)(2,1)} %param.11) | copy-start | bytes 786436
  52.3 24.1 %copy-start.3 = (bf16[256,256]{1,0:T(8,128)(2,1)S(1)}, bf16[256,256]{1,0:T(8,128)(2,1)}, u32[]{:S(2)}) copy-start(bf16[256,256]{1,0:T(8,128)(2,1)} %constant.105.clone.wi_ref) | copy-start | bytes 393220
  52.3 24.1 %copy-start.4 = (bf16[256,256]{1,0:T(8,128)(2,1)S(1)}, bf16[256,256]{1,0:T(8,128)(2,1)}, u32[]{:S(2)}) copy-start(bf16[256,256]{1,0:T(8,128)(2,1)} %constant.104.clone.wr_ref) | copy-start | bytes 393220
  52.3 24.1 %copy-start.6 = (s32[1,1,1,2]{3,2,1,0:T(1,128)S(1)}, s32[1,1,1,2]{3,2,1,0:T(1,128)}, u32[]{:S(2)}) copy-start(s32[1,1,1,2]{3,2,1,0:T(1,128)} %param.12) | copy-start | bytes 28
  97.1 15.9 %all-to-all-start.4 = ((bf16[8,2,48,256]{3,2,1,0:T(8,128)(2,1)}), bf16[8,2,48,256]{3,2,1,0:T(8,128)(2,1)S(1)}, u32[]{:S(2)}, u32[]{:S(2)}) async-start(bf16[8,2,48,256]{3,2,1,0:T(8,128)(2,1)} %get-tuple-element.39), calls=%async_computation.4 | async-start | bytes 786432 | tf_op jit(solution)/shard_map/all_to_all | solution.py:299
  103.5 16.0 %collective-permute-start.4 = (bf16[48,1536]{1,0:T(8,128)(2,1)S(1)}, bf16[48,1536]{1,0:T(8,128)(2,1)S(1)}, u32[]{:S(2)}, u32[]{:S(2)}) collective-permute-start(bf16[48,1536]{1,0:T(8,128)(2,1)S(1)} %get-tuple-element.42), channel_id=1, source_target_pairs={{0,8},{8,16},{16,24},{24,0},{1,9},{9,17},{17,25},{25,1},{2,10},{10... | collective-permute-start | bytes 442376 | tf_op jit(solution)/shard_map/ppermute | solution.py:296
  105.4 14.1 %collective-permute-start.5 = (bf16[48,1536]{1,0:T(8,128)(2,1)S(1)}, bf16[48,1536]{1,0:T(8,128)(2,1)S(1)}, u32[]{:S(2)}, u32[]{:S(2)}) collective-permute-start(bf16[48,1536]{1,0:T(8,128)(2,1)S(1)} %get-tuple-element.43), channel_id=1, source_target_pairs={{0,16},{8,24},{16,0},{24,8},{1,17},{9,25},{17,1},{25,9},{2,18},{10... | collective-permute-start | bytes 442376 | tf_op jit(solution)/shard_map/ppermute | solution.py:296
  107.3 12.1 %collective-permute-start.6 = (bf16[48,1536]{1,0:T(8,128)(2,1)S(1)}, bf16[48,1536]{1,0:T(8,128)(2,1)S(1)}, u32[]{:S(2)}, u32[]{:S(2)}) collective-permute-start(bf16[48,1536]{1,0:T(8,128)(2,1)S(1)} %get-tuple-element.44), channel_id=1, source_target_pairs={{0,24},{8,0},{16,8},{24,16},{1,25},{9,1},{17,9},{25,17},{2,26},{10... | collective-permute-start | bytes 442376 | tf_op jit(solution)/shard_map/ppermute | solution.py:296
  115.9 12.8 %all-to-all-start.5 = ((bf16[4,48,1536]{2,1,0:T(8,128)(2,1)}), bf16[4,48,1536]{2,1,0:T(8,128)(2,1)S(1)}, u32[]{:S(2)}, u32[]{:S(2)}) async-start(bf16[4,48,1536]{2,1,0:T(8,128)(2,1)} %shard_map.95), calls=%async_computation.5 | async-start | bytes 1179648 | tf_op jit(solution)/shard_map/all_to_all | solution.py:305
  119.5 15.3 %collective-permute-start.7 = (bf16[48,1536]{1,0:T(8,128)(2,1)S(1)}, bf16[48,1536]{1,0:T(8,128)(2,1)S(1)}, u32[]{:S(2)}, u32[]{:S(2)}) collective-permute-start(bf16[48,1536]{1,0:T(8,128)(2,1)S(1)} %add_convert_fusion.2), channel_id=1, source_target_pairs={{0,449},{1,450},{2,451},{3,452},{4,453},{5,454},{6,455},{32,481},{... | collective-permute-start | bytes 442376 | tf_op jit(solution)/shard_map/ppermute | solution.py:293
  134.9 40.1 %copy-start = (bf16[2,1,192,1536]{3,2,1,0:T(8,128)(2,1)S(1)}, bf16[2,1,192,1536]{3,2,1,0:T(8,128)(2,1)}, u32[]{:S(2)}) copy-start(bf16[2,1,192,1536]{3,2,1,0:T(8,128)(2,1)} %param.9) | copy-start | bytes 3538948
  134.9 18.9 %collective-permute-start.8 = (bf16[48,1536]{1,0:T(8,128)(2,1)S(1)}, bf16[48,1536]{1,0:T(8,128)(2,1)S(1)}, u32[]{:S(2)}, u32[]{:S(2)}) collective-permute-start(bf16[48,1536]{1,0:T(8,128)(2,1)S(1)} %add_convert_fusion.1), channel_id=1, source_target_pairs={{0,256},{32,288},{64,320},{96,352},{128,384},{160,416},{192,448},{... | collective-permute-start | bytes 442376 | tf_op jit(solution)/shard_map/ppermute | solution.py:284
  171.5 5.1 %collective-permute-start.9 = (bf16[192,1536]{1,0:T(8,128)(2,1)S(1)}, bf16[192,1536]{1,0:T(8,128)(2,1)S(1)}, u32[]{:S(2)}, u32[]{:S(2)}) collective-permute-start(bf16[192,1536]{1,0:T(8,128)(2,1)S(1)} %bitcast.24), channel_id=1, source_target_pairs={{0,32},{32,0},{64,96},{96,64},{128,160},{160,128},{192,224},{224,1... | collective-permute-start | bytes 1769480 | tf_op jit(solution)/shard_map/ppermute | solution.py:284

commit v9 on v8

--- a/solution.py
+++ b/solution.py
@@ -235,6 +235,18 @@
     return call(place_body, outs, [pltpu.VMEM((slabs, *shape), jnp.float32)], *facts, windows)
 
 
+def sum_body(*refs):
+    *terms, out = refs
+    total = sum(term[...].astype(jnp.float32) for term in terms).astype(out.dtype)
+    for k in range(out.shape[0]):
+        out[k] = total
+
+
+def sum_copies(terms, copies):
+    out = jax.ShapeDtypeStruct((copies, *terms[0].shape), jnp.bfloat16)
+    return call(sum_body, [out], [], *terms)[0]
+
+
 def step_body(part_ref, layer, gradient, *refs):
     out, made, sems = refs[-3:]
     part = part_ref[0]
@@ -315,14 +327,13 @@
     def rows_of(block):
         return lax.dynamic_slice(own_part, (block * block_rows, 0), (block_rows, columns))
 
-    after, own, counts = lax.optimization_barrier((rows_of(3 - place_z), rows_of(place_z), counts))
-    after = mirrored(after, -1)
+    after = mirrored(rows_of(3 - place_z), -1)
+    own = rows_of(place_z)
 
     slot_rows, count = offsets.reshape(slots), counts.reshape(1)
     line = jax.ShapeDtypeStruct((8, LANE), jnp.int32)
     meta = call(facts_body, [line], [], slot_rows, column_starts.reshape(slots), count, angle_ids)[0]
     eight = to_eight(meta)
-    eight, own = lax.optimization_barrier((eight, own))
     facts = (eight, slab.reshape(1).astype(jnp.int32))
     own = of_slabs(own)
     after, own = lax.optimization_barrier((after, own))
@@ -339,9 +350,7 @@
     own = jnp.sum(own.astype(f32), axis=0)
 
     total = lax.optimization_barrier((own + spill.astype(f32)).astype(bf16))
-    total = (total.astype(f32) + swap(total, 8).astype(f32)).astype(bf16)
-
-    total = to_four(jnp.broadcast_to(total, (4, *total.shape))).reshape(tile_rows, columns)
+    total = to_four(sum_copies([total, swap(total, 8)], 4)).reshape(tile_rows, columns)
     new = step(core, layer, total)
     return step(1 - core, layer, swap(total, 1), new).reshape(volume.shape)
 

time: 181 us -> 179 us (0.989)
  the two profiles are of different devices: /device:TPU:1 before, /device:TPU:27 now
where the time goes in v9:
time: 179 us
  starting transfers between devices  57.4 us (32%)
  blocking collectives  57 us (32%)
  waiting for transfers between devices  44.4 us (25%)
  Pallas kernels  14.9 us (8%)
  local copies, waits for them, and re-layouts  3.27 us (2%)
    all_to_all x2, blocking collectives, to_eight(): lax.all_to_all(value, 'angle', 0, 0, axis_index_groups=eight_groups, tile...  39.4 us
    ppermute x6, starting transfers between devices, to_slab(): lax.ppermute(value, 'slab', [(i, (i + by) % slabs) for i in range(slabs)])  18.7 us
    all_to_all x1, blocking collectives, to_four(): lax.all_to_all(value, 'angle', 0, 0, axis_index_groups=four_groups, tiled...  17.7 us
    ppermute x2, waiting for transfers between devices, swap(): return lax.ppermute(value, 'angle', [(i, i ^ by) for i in range(angles)])  16.3 us
    ppermute x2, starting transfers between devices, mirrored(): return lax.ppermute(value, ('angle', 'tile'), pairs)  13.2 us
    pallas_call x7, Pallas kernels, call(): pl.pallas_call(body, out_shape=out_shape, in_specs=[smem if x.dtype == jn...  12.7 us
    all_to_all x2, waiting for transfers between devices, to_slabs(): return lax.all_to_all(value, 'slab', 0, 0, tiled=True)  12.6 us
    all_to_all x2, starting transfers between devices, to_eight(): lax.all_to_all(value, 'angle', 0, 0, axis_index_groups=eight_groups, tile...  11.9 us
  transfers between devices with their start and end apart: 14, of which 7 were waited for; matrix products, arithmetic and copies ran while one was open for 0% of the time, Pallas kernels for 5%

profile of v9, /device:TPU:27, one launch (start us, length us, event | category | flops | bytes accessed | tf_op | source)
XLA Modules:
  0.0 178.7 jit_solution(11388624534214777347)
XLA Ops:
  0.0 1.1 dynamic-slice_bitcast_fusion
  1.1 11.3 %collective-permute-start = (bf16[48,1536]{1,0:T(8,128)(2,1)S(1)}, bf16[48,1536]{1,0:T(8,128)(2,1)S(1)}, u32[]{:S(2)}, u32[]{:S(2)}) collective-permute-start(bf16[48,1536]{1,0:T(8,128)(2,1)S(1)} %get-tuple-element.36), channel_id=1, source_target_pairs={{1,448},{2,449},{3,450},{4,451},{5,452},{6,453},{7,454},{33,480},{... | collective-permute-start | bytes 442376 | tf_op jit(solution)/shard_map/ppermute | solution.py:305
  12.4 2.2 %collective-permute-start.3 = (bf16[48,1536]{1,0:T(8,128)(2,1)S(1)}, bf16[48,1536]{1,0:T(8,128)(2,1)S(1)}, u32[]{:S(2)}, u32[]{:S(2)}) collective-permute-start(bf16[48,1536]{1,0:T(8,128)(2,1)S(1)} %get-tuple-element.21.refs_0_), channel_id=1, source_target_pairs={{0,24},{8,0},{16,8},{24,16},{1,25},{9,1},{17,9},{25,17},{2,26},{10... | collective-permute-start | bytes 442376 | tf_op jit(solution)/shard_map/ppermute | solution.py:308
  14.5 4.0 %collective-permute-start.2 = (bf16[48,1536]{1,0:T(8,128)(2,1)S(1)}, bf16[48,1536]{1,0:T(8,128)(2,1)S(1)}, u32[]{:S(2)}, u32[]{:S(2)}) collective-permute-start(bf16[48,1536]{1,0:T(8,128)(2,1)S(1)} %get-tuple-element.21.refs_0_), channel_id=1, source_target_pairs={{0,16},{8,24},{16,0},{24,8},{1,17},{9,25},{17,1},{25,9},{2,18},{10... | collective-permute-start | bytes 442376 | tf_op jit(solution)/shard_map/ppermute | solution.py:308
  18.6 3.4 %collective-permute-start.1 = (bf16[48,1536]{1,0:T(8,128)(2,1)S(1)}, bf16[48,1536]{1,0:T(8,128)(2,1)S(1)}, u32[]{:S(2)}, u32[]{:S(2)}) collective-permute-start(bf16[48,1536]{1,0:T(8,128)(2,1)S(1)} %get-tuple-element.21.refs_0_), channel_id=1, source_target_pairs={{0,8},{8,16},{16,24},{24,0},{1,9},{9,17},{17,25},{25,1},{2,10},{10... | collective-permute-start | bytes 442376 | tf_op jit(solution)/shard_map/ppermute | solution.py:308
  24.7 1.1 shard_map.91
  25.8 7.7 %all-to-all-start = ((s32[8,1,128]{2,1,0:T(1,128)}), s32[8,1,128]{2,1,0:T(1,128)S(1)}, u32[]{:S(2)}, u32[]{:S(2)}) async-start(s32[8,1,128]{2,1,0:T(1,128)} %bitcast.6), calls=%async_computation | async-start | bytes 8192 | tf_op jit(solution)/shard_map/all_to_all | solution.py:311
  33.5 4.8 %all-to-all-done = s32[8,1,128]{2,1,0:T(1,128)S(1)} async-done(((s32[8,1,128]{2,1,0:T(1,128)}), s32[8,1,128]{2,1,0:T(1,128)S(1)}, u32[]{:S(2)}, u32[]{:S(2)}) %all-to-all-start) | async-done | bytes 4128 | tf_op jit(solution)/shard_map/all_to_all | solution.py:311
  38.2 0.9 broadcast_in_dim.3
  39.1 3.5 %all-to-all-start.1 = ((bf16[4,48,1536]{2,1,0:T(8,128)(2,1)}), bf16[4,48,1536]{2,1,0:T(8,128)(2,1)S(1)}, u32[]{:S(2)}, u32[]{:S(2)}) async-start(bf16[4,48,1536]{2,1,0:T(8,128)(2,1)} %broadcast_in_dim.3), calls=%async_computation.1 | async-start | bytes 1179648 | tf_op jit(solution)/shard_map/all_to_all | solution.py:317
  42.6 1.7 shard_map.92.done
  44.3 6.4 %all-to-all-done.1.blocks = bf16[4,48,1536]{2,1,0:T(8,128)(2,1)S(1)} async-done(((bf16[4,48,1536]{2,1,0:T(8,128)(2,1)}), bf16[4,48,1536]{2,1,0:T(8,128)(2,1)S(1)}, u32[]{:S(2)}, u32[]{:S(2)}) %all-to-all-start.1) | async-done | bytes 589856 | tf_op jit(solution)/shard_map/all_to_all | solution.py:317
  50.7 1.7 shard_map.93
  52.4 24.3 %all_to_all.41.windows = bf16[8,2,2,48,256]{4,3,2,1,0:T(8,128)(2,1)S(1)} all-to-all(bf16[8,2,2,48,256]{4,3,2,1,0:T(8,128)(2,1)S(1)} %shard_map.93), channel_id=1, replica_groups={{0,32,64,96,128,160,192,224},{256,288,320,352,384,416,448,480},{1,33,65..., dimensions={0} | all-to-all | bytes 1572864 | tf_op jit(solution)/shard_map/all_to_all | solution.py:311
  76.7 3.4 %shard_map.94 = (bf16[8,2,48,256]{3,2,1,0:T(8,128)(2,1)}, bf16[8,2,48,256]{3,2,1,0:T(8,128)(2,1)S(1)}) custom-call(s32[2]{0:T(128)S(1)} %bitcast.32, s32[1]{0:T(128)} %bitcast.21.count_ref, bf16[8,2,2,48,256]{4,3,2,1,0:T(8,128)(2,1)S(1)} %all_to_all.41.windows, f32[2,256,256]{2,1,0:T(8,128)S(1)} %copy-done.1, bf16[2,256,256]{2,1,0:T(8,128)(2,1)S(1)} %bitcast.26, ...), custom_call_target="tpu_custom_call" | custom-call | tf_op jit(solution)/shard_map/pallas_call | solution.py:45
  80.2 15.1 %all_to_all.42.windows = bf16[8,2,48,256]{3,2,1,0:T(8,128)(2,1)S(1)} all-to-all(bf16[8,2,48,256]{3,2,1,0:T(8,128)(2,1)S(1)} %get-tuple-element.27), channel_id=1, replica_groups={{0,32,64,96,128,160,192,224},{256,288,320,352,384,416,448,480},{1,33,65..., dimensions={0} | all-to-all | bytes 786432 | tf_op jit(solution)/shard_map/all_to_all | solution.py:311
  95.3 4.2 %all-to-all-start.4 = ((bf16[8,2,48,256]{3,2,1,0:T(8,128)(2,1)}), bf16[8,2,48,256]{3,2,1,0:T(8,128)(2,1)S(1)}, u32[]{:S(2)}, u32[]{:S(2)}) async-start(bf16[8,2,48,256]{3,2,1,0:T(8,128)(2,1)} %get-tuple-element.29), calls=%async_computation.4 | async-start | bytes 786432 | tf_op jit(solution)/shard_map/all_to_all | solution.py:311
  99.5 2.0 %shard_map.96 = (f32[48,1536]{1,0:T(8,128)S(1)}, bf16[48,1536]{1,0:T(8,128)(2,1)S(1)}, bf16[48,1536]{1,0:T(8,128)(2,1)S(1)}, bf16[48,1536]{1,0:T(8,128)(2,1)S(1)}) custom-call(s32[8,128]{1,0:T(8,128)S(1)} %bitcast.29, s32[1]{0:T(128)} %bitcast.8.slab_ref, bf16[8,2,48,256]{3,2,1,0:T(8,128)(2,1)S(1)} %all_to_all.42.windows), custom_call_target="tpu_custom_call" | custom-call | tf_op jit(solution)/shard_map/pallas_call | solution.py:45
  101.5 1.9 %collective-permute-start.4 = (bf16[48,1536]{1,0:T(8,128)(2,1)S(1)}, bf16[48,1536]{1,0:T(8,128)(2,1)S(1)}, u32[]{:S(2)}, u32[]{:S(2)}) collective-permute-start(bf16[48,1536]{1,0:T(8,128)(2,1)S(1)} %get-tuple-element.32), channel_id=1, source_target_pairs={{0,8},{8,16},{16,24},{24,0},{1,9},{9,17},{17,25},{25,1},{2,10},{10... | collective-permute-start | bytes 442376 | tf_op jit(solution)/shard_map/ppermute | solution.py:308
  103.4 4.9 %collective-permute-start.5 = (bf16[48,1536]{1,0:T(8,128)(2,1)S(1)}, bf16[48,1536]{1,0:T(8,128)(2,1)S(1)}, u32[]{:S(2)}, u32[]{:S(2)}) collective-permute-start(bf16[48,1536]{1,0:T(8,128)(2,1)S(1)} %get-tuple-element.33), channel_id=1, source_target_pairs={{0,16},{8,24},{16,0},{24,8},{1,17},{9,25},{17,1},{25,9},{2,18},{10... | collective-permute-start | bytes 442376 | tf_op jit(solution)/shard_map/ppermute | solution.py:308
  108.3 2.3 %collective-permute-start.6 = (bf16[48,1536]{1,0:T(8,128)(2,1)S(1)}, bf16[48,1536]{1,0:T(8,128)(2,1)S(1)}, u32[]{:S(2)}, u32[]{:S(2)}) collective-permute-start(bf16[48,1536]{1,0:T(8,128)(2,1)S(1)} %get-tuple-element.34), channel_id=1, source_target_pairs={{0,24},{8,0},{16,8},{24,16},{1,25},{9,1},{17,9},{25,17},{2,26},{10... | collective-permute-start | bytes 442376 | tf_op jit(solution)/shard_map/ppermute | solution.py:308
  111.2 2.8 %shard_map.95 = bf16[4,48,1536]{2,1,0:T(8,128)(2,1)} custom-call(s32[8,128]{1,0:T(8,128)S(1)} %bitcast.30, s32[1]{0:T(128)} %bitcast.8.slab_ref, bf16[8,2,48,256]{3,2,1,0:T(8,128)(2,1)S(1)} %all-to-all-done.4.windows), custom_call_target="tpu_custom_call" | custom-call | tf_op jit(solution)/shard_map/pallas_call | solution.py:45
  113.9 4.6 %all-to-all-start.5 = ((bf16[4,48,1536]{2,1,0:T(8,128)(2,1)}), bf16[4,48,1536]{2,1,0:T(8,128)(2,1)S(1)}, u32[]{:S(2)}, u32[]{:S(2)}) async-start(bf16[4,48,1536]{2,1,0:T(8,128)(2,1)} %shard_map.95), calls=%async_computation.5 | async-start | bytes 1179648 | tf_op jit(solution)/shard_map/all_to_all | solution.py:317
  118.7 1.9 %collective-permute-start.7 = (bf16[48,1536]{1,0:T(8,128)(2,1)S(1)}, bf16[48,1536]{1,0:T(8,128)(2,1)S(1)}, u32[]{:S(2)}, u32[]{:S(2)}) collective-permute-start(bf16[48,1536]{1,0:T(8,128)(2,1)S(1)} %add_convert_fusion.1), channel_id=1, source_target_pairs={{0,449},{1,450},{2,451},{3,452},{4,453},{5,454},{6,455},{32,481},{... | collective-permute-start | bytes 442376 | tf_op jit(solution)/shard_map/ppermute | solution.py:305
  120.6 6.2 %all-to-all-done.5 = bf16[4,48,1536]{2,1,0:T(8,128)(2,1)S(1)} async-done(((bf16[4,48,1536]{2,1,0:T(8,128)(2,1)}), bf16[4,48,1536]{2,1,0:T(8,128)(2,1)S(1)}, u32[]{:S(2)}, u32[]{:S(2)}) %all-to-all-start.5) | async-done | bytes 589856 | tf_op jit(solution)/shard_map/all_to_all | solution.py:317
  126.8 10.1 %collective-permute-done.7 = bf16[48,1536]{1,0:T(8,128)(2,1)S(1)} collective-permute-done((bf16[48,1536]{1,0:T(8,128)(2,1)S(1)}, bf16[48,1536]{1,0:T(8,128)(2,1)S(1)}, u32[]{:S(2)}, u32[]{:S(2)}) %collective-permute-start.7) | collective-permute-done | bytes 147488 | tf_op jit(solution)/shard_map/ppermute | solution.py:305
  137.0 2.1 %collective-permute-start.8 = (bf16[48,1536]{1,0:T(8,128)(2,1)S(1)}, bf16[48,1536]{1,0:T(8,128)(2,1)S(1)}, u32[]{:S(2)}, u32[]{:S(2)}) collective-permute-start(bf16[48,1536]{1,0:T(8,128)(2,1)S(1)} %add_convert_fusion.refs_0_), channel_id=1, source_target_pairs={{0,256},{32,288},{64,320},{96,352},{128,384},{160,416},{192,448},{... | collective-permute-start | bytes 442376 | tf_op jit(solution)/shard_map/ppermute | solution.py:296
  139.1 15.8 %collective-permute-done.8.refs_1_ = bf16[48,1536]{1,0:T(8,128)(2,1)S(1)} collective-permute-done((bf16[48,1536]{1,0:T(8,128)(2,1)S(1)}, bf16[48,1536]{1,0:T(8,128)(2,1)S(1)}, u32[]{:S(2)}, u32[]{:S(2)}) %collective-permute-start.8) | collective-permute-done | bytes 147488 | tf_op jit(solution)/shard_map/ppermute | solution.py:296
  154.9 17.7 %all_to_all.43 = bf16[4,48,1536]{2,1,0:T(8,128)(2,1)S(1)} all-to-all(bf16[4,48,1536]{2,1,0:T(8,128)(2,1)S(1)} %shard_map.97), channel_id=1, replica_groups={{0,64,128,192},{32,96,160,224},{256,320,384,448},{288,352,416,480},{1,6..., dimensions={0} | all-to-all | bytes 1179648 | tf_op jit(solution)/shard_map/all_to_all | solution.py:314
  172.5 3.5 %collective-permute-start.9 = (bf16[192,1536]{1,0:T(8,128)(2,1)S(1)}, bf16[192,1536]{1,0:T(8,128)(2,1)S(1)}, u32[]{:S(2)}, u32[]{:S(2)}) collective-permute-start(bf16[192,1536]{1,0:T(8,128)(2,1)S(1)} %bitcast.24), channel_id=1, source_target_pairs={{0,32},{32,0},{64,96},{96,64},{128,160},{160,128},{192,224},{224,1... | collective-permute-start | bytes 1769480 | tf_op jit(solution)/shard_map/ppermute | solution.py:296
  176.0 1.1 shard_map.98.refs_0_
  177.6 1.1 shard_map.99
  (29 shorter events, 2.8 us)
Async XLA Ops:
  1.1 32.4 %collective-permute-start = (bf16[48,1536]{1,0:T(8,128)(2,1)S(1)}, bf16[48,1536]{1,0:T(8,128)(2,1)S(1)}, u32[]{:S(2)}, u32[]{:S(2)}) collective-permute-start(bf16[48,1536]{1,0:T(8,128)(2,1)S(1)} %get-tuple-element.36), channel_id=1, source_target_pairs={{1,448},{2,449},{3,450},{4,451},{5,452},{6,453},{7,454},{33,480},{... | collective-permute-start | bytes 442376 | tf_op jit(solution)/shard_map/ppermute | solution.py:305
  12.4 21.1 %collective-permute-start.3 = (bf16[48,1536]{1,0:T(8,128)(2,1)S(1)}, bf16[48,1536]{1,0:T(8,128)(2,1)S(1)}, u32[]{:S(2)}, u32[]{:S(2)}) collective-permute-start(bf16[48,1536]{1,0:T(8,128)(2,1)S(1)} %get-tuple-element.21.refs_0_), channel_id=1, source_target_pairs={{0,24},{8,0},{16,8},{24,16},{1,25},{9,1},{17,9},{25,17},{2,26},{10... | collective-permute-start | bytes 442376 | tf_op jit(solution)/shard_map/ppermute | solution.py:308
  14.5 18.9 %collective-permute-start.2 = (bf16[48,1536]{1,0:T(8,128)(2,1)S(1)}, bf16[48,1536]{1,0:T(8,128)(2,1)S(1)}, u32[]{:S(2)}, u32[]{:S(2)}) collective-permute-start(bf16[48,1536]{1,0:T(8,128)(2,1)S(1)} %get-tuple-element.21.refs_0_), channel_id=1, source_target_pairs={{0,16},{8,24},{16,0},{24,8},{1,17},{9,25},{17,1},{25,9},{2,18},{10... | collective-permute-start | bytes 442376 | tf_op jit(solution)/shard_map/ppermute | solution.py:308
  18.6 14.9 %collective-permute-start.1 = (bf16[48,1536]{1,0:T(8,128)(2,1)S(1)}, bf16[48,1536]{1,0:T(8,128)(2,1)S(1)}, u32[]{:S(2)}, u32[]{:S(2)}) collective-permute-start(bf16[48,1536]{1,0:T(8,128)(2,1)S(1)} %get-tuple-element.21.refs_0_), channel_id=1, source_target_pairs={{0,8},{8,16},{16,24},{24,0},{1,9},{9,17},{17,25},{25,1},{2,10},{10... | collective-permute-start | bytes 442376 | tf_op jit(solution)/shard_map/ppermute | solution.py:308
  23.3 0.7 copy-start.5
  24.0 0.7 copy-start.7
  25.8 12.5 %all-to-all-start = ((s32[8,1,128]{2,1,0:T(1,128)}), s32[8,1,128]{2,1,0:T(1,128)S(1)}, u32[]{:S(2)}, u32[]{:S(2)}) async-start(s32[8,1,128]{2,1,0:T(1,128)} %bitcast.6), calls=%async_computation | async-start | bytes 8192 | tf_op jit(solution)/shard_map/all_to_all | solution.py:311
  39.1 11.6 %all-to-all-start.1 = ((bf16[4,48,1536]{2,1,0:T(8,128)(2,1)}), bf16[4,48,1536]{2,1,0:T(8,128)(2,1)S(1)}, u32[]{:S(2)}, u32[]{:S(2)}) async-start(bf16[4,48,1536]{2,1,0:T(8,128)(2,1)} %broadcast_in_dim.3), calls=%async_computation.1 | async-start | bytes 1179648 | tf_op jit(solution)/shard_map/all_to_all | solution.py:317
  52.4 24.3 %copy-start.1 = (f32[2,256,256]{2,1,0:T(8,128)S(1)}, f32[2,256,256]{2,1,0:T(8,128)}, u32[]{:S(2)}) copy-start(f32[2,256,256]{2,1,0:T(8,128)} %probe.1) | copy-start | bytes 1572868
  52.4 24.3 %copy-start.2 = (bf16[1,1,1,2,256,256]{5,4,3,2,1,0:T(8,128)(2,1)S(1)}, bf16[1,1,1,2,256,256]{5,4,3,2,1,0:T(8,128)(2,1)}, u32[]{:S(2)}) copy-start(bf16[1,1,1,2,256,256]{5,4,3,2,1,0:T(8,128)(2,1)} %param.11) | copy-start | bytes 786436
  52.4 24.3 %copy-start.3 = (bf16[256,256]{1,0:T(8,128)(2,1)S(1)}, bf16[256,256]{1,0:T(8,128)(2,1)}, u32[]{:S(2)}) copy-start(bf16[256,256]{1,0:T(8,128)(2,1)} %constant.105.clone.wi_ref) | copy-start | bytes 393220
  52.4 24.3 %copy-start.4 = (bf16[256,256]{1,0:T(8,128)(2,1)S(1)}, bf16[256,256]{1,0:T(8,128)(2,1)}, u32[]{:S(2)}) copy-start(bf16[256,256]{1,0:T(8,128)(2,1)} %constant.104.clone.wr_ref) | copy-start | bytes 393220
  52.4 24.3 %copy-start.6 = (s32[1,1,1,2]{3,2,1,0:T(1,128)S(1)}, s32[1,1,1,2]{3,2,1,0:T(1,128)}, u32[]{:S(2)}) copy-start(s32[1,1,1,2]{3,2,1,0:T(1,128)} %param.12) | copy-start | bytes 28
  95.3 15.9 %all-to-all-start.4 = ((bf16[8,2,48,256]{3,2,1,0:T(8,128)(2,1)}), bf16[8,2,48,256]{3,2,1,0:T(8,128)(2,1)S(1)}, u32[]{:S(2)}, u32[]{:S(2)}) async-start(bf16[8,2,48,256]{3,2,1,0:T(8,128)(2,1)} %get-tuple-element.29), calls=%async_computation.4 | async-start | bytes 786432 | tf_op jit(solution)/shard_map/all_to_all | solution.py:311
  101.5 17.1 %collective-permute-start.4 = (bf16[48,1536]{1,0:T(8,128)(2,1)S(1)}, bf16[48,1536]{1,0:T(8,128)(2,1)S(1)}, u32[]{:S(2)}, u32[]{:S(2)}) collective-permute-start(bf16[48,1536]{1,0:T(8,128)(2,1)S(1)} %get-tuple-element.32), channel_id=1, source_target_pairs={{0,8},{8,16},{16,24},{24,0},{1,9},{9,17},{17,25},{25,1},{2,10},{10... | collective-permute-start | bytes 442376 | tf_op jit(solution)/shard_map/ppermute | solution.py:308
  103.4 15.2 %collective-permute-start.5 = (bf16[48,1536]{1,0:T(8,128)(2,1)S(1)}, bf16[48,1536]{1,0:T(8,128)(2,1)S(1)}, u32[]{:S(2)}, u32[]{:S(2)}) collective-permute-start(bf16[48,1536]{1,0:T(8,128)(2,1)S(1)} %get-tuple-element.33), channel_id=1, source_target_pairs={{0,16},{8,24},{16,0},{24,8},{1,17},{9,25},{17,1},{25,9},{2,18},{10... | collective-permute-start | bytes 442376 | tf_op jit(solution)/shard_map/ppermute | solution.py:308
  108.3 10.3 %collective-permute-start.6 = (bf16[48,1536]{1,0:T(8,128)(2,1)S(1)}, bf16[48,1536]{1,0:T(8,128)(2,1)S(1)}, u32[]{:S(2)}, u32[]{:S(2)}) collective-permute-start(bf16[48,1536]{1,0:T(8,128)(2,1)S(1)} %get-tuple-element.34), channel_id=1, source_target_pairs={{0,24},{8,0},{16,8},{24,16},{1,25},{9,1},{17,9},{25,17},{2,26},{10... | collective-permute-start | bytes 442376 | tf_op jit(solution)/shard_map/ppermute | solution.py:308
  113.9 12.8 %all-to-all-start.5 = ((bf16[4,48,1536]{2,1,0:T(8,128)(2,1)}), bf16[4,48,1536]{2,1,0:T(8,128)(2,1)S(1)}, u32[]{:S(2)}, u32[]{:S(2)}) async-start(bf16[4,48,1536]{2,1,0:T(8,128)(2,1)} %shard_map.95), calls=%async_computation.5 | async-start | bytes 1179648 | tf_op jit(solution)/shard_map/all_to_all | solution.py:317
  118.7 18.3 %collective-permute-start.7 = (bf16[48,1536]{1,0:T(8,128)(2,1)S(1)}, bf16[48,1536]{1,0:T(8,128)(2,1)S(1)}, u32[]{:S(2)}, u32[]{:S(2)}) collective-permute-start(bf16[48,1536]{1,0:T(8,128)(2,1)S(1)} %add_convert_fusion.1), channel_id=1, source_target_pairs={{0,449},{1,450},{2,451},{3,452},{4,453},{5,454},{6,455},{32,481},{... | collective-permute-start | bytes 442376 | tf_op jit(solution)/shard_map/ppermute | solution.py:305
  137.0 39.0 %copy-start = (bf16[2,1,192,1536]{3,2,1,0:T(8,128)(2,1)S(1)}, bf16[2,1,192,1536]{3,2,1,0:T(8,128)(2,1)}, u32[]{:S(2)}) copy-start(bf16[2,1,192,1536]{3,2,1,0:T(8,128)(2,1)} %param.9) | copy-start | bytes 3538948
  137.0 17.8 %collective-permute-start.8 = (bf16[48,1536]{1,0:T(8,128)(2,1)S(1)}, bf16[48,1536]{1,0:T(8,128)(2,1)S(1)}, u32[]{:S(2)}, u32[]{:S(2)}) collective-permute-start(bf16[48,1536]{1,0:T(8,128)(2,1)S(1)} %add_convert_fusion.refs_0_), channel_id=1, source_target_pairs={{0,256},{32,288},{64,320},{96,352},{128,384},{160,416},{192,448},{... | collective-permute-start | bytes 442376 | tf_op jit(solution)/shard_map/ppermute | solution.py:296
  172.5 5.1 %collective-permute-start.9 = (bf16[192,1536]{1,0:T(8,128)(2,1)S(1)}, bf16[192,1536]{1,0:T(8,128)(2,1)S(1)}, u32[]{:S(2)}, u32[]{:S(2)}) collective-permute-start(bf16[192,1536]{1,0:T(8,128)(2,1)S(1)} %bitcast.24), channel_id=1, source_target_pairs={{0,32},{32,0},{64,96},{96,64},{128,160},{160,128},{192,224},{224,1... | collective-permute-start | bytes 1769480 | tf_op jit(solution)/shard_map/ppermute | solution.py:296

commit v10 on v9

--- a/solution.py
+++ b/solution.py
@@ -89,7 +89,7 @@
         return starts, left & (LANE - 1)
 
 
-def cut_body(absolute, facts_ref, slab_ref, *refs):
+def cut_body(facts_ref, slab_ref, *refs):
     blocks, out = refs[:-1], refs[-1]
     angles, slots, rows, width = out.shape
     facts = Facts(facts_ref, slab_ref, slots, len(blocks), blocks[0].shape[1])
@@ -101,8 +101,7 @@
             def _():
                 total = [jnp.zeros((rows, LANE), jnp.float32)] * 2
                 for k, block in enumerate(blocks):
-                    layer = k if absolute else facts.layer(-k)
-                    starts, inside = facts.columns_of(angle, slot, layer)
+                    starts, inside = facts.columns_of(angle, slot, facts.layer(-k))
                     turned = [
                         pltpu.roll(block[:, pl.ds(start, LANE)].astype(jnp.float32), (LANE - inside) & (LANE - 1), 1)
                         for start in starts
@@ -114,18 +113,7 @@
 
 def cut_windows(facts, blocks, angles, slots, width):
     out = jax.ShapeDtypeStruct((angles, slots, blocks[0].shape[0], width), jnp.bfloat16)
-    return call(functools.partial(cut_body, False), [out], [], *facts, *blocks)[0]
-
-
-def cut_rest(facts, blocks, done, which):
-    angles, slots, rows, width = done.shape
-    out = jax.ShapeDtypeStruct((angles, 2, slots, rows, width), jnp.bfloat16)
-
-    def body(facts_ref, slab_ref, blocks, done, out):
-        out[:, 1 - which] = done[...]
-        cut_body(True, facts_ref, slab_ref, *(blocks.at[k] for k in range(blocks.shape[0])), out.at[:, which])
-
-    return call(body, [out], [], *facts, blocks, done)[0]
+    return call(cut_body, [out], [], *facts, *blocks)[0]
 
 
 def cos_sin(angle):
@@ -147,8 +135,8 @@
     )
 
 
-def patch_body(row_ref, count_ref, windows, probe, patterns, wr_ref, wi_ref, own_out, next_out):
-    angles, _, slots, rows, width = windows.shape
+def patch_body(row_ref, count_ref, own_in, next_in, probe, patterns, wr_ref, wi_ref, own_out, next_out):
+    angles, slots, rows, width = own_in.shape
     f32, bf16 = jnp.float32, jnp.bfloat16
     blocks = angles // 2
     tall = 2 * blocks * rows
@@ -160,7 +148,7 @@
             pick = one_hot(width, tall, -row)
             window = []
             for part in range(2):
-                held = [windows[2 * k + part, tile, slot] for tile in range(2) for k in range(blocks)]
+                held = [ref[2 * k + part, slot] for ref in (own_in, next_in) for k in range(blocks)]
                 window.append(dot(pick, jnp.concatenate(held, axis=0)))
             phase, absorption = window
             magnitude = jnp.exp(-absorption)
@@ -196,10 +184,9 @@
                     next_out[2 * (blocks - 1 - k) + part, slot] = below
 
 
-def patch_gradients(slot_rows, count, windows, probe_wave, patterns, tables):
-    angles, _, slots, rows, width = windows.shape
-    out = jax.ShapeDtypeStruct((angles, slots, rows, width), jnp.bfloat16)
-    return call(patch_body, [out, out], [], slot_rows, count, windows, probe_wave, patterns, *tables)
+def patch_gradients(slot_rows, count, own, after, probe_wave, patterns, tables):
+    out = jax.ShapeDtypeStruct(own.shape, jnp.bfloat16)
+    return call(patch_body, [out, out], [], slot_rows, count, own, after, probe_wave, patterns, *tables)
 
 
 def place_body(facts_ref, slab_ref, windows, *refs):
@@ -338,11 +325,11 @@
     own = of_slabs(own)
     after, own = lax.optimization_barrier((after, own))
     own = cut_windows(facts, own, 8, slots, width)
-    after = to_slabs(jnp.broadcast_to(after, (slabs, *after.shape)))
+    own, after = to_eight(own), of_slabs(after)
     after, own = lax.optimization_barrier((after, own))
-    windows = to_eight(cut_rest(facts, after, own, 1))
-
-    own, after = patch_gradients(slot_rows, count, windows, probe_wave, patterns, tables)
+    after = to_eight(cut_windows(facts, after, 8, slots, width))
+
+    own, after = patch_gradients(slot_rows, count, own, after, probe_wave, patterns, tables)
     after, own = lax.optimization_barrier((to_eight(after), own))
     own = to_eight(own)
     spill = mirrored(over_slabs(*place_windows(facts, after, slabs, columns)).astype(bf16), 1)

time: 179 us -> 182 us (1.017)
  starting transfers between devices: 57.4 us -> 68.6 us
  blocking collectives: 57 us -> 50.1 us
  waiting for transfers between devices: 44.4 us -> 42.2 us
    ppermute x6 -> x9, starting transfers between devices: 18.7 us -> 28.2 us  [to_slab(): lax.ppermute(value, 'slab', [(i, (i + by) % slabs) for i in range(slabs)])]
    all_to_all x2, blocking collectives: 39.4 us -> 32.5 us  [to_eight(): lax.all_to_all(value, 'angle', 0, 0, axis_index_groups=eight_groups, tile...]
    all_to_all x2 -> x1, waiting for transfers between devices: 12.6 us -> 6.17 us  [to_slabs(): return lax.all_to_all(value, 'slab', 0, 0, tiled=True)]
    ppermute x6 -> x9, waiting for transfers between devices: 0.02 us -> 4.82 us  [to_slab(): lax.ppermute(value, 'slab', [(i, (i + by) % slabs) for i in range(slabs)])]
    all_to_all x2 -> x3, starting transfers between devices: 11.9 us -> 16.1 us  [to_eight(): lax.all_to_all(value, 'angle', 0, 0, axis_index_groups=eight_groups, tile...]
    all_to_all x2 -> x1, starting transfers between devices: 8.08 us -> 5.58 us  [to_slabs(): return lax.all_to_all(value, 'slab', 0, 0, tiled=True)]
    all_to_all x2 -> x3, waiting for transfers between devices: 5.4 us -> 4.79 us  [to_eight(): lax.all_to_all(value, 'angle', 0, 0, axis_index_groups=eight_groups, tile...]
  transfers between devices with their start and end apart: 14 -> 17, of which waited for: 7 -> 7; matrix products, arithmetic and copies ran while one was open for 0% -> 0% of each run, Pallas kernels for 5% -> 4%
where the time goes in v10:
time: 182 us; the launch traced here: 181 us
  starting transfers between devices  68.6 us (38%)
  blocking collectives  50.1 us (28%)
  waiting for transfers between devices  42.2 us (23%)
  Pallas kernels  15.6 us (9%)
  local copies, waits for them, and re-layouts  2.4 us (1%)
    all_to_all x2, blocking collectives, to_eight(): lax.all_to_all(value, 'angle', 0, 0, axis_index_groups=eight_groups, tile...  32.5 us
    ppermute x9, starting transfers between devices, to_slab(): lax.ppermute(value, 'slab', [(i, (i + by) % slabs) for i in range(slabs)])  28.2 us
    all_to_all x1, blocking collectives, to_four(): lax.all_to_all(value, 'angle', 0, 0, axis_index_groups=four_groups, tiled...  17.7 us
    ppermute x2, waiting for transfers between devices, swap(): return lax.ppermute(value, 'angle', [(i, i ^ by) for i in range(angles)])  16.4 us
    all_to_all x3, starting transfers between devices, to_eight(): lax.all_to_all(value, 'angle', 0, 0, axis_index_groups=eight_groups, tile...  16.1 us
    pallas_call x7, Pallas kernels, call(): pl.pallas_call(body, out_shape=out_shape, in_specs=[smem if x.dtype == jn...  13.4 us
    ppermute x2, starting transfers between devices, mirrored(): return lax.ppermute(value, ('angle', 'tile'), pairs)  13.2 us
    ppermute x2, waiting for transfers between devices, mirrored(): return lax.ppermute(value, ('angle', 'tile'), pairs)  10 us
  transfers between devices with their start and end apart: 17, of which 7 were waited for; matrix products, arithmetic and copies ran while one was open for 0% of the time, Pallas kernels for 4%

profile of v10, /device:TPU:27, one launch (start us, length us, event | category | flops | bytes accessed | tf_op | source)
XLA Modules:
  0.0 180.7 jit_solution(3992721542281878507)
XLA Ops:
  1.1 11.3 %collective-permute-start = (bf16[48,1536]{1,0:T(8,128)(2,1)S(1)}, bf16[48,1536]{1,0:T(8,128)(2,1)S(1)}, u32[]{:S(2)}, u32[]{:S(2)}) collective-permute-start(bf16[48,1536]{1,0:T(8,128)(2,1)S(1)} %get-tuple-element.42), channel_id=1, source_target_pairs={{1,448},{2,449},{3,450},{4,451},{5,452},{6,453},{7,454},{33,480},{... | collective-permute-start | bytes 442376 | tf_op jit(solution)/shard_map/ppermute | solution.py:292
  12.4 2.2 %collective-permute-start.3 = (bf16[48,1536]{1,0:T(8,128)(2,1)S(1)}, bf16[48,1536]{1,0:T(8,128)(2,1)S(1)}, u32[]{:S(2)}, u32[]{:S(2)}) collective-permute-start(bf16[48,1536]{1,0:T(8,128)(2,1)S(1)} %get-tuple-element.24.refs_0_), channel_id=1, source_target_pairs={{0,24},{8,0},{16,8},{24,16},{1,25},{9,1},{17,9},{25,17},{2,26},{10... | collective-permute-start | bytes 442376 | tf_op jit(solution)/shard_map/ppermute | solution.py:295
  14.5 4.0 %collective-permute-start.2 = (bf16[48,1536]{1,0:T(8,128)(2,1)S(1)}, bf16[48,1536]{1,0:T(8,128)(2,1)S(1)}, u32[]{:S(2)}, u32[]{:S(2)}) collective-permute-start(bf16[48,1536]{1,0:T(8,128)(2,1)S(1)} %get-tuple-element.24.refs_0_), channel_id=1, source_target_pairs={{0,16},{8,24},{16,0},{24,8},{1,17},{9,25},{17,1},{25,9},{2,18},{10... | collective-permute-start | bytes 442376 | tf_op jit(solution)/shard_map/ppermute | solution.py:295
  18.6 3.4 %collective-permute-start.1 = (bf16[48,1536]{1,0:T(8,128)(2,1)S(1)}, bf16[48,1536]{1,0:T(8,128)(2,1)S(1)}, u32[]{:S(2)}, u32[]{:S(2)}) collective-permute-start(bf16[48,1536]{1,0:T(8,128)(2,1)S(1)} %get-tuple-element.24.refs_0_), channel_id=1, source_target_pairs={{0,8},{8,16},{16,24},{24,0},{1,9},{9,17},{17,25},{25,1},{2,10},{10... | collective-permute-start | bytes 442376 | tf_op jit(solution)/shard_map/ppermute | solution.py:295
  24.7 1.1 shard_map.91
  25.8 7.7 %all-to-all-start = ((s32[8,1,128]{2,1,0:T(1,128)}), s32[8,1,128]{2,1,0:T(1,128)S(1)}, u32[]{:S(2)}, u32[]{:S(2)}) async-start(s32[8,1,128]{2,1,0:T(1,128)} %bitcast.6), calls=%async_computation | async-start | bytes 8192 | tf_op jit(solution)/shard_map/all_to_all | solution.py:298
  33.5 4.8 %all-to-all-done = s32[8,1,128]{2,1,0:T(1,128)S(1)} async-done(((s32[8,1,128]{2,1,0:T(1,128)}), s32[8,1,128]{2,1,0:T(1,128)S(1)}, u32[]{:S(2)}, u32[]{:S(2)}) %all-to-all-start) | async-done | bytes 4128 | tf_op jit(solution)/shard_map/all_to_all | solution.py:298
  38.2 2.4 %shard_map.92 = bf16[8,2,48,256]{3,2,1,0:T(8,128)(2,1)} custom-call(s32[8,128]{1,0:T(8,128)S(1)} %bitcast.27, s32[1]{0:T(128)} %bitcast.8.slab_ref, bf16[48,1536]{1,0:T(8,128)(2,1)S(1)} %get-tuple-element.24.refs_0_, bf16[48,1536]{1,0:T(8,128)(2,1)S(1)} %collective-permute-done.1.refs_1_, bf16[48,1536]{1,0:T(8,128)(2,1)S(1)} %collective-permute-done.2.refs_2_, ...), custom_call_target="tpu_custom_call" | custom-call | tf_op jit(solution)/shard_map/pallas_call | solution.py:45
  40.7 4.2 %all-to-all-start.1 = ((bf16[8,2,48,256]{3,2,1,0:T(8,128)(2,1)}), bf16[8,2,48,256]{3,2,1,0:T(8,128)(2,1)S(1)}, u32[]{:S(2)}, u32[]{:S(2)}) async-start(bf16[8,2,48,256]{3,2,1,0:T(8,128)(2,1)} %shard_map.92), calls=%async_computation.1 | async-start | bytes 786432 | tf_op jit(solution)/shard_map/all_to_all | solution.py:298
  44.9 1.9 %collective-permute-start.6 = (bf16[48,1536]{1,0:T(8,128)(2,1)S(1)}, bf16[48,1536]{1,0:T(8,128)(2,1)S(1)}, u32[]{:S(2)}, u32[]{:S(2)}) collective-permute-start(bf16[48,1536]{1,0:T(8,128)(2,1)S(1)} %collective-permute-done.refs_0_), channel_id=1, source_target_pairs={{0,24},{8,0},{16,8},{24,16},{1,25},{9,1},{17,9},{25,17},{2,26},{10... | collective-permute-start | bytes 442376 | tf_op jit(solution)/shard_map/ppermute | solution.py:295
  46.8 3.0 %collective-permute-start.5 = (bf16[48,1536]{1,0:T(8,128)(2,1)S(1)}, bf16[48,1536]{1,0:T(8,128)(2,1)S(1)}, u32[]{:S(2)}, u32[]{:S(2)}) collective-permute-start(bf16[48,1536]{1,0:T(8,128)(2,1)S(1)} %collective-permute-done.refs_0_), channel_id=1, source_target_pairs={{0,16},{8,24},{16,0},{24,8},{1,17},{9,25},{17,1},{25,9},{2,18},{10... | collective-permute-start | bytes 442376 | tf_op jit(solution)/shard_map/ppermute | solution.py:295
  49.9 4.0 %collective-permute-start.4 = (bf16[48,1536]{1,0:T(8,128)(2,1)S(1)}, bf16[48,1536]{1,0:T(8,128)(2,1)S(1)}, u32[]{:S(2)}, u32[]{:S(2)}) collective-permute-start(bf16[48,1536]{1,0:T(8,128)(2,1)S(1)} %collective-permute-done.refs_0_), channel_id=1, source_target_pairs={{0,8},{8,16},{16,24},{24,0},{1,9},{9,17},{17,25},{25,1},{2,10},{10... | collective-permute-start | bytes 442376 | tf_op jit(solution)/shard_map/ppermute | solution.py:295
  53.9 1.4 collective-permute-done.5.refs_2_
  55.3 3.4 %collective-permute-done.4.refs_1_ = bf16[48,1536]{1,0:T(8,128)(2,1)S(1)} collective-permute-done((bf16[48,1536]{1,0:T(8,128)(2,1)S(1)}, bf16[48,1536]{1,0:T(8,128)(2,1)S(1)}, u32[]{:S(2)}, u32[]{:S(2)}) %collective-permute-start.4) | collective-permute-done | bytes 147488 | tf_op jit(solution)/shard_map/ppermute | solution.py:295
  58.7 1.7 shard_map.93
  60.3 17.5 %all_to_all.41.next_in = bf16[8,2,48,256]{3,2,1,0:T(8,128)(2,1)S(1)} all-to-all(bf16[8,2,48,256]{3,2,1,0:T(8,128)(2,1)S(1)} %shard_map.93), channel_id=1, replica_groups={{0,32,64,96,128,160,192,224},{256,288,320,352,384,416,448,480},{1,33,65..., dimensions={0} | all-to-all | bytes 786432 | tf_op jit(solution)/shard_map/all_to_all | solution.py:298
  77.9 3.4 %shard_map.94 = (bf16[8,2,48,256]{3,2,1,0:T(8,128)(2,1)}, bf16[8,2,48,256]{3,2,1,0:T(8,128)(2,1)S(1)}) custom-call(s32[2]{0:T(128)S(1)} %bitcast.32, s32[1]{0:T(128)} %bitcast.21.count_ref, bf16[8,2,48,256]{3,2,1,0:T(8,128)(2,1)S(1)} %all-to-all-done.1.own_in, bf16[8,2,48,256]{3,2,1,0:T(8,128)(2,1)S(1)} %all_to_all.41.next_in, f32[2,256,256]{2,1,0:T(8,128)S(1)} %copy-done.1, ...), custom_call_target="tpu_custom_call" | custom-call | tf_op jit(solution)/shard_map/pallas_call | solution.py:45
  81.3 14.9 %all_to_all.42.windows = bf16[8,2,48,256]{3,2,1,0:T(8,128)(2,1)S(1)} all-to-all(bf16[8,2,48,256]{3,2,1,0:T(8,128)(2,1)S(1)} %get-tuple-element.33), channel_id=1, replica_groups={{0,32,64,96,128,160,192,224},{256,288,320,352,384,416,448,480},{1,33,65..., dimensions={0} | all-to-all | bytes 786432 | tf_op jit(solution)/shard_map/all_to_all | solution.py:298
  96.2 4.2 %all-to-all-start.4 = ((bf16[8,2,48,256]{3,2,1,0:T(8,128)(2,1)}), bf16[8,2,48,256]{3,2,1,0:T(8,128)(2,1)S(1)}, u32[]{:S(2)}, u32[]{:S(2)}) async-start(bf16[8,2,48,256]{3,2,1,0:T(8,128)(2,1)} %get-tuple-element.35), calls=%async_computation.4 | async-start | bytes 786432 | tf_op jit(solution)/shard_map/all_to_all | solution.py:298
  100.5 2.0 %shard_map.96 = (f32[48,1536]{1,0:T(8,128)S(1)}, bf16[48,1536]{1,0:T(8,128)(2,1)S(1)}, bf16[48,1536]{1,0:T(8,128)(2,1)S(1)}, bf16[48,1536]{1,0:T(8,128)(2,1)S(1)}) custom-call(s32[8,128]{1,0:T(8,128)S(1)} %bitcast.29, s32[1]{0:T(128)} %bitcast.8.slab_ref, bf16[8,2,48,256]{3,2,1,0:T(8,128)(2,1)S(1)} %all_to_all.42.windows), custom_call_target="tpu_custom_call" | custom-call | tf_op jit(solution)/shard_map/pallas_call | solution.py:45
  102.4 3.2 %collective-permute-start.7 = (bf16[48,1536]{1,0:T(8,128)(2,1)S(1)}, bf16[48,1536]{1,0:T(8,128)(2,1)S(1)}, u32[]{:S(2)}, u32[]{:S(2)}) collective-permute-start(bf16[48,1536]{1,0:T(8,128)(2,1)S(1)} %get-tuple-element.38), channel_id=1, source_target_pairs={{0,8},{8,16},{16,24},{24,0},{1,9},{9,17},{17,25},{25,1},{2,10},{10... | collective-permute-start | bytes 442376 | tf_op jit(solution)/shard_map/ppermute | solution.py:295
  105.6 4.6 %collective-permute-start.8 = (bf16[48,1536]{1,0:T(8,128)(2,1)S(1)}, bf16[48,1536]{1,0:T(8,128)(2,1)S(1)}, u32[]{:S(2)}, u32[]{:S(2)}) collective-permute-start(bf16[48,1536]{1,0:T(8,128)(2,1)S(1)} %get-tuple-element.39), channel_id=1, source_target_pairs={{0,16},{8,24},{16,0},{24,8},{1,17},{9,25},{17,1},{25,9},{2,18},{10... | collective-permute-start | bytes 442376 | tf_op jit(solution)/shard_map/ppermute | solution.py:295
  110.2 1.9 %collective-permute-start.9 = (bf16[48,1536]{1,0:T(8,128)(2,1)S(1)}, bf16[48,1536]{1,0:T(8,128)(2,1)S(1)}, u32[]{:S(2)}, u32[]{:S(2)}) collective-permute-start(bf16[48,1536]{1,0:T(8,128)(2,1)S(1)} %get-tuple-element.40), channel_id=1, source_target_pairs={{0,24},{8,0},{16,8},{24,16},{1,25},{9,1},{17,9},{25,17},{2,26},{10... | collective-permute-start | bytes 442376 | tf_op jit(solution)/shard_map/ppermute | solution.py:295
  112.2 2.8 %shard_map.95 = bf16[4,48,1536]{2,1,0:T(8,128)(2,1)} custom-call(s32[8,128]{1,0:T(8,128)S(1)} %bitcast.30, s32[1]{0:T(128)} %bitcast.8.slab_ref, bf16[8,2,48,256]{3,2,1,0:T(8,128)(2,1)S(1)} %all-to-all-done.4.windows), custom_call_target="tpu_custom_call" | custom-call | tf_op jit(solution)/shard_map/pallas_call | solution.py:45
  114.9 5.6 %all-to-all-start.5 = ((bf16[4,48,1536]{2,1,0:T(8,128)(2,1)}), bf16[4,48,1536]{2,1,0:T(8,128)(2,1)S(1)}, u32[]{:S(2)}, u32[]{:S(2)}) async-start(bf16[4,48,1536]{2,1,0:T(8,128)(2,1)} %shard_map.95), calls=%async_computation.5 | async-start | bytes 1179648 | tf_op jit(solution)/shard_map/all_to_all | solution.py:304
  120.6 1.9 %collective-permute-start.10 = (bf16[48,1536]{1,0:T(8,128)(2,1)S(1)}, bf16[48,1536]{1,0:T(8,128)(2,1)S(1)}, u32[]{:S(2)}, u32[]{:S(2)}) collective-permute-start(bf16[48,1536]{1,0:T(8,128)(2,1)S(1)} %add_convert_fusion.1), channel_id=1, source_target_pairs={{0,449},{1,450},{2,451},{3,452},{4,453},{5,454},{6,455},{32,481},{... | collective-permute-start | bytes 442376 | tf_op jit(solution)/shard_map/ppermute | solution.py:292
  122.5 6.2 %all-to-all-done.5 = bf16[4,48,1536]{2,1,0:T(8,128)(2,1)S(1)} async-done(((bf16[4,48,1536]{2,1,0:T(8,128)(2,1)}), bf16[4,48,1536]{2,1,0:T(8,128)(2,1)S(1)}, u32[]{:S(2)}, u32[]{:S(2)}) %all-to-all-start.5) | async-done | bytes 589856 | tf_op jit(solution)/shard_map/all_to_all | solution.py:304
  128.8 10.0 %collective-permute-done.10 = bf16[48,1536]{1,0:T(8,128)(2,1)S(1)} collective-permute-done((bf16[48,1536]{1,0:T(8,128)(2,1)S(1)}, bf16[48,1536]{1,0:T(8,128)(2,1)S(1)}, u32[]{:S(2)}, u32[]{:S(2)}) %collective-permute-start.10) | collective-permute-done | bytes 147488 | tf_op jit(solution)/shard_map/ppermute | solution.py:292
  138.9 2.1 %collective-permute-start.11 = (bf16[48,1536]{1,0:T(8,128)(2,1)S(1)}, bf16[48,1536]{1,0:T(8,128)(2,1)S(1)}, u32[]{:S(2)}, u32[]{:S(2)}) collective-permute-start(bf16[48,1536]{1,0:T(8,128)(2,1)S(1)} %add_convert_fusion.refs_0_), channel_id=1, source_target_pairs={{0,256},{32,288},{64,320},{96,352},{128,384},{160,416},{192,448},{... | collective-permute-start | bytes 442376 | tf_op jit(solution)/shard_map/ppermute | solution.py:283
  140.9 15.9 %collective-permute-done.11.refs_1_ = bf16[48,1536]{1,0:T(8,128)(2,1)S(1)} collective-permute-done((bf16[48,1536]{1,0:T(8,128)(2,1)S(1)}, bf16[48,1536]{1,0:T(8,128)(2,1)S(1)}, u32[]{:S(2)}, u32[]{:S(2)}) %collective-permute-start.11) | collective-permute-done | bytes 147488 | tf_op jit(solution)/shard_map/ppermute | solution.py:283
  156.9 17.7 %all_to_all.43 = bf16[4,48,1536]{2,1,0:T(8,128)(2,1)S(1)} all-to-all(bf16[4,48,1536]{2,1,0:T(8,128)(2,1)S(1)} %shard_map.97), channel_id=1, replica_groups={{0,64,128,192},{32,96,160,224},{256,320,384,448},{288,352,416,480},{1,6..., dimensions={0} | all-to-all | bytes 1179648 | tf_op jit(solution)/shard_map/all_to_all | solution.py:301
  174.6 3.5 %collective-permute-start.12 = (bf16[192,1536]{1,0:T(8,128)(2,1)S(1)}, bf16[192,1536]{1,0:T(8,128)(2,1)S(1)}, u32[]{:S(2)}, u32[]{:S(2)}) collective-permute-start(bf16[192,1536]{1,0:T(8,128)(2,1)S(1)} %bitcast.24), channel_id=1, source_target_pairs={{0,32},{32,0},{64,96},{96,64},{128,160},{160,128},{192,224},{224,1... | collective-permute-start | bytes 1769480 | tf_op jit(solution)/shard_map/ppermute | solution.py:283
  (34 shorter events, 5.3 us)
Async XLA Ops:
  1.1 32.4 %collective-permute-start = (bf16[48,1536]{1,0:T(8,128)(2,1)S(1)}, bf16[48,1536]{1,0:T(8,128)(2,1)S(1)}, u32[]{:S(2)}, u32[]{:S(2)}) collective-permute-start(bf16[48,1536]{1,0:T(8,128)(2,1)S(1)} %get-tuple-element.42), channel_id=1, source_target_pairs={{1,448},{2,449},{3,450},{4,451},{5,452},{6,453},{7,454},{33,480},{... | collective-permute-start | bytes 442376 | tf_op jit(solution)/shard_map/ppermute | solution.py:292
  12.4 21.1 %collective-permute-start.3 = (bf16[48,1536]{1,0:T(8,128)(2,1)S(1)}, bf16[48,1536]{1,0:T(8,128)(2,1)S(1)}, u32[]{:S(2)}, u32[]{:S(2)}) collective-permute-start(bf16[48,1536]{1,0:T(8,128)(2,1)S(1)} %get-tuple-element.24.refs_0_), channel_id=1, source_target_pairs={{0,24},{8,0},{16,8},{24,16},{1,25},{9,1},{17,9},{25,17},{2,26},{10... | collective-permute-start | bytes 442376 | tf_op jit(solution)/shard_map/ppermute | solution.py:295
  14.5 18.9 %collective-permute-start.2 = (bf16[48,1536]{1,0:T(8,128)(2,1)S(1)}, bf16[48,1536]{1,0:T(8,128)(2,1)S(1)}, u32[]{:S(2)}, u32[]{:S(2)}) collective-permute-start(bf16[48,1536]{1,0:T(8,128)(2,1)S(1)} %get-tuple-element.24.refs_0_), channel_id=1, source_target_pairs={{0,16},{8,24},{16,0},{24,8},{1,17},{9,25},{17,1},{25,9},{2,18},{10... | collective-permute-start | bytes 442376 | tf_op jit(solution)/shard_map/ppermute | solution.py:295
  18.6 14.9 %collective-permute-start.1 = (bf16[48,1536]{1,0:T(8,128)(2,1)S(1)}, bf16[48,1536]{1,0:T(8,128)(2,1)S(1)}, u32[]{:S(2)}, u32[]{:S(2)}) collective-permute-start(bf16[48,1536]{1,0:T(8,128)(2,1)S(1)} %get-tuple-element.24.refs_0_), channel_id=1, source_target_pairs={{0,8},{8,16},{16,24},{24,0},{1,9},{9,17},{17,25},{25,1},{2,10},{10... | collective-permute-start | bytes 442376 | tf_op jit(solution)/shard_map/ppermute | solution.py:295
  23.3 0.7 copy-start.5
  24.0 0.7 copy-start.7
  25.8 12.5 %all-to-all-start = ((s32[8,1,128]{2,1,0:T(1,128)}), s32[8,1,128]{2,1,0:T(1,128)S(1)}, u32[]{:S(2)}, u32[]{:S(2)}) async-start(s32[8,1,128]{2,1,0:T(1,128)} %bitcast.6), calls=%async_computation | async-start | bytes 8192 | tf_op jit(solution)/shard_map/all_to_all | solution.py:298
  40.7 37.2 %copy-start.1 = (f32[2,256,256]{2,1,0:T(8,128)S(1)}, f32[2,256,256]{2,1,0:T(8,128)}, u32[]{:S(2)}) copy-start(f32[2,256,256]{2,1,0:T(8,128)} %probe.1) | copy-start | bytes 1572868
  40.7 37.2 %copy-start.2 = (bf16[1,1,1,2,256,256]{5,4,3,2,1,0:T(8,128)(2,1)S(1)}, bf16[1,1,1,2,256,256]{5,4,3,2,1,0:T(8,128)(2,1)}, u32[]{:S(2)}) copy-start(bf16[1,1,1,2,256,256]{5,4,3,2,1,0:T(8,128)(2,1)} %param.11) | copy-start | bytes 786436
  40.7 37.2 %copy-start.3 = (bf16[256,256]{1,0:T(8,128)(2,1)S(1)}, bf16[256,256]{1,0:T(8,128)(2,1)}, u32[]{:S(2)}) copy-start(bf16[256,256]{1,0:T(8,128)(2,1)} %constant.105.clone.wi_ref) | copy-start | bytes 393220
  40.7 37.2 %copy-start.4 = (bf16[256,256]{1,0:T(8,128)(2,1)S(1)}, bf16[256,256]{1,0:T(8,128)(2,1)}, u32[]{:S(2)}) copy-start(bf16[256,256]{1,0:T(8,128)(2,1)} %constant.104.clone.wr_ref) | copy-start | bytes 393220
  40.7 37.2 %copy-start.6 = (s32[1,1,1,2]{3,2,1,0:T(1,128)S(1)}, s32[1,1,1,2]{3,2,1,0:T(1,128)}, u32[]{:S(2)}) copy-start(s32[1,1,1,2]{3,2,1,0:T(1,128)} %param.12) | copy-start | bytes 28
  40.7 17.9 %all-to-all-start.1 = ((bf16[8,2,48,256]{3,2,1,0:T(8,128)(2,1)}), bf16[8,2,48,256]{3,2,1,0:T(8,128)(2,1)S(1)}, u32[]{:S(2)}, u32[]{:S(2)}) async-start(bf16[8,2,48,256]{3,2,1,0:T(8,128)(2,1)} %shard_map.92), calls=%async_computation.1 | async-start | bytes 786432 | tf_op jit(solution)/shard_map/all_to_all | solution.py:298
  44.9 8.9 %collective-permute-start.6 = (bf16[48,1536]{1,0:T(8,128)(2,1)S(1)}, bf16[48,1536]{1,0:T(8,128)(2,1)S(1)}, u32[]{:S(2)}, u32[]{:S(2)}) collective-permute-start(bf16[48,1536]{1,0:T(8,128)(2,1)S(1)} %collective-permute-done.refs_0_), channel_id=1, source_target_pairs={{0,24},{8,0},{16,8},{24,16},{1,25},{9,1},{17,9},{25,17},{2,26},{10... | collective-permute-start | bytes 442376 | tf_op jit(solution)/shard_map/ppermute | solution.py:295
  46.8 8.5 %collective-permute-start.5 = (bf16[48,1536]{1,0:T(8,128)(2,1)S(1)}, bf16[48,1536]{1,0:T(8,128)(2,1)S(1)}, u32[]{:S(2)}, u32[]{:S(2)}) collective-permute-start(bf16[48,1536]{1,0:T(8,128)(2,1)S(1)} %collective-permute-done.refs_0_), channel_id=1, source_target_pairs={{0,16},{8,24},{16,0},{24,8},{1,17},{9,25},{17,1},{25,9},{2,18},{10... | collective-permute-start | bytes 442376 | tf_op jit(solution)/shard_map/ppermute | solution.py:295
  49.9 8.8 %collective-permute-start.4 = (bf16[48,1536]{1,0:T(8,128)(2,1)S(1)}, bf16[48,1536]{1,0:T(8,128)(2,1)S(1)}, u32[]{:S(2)}, u32[]{:S(2)}) collective-permute-start(bf16[48,1536]{1,0:T(8,128)(2,1)S(1)} %collective-permute-done.refs_0_), channel_id=1, source_target_pairs={{0,8},{8,16},{16,24},{24,0},{1,9},{9,17},{17,25},{25,1},{2,10},{10... | collective-permute-start | bytes 442376 | tf_op jit(solution)/shard_map/ppermute | solution.py:295
  96.2 15.9 %all-to-all-start.4 = ((bf16[8,2,48,256]{3,2,1,0:T(8,128)(2,1)}), bf16[8,2,48,256]{3,2,1,0:T(8,128)(2,1)S(1)}, u32[]{:S(2)}, u32[]{:S(2)}) async-start(bf16[8,2,48,256]{3,2,1,0:T(8,128)(2,1)} %get-tuple-element.35), calls=%async_computation.4 | async-start | bytes 786432 | tf_op jit(solution)/shard_map/all_to_all | solution.py:298
  102.4 18.1 %collective-permute-start.7 = (bf16[48,1536]{1,0:T(8,128)(2,1)S(1)}, bf16[48,1536]{1,0:T(8,128)(2,1)S(1)}, u32[]{:S(2)}, u32[]{:S(2)}) collective-permute-start(bf16[48,1536]{1,0:T(8,128)(2,1)S(1)} %get-tuple-element.38), channel_id=1, source_target_pairs={{0,8},{8,16},{16,24},{24,0},{1,9},{9,17},{17,25},{25,1},{2,10},{10... | collective-permute-start | bytes 442376 | tf_op jit(solution)/shard_map/ppermute | solution.py:295
  105.6 14.9 %collective-permute-start.8 = (bf16[48,1536]{1,0:T(8,128)(2,1)S(1)}, bf16[48,1536]{1,0:T(8,128)(2,1)S(1)}, u32[]{:S(2)}, u32[]{:S(2)}) collective-permute-start(bf16[48,1536]{1,0:T(8,128)(2,1)S(1)} %get-tuple-element.39), channel_id=1, source_target_pairs={{0,16},{8,24},{16,0},{24,8},{1,17},{9,25},{17,1},{25,9},{2,18},{10... | collective-permute-start | bytes 442376 | tf_op jit(solution)/shard_map/ppermute | solution.py:295
  110.2 10.3 %collective-permute-start.9 = (bf16[48,1536]{1,0:T(8,128)(2,1)S(1)}, bf16[48,1536]{1,0:T(8,128)(2,1)S(1)}, u32[]{:S(2)}, u32[]{:S(2)}) collective-permute-start(bf16[48,1536]{1,0:T(8,128)(2,1)S(1)} %get-tuple-element.40), channel_id=1, source_target_pairs={{0,24},{8,0},{16,8},{24,16},{1,25},{9,1},{17,9},{25,17},{2,26},{10... | collective-permute-start | bytes 442376 | tf_op jit(solution)/shard_map/ppermute | solution.py:295
  114.9 13.8 %all-to-all-start.5 = ((bf16[4,48,1536]{2,1,0:T(8,128)(2,1)}), bf16[4,48,1536]{2,1,0:T(8,128)(2,1)S(1)}, u32[]{:S(2)}, u32[]{:S(2)}) async-start(bf16[4,48,1536]{2,1,0:T(8,128)(2,1)} %shard_map.95), calls=%async_computation.5 | async-start | bytes 1179648 | tf_op jit(solution)/shard_map/all_to_all | solution.py:304
  120.6 18.2 %collective-permute-start.10 = (bf16[48,1536]{1,0:T(8,128)(2,1)S(1)}, bf16[48,1536]{1,0:T(8,128)(2,1)S(1)}, u32[]{:S(2)}, u32[]{:S(2)}) collective-permute-start(bf16[48,1536]{1,0:T(8,128)(2,1)S(1)} %add_convert_fusion.1), channel_id=1, source_target_pairs={{0,449},{1,450},{2,451},{3,452},{4,453},{5,454},{6,455},{32,481},{... | collective-permute-start | bytes 442376 | tf_op jit(solution)/shard_map/ppermute | solution.py:292
  138.8 39.2 %copy-start = (bf16[2,1,192,1536]{3,2,1,0:T(8,128)(2,1)S(1)}, bf16[2,1,192,1536]{3,2,1,0:T(8,128)(2,1)}, u32[]{:S(2)}) copy-start(bf16[2,1,192,1536]{3,2,1,0:T(8,128)(2,1)} %param.9) | copy-start | bytes 3538948
  138.9 18.0 %collective-permute-start.11 = (bf16[48,1536]{1,0:T(8,128)(2,1)S(1)}, bf16[48,1536]{1,0:T(8,128)(2,1)S(1)}, u32[]{:S(2)}, u32[]{:S(2)}) collective-permute-start(bf16[48,1536]{1,0:T(8,128)(2,1)S(1)} %add_convert_fusion.refs_0_), channel_id=1, source_target_pairs={{0,256},{32,288},{64,320},{96,352},{128,384},{160,416},{192,448},{... | collective-permute-start | bytes 442376 | tf_op jit(solution)/shard_map/ppermute | solution.py:283
  174.6 5.1 %collective-permute-start.12 = (bf16[192,1536]{1,0:T(8,128)(2,1)S(1)}, bf16[192,1536]{1,0:T(8,128)(2,1)S(1)}, u32[]{:S(2)}, u32[]{:S(2)}) collective-permute-start(bf16[192,1536]{1,0:T(8,128)(2,1)S(1)} %bitcast.24), channel_id=1, source_target_pairs={{0,32},{32,0},{64,96},{96,64},{128,160},{160,128},{192,224},{224,1... | collective-permute-start | bytes 1769480 | tf_op jit(solution)/shard_map/ppermute | solution.py:283

commit v11 on v9

--- a/solution.py
+++ b/solution.py
@@ -89,7 +89,7 @@
         return starts, left & (LANE - 1)
 
 
-def cut_body(absolute, facts_ref, slab_ref, *refs):
+def cut_body(facts_ref, slab_ref, *refs):
     blocks, out = refs[:-1], refs[-1]
     angles, slots, rows, width = out.shape
     facts = Facts(facts_ref, slab_ref, slots, len(blocks), blocks[0].shape[1])
@@ -101,8 +101,7 @@
             def _():
                 total = [jnp.zeros((rows, LANE), jnp.float32)] * 2
                 for k, block in enumerate(blocks):
-                    layer = k if absolute else facts.layer(-k)
-                    starts, inside = facts.columns_of(angle, slot, layer)
+                    starts, inside = facts.columns_of(angle, slot, facts.layer(-k))
                     turned = [
                         pltpu.roll(block[:, pl.ds(start, LANE)].astype(jnp.float32), (LANE - inside) & (LANE - 1), 1)
                         for start in starts
@@ -114,18 +113,19 @@
 
 def cut_windows(facts, blocks, angles, slots, width):
     out = jax.ShapeDtypeStruct((angles, slots, blocks[0].shape[0], width), jnp.bfloat16)
-    return call(functools.partial(cut_body, False), [out], [], *facts, *blocks)[0]
+    return call(cut_body, [out], [], *facts, *blocks)[0]
 
 
 def cut_rest(facts, blocks, done, which):
     angles, slots, rows, width = done.shape
     out = jax.ShapeDtypeStruct((angles, 2, slots, rows, width), jnp.bfloat16)
 
-    def body(facts_ref, slab_ref, blocks, done, out):
+    def body(facts_ref, slab_ref, *refs):
+        *blocks, done, out = refs
         out[:, 1 - which] = done[...]
-        cut_body(True, facts_ref, slab_ref, *(blocks.at[k] for k in range(blocks.shape[0])), out.at[:, which])
-
-    return call(body, [out], [], *facts, blocks, done)[0]
+        cut_body(facts_ref, slab_ref, *blocks, out.at[:, which])
+
+    return call(body, [out], [], *facts, *blocks, done)[0]
 
 
 def cos_sin(angle):
@@ -336,9 +336,8 @@
     eight = to_eight(meta)
     facts = (eight, slab.reshape(1).astype(jnp.int32))
     own = of_slabs(own)
-    after, own = lax.optimization_barrier((after, own))
-    own = cut_windows(facts, own, 8, slots, width)
-    after = to_slabs(jnp.broadcast_to(after, (slabs, *after.shape)))
+    after, own, facts = lax.optimization_barrier((after, own, facts))
+    own, after = cut_windows(facts, own, 8, slots, width), of_slabs(after)
     after, own = lax.optimization_barrier((after, own))
     windows = to_eight(cut_rest(facts, after, own, 1))
 

time: 179 us -> 181 us (1.011)
  starting transfers between devices: 57.4 us -> 64.5 us
  waiting for transfers between devices: 44.4 us -> 40.1 us
    ppermute x6 -> x9, starting transfers between devices: 18.7 us -> 28.3 us  [to_slab(): lax.ppermute(value, 'slab', [(i, (i + by) % slabs) for i in range(slabs)])]
    all_to_all x2 -> x1, waiting for transfers between devices: 12.6 us -> 6.17 us  [to_slabs(): return lax.all_to_all(value, 'slab', 0, 0, tiled=True)]
    ppermute x6 -> x9, waiting for transfers between devices: 0.02 us -> 2.68 us  [to_slab(): lax.ppermute(value, 'slab', [(i, (i + by) % slabs) for i in range(slabs)])]
    all_to_all x2 -> x1, starting transfers between devices: 8.08 us -> 5.6 us  [to_slabs(): return lax.all_to_all(value, 'slab', 0, 0, tiled=True)]
  transfers between devices with their start and end apart: 14 -> 16, of which waited for: 7 -> 6; matrix products, arithmetic and copies ran while one was open for 0% -> 0% of each run, Pallas kernels for 5% -> 5%
where the time goes in v11:
time: 181 us
  starting transfers between devices  64.5 us (36%)
  blocking collectives  57 us (31%)
  waiting for transfers between devices  40.1 us (22%)
  Pallas kernels  14.9 us (8%)
  local copies, waits for them, and re-layouts  2.41 us (1%)
    all_to_all x2, blocking collectives, to_eight(): lax.all_to_all(value, 'angle', 0, 0, axis_index_groups=eight_groups, tile...  39.3 us
    ppermute x9, starting transfers between devices, to_slab(): lax.ppermute(value, 'slab', [(i, (i + by) % slabs) for i in range(slabs)])  28.3 us
    all_to_all x1, blocking collectives, to_four(): lax.all_to_all(value, 'angle', 0, 0, axis_index_groups=four_groups, tiled...  17.7 us
    ppermute x2, waiting for transfers between devices, swap(): return lax.ppermute(value, 'angle', [(i, i ^ by) for i in range(angles)])  16.4 us
    ppermute x2, starting transfers between devices, mirrored(): return lax.ppermute(value, ('angle', 'tile'), pairs)  13.2 us
    pallas_call x7, Pallas kernels, call(): pl.pallas_call(body, out_shape=out_shape, in_specs=[smem if x.dtype == jn...  12.7 us
    all_to_all x2, starting transfers between devices, to_eight(): lax.all_to_all(value, 'angle', 0, 0, axis_index_groups=eight_groups, tile...  11.9 us
    ppermute x2, waiting for transfers between devices, mirrored(): return lax.ppermute(value, ('angle', 'tile'), pairs)  10 us
  transfers between devices with their start and end apart: 16, of which 6 were waited for; matrix products, arithmetic and copies ran while one was open for 0% of the time, Pallas kernels for 5%

profile of v11, /device:TPU:27, one launch (start us, length us, event | category | flops | bytes accessed | tf_op | source)
XLA Modules:
  0.0 180.6 jit_solution(17890757604833517405)
XLA Ops:
  1.1 11.3 %collective-permute-start = (bf16[48,1536]{1,0:T(8,128)(2,1)S(1)}, bf16[48,1536]{1,0:T(8,128)(2,1)S(1)}, u32[]{:S(2)}, u32[]{:S(2)}) collective-permute-start(bf16[48,1536]{1,0:T(8,128)(2,1)S(1)} %get-tuple-element.46), channel_id=1, source_target_pairs={{1,448},{2,449},{3,450},{4,451},{5,452},{6,453},{7,454},{33,480},{... | collective-permute-start | bytes 442376 | tf_op jit(solution)/shard_map/ppermute | solution.py:305
  12.4 2.2 %collective-permute-start.3 = (bf16[48,1536]{1,0:T(8,128)(2,1)S(1)}, bf16[48,1536]{1,0:T(8,128)(2,1)S(1)}, u32[]{:S(2)}, u32[]{:S(2)}) collective-permute-start(bf16[48,1536]{1,0:T(8,128)(2,1)S(1)} %get-tuple-element.28.refs_0_), channel_id=1, source_target_pairs={{0,24},{8,0},{16,8},{24,16},{1,25},{9,1},{17,9},{25,17},{2,26},{10... | collective-permute-start | bytes 442376 | tf_op jit(solution)/shard_map/ppermute | solution.py:308
  14.5 4.0 %collective-permute-start.2 = (bf16[48,1536]{1,0:T(8,128)(2,1)S(1)}, bf16[48,1536]{1,0:T(8,128)(2,1)S(1)}, u32[]{:S(2)}, u32[]{:S(2)}) collective-permute-start(bf16[48,1536]{1,0:T(8,128)(2,1)S(1)} %get-tuple-element.28.refs_0_), channel_id=1, source_target_pairs={{0,16},{8,24},{16,0},{24,8},{1,17},{9,25},{17,1},{25,9},{2,18},{10... | collective-permute-start | bytes 442376 | tf_op jit(solution)/shard_map/ppermute | solution.py:308
  18.6 3.4 %collective-permute-start.1 = (bf16[48,1536]{1,0:T(8,128)(2,1)S(1)}, bf16[48,1536]{1,0:T(8,128)(2,1)S(1)}, u32[]{:S(2)}, u32[]{:S(2)}) collective-permute-start(bf16[48,1536]{1,0:T(8,128)(2,1)S(1)} %get-tuple-element.28.refs_0_), channel_id=1, source_target_pairs={{0,8},{8,16},{16,24},{24,0},{1,9},{9,17},{17,25},{25,1},{2,10},{10... | collective-permute-start | bytes 442376 | tf_op jit(solution)/shard_map/ppermute | solution.py:308
  24.7 1.1 shard_map.91
  25.8 7.7 %all-to-all-start = ((s32[8,1,128]{2,1,0:T(1,128)}), s32[8,1,128]{2,1,0:T(1,128)S(1)}, u32[]{:S(2)}, u32[]{:S(2)}) async-start(s32[8,1,128]{2,1,0:T(1,128)} %bitcast.8), calls=%async_computation | async-start | bytes 8192 | tf_op jit(solution)/shard_map/all_to_all | solution.py:311
  33.5 4.8 %all-to-all-done = s32[8,1,128]{2,1,0:T(1,128)S(1)} async-done(((s32[8,1,128]{2,1,0:T(1,128)}), s32[8,1,128]{2,1,0:T(1,128)S(1)}, u32[]{:S(2)}, u32[]{:S(2)}) %all-to-all-start) | async-done | bytes 4128 | tf_op jit(solution)/shard_map/all_to_all | solution.py:311
  38.3 1.9 %collective-permute-start.6 = (bf16[48,1536]{1,0:T(8,128)(2,1)S(1)}, bf16[48,1536]{1,0:T(8,128)(2,1)S(1)}, u32[]{:S(2)}, u32[]{:S(2)}) collective-permute-start(bf16[48,1536]{1,0:T(8,128)(2,1)S(1)} %collective-permute-done.refs_0_), channel_id=1, source_target_pairs={{0,24},{8,0},{16,8},{24,16},{1,25},{9,1},{17,9},{25,17},{2,26},{10... | collective-permute-start | bytes 442376 | tf_op jit(solution)/shard_map/ppermute | solution.py:308
  40.2 3.0 %collective-permute-start.5 = (bf16[48,1536]{1,0:T(8,128)(2,1)S(1)}, bf16[48,1536]{1,0:T(8,128)(2,1)S(1)}, u32[]{:S(2)}, u32[]{:S(2)}) collective-permute-start(bf16[48,1536]{1,0:T(8,128)(2,1)S(1)} %collective-permute-done.refs_0_), channel_id=1, source_target_pairs={{0,16},{8,24},{16,0},{24,8},{1,17},{9,25},{17,1},{25,9},{2,18},{10... | collective-permute-start | bytes 442376 | tf_op jit(solution)/shard_map/ppermute | solution.py:308
  43.2 4.0 %collective-permute-start.4 = (bf16[48,1536]{1,0:T(8,128)(2,1)S(1)}, bf16[48,1536]{1,0:T(8,128)(2,1)S(1)}, u32[]{:S(2)}, u32[]{:S(2)}) collective-permute-start(bf16[48,1536]{1,0:T(8,128)(2,1)S(1)} %collective-permute-done.refs_0_), channel_id=1, source_target_pairs={{0,8},{8,16},{16,24},{24,0},{1,9},{9,17},{17,25},{25,1},{2,10},{10... | collective-permute-start | bytes 442376 | tf_op jit(solution)/shard_map/ppermute | solution.py:308
  47.2 1.7 shard_map.92.refs_4_
  48.9 2.7 %collective-permute-done.4.refs_1_ = bf16[48,1536]{1,0:T(8,128)(2,1)S(1)} collective-permute-done((bf16[48,1536]{1,0:T(8,128)(2,1)S(1)}, bf16[48,1536]{1,0:T(8,128)(2,1)S(1)}, u32[]{:S(2)}, u32[]{:S(2)}) %collective-permute-start.4) | collective-permute-done | bytes 147488 | tf_op jit(solution)/shard_map/ppermute | solution.py:308
  51.6 1.7 shard_map.93
  53.4 24.2 %all_to_all.37.windows = bf16[8,2,2,48,256]{4,3,2,1,0:T(8,128)(2,1)S(1)} all-to-all(bf16[8,2,2,48,256]{4,3,2,1,0:T(8,128)(2,1)S(1)} %shard_map.93), channel_id=1, replica_groups={{0,32,64,96,128,160,192,224},{256,288,320,352,384,416,448,480},{1,33,65..., dimensions={0} | all-to-all | bytes 1572864 | tf_op jit(solution)/shard_map/all_to_all | solution.py:311
  77.6 3.4 %shard_map.94 = (bf16[8,2,48,256]{3,2,1,0:T(8,128)(2,1)}, bf16[8,2,48,256]{3,2,1,0:T(8,128)(2,1)S(1)}) custom-call(s32[2]{0:T(128)S(1)} %bitcast.32, s32[1]{0:T(128)} %bitcast.21.count_ref, bf16[8,2,2,48,256]{4,3,2,1,0:T(8,128)(2,1)S(1)} %all_to_all.37.windows, f32[2,256,256]{2,1,0:T(8,128)S(1)} %copy-done.1, bf16[2,256,256]{2,1,0:T(8,128)(2,1)S(1)} %bitcast.26, ...), custom_call_target="tpu_custom_call" | custom-call | tf_op jit(solution)/shard_map/pallas_call | solution.py:45
  81.0 15.1 %all_to_all.38.windows = bf16[8,2,48,256]{3,2,1,0:T(8,128)(2,1)S(1)} all-to-all(bf16[8,2,48,256]{3,2,1,0:T(8,128)(2,1)S(1)} %get-tuple-element.37), channel_id=1, replica_groups={{0,32,64,96,128,160,192,224},{256,288,320,352,384,416,448,480},{1,33,65..., dimensions={0} | all-to-all | bytes 786432 | tf_op jit(solution)/shard_map/all_to_all | solution.py:311
  96.1 4.2 %all-to-all-start.3 = ((bf16[8,2,48,256]{3,2,1,0:T(8,128)(2,1)}), bf16[8,2,48,256]{3,2,1,0:T(8,128)(2,1)S(1)}, u32[]{:S(2)}, u32[]{:S(2)}) async-start(bf16[8,2,48,256]{3,2,1,0:T(8,128)(2,1)} %get-tuple-element.39), calls=%async_computation.3 | async-start | bytes 786432 | tf_op jit(solution)/shard_map/all_to_all | solution.py:311
  100.3 2.0 %shard_map.96 = (f32[48,1536]{1,0:T(8,128)S(1)}, bf16[48,1536]{1,0:T(8,128)(2,1)S(1)}, bf16[48,1536]{1,0:T(8,128)(2,1)S(1)}, bf16[48,1536]{1,0:T(8,128)(2,1)S(1)}) custom-call(s32[8,128]{1,0:T(8,128)S(1)} %bitcast.29, s32[1]{0:T(128)} %bitcast.10.slab_ref, bf16[8,2,48,256]{3,2,1,0:T(8,128)(2,1)S(1)} %all_to_all.38.windows), custom_call_target="tpu_custom_call" | custom-call | tf_op jit(solution)/shard_map/pallas_call | solution.py:45
  102.3 3.3 %collective-permute-start.7 = (bf16[48,1536]{1,0:T(8,128)(2,1)S(1)}, bf16[48,1536]{1,0:T(8,128)(2,1)S(1)}, u32[]{:S(2)}, u32[]{:S(2)}) collective-permute-start(bf16[48,1536]{1,0:T(8,128)(2,1)S(1)} %get-tuple-element.42), channel_id=1, source_target_pairs={{0,8},{8,16},{16,24},{24,0},{1,9},{9,17},{17,25},{25,1},{2,10},{10... | collective-permute-start | bytes 442376 | tf_op jit(solution)/shard_map/ppermute | solution.py:308
  105.6 4.6 %collective-permute-start.8 = (bf16[48,1536]{1,0:T(8,128)(2,1)S(1)}, bf16[48,1536]{1,0:T(8,128)(2,1)S(1)}, u32[]{:S(2)}, u32[]{:S(2)}) collective-permute-start(bf16[48,1536]{1,0:T(8,128)(2,1)S(1)} %get-tuple-element.43), channel_id=1, source_target_pairs={{0,16},{8,24},{16,0},{24,8},{1,17},{9,25},{17,1},{25,9},{2,18},{10... | collective-permute-start | bytes 442376 | tf_op jit(solution)/shard_map/ppermute | solution.py:308
  110.2 1.9 %collective-permute-start.9 = (bf16[48,1536]{1,0:T(8,128)(2,1)S(1)}, bf16[48,1536]{1,0:T(8,128)(2,1)S(1)}, u32[]{:S(2)}, u32[]{:S(2)}) collective-permute-start(bf16[48,1536]{1,0:T(8,128)(2,1)S(1)} %get-tuple-element.44), channel_id=1, source_target_pairs={{0,24},{8,0},{16,8},{24,16},{1,25},{9,1},{17,9},{25,17},{2,26},{10... | collective-permute-start | bytes 442376 | tf_op jit(solution)/shard_map/ppermute | solution.py:308
  112.1 2.8 %shard_map.95 = bf16[4,48,1536]{2,1,0:T(8,128)(2,1)} custom-call(s32[8,128]{1,0:T(8,128)S(1)} %bitcast.30, s32[1]{0:T(128)} %bitcast.10.slab_ref, bf16[8,2,48,256]{3,2,1,0:T(8,128)(2,1)S(1)} %all-to-all-done.3.windows), custom_call_target="tpu_custom_call" | custom-call | tf_op jit(solution)/shard_map/pallas_call | solution.py:45
  114.8 5.6 %all-to-all-start.4 = ((bf16[4,48,1536]{2,1,0:T(8,128)(2,1)}), bf16[4,48,1536]{2,1,0:T(8,128)(2,1)S(1)}, u32[]{:S(2)}, u32[]{:S(2)}) async-start(bf16[4,48,1536]{2,1,0:T(8,128)(2,1)} %shard_map.95), calls=%async_computation.4 | async-start | bytes 1179648 | tf_op jit(solution)/shard_map/all_to_all | solution.py:317
  120.5 1.9 %collective-permute-start.10 = (bf16[48,1536]{1,0:T(8,128)(2,1)S(1)}, bf16[48,1536]{1,0:T(8,128)(2,1)S(1)}, u32[]{:S(2)}, u32[]{:S(2)}) collective-permute-start(bf16[48,1536]{1,0:T(8,128)(2,1)S(1)} %add_convert_fusion.1), channel_id=1, source_target_pairs={{0,449},{1,450},{2,451},{3,452},{4,453},{5,454},{6,455},{32,481},{... | collective-permute-start | bytes 442376 | tf_op jit(solution)/shard_map/ppermute | solution.py:305
  122.5 6.2 %all-to-all-done.4 = bf16[4,48,1536]{2,1,0:T(8,128)(2,1)S(1)} async-done(((bf16[4,48,1536]{2,1,0:T(8,128)(2,1)}), bf16[4,48,1536]{2,1,0:T(8,128)(2,1)S(1)}, u32[]{:S(2)}, u32[]{:S(2)}) %all-to-all-start.4) | async-done | bytes 589856 | tf_op jit(solution)/shard_map/all_to_all | solution.py:317
  128.7 10.0 %collective-permute-done.10 = bf16[48,1536]{1,0:T(8,128)(2,1)S(1)} collective-permute-done((bf16[48,1536]{1,0:T(8,128)(2,1)S(1)}, bf16[48,1536]{1,0:T(8,128)(2,1)S(1)}, u32[]{:S(2)}, u32[]{:S(2)}) %collective-permute-start.10) | collective-permute-done | bytes 147488 | tf_op jit(solution)/shard_map/ppermute | solution.py:305
  138.8 2.1 %collective-permute-start.11 = (bf16[48,1536]{1,0:T(8,128)(2,1)S(1)}, bf16[48,1536]{1,0:T(8,128)(2,1)S(1)}, u32[]{:S(2)}, u32[]{:S(2)}) collective-permute-start(bf16[48,1536]{1,0:T(8,128)(2,1)S(1)} %add_convert_fusion.refs_0_), channel_id=1, source_target_pairs={{0,256},{32,288},{64,320},{96,352},{128,384},{160,416},{192,448},{... | collective-permute-start | bytes 442376 | tf_op jit(solution)/shard_map/ppermute | solution.py:296
  140.8 15.9 %collective-permute-done.11.refs_1_ = bf16[48,1536]{1,0:T(8,128)(2,1)S(1)} collective-permute-done((bf16[48,1536]{1,0:T(8,128)(2,1)S(1)}, bf16[48,1536]{1,0:T(8,128)(2,1)S(1)}, u32[]{:S(2)}, u32[]{:S(2)}) %collective-permute-start.11) | collective-permute-done | bytes 147488 | tf_op jit(solution)/shard_map/ppermute | solution.py:296
  156.8 17.7 %all_to_all.39 = bf16[4,48,1536]{2,1,0:T(8,128)(2,1)S(1)} all-to-all(bf16[4,48,1536]{2,1,0:T(8,128)(2,1)S(1)} %shard_map.97), channel_id=1, replica_groups={{0,64,128,192},{32,96,160,224},{256,320,384,448},{288,352,416,480},{1,6..., dimensions={0} | all-to-all | bytes 1179648 | tf_op jit(solution)/shard_map/all_to_all | solution.py:314
  174.5 3.4 %collective-permute-start.12 = (bf16[192,1536]{1,0:T(8,128)(2,1)S(1)}, bf16[192,1536]{1,0:T(8,128)(2,1)S(1)}, u32[]{:S(2)}, u32[]{:S(2)}) collective-permute-start(bf16[192,1536]{1,0:T(8,128)(2,1)S(1)} %bitcast.24), channel_id=1, source_target_pairs={{0,32},{32,0},{64,96},{96,64},{128,160},{160,128},{192,224},{224,1... | collective-permute-start | bytes 1769480 | tf_op jit(solution)/shard_map/ppermute | solution.py:296
  178.0 1.1 shard_map.98.refs_0_
  179.6 1.1 shard_map.99
  (32 shorter events, 3.2 us)
Async XLA Ops:
  1.1 37.2 %collective-permute-start = (bf16[48,1536]{1,0:T(8,128)(2,1)S(1)}, bf16[48,1536]{1,0:T(8,128)(2,1)S(1)}, u32[]{:S(2)}, u32[]{:S(2)}) collective-permute-start(bf16[48,1536]{1,0:T(8,128)(2,1)S(1)} %get-tuple-element.46), channel_id=1, source_target_pairs={{1,448},{2,449},{3,450},{4,451},{5,452},{6,453},{7,454},{33,480},{... | collective-permute-start | bytes 442376 | tf_op jit(solution)/shard_map/ppermute | solution.py:305
  12.4 25.9 %collective-permute-start.3 = (bf16[48,1536]{1,0:T(8,128)(2,1)S(1)}, bf16[48,1536]{1,0:T(8,128)(2,1)S(1)}, u32[]{:S(2)}, u32[]{:S(2)}) collective-permute-start(bf16[48,1536]{1,0:T(8,128)(2,1)S(1)} %get-tuple-element.28.refs_0_), channel_id=1, source_target_pairs={{0,24},{8,0},{16,8},{24,16},{1,25},{9,1},{17,9},{25,17},{2,26},{10... | collective-permute-start | bytes 442376 | tf_op jit(solution)/shard_map/ppermute | solution.py:308
  14.5 23.7 %collective-permute-start.2 = (bf16[48,1536]{1,0:T(8,128)(2,1)S(1)}, bf16[48,1536]{1,0:T(8,128)(2,1)S(1)}, u32[]{:S(2)}, u32[]{:S(2)}) collective-permute-start(bf16[48,1536]{1,0:T(8,128)(2,1)S(1)} %get-tuple-element.28.refs_0_), channel_id=1, source_target_pairs={{0,16},{8,24},{16,0},{24,8},{1,17},{9,25},{17,1},{25,9},{2,18},{10... | collective-permute-start | bytes 442376 | tf_op jit(solution)/shard_map/ppermute | solution.py:308
  18.6 19.7 %collective-permute-start.1 = (bf16[48,1536]{1,0:T(8,128)(2,1)S(1)}, bf16[48,1536]{1,0:T(8,128)(2,1)S(1)}, u32[]{:S(2)}, u32[]{:S(2)}) collective-permute-start(bf16[48,1536]{1,0:T(8,128)(2,1)S(1)} %get-tuple-element.28.refs_0_), channel_id=1, source_target_pairs={{0,8},{8,16},{16,24},{24,0},{1,9},{9,17},{17,25},{25,1},{2,10},{10... | collective-permute-start | bytes 442376 | tf_op jit(solution)/shard_map/ppermute | solution.py:308
  23.3 0.7 copy-start.5
  24.0 0.7 copy-start.7
  25.8 12.5 %all-to-all-start = ((s32[8,1,128]{2,1,0:T(1,128)}), s32[8,1,128]{2,1,0:T(1,128)S(1)}, u32[]{:S(2)}, u32[]{:S(2)}) async-start(s32[8,1,128]{2,1,0:T(1,128)} %bitcast.8), calls=%async_computation | async-start | bytes 8192 | tf_op jit(solution)/shard_map/all_to_all | solution.py:311
  38.3 10.6 %collective-permute-start.6 = (bf16[48,1536]{1,0:T(8,128)(2,1)S(1)}, bf16[48,1536]{1,0:T(8,128)(2,1)S(1)}, u32[]{:S(2)}, u32[]{:S(2)}) collective-permute-start(bf16[48,1536]{1,0:T(8,128)(2,1)S(1)} %collective-permute-done.refs_0_), channel_id=1, source_target_pairs={{0,24},{8,0},{16,8},{24,16},{1,25},{9,1},{17,9},{25,17},{2,26},{10... | collective-permute-start | bytes 442376 | tf_op jit(solution)/shard_map/ppermute | solution.py:308
  40.2 8.7 %collective-permute-start.5 = (bf16[48,1536]{1,0:T(8,128)(2,1)S(1)}, bf16[48,1536]{1,0:T(8,128)(2,1)S(1)}, u32[]{:S(2)}, u32[]{:S(2)}) collective-permute-start(bf16[48,1536]{1,0:T(8,128)(2,1)S(1)} %collective-permute-done.refs_0_), channel_id=1, source_target_pairs={{0,16},{8,24},{16,0},{24,8},{1,17},{9,25},{17,1},{25,9},{2,18},{10... | collective-permute-start | bytes 442376 | tf_op jit(solution)/shard_map/ppermute | solution.py:308
  43.2 8.4 %collective-permute-start.4 = (bf16[48,1536]{1,0:T(8,128)(2,1)S(1)}, bf16[48,1536]{1,0:T(8,128)(2,1)S(1)}, u32[]{:S(2)}, u32[]{:S(2)}) collective-permute-start(bf16[48,1536]{1,0:T(8,128)(2,1)S(1)} %collective-permute-done.refs_0_), channel_id=1, source_target_pairs={{0,8},{8,16},{16,24},{24,0},{1,9},{9,17},{17,25},{25,1},{2,10},{10... | collective-permute-start | bytes 442376 | tf_op jit(solution)/shard_map/ppermute | solution.py:308
  53.3 24.2 %copy-start.1 = (f32[2,256,256]{2,1,0:T(8,128)S(1)}, f32[2,256,256]{2,1,0:T(8,128)}, u32[]{:S(2)}) copy-start(f32[2,256,256]{2,1,0:T(8,128)} %probe.1) | copy-start | bytes 1572868
  53.3 24.2 %copy-start.2 = (bf16[1,1,1,2,256,256]{5,4,3,2,1,0:T(8,128)(2,1)S(1)}, bf16[1,1,1,2,256,256]{5,4,3,2,1,0:T(8,128)(2,1)}, u32[]{:S(2)}) copy-start(bf16[1,1,1,2,256,256]{5,4,3,2,1,0:T(8,128)(2,1)} %param.11) | copy-start | bytes 786436
  53.3 24.2 %copy-start.3 = (bf16[256,256]{1,0:T(8,128)(2,1)S(1)}, bf16[256,256]{1,0:T(8,128)(2,1)}, u32[]{:S(2)}) copy-start(bf16[256,256]{1,0:T(8,128)(2,1)} %constant.105.clone.wi_ref) | copy-start | bytes 393220
  53.3 24.2 %copy-start.4 = (bf16[256,256]{1,0:T(8,128)(2,1)S(1)}, bf16[256,256]{1,0:T(8,128)(2,1)}, u32[]{:S(2)}) copy-start(bf16[256,256]{1,0:T(8,128)(2,1)} %constant.104.clone.wr_ref) | copy-start | bytes 393220
  53.4 24.2 %copy-start.6 = (s32[1,1,1,2]{3,2,1,0:T(1,128)S(1)}, s32[1,1,1,2]{3,2,1,0:T(1,128)}, u32[]{:S(2)}) copy-start(s32[1,1,1,2]{3,2,1,0:T(1,128)} %param.12) | copy-start | bytes 28
  96.1 16.0 %all-to-all-start.3 = ((bf16[8,2,48,256]{3,2,1,0:T(8,128)(2,1)}), bf16[8,2,48,256]{3,2,1,0:T(8,128)(2,1)S(1)}, u32[]{:S(2)}, u32[]{:S(2)}) async-start(bf16[8,2,48,256]{3,2,1,0:T(8,128)(2,1)} %get-tuple-element.39), calls=%async_computation.3 | async-start | bytes 786432 | tf_op jit(solution)/shard_map/all_to_all | solution.py:311
  102.3 18.1 %collective-permute-start.7 = (bf16[48,1536]{1,0:T(8,128)(2,1)S(1)}, bf16[48,1536]{1,0:T(8,128)(2,1)S(1)}, u32[]{:S(2)}, u32[]{:S(2)}) collective-permute-start(bf16[48,1536]{1,0:T(8,128)(2,1)S(1)} %get-tuple-element.42), channel_id=1, source_target_pairs={{0,8},{8,16},{16,24},{24,0},{1,9},{9,17},{17,25},{25,1},{2,10},{10... | collective-permute-start | bytes 442376 | tf_op jit(solution)/shard_map/ppermute | solution.py:308
  105.6 14.9 %collective-permute-start.8 = (bf16[48,1536]{1,0:T(8,128)(2,1)S(1)}, bf16[48,1536]{1,0:T(8,128)(2,1)S(1)}, u32[]{:S(2)}, u32[]{:S(2)}) collective-permute-start(bf16[48,1536]{1,0:T(8,128)(2,1)S(1)} %get-tuple-element.43), channel_id=1, source_target_pairs={{0,16},{8,24},{16,0},{24,8},{1,17},{9,25},{17,1},{25,9},{2,18},{10... | collective-permute-start | bytes 442376 | tf_op jit(solution)/shard_map/ppermute | solution.py:308
  110.2 10.3 %collective-permute-start.9 = (bf16[48,1536]{1,0:T(8,128)(2,1)S(1)}, bf16[48,1536]{1,0:T(8,128)(2,1)S(1)}, u32[]{:S(2)}, u32[]{:S(2)}) collective-permute-start(bf16[48,1536]{1,0:T(8,128)(2,1)S(1)} %get-tuple-element.44), channel_id=1, source_target_pairs={{0,24},{8,0},{16,8},{24,16},{1,25},{9,1},{17,9},{25,17},{2,26},{10... | collective-permute-start | bytes 442376 | tf_op jit(solution)/shard_map/ppermute | solution.py:308
  114.8 13.8 %all-to-all-start.4 = ((bf16[4,48,1536]{2,1,0:T(8,128)(2,1)}), bf16[4,48,1536]{2,1,0:T(8,128)(2,1)S(1)}, u32[]{:S(2)}, u32[]{:S(2)}) async-start(bf16[4,48,1536]{2,1,0:T(8,128)(2,1)} %shard_map.95), calls=%async_computation.4 | async-start | bytes 1179648 | tf_op jit(solution)/shard_map/all_to_all | solution.py:317
  120.5 18.2 %collective-permute-start.10 = (bf16[48,1536]{1,0:T(8,128)(2,1)S(1)}, bf16[48,1536]{1,0:T(8,128)(2,1)S(1)}, u32[]{:S(2)}, u32[]{:S(2)}) collective-permute-start(bf16[48,1536]{1,0:T(8,128)(2,1)S(1)} %add_convert_fusion.1), channel_id=1, source_target_pairs={{0,449},{1,450},{2,451},{3,452},{4,453},{5,454},{6,455},{32,481},{... | collective-permute-start | bytes 442376 | tf_op jit(solution)/shard_map/ppermute | solution.py:305
  138.8 39.2 %copy-start = (bf16[2,1,192,1536]{3,2,1,0:T(8,128)(2,1)S(1)}, bf16[2,1,192,1536]{3,2,1,0:T(8,128)(2,1)}, u32[]{:S(2)}) copy-start(bf16[2,1,192,1536]{3,2,1,0:T(8,128)(2,1)} %param.9) | copy-start | bytes 3538948
  138.8 18.0 %collective-permute-start.11 = (bf16[48,1536]{1,0:T(8,128)(2,1)S(1)}, bf16[48,1536]{1,0:T(8,128)(2,1)S(1)}, u32[]{:S(2)}, u32[]{:S(2)}) collective-permute-start(bf16[48,1536]{1,0:T(8,128)(2,1)S(1)} %add_convert_fusion.refs_0_), channel_id=1, source_target_pairs={{0,256},{32,288},{64,320},{96,352},{128,384},{160,416},{192,448},{... | collective-permute-start | bytes 442376 | tf_op jit(solution)/shard_map/ppermute | solution.py:296
  174.5 5.1 %collective-permute-start.12 = (bf16[192,1536]{1,0:T(8,128)(2,1)S(1)}, bf16[192,1536]{1,0:T(8,128)(2,1)S(1)}, u32[]{:S(2)}, u32[]{:S(2)}) collective-permute-start(bf16[192,1536]{1,0:T(8,128)(2,1)S(1)} %bitcast.24), channel_id=1, source_target_pairs={{0,32},{32,0},{64,96},{96,64},{128,160},{160,128},{192,224},{224,1... | collective-permute-start | bytes 1769480 | tf_op jit(solution)/shard_map/ppermute | solution.py:296

commit v12 on v9

--- a/solution.py
+++ b/solution.py
@@ -322,6 +322,13 @@
     def over_slabs(kept, *sent):
         return sum((to_slab(block, k + 1).astype(f32) for k, block in enumerate(sent)), kept)
 
+    def live_to_eight(value, axis):
+        def first(value):
+            sent = to_eight(lax.slice_in_dim(value, 0, 1, axis=axis))
+            return jnp.concatenate([sent, lax.slice_in_dim(value, 1, slots, axis=axis)], axis=axis)
+
+        return lax.cond(more, to_eight, first, value)
+
     own_part = lax.dynamic_index_in_dim(layer, core, 0, keepdims=False)
 
     def rows_of(block):
@@ -335,15 +342,16 @@
     meta = call(facts_body, [line], [], slot_rows, column_starts.reshape(slots), count, angle_ids)[0]
     eight = to_eight(meta)
     facts = (eight, slab.reshape(1).astype(jnp.int32))
+    more = jnp.max(eight[:, 5 : 3 * slots : 3]) > 0
     own = of_slabs(own)
     after, own = lax.optimization_barrier((after, own))
     own = cut_windows(facts, own, 8, slots, width)
     after = to_slabs(jnp.broadcast_to(after, (slabs, *after.shape)))
     after, own = lax.optimization_barrier((after, own))
-    windows = to_eight(cut_rest(facts, after, own, 1))
+    windows = live_to_eight(cut_rest(facts, after, own, 1), 2)
 
     own, after = patch_gradients(slot_rows, count, windows, probe_wave, patterns, tables)
-    after, own = lax.optimization_barrier((to_eight(after), own))
+    after, own = lax.optimization_barrier((live_to_eight(after, 1), own))
     own = to_eight(own)
     spill = mirrored(over_slabs(*place_windows(facts, after, slabs, columns)).astype(bf16), 1)
     own = to_slabs(place_windows(facts, own, slabs, columns, together=True)[0])

time: 179 us -> 169 us (0.944)
  the two profiles are of different devices: /device:TPU:27 before, /device:TPU:1 now
where the time goes in v12:
time: 169 us; the launch traced here: 168 us
  blocking collectives  59.2 us (35%)
  starting transfers between devices  47.2 us (28%)
  waiting for transfers between devices  39.6 us (23%)
  Pallas kernels  15.3 us (9%)
  local copies, waits for them, and re-layouts  3.27 us (2%)
  between operations  2.18 us (1%)
    all_to_all x2, blocking collectives, to_eight(): lax.all_to_all(value, 'angle', 0, 0, axis_index_groups=eight_groups, tile...  41.6 us
    ppermute x6, starting transfers between devices, to_slab(): lax.ppermute(value, 'slab', [(i, (i + by) % slabs) for i in range(slabs)])  18.6 us
    all_to_all x1, blocking collectives, to_four(): lax.all_to_all(value, 'angle', 0, 0, axis_index_groups=four_groups, tiled...  17.7 us
    ppermute x2, waiting for transfers between devices, swap(): return lax.ppermute(value, 'angle', [(i, i ^ by) for i in range(angles)])  14.7 us
    all_to_all x2, waiting for transfers between devices, to_slabs(): return lax.all_to_all(value, 'slab', 0, 0, tiled=True)  14 us
    pallas_call x7, Pallas kernels, call(): pl.pallas_call(body, out_shape=out_shape, in_specs=[smem if x.dtype == jn...  13.2 us
    all_to_all x2, starting transfers between devices, to_eight(): lax.all_to_all(value, 'angle', 0, 0, axis_index_groups=eight_groups, tile...  11.9 us
    all_to_all x2, starting transfers between devices, to_slabs(): return lax.all_to_all(value, 'slab', 0, 0, tiled=True)  8.59 us
  transfers between devices with their start and end apart: 14, of which 8 were waited for; matrix products, arithmetic and copies ran while one was open for 1% of the time, Pallas kernels for 5%

profile of v12, /device:TPU:1, one launch (start us, length us, event | category | flops | bytes accessed | tf_op | source)
XLA Modules:
  0.0 167.8 jit_solution(8831271323387913909)
XLA Ops:
  1.1 1.3 collective-permute-start
  2.4 5.2 %collective-permute-start.3 = (bf16[48,1536]{1,0:T(8,128)(2,1)S(1)}, bf16[48,1536]{1,0:T(8,128)(2,1)S(1)}, u32[]{:S(2)}, u32[]{:S(2)}) collective-permute-start(bf16[48,1536]{1,0:T(8,128)(2,1)S(1)} %get-tuple-element.31.refs_0_), channel_id=1, source_target_pairs={{0,24},{8,0},{16,8},{24,16},{1,25},{9,1},{17,9},{25,17},{2,26},{10... | collective-permute-start | bytes 442376 | tf_op jit(solution)/shard_map/ppermute | solution.py:308
  7.6 2.4 %collective-permute-start.2 = (bf16[48,1536]{1,0:T(8,128)(2,1)S(1)}, bf16[48,1536]{1,0:T(8,128)(2,1)S(1)}, u32[]{:S(2)}, u32[]{:S(2)}) collective-permute-start(bf16[48,1536]{1,0:T(8,128)(2,1)S(1)} %get-tuple-element.31.refs_0_), channel_id=1, source_target_pairs={{0,16},{8,24},{16,0},{24,8},{1,17},{9,25},{17,1},{25,9},{2,18},{10... | collective-permute-start | bytes 442376 | tf_op jit(solution)/shard_map/ppermute | solution.py:308
  10.0 2.5 %collective-permute-start.1 = (bf16[48,1536]{1,0:T(8,128)(2,1)S(1)}, bf16[48,1536]{1,0:T(8,128)(2,1)S(1)}, u32[]{:S(2)}, u32[]{:S(2)}) collective-permute-start(bf16[48,1536]{1,0:T(8,128)(2,1)S(1)} %get-tuple-element.31.refs_0_), channel_id=1, source_target_pairs={{0,8},{8,16},{16,24},{24,0},{1,9},{9,17},{17,25},{25,1},{2,10},{10... | collective-permute-start | bytes 442376 | tf_op jit(solution)/shard_map/ppermute | solution.py:308
  15.2 1.1 shard_map.91
  16.3 7.7 %all-to-all-start.4 = ((s32[8,1,128]{2,1,0:T(1,128)}), s32[8,1,128]{2,1,0:T(1,128)S(1)}, u32[]{:S(2)}, u32[]{:S(2)}) async-start(s32[8,1,128]{2,1,0:T(1,128)} %bitcast.6), calls=%async_computation.4 | async-start | bytes 8192 | tf_op jit(solution)/shard_map/all_to_all | solution.py:311
  24.0 2.4 %collective-permute-done = bf16[48,1536]{1,0:T(8,128)(2,1)S(1)} collective-permute-done((bf16[48,1536]{1,0:T(8,128)(2,1)S(1)}, bf16[48,1536]{1,0:T(8,128)(2,1)S(1)}, u32[]{:S(2)}, u32[]{:S(2)}) %collective-permute-start) | collective-permute-done | bytes 147488 | tf_op jit(solution)/shard_map/ppermute | solution.py:305
  26.4 2.4 %all-to-all-done.4 = s32[8,1,128]{2,1,0:T(1,128)S(1)} async-done(((s32[8,1,128]{2,1,0:T(1,128)}), s32[8,1,128]{2,1,0:T(1,128)S(1)}, u32[]{:S(2)}, u32[]{:S(2)}) %all-to-all-start.4) | async-done | bytes 4128 | tf_op jit(solution)/shard_map/all_to_all | solution.py:311
  29.7 5.1 %all-to-all-start.5 = ((bf16[4,48,1536]{2,1,0:T(8,128)(2,1)}), bf16[4,48,1536]{2,1,0:T(8,128)(2,1)S(1)}, u32[]{:S(2)}, u32[]{:S(2)}) async-start(bf16[4,48,1536]{2,1,0:T(8,128)(2,1)} %broadcast_in_dim.3), calls=%async_computation.5 | async-start | bytes 1179648 | tf_op jit(solution)/shard_map/all_to_all | solution.py:317
  36.1 1.8 %shard_map.92.done = bf16[8,2,48,256]{3,2,1,0:T(8,128)(2,1)S(1)} custom-call(s32[8,128]{1,0:T(8,128)S(1)} %bitcast.28, s32[1]{0:T(128)} %bitcast.8.slab_ref, bf16[48,1536]{1,0:T(8,128)(2,1)S(1)} %get-tuple-element.31.refs_0_, bf16[48,1536]{1,0:T(8,128)(2,1)S(1)} %collective-permute-done.1.refs_1_, bf16[48,1536]{1,0:T(8,128)(2,1)S(1)} %collective-permute-done.2.refs_2_, ...), custom_call_target="tpu_custom_call" | custom-call | tf_op jit(solution)/shard_map/pallas_call | solution.py:45
  38.0 6.1 %all-to-all-done.5.blocks = bf16[4,48,1536]{2,1,0:T(8,128)(2,1)S(1)} async-done(((bf16[4,48,1536]{2,1,0:T(8,128)(2,1)}), bf16[4,48,1536]{2,1,0:T(8,128)(2,1)S(1)}, u32[]{:S(2)}, u32[]{:S(2)}) %all-to-all-start.5) | async-done | bytes 589856 | tf_op jit(solution)/shard_map/all_to_all | solution.py:317
  44.0 1.8 %shard_map.93 = bf16[8,2,2,48,256]{4,3,2,1,0:T(8,128)(2,1)S(1)} custom-call(s32[8,128]{1,0:T(8,128)S(1)} %bitcast.29, s32[1]{0:T(128)} %bitcast.8.slab_ref, bf16[4,48,1536]{2,1,0:T(8,128)(2,1)S(1)} %all-to-all-done.5.blocks, bf16[8,2,48,256]{3,2,1,0:T(8,128)(2,1)S(1)} %shard_map.92.done), custom_call_target="tpu_custom_call" | custom-call | tf_op jit(solution)/shard_map/pallas_call | solution.py:45
  45.9 24.4 %conditional.2 = (bf16[8,2,2,48,256]{4,3,2,1,0:T(8,128)(2,1)S(1)}) conditional(s32[]{:T(128)} %convert_element_type.25, bf16[8,2,2,48,256]{4,3,2,1,0:T(8,128)(2,1)S(1)} %shard_map.93, bf16[8,2,2,48,256]{4,3,2,1,0:T(8,128)(2,1)S(1)} %shard_map.93), branch_computations={%region_1.2_spmd, %region_2.3_spmd} | conditional | flops 393216 | bytes 3932168 | solution.py:330
  45.9 24.4 %all_to_all.48 = bf16[8,2,2,48,256]{4,3,2,1,0:T(8,128)(2,1)S(1)} all-to-all(bf16[8,2,2,48,256]{4,3,2,1,0:T(8,128)(2,1)S(1)} %param.1), channel_id=1, replica_groups={{0,32,64,96,128,160,192,224},{256,288,320,352,384,416,448,480},{1,33,65..., dimensions={0} | all-to-all | bytes 1572864 | tf_op jit(solution)/shard_map/cond/branch_1_fun/all_to_all | solution.py:311
  70.3 3.4 %shard_map.94 = (bf16[8,2,48,256]{3,2,1,0:T(8,128)(2,1)}, bf16[8,2,48,256]{3,2,1,0:T(8,128)(2,1)S(1)}) custom-call(s32[2]{0:T(128)S(1)} %bitcast.33, s32[1]{0:T(128)} %bitcast.21.count_ref, bf16[8,2,2,48,256]{4,3,2,1,0:T(8,128)(2,1)S(1)} %get-tuple-element.51.windows, f32[2,256,256]{2,1,0:T(8,128)S(1)} %copy-done.1, bf16[2,256,256]{2,1,0:T(8,128)(2,1)S(1)} %bitcast.26, ...), custom_call_target="tpu_custom_call" | custom-call | tf_op jit(solution)/shard_map/pallas_call | solution.py:45
  73.7 17.2 %conditional.3 = (bf16[8,2,48,256]{3,2,1,0:T(8,128)(2,1)S(1)}) conditional(s32[]{:T(128)} %convert_element_type.25, bf16[8,2,48,256]{3,2,1,0:T(8,128)(2,1)S(1)} %get-tuple-element.37, bf16[8,2,48,256]{3,2,1,0:T(8,128)(2,1)S(1)} %get-tuple-element.37), branch_computations={%region_3.4_spmd, %region_4.5_spmd} | conditional | flops 196608 | bytes 1966088 | solution.py:330
  73.7 17.2 %all_to_all.50 = bf16[8,2,48,256]{3,2,1,0:T(8,128)(2,1)S(1)} all-to-all(bf16[8,2,48,256]{3,2,1,0:T(8,128)(2,1)S(1)} %param.3), channel_id=1, replica_groups={{0,32,64,96,128,160,192,224},{256,288,320,352,384,416,448,480},{1,33,65..., dimensions={0} | all-to-all | bytes 786432 | tf_op jit(solution)/shard_map/cond/branch_1_fun/all_to_all | solution.py:311
  91.0 4.2 %all-to-all-start.6 = ((bf16[8,2,48,256]{3,2,1,0:T(8,128)(2,1)}), bf16[8,2,48,256]{3,2,1,0:T(8,128)(2,1)S(1)}, u32[]{:S(2)}, u32[]{:S(2)}) async-start(bf16[8,2,48,256]{3,2,1,0:T(8,128)(2,1)} %get-tuple-element.39), calls=%async_computation.6 | async-start | bytes 786432 | tf_op jit(solution)/shard_map/all_to_all | solution.py:311
  95.2 2.1 %shard_map.96 = (f32[48,1536]{1,0:T(8,128)S(1)}, bf16[48,1536]{1,0:T(8,128)(2,1)S(1)}, bf16[48,1536]{1,0:T(8,128)(2,1)S(1)}, bf16[48,1536]{1,0:T(8,128)(2,1)S(1)}) custom-call(s32[8,128]{1,0:T(8,128)S(1)} %bitcast.30, s32[1]{0:T(128)} %bitcast.8.slab_ref, bf16[8,2,48,256]{3,2,1,0:T(8,128)(2,1)S(1)} %get-tuple-element.52.windows), custom_call_target="tpu_custom_call" | custom-call | tf_op jit(solution)/shard_map/pallas_call | solution.py:45
  97.3 1.9 %collective-permute-start.4 = (bf16[48,1536]{1,0:T(8,128)(2,1)S(1)}, bf16[48,1536]{1,0:T(8,128)(2,1)S(1)}, u32[]{:S(2)}, u32[]{:S(2)}) collective-permute-start(bf16[48,1536]{1,0:T(8,128)(2,1)S(1)} %get-tuple-element.42), channel_id=1, source_target_pairs={{0,8},{8,16},{16,24},{24,0},{1,9},{9,17},{17,25},{25,1},{2,10},{10... | collective-permute-start | bytes 442376 | tf_op jit(solution)/shard_map/ppermute | solution.py:308
  99.2 1.9 %collective-permute-start.5 = (bf16[48,1536]{1,0:T(8,128)(2,1)S(1)}, bf16[48,1536]{1,0:T(8,128)(2,1)S(1)}, u32[]{:S(2)}, u32[]{:S(2)}) collective-permute-start(bf16[48,1536]{1,0:T(8,128)(2,1)S(1)} %get-tuple-element.43), channel_id=1, source_target_pairs={{0,16},{8,24},{16,0},{24,8},{1,17},{9,25},{17,1},{25,9},{2,18},{10... | collective-permute-start | bytes 442376 | tf_op jit(solution)/shard_map/ppermute | solution.py:308
  101.1 4.6 %collective-permute-start.6 = (bf16[48,1536]{1,0:T(8,128)(2,1)S(1)}, bf16[48,1536]{1,0:T(8,128)(2,1)S(1)}, u32[]{:S(2)}, u32[]{:S(2)}) collective-permute-start(bf16[48,1536]{1,0:T(8,128)(2,1)S(1)} %get-tuple-element.44), channel_id=1, source_target_pairs={{0,24},{8,0},{16,8},{24,16},{1,25},{9,1},{17,9},{25,17},{2,26},{10... | collective-permute-start | bytes 442376 | tf_op jit(solution)/shard_map/ppermute | solution.py:308
  105.7 1.1 all-to-all-done.6.windows
  106.9 2.9 %shard_map.95 = bf16[4,48,1536]{2,1,0:T(8,128)(2,1)} custom-call(s32[8,128]{1,0:T(8,128)S(1)} %bitcast.31, s32[1]{0:T(128)} %bitcast.8.slab_ref, bf16[8,2,48,256]{3,2,1,0:T(8,128)(2,1)S(1)} %all-to-all-done.6.windows), custom_call_target="tpu_custom_call" | custom-call | tf_op jit(solution)/shard_map/pallas_call | solution.py:45
  109.8 3.5 %all-to-all-start.7 = ((bf16[4,48,1536]{2,1,0:T(8,128)(2,1)}), bf16[4,48,1536]{2,1,0:T(8,128)(2,1)S(1)}, u32[]{:S(2)}, u32[]{:S(2)}) async-start(bf16[4,48,1536]{2,1,0:T(8,128)(2,1)} %shard_map.95), calls=%async_computation.7 | async-start | bytes 1179648 | tf_op jit(solution)/shard_map/all_to_all | solution.py:317
  113.4 1.3 collective-permute-start.7
  114.7 7.9 %all-to-all-done.7 = bf16[4,48,1536]{2,1,0:T(8,128)(2,1)S(1)} async-done(((bf16[4,48,1536]{2,1,0:T(8,128)(2,1)}), bf16[4,48,1536]{2,1,0:T(8,128)(2,1)S(1)}, u32[]{:S(2)}, u32[]{:S(2)}) %all-to-all-start.7) | async-done | bytes 589856 | tf_op jit(solution)/shard_map/all_to_all | solution.py:317
  122.7 5.0 %collective-permute-done.7 = bf16[48,1536]{1,0:T(8,128)(2,1)S(1)} collective-permute-done((bf16[48,1536]{1,0:T(8,128)(2,1)S(1)}, bf16[48,1536]{1,0:T(8,128)(2,1)S(1)}, u32[]{:S(2)}, u32[]{:S(2)}) %collective-permute-start.7) | collective-permute-done | bytes 147488 | tf_op jit(solution)/shard_map/ppermute | solution.py:305
  127.7 2.1 %collective-permute-start.8 = (bf16[48,1536]{1,0:T(8,128)(2,1)S(1)}, bf16[48,1536]{1,0:T(8,128)(2,1)S(1)}, u32[]{:S(2)}, u32[]{:S(2)}) collective-permute-start(bf16[48,1536]{1,0:T(8,128)(2,1)S(1)} %add_convert_fusion.refs_0_), channel_id=1, source_target_pairs={{0,256},{32,288},{64,320},{96,352},{128,384},{160,416},{192,448},{... | collective-permute-start | bytes 442376 | tf_op jit(solution)/shard_map/ppermute | solution.py:296
  129.8 14.1 %collective-permute-done.8.refs_1_ = bf16[48,1536]{1,0:T(8,128)(2,1)S(1)} collective-permute-done((bf16[48,1536]{1,0:T(8,128)(2,1)S(1)}, bf16[48,1536]{1,0:T(8,128)(2,1)S(1)}, u32[]{:S(2)}, u32[]{:S(2)}) %collective-permute-start.8) | collective-permute-done | bytes 147488 | tf_op jit(solution)/shard_map/ppermute | solution.py:296
  143.9 17.7 %all_to_all.51 = bf16[4,48,1536]{2,1,0:T(8,128)(2,1)S(1)} all-to-all(bf16[4,48,1536]{2,1,0:T(8,128)(2,1)S(1)} %shard_map.97), channel_id=1, replica_groups={{0,64,128,192},{32,96,160,224},{256,320,384,448},{288,352,416,480},{1,6..., dimensions={0} | all-to-all | bytes 1179648 | tf_op jit(solution)/shard_map/all_to_all | solution.py:314
  161.6 3.5 %collective-permute-start.9 = (bf16[192,1536]{1,0:T(8,128)(2,1)S(1)}, bf16[192,1536]{1,0:T(8,128)(2,1)S(1)}, u32[]{:S(2)}, u32[]{:S(2)}) collective-permute-start(bf16[192,1536]{1,0:T(8,128)(2,1)S(1)} %bitcast.24), channel_id=1, source_target_pairs={{0,32},{32,0},{64,96},{96,64},{128,160},{160,128},{192,224},{224,1... | collective-permute-start | bytes 1769480 | tf_op jit(solution)/shard_map/ppermute | solution.py:296
  (32 shorter events, 6.9 us)
Async XLA Ops:
  1.1 25.3 %collective-permute-start = (bf16[48,1536]{1,0:T(8,128)(2,1)S(1)}, bf16[48,1536]{1,0:T(8,128)(2,1)S(1)}, u32[]{:S(2)}, u32[]{:S(2)}) collective-permute-start(bf16[48,1536]{1,0:T(8,128)(2,1)S(1)} %get-tuple-element.50), channel_id=1, source_target_pairs={{1,448},{2,449},{3,450},{4,451},{5,452},{6,453},{7,454},{33,480},{... | collective-permute-start | bytes 442376 | tf_op jit(solution)/shard_map/ppermute | solution.py:305
  2.4 24.0 %collective-permute-start.3 = (bf16[48,1536]{1,0:T(8,128)(2,1)S(1)}, bf16[48,1536]{1,0:T(8,128)(2,1)S(1)}, u32[]{:S(2)}, u32[]{:S(2)}) collective-permute-start(bf16[48,1536]{1,0:T(8,128)(2,1)S(1)} %get-tuple-element.31.refs_0_), channel_id=1, source_target_pairs={{0,24},{8,0},{16,8},{24,16},{1,25},{9,1},{17,9},{25,17},{2,26},{10... | collective-permute-start | bytes 442376 | tf_op jit(solution)/shard_map/ppermute | solution.py:308
  7.6 18.8 %collective-permute-start.2 = (bf16[48,1536]{1,0:T(8,128)(2,1)S(1)}, bf16[48,1536]{1,0:T(8,128)(2,1)S(1)}, u32[]{:S(2)}, u32[]{:S(2)}) collective-permute-start(bf16[48,1536]{1,0:T(8,128)(2,1)S(1)} %get-tuple-element.31.refs_0_), channel_id=1, source_target_pairs={{0,16},{8,24},{16,0},{24,8},{1,17},{9,25},{17,1},{25,9},{2,18},{10... | collective-permute-start | bytes 442376 | tf_op jit(solution)/shard_map/ppermute | solution.py:308
  10.0 16.3 %collective-permute-start.1 = (bf16[48,1536]{1,0:T(8,128)(2,1)S(1)}, bf16[48,1536]{1,0:T(8,128)(2,1)S(1)}, u32[]{:S(2)}, u32[]{:S(2)}) collective-permute-start(bf16[48,1536]{1,0:T(8,128)(2,1)S(1)} %get-tuple-element.31.refs_0_), channel_id=1, source_target_pairs={{0,8},{8,16},{16,24},{24,0},{1,9},{9,17},{17,25},{25,1},{2,10},{10... | collective-permute-start | bytes 442376 | tf_op jit(solution)/shard_map/ppermute | solution.py:308
  13.8 0.7 copy-start.5
  14.5 0.7 copy-start.7
  16.3 12.5 %all-to-all-start.4 = ((s32[8,1,128]{2,1,0:T(1,128)}), s32[8,1,128]{2,1,0:T(1,128)S(1)}, u32[]{:S(2)}, u32[]{:S(2)}) async-start(s32[8,1,128]{2,1,0:T(1,128)} %bitcast.6), calls=%async_computation.4 | async-start | bytes 8192 | tf_op jit(solution)/shard_map/all_to_all | solution.py:311
  29.7 14.3 %all-to-all-start.5 = ((bf16[4,48,1536]{2,1,0:T(8,128)(2,1)}), bf16[4,48,1536]{2,1,0:T(8,128)(2,1)S(1)}, u32[]{:S(2)}, u32[]{:S(2)}) async-start(bf16[4,48,1536]{2,1,0:T(8,128)(2,1)} %broadcast_in_dim.3), calls=%async_computation.5 | async-start | bytes 1179648 | tf_op jit(solution)/shard_map/all_to_all | solution.py:317
  45.8 24.5 %copy-start.1 = (f32[2,256,256]{2,1,0:T(8,128)S(1)}, f32[2,256,256]{2,1,0:T(8,128)}, u32[]{:S(2)}) copy-start(f32[2,256,256]{2,1,0:T(8,128)} %probe.1) | copy-start | bytes 1572868
  45.9 24.5 %copy-start.2 = (bf16[1,1,1,2,256,256]{5,4,3,2,1,0:T(8,128)(2,1)S(1)}, bf16[1,1,1,2,256,256]{5,4,3,2,1,0:T(8,128)(2,1)}, u32[]{:S(2)}) copy-start(bf16[1,1,1,2,256,256]{5,4,3,2,1,0:T(8,128)(2,1)} %param.15) | copy-start | bytes 786436
  45.9 24.4 %copy-start.3 = (bf16[256,256]{1,0:T(8,128)(2,1)S(1)}, bf16[256,256]{1,0:T(8,128)(2,1)}, u32[]{:S(2)}) copy-start(bf16[256,256]{1,0:T(8,128)(2,1)} %constant.107.clone.wi_ref) | copy-start | bytes 393220
  45.9 24.4 %copy-start.4 = (bf16[256,256]{1,0:T(8,128)(2,1)S(1)}, bf16[256,256]{1,0:T(8,128)(2,1)}, u32[]{:S(2)}) copy-start(bf16[256,256]{1,0:T(8,128)(2,1)} %constant.106.clone.wr_ref) | copy-start | bytes 393220
  45.9 24.4 %copy-start.6 = (s32[1,1,1,2]{3,2,1,0:T(1,128)S(1)}, s32[1,1,1,2]{3,2,1,0:T(1,128)}, u32[]{:S(2)}) copy-start(s32[1,1,1,2]{3,2,1,0:T(1,128)} %param.16) | copy-start | bytes 28
  91.0 15.9 %all-to-all-start.6 = ((bf16[8,2,48,256]{3,2,1,0:T(8,128)(2,1)}), bf16[8,2,48,256]{3,2,1,0:T(8,128)(2,1)S(1)}, u32[]{:S(2)}, u32[]{:S(2)}) async-start(bf16[8,2,48,256]{3,2,1,0:T(8,128)(2,1)} %get-tuple-element.39), calls=%async_computation.6 | async-start | bytes 786432 | tf_op jit(solution)/shard_map/all_to_all | solution.py:311
  97.3 16.0 %collective-permute-start.4 = (bf16[48,1536]{1,0:T(8,128)(2,1)S(1)}, bf16[48,1536]{1,0:T(8,128)(2,1)S(1)}, u32[]{:S(2)}, u32[]{:S(2)}) collective-permute-start(bf16[48,1536]{1,0:T(8,128)(2,1)S(1)} %get-tuple-element.42), channel_id=1, source_target_pairs={{0,8},{8,16},{16,24},{24,0},{1,9},{9,17},{17,25},{25,1},{2,10},{10... | collective-permute-start | bytes 442376 | tf_op jit(solution)/shard_map/ppermute | solution.py:308
  99.2 14.1 %collective-permute-start.5 = (bf16[48,1536]{1,0:T(8,128)(2,1)S(1)}, bf16[48,1536]{1,0:T(8,128)(2,1)S(1)}, u32[]{:S(2)}, u32[]{:S(2)}) collective-permute-start(bf16[48,1536]{1,0:T(8,128)(2,1)S(1)} %get-tuple-element.43), channel_id=1, source_target_pairs={{0,16},{8,24},{16,0},{24,8},{1,17},{9,25},{17,1},{25,9},{2,18},{10... | collective-permute-start | bytes 442376 | tf_op jit(solution)/shard_map/ppermute | solution.py:308
  101.1 12.1 %collective-permute-start.6 = (bf16[48,1536]{1,0:T(8,128)(2,1)S(1)}, bf16[48,1536]{1,0:T(8,128)(2,1)S(1)}, u32[]{:S(2)}, u32[]{:S(2)}) collective-permute-start(bf16[48,1536]{1,0:T(8,128)(2,1)S(1)} %get-tuple-element.44), channel_id=1, source_target_pairs={{0,24},{8,0},{16,8},{24,16},{1,25},{9,1},{17,9},{25,17},{2,26},{10... | collective-permute-start | bytes 442376 | tf_op jit(solution)/shard_map/ppermute | solution.py:308
  109.8 12.8 %all-to-all-start.7 = ((bf16[4,48,1536]{2,1,0:T(8,128)(2,1)}), bf16[4,48,1536]{2,1,0:T(8,128)(2,1)S(1)}, u32[]{:S(2)}, u32[]{:S(2)}) async-start(bf16[4,48,1536]{2,1,0:T(8,128)(2,1)} %shard_map.95), calls=%async_computation.7 | async-start | bytes 1179648 | tf_op jit(solution)/shard_map/all_to_all | solution.py:317
  113.4 14.3 %collective-permute-start.7 = (bf16[48,1536]{1,0:T(8,128)(2,1)S(1)}, bf16[48,1536]{1,0:T(8,128)(2,1)S(1)}, u32[]{:S(2)}, u32[]{:S(2)}) collective-permute-start(bf16[48,1536]{1,0:T(8,128)(2,1)S(1)} %add_convert_fusion.1), channel_id=1, source_target_pairs={{0,449},{1,450},{2,451},{3,452},{4,453},{5,454},{6,455},{32,481},{... | collective-permute-start | bytes 442376 | tf_op jit(solution)/shard_map/ppermute | solution.py:305
  127.7 37.4 %copy-start = (bf16[2,1,192,1536]{3,2,1,0:T(8,128)(2,1)S(1)}, bf16[2,1,192,1536]{3,2,1,0:T(8,128)(2,1)}, u32[]{:S(2)}) copy-start(bf16[2,1,192,1536]{3,2,1,0:T(8,128)(2,1)} %param.13) | copy-start | bytes 3538948
  127.7 16.2 %collective-permute-start.8 = (bf16[48,1536]{1,0:T(8,128)(2,1)S(1)}, bf16[48,1536]{1,0:T(8,128)(2,1)S(1)}, u32[]{:S(2)}, u32[]{:S(2)}) collective-permute-start(bf16[48,1536]{1,0:T(8,128)(2,1)S(1)} %add_convert_fusion.refs_0_), channel_id=1, source_target_pairs={{0,256},{32,288},{64,320},{96,352},{128,384},{160,416},{192,448},{... | collective-permute-start | bytes 442376 | tf_op jit(solution)/shard_map/ppermute | solution.py:296
  161.6 5.1 %collective-permute-start.9 = (bf16[192,1536]{1,0:T(8,128)(2,1)S(1)}, bf16[192,1536]{1,0:T(8,128)(2,1)S(1)}, u32[]{:S(2)}, u32[]{:S(2)}) collective-permute-start(bf16[192,1536]{1,0:T(8,128)(2,1)S(1)} %bitcast.24), channel_id=1, source_target_pairs={{0,32},{32,0},{64,96},{96,64},{128,160},{160,128},{192,224},{224,1... | collective-permute-start | bytes 1769480 | tf_op jit(solution)/shard_map/ppermute | solution.py:296

commit v13 on v12

--- a/solution.py
+++ b/solution.py
@@ -216,22 +216,19 @@
             def _():
                 window = windows[angle, slot].astype(jnp.float32)
                 for k in range(slabs):
-                    layer = facts.layer(k) if len(outs) > 1 else k
-                    starts, inside = facts.columns_of(angle, slot, layer)
+                    starts, inside = facts.columns_of(angle, slot, facts.layer(k))
                     first, second = (pltpu.roll(window[:, i * LANE : (i + 1) * LANE], inside, 1) for i in range(2))
                     there = lane < inside
                     total[k, :, pl.ds(starts[0], LANE)] += jnp.where(there, 0.0, first)
                     total[k, :, pl.ds(starts[1], LANE)] += jnp.where(there, first, second)
                     total[k, :, pl.ds(starts[2], LANE)] += jnp.where(there, second, 0.0)
     for k, out in enumerate(outs):
-        out[...] = (total[k] if len(outs) > 1 else total[...]).astype(out.dtype)
-
-
-def place_windows(facts, windows, slabs, columns, together=False):
+        out[...] = total[k].astype(out.dtype)
+
+
+def place_windows(facts, windows, slabs, columns):
     shape = (windows.shape[2], columns)
     outs = [jax.ShapeDtypeStruct(shape, jnp.bfloat16 if k else jnp.float32) for k in range(slabs)]
-    if together:
-        outs = [jax.ShapeDtypeStruct((slabs, *shape), jnp.bfloat16)]
     return call(place_body, outs, [pltpu.VMEM((slabs, *shape), jnp.float32)], *facts, windows)
 
 
@@ -354,8 +351,7 @@
     after, own = lax.optimization_barrier((live_to_eight(after, 1), own))
     own = to_eight(own)
     spill = mirrored(over_slabs(*place_windows(facts, after, slabs, columns)).astype(bf16), 1)
-    own = to_slabs(place_windows(facts, own, slabs, columns, together=True)[0])
-    own = jnp.sum(own.astype(f32), axis=0)
+    own = over_slabs(*place_windows(facts, own, slabs, columns))
 
     total = lax.optimization_barrier((own + spill.astype(f32)).astype(bf16))
     total = to_four(sum_copies([total, swap(total, 8)], 4)).reshape(tile_rows, columns)

time: 169 us -> 173 us (1.024)
  starting transfers between devices: 47.2 us -> 53.7 us
    ppermute x6 -> x9, starting transfers between devices: 18.6 us -> 28.5 us  [to_slab(): lax.ppermute(value, 'slab', [(i, (i + by) % slabs) for i in range(slabs)])]
    ppermute x6 -> x9, waiting for transfers between devices: 0.02 us -> 9.26 us  [to_slab(): lax.ppermute(value, 'slab', [(i, (i + by) % slabs) for i in range(slabs)])]
    all_to_all x2 -> x1, waiting for transfers between devices: 14 us -> 6.16 us  [to_slabs(): return lax.all_to_all(value, 'slab', 0, 0, tiled=True)]
    ppermute x2, waiting for transfers between devices: 7.34 us -> 2.36 us  [mirrored(): return lax.ppermute(value, ('angle', 'tile'), pairs)]
    ppermute x2, waiting for transfers between devices: 14.7 us -> 18.7 us  [swap(): return lax.ppermute(value, 'angle', [(i, i ^ by) for i in range(angles)])]
    all_to_all x2 -> x1, starting transfers between devices: 8.59 us -> 5.11 us  [to_slabs(): return lax.all_to_all(value, 'slab', 0, 0, tiled=True)]
  transfers between devices with their start and end apart: 14 -> 16, of which waited for: 8 -> 9; matrix products, arithmetic and copies ran while one was open for 1% -> 0% of each run, Pallas kernels for 5% -> 5%
where the time goes in v13:
time: 173 us
  blocking collectives  59.1 us (34%)
  starting transfers between devices  53.7 us (31%)
  waiting for transfers between devices  38.9 us (22%)
  Pallas kernels  14.6 us (8%)
  local copies, waits for them, and re-layouts  3.27 us (2%)
  between operations  2.13 us (1%)
    all_to_all x2, blocking collectives, to_eight(): lax.all_to_all(value, 'angle', 0, 0, axis_index_groups=eight_groups, tile...  41.6 us
    ppermute x9, starting transfers between devices, to_slab(): lax.ppermute(value, 'slab', [(i, (i + by) % slabs) for i in range(slabs)])  28.5 us
    ppermute x2, waiting for transfers between devices, swap(): return lax.ppermute(value, 'angle', [(i, i ^ by) for i in range(angles)])  18.7 us
    all_to_all x1, blocking collectives, to_four(): lax.all_to_all(value, 'angle', 0, 0, axis_index_groups=four_groups, tiled...  17.5 us
    pallas_call x7, Pallas kernels, call(): pl.pallas_call(body, out_shape=out_shape, in_specs=[smem if x.dtype == jn...  12.4 us
    all_to_all x2, starting transfers between devices, to_eight(): lax.all_to_all(value, 'angle', 0, 0, axis_index_groups=eight_groups, tile...  11.9 us
    ppermute x9, waiting for transfers between devices, to_slab(): lax.ppermute(value, 'slab', [(i, (i + by) % slabs) for i in range(slabs)])  9.26 us
    all_to_all x1, waiting for transfers between devices, to_slabs(): return lax.all_to_all(value, 'slab', 0, 0, tiled=True)  6.16 us
  transfers between devices with their start and end apart: 16, of which 9 were waited for; matrix products, arithmetic and copies ran while one was open for 0% of the time, Pallas kernels for 5%

profile of v13, /device:TPU:1, one launch (start us, length us, event | category | flops | bytes accessed | tf_op | source)
XLA Modules:
  0.0 172.5 jit_solution(16888859641255674997)
XLA Ops:
  2.4 5.2 %collective-permute-start.3 = (bf16[48,1536]{1,0:T(8,128)(2,1)S(1)}, bf16[48,1536]{1,0:T(8,128)(2,1)S(1)}, u32[]{:S(2)}, u32[]{:S(2)}) collective-permute-start(bf16[48,1536]{1,0:T(8,128)(2,1)S(1)} %get-tuple-element.35.refs_0_), channel_id=1, source_target_pairs={{0,24},{8,0},{16,8},{24,16},{1,25},{9,1},{17,9},{25,17},{2,26},{10... | collective-permute-start | bytes 442376 | tf_op jit(solution)/shard_map/ppermute | solution.py:305
  7.6 2.4 %collective-permute-start.2 = (bf16[48,1536]{1,0:T(8,128)(2,1)S(1)}, bf16[48,1536]{1,0:T(8,128)(2,1)S(1)}, u32[]{:S(2)}, u32[]{:S(2)}) collective-permute-start(bf16[48,1536]{1,0:T(8,128)(2,1)S(1)} %get-tuple-element.35.refs_0_), channel_id=1, source_target_pairs={{0,16},{8,24},{16,0},{24,8},{1,17},{9,25},{17,1},{25,9},{2,18},{10... | collective-permute-start | bytes 442376 | tf_op jit(solution)/shard_map/ppermute | solution.py:305
  10.0 2.5 %collective-permute-start.1 = (bf16[48,1536]{1,0:T(8,128)(2,1)S(1)}, bf16[48,1536]{1,0:T(8,128)(2,1)S(1)}, u32[]{:S(2)}, u32[]{:S(2)}) collective-permute-start(bf16[48,1536]{1,0:T(8,128)(2,1)S(1)} %get-tuple-element.35.refs_0_), channel_id=1, source_target_pairs={{0,8},{8,16},{16,24},{24,0},{1,9},{9,17},{17,25},{25,1},{2,10},{10... | collective-permute-start | bytes 442376 | tf_op jit(solution)/shard_map/ppermute | solution.py:305
  16.3 7.7 %all-to-all-start.4 = ((s32[8,1,128]{2,1,0:T(1,128)}), s32[8,1,128]{2,1,0:T(1,128)S(1)}, u32[]{:S(2)}, u32[]{:S(2)}) async-start(s32[8,1,128]{2,1,0:T(1,128)} %bitcast.6), calls=%async_computation.4 | async-start | bytes 8192 | tf_op jit(solution)/shard_map/all_to_all | solution.py:308
  24.0 2.4 %collective-permute-done = bf16[48,1536]{1,0:T(8,128)(2,1)S(1)} collective-permute-done((bf16[48,1536]{1,0:T(8,128)(2,1)S(1)}, bf16[48,1536]{1,0:T(8,128)(2,1)S(1)}, u32[]{:S(2)}, u32[]{:S(2)}) %collective-permute-start) | collective-permute-done | bytes 147488 | tf_op jit(solution)/shard_map/ppermute | solution.py:302
  26.4 2.4 %all-to-all-done.4 = s32[8,1,128]{2,1,0:T(1,128)S(1)} async-done(((s32[8,1,128]{2,1,0:T(1,128)}), s32[8,1,128]{2,1,0:T(1,128)S(1)}, u32[]{:S(2)}, u32[]{:S(2)}) %all-to-all-start.4) | async-done | bytes 4128 | tf_op jit(solution)/shard_map/all_to_all | solution.py:308
  29.7 5.1 %all-to-all-start.5 = ((bf16[4,48,1536]{2,1,0:T(8,128)(2,1)}), bf16[4,48,1536]{2,1,0:T(8,128)(2,1)S(1)}, u32[]{:S(2)}, u32[]{:S(2)}) async-start(bf16[4,48,1536]{2,1,0:T(8,128)(2,1)} %broadcast_in_dim.3), calls=%async_computation.5 | async-start | bytes 1179648 | tf_op jit(solution)/shard_map/all_to_all | solution.py:314
  36.0 1.8 %shard_map.92.done = bf16[8,2,48,256]{3,2,1,0:T(8,128)(2,1)S(1)} custom-call(s32[8,128]{1,0:T(8,128)S(1)} %bitcast.28, s32[1]{0:T(128)} %bitcast.8.slab_ref, bf16[48,1536]{1,0:T(8,128)(2,1)S(1)} %get-tuple-element.35.refs_0_, bf16[48,1536]{1,0:T(8,128)(2,1)S(1)} %collective-permute-done.1.refs_1_, bf16[48,1536]{1,0:T(8,128)(2,1)S(1)} %collective-permute-done.2.refs_2_, ...), custom_call_target="tpu_custom_call" | custom-call | tf_op jit(solution)/shard_map/pallas_call | solution.py:45
  37.9 6.2 %all-to-all-done.5.blocks = bf16[4,48,1536]{2,1,0:T(8,128)(2,1)S(1)} async-done(((bf16[4,48,1536]{2,1,0:T(8,128)(2,1)}), bf16[4,48,1536]{2,1,0:T(8,128)(2,1)S(1)}, u32[]{:S(2)}, u32[]{:S(2)}) %all-to-all-start.5) | async-done | bytes 589856 | tf_op jit(solution)/shard_map/all_to_all | solution.py:314
  44.0 1.8 %shard_map.93 = bf16[8,2,2,48,256]{4,3,2,1,0:T(8,128)(2,1)S(1)} custom-call(s32[8,128]{1,0:T(8,128)S(1)} %bitcast.29, s32[1]{0:T(128)} %bitcast.8.slab_ref, bf16[4,48,1536]{2,1,0:T(8,128)(2,1)S(1)} %all-to-all-done.5.blocks, bf16[8,2,48,256]{3,2,1,0:T(8,128)(2,1)S(1)} %shard_map.92.done), custom_call_target="tpu_custom_call" | custom-call | tf_op jit(solution)/shard_map/pallas_call | solution.py:45
  45.9 24.4 %conditional.2 = (bf16[8,2,2,48,256]{4,3,2,1,0:T(8,128)(2,1)S(1)}) conditional(s32[]{:T(128)} %convert_element_type.31, bf16[8,2,2,48,256]{4,3,2,1,0:T(8,128)(2,1)S(1)} %shard_map.93, bf16[8,2,2,48,256]{4,3,2,1,0:T(8,128)(2,1)S(1)} %shard_map.93), branch_computations={%region_1.2_spmd, %region_2.3_spmd} | conditional | flops 393216 | bytes 3932168 | solution.py:327
  45.9 24.4 %all_to_all.43 = bf16[8,2,2,48,256]{4,3,2,1,0:T(8,128)(2,1)S(1)} all-to-all(bf16[8,2,2,48,256]{4,3,2,1,0:T(8,128)(2,1)S(1)} %param.1), channel_id=1, replica_groups={{0,32,64,96,128,160,192,224},{256,288,320,352,384,416,448,480},{1,33,65..., dimensions={0} | all-to-all | bytes 1572864 | tf_op jit(solution)/shard_map/cond/branch_1_fun/all_to_all | solution.py:308
  70.3 3.4 %shard_map.94 = (bf16[8,2,48,256]{3,2,1,0:T(8,128)(2,1)}, bf16[8,2,48,256]{3,2,1,0:T(8,128)(2,1)S(1)}) custom-call(s32[2]{0:T(128)S(1)} %bitcast.33, s32[1]{0:T(128)} %bitcast.21.count_ref, bf16[8,2,2,48,256]{4,3,2,1,0:T(8,128)(2,1)S(1)} %get-tuple-element.59.windows, f32[2,256,256]{2,1,0:T(8,128)S(1)} %copy-done.1, bf16[2,256,256]{2,1,0:T(8,128)(2,1)S(1)} %bitcast.26, ...), custom_call_target="tpu_custom_call" | custom-call | tf_op jit(solution)/shard_map/pallas_call | solution.py:45
  73.7 17.2 %conditional.3 = (bf16[8,2,48,256]{3,2,1,0:T(8,128)(2,1)S(1)}) conditional(s32[]{:T(128)} %convert_element_type.31, bf16[8,2,48,256]{3,2,1,0:T(8,128)(2,1)S(1)} %get-tuple-element.41, bf16[8,2,48,256]{3,2,1,0:T(8,128)(2,1)S(1)} %get-tuple-element.41), branch_computations={%region_3.4_spmd, %region_4.5_spmd} | conditional | flops 196608 | bytes 1966088 | solution.py:327
  73.7 17.2 %all_to_all.45 = bf16[8,2,48,256]{3,2,1,0:T(8,128)(2,1)S(1)} all-to-all(bf16[8,2,48,256]{3,2,1,0:T(8,128)(2,1)S(1)} %param.3), channel_id=1, replica_groups={{0,32,64,96,128,160,192,224},{256,288,320,352,384,416,448,480},{1,33,65..., dimensions={0} | all-to-all | bytes 786432 | tf_op jit(solution)/shard_map/cond/branch_1_fun/all_to_all | solution.py:308
  91.0 4.2 %all-to-all-start.6 = ((bf16[8,2,48,256]{3,2,1,0:T(8,128)(2,1)}), bf16[8,2,48,256]{3,2,1,0:T(8,128)(2,1)S(1)}, u32[]{:S(2)}, u32[]{:S(2)}) async-start(bf16[8,2,48,256]{3,2,1,0:T(8,128)(2,1)} %get-tuple-element.43), calls=%async_computation.6 | async-start | bytes 786432 | tf_op jit(solution)/shard_map/all_to_all | solution.py:308
  95.2 2.1 %shard_map.96 = (f32[48,1536]{1,0:T(8,128)S(1)}, bf16[48,1536]{1,0:T(8,128)(2,1)S(1)}, bf16[48,1536]{1,0:T(8,128)(2,1)S(1)}, bf16[48,1536]{1,0:T(8,128)(2,1)S(1)}) custom-call(s32[8,128]{1,0:T(8,128)S(1)} %bitcast.30, s32[1]{0:T(128)} %bitcast.8.slab_ref, bf16[8,2,48,256]{3,2,1,0:T(8,128)(2,1)S(1)} %get-tuple-element.60.windows), custom_call_target="tpu_custom_call" | custom-call | tf_op jit(solution)/shard_map/pallas_call | solution.py:45
  97.3 1.9 %collective-permute-start.7 = (bf16[48,1536]{1,0:T(8,128)(2,1)S(1)}, bf16[48,1536]{1,0:T(8,128)(2,1)S(1)}, u32[]{:S(2)}, u32[]{:S(2)}) collective-permute-start(bf16[48,1536]{1,0:T(8,128)(2,1)S(1)} %get-tuple-element.50), channel_id=1, source_target_pairs={{0,8},{8,16},{16,24},{24,0},{1,9},{9,17},{17,25},{25,1},{2,10},{10... | collective-permute-start | bytes 442376 | tf_op jit(solution)/shard_map/ppermute | solution.py:305
  99.2 1.9 %collective-permute-start.8 = (bf16[48,1536]{1,0:T(8,128)(2,1)S(1)}, bf16[48,1536]{1,0:T(8,128)(2,1)S(1)}, u32[]{:S(2)}, u32[]{:S(2)}) collective-permute-start(bf16[48,1536]{1,0:T(8,128)(2,1)S(1)} %get-tuple-element.51), channel_id=1, source_target_pairs={{0,16},{8,24},{16,0},{24,8},{1,17},{9,25},{17,1},{25,9},{2,18},{10... | collective-permute-start | bytes 442376 | tf_op jit(solution)/shard_map/ppermute | solution.py:305
  101.1 4.6 %collective-permute-start.9 = (bf16[48,1536]{1,0:T(8,128)(2,1)S(1)}, bf16[48,1536]{1,0:T(8,128)(2,1)S(1)}, u32[]{:S(2)}, u32[]{:S(2)}) collective-permute-start(bf16[48,1536]{1,0:T(8,128)(2,1)S(1)} %get-tuple-element.52), channel_id=1, source_target_pairs={{0,24},{8,0},{16,8},{24,16},{1,25},{9,1},{17,9},{25,17},{2,26},{10... | collective-permute-start | bytes 442376 | tf_op jit(solution)/shard_map/ppermute | solution.py:305
  105.7 3.1 %collective-permute-done.7 = bf16[48,1536]{1,0:T(8,128)(2,1)S(1)} collective-permute-done((bf16[48,1536]{1,0:T(8,128)(2,1)S(1)}, bf16[48,1536]{1,0:T(8,128)(2,1)S(1)}, u32[]{:S(2)}, u32[]{:S(2)}) %collective-permute-start.7) | collective-permute-done | bytes 147488 | tf_op jit(solution)/shard_map/ppermute | solution.py:305
  108.9 2.2 %collective-permute-done.9 = bf16[48,1536]{1,0:T(8,128)(2,1)S(1)} collective-permute-done((bf16[48,1536]{1,0:T(8,128)(2,1)S(1)}, bf16[48,1536]{1,0:T(8,128)(2,1)S(1)}, u32[]{:S(2)}, u32[]{:S(2)}) %collective-permute-start.9) | collective-permute-done | bytes 147488 | tf_op jit(solution)/shard_map/ppermute | solution.py:305
  111.1 1.3 collective-permute-start.10
  112.4 2.1 %shard_map.95 = (f32[48,1536]{1,0:T(8,128)S(1)}, bf16[48,1536]{1,0:T(8,128)(2,1)S(1)}, bf16[48,1536]{1,0:T(8,128)(2,1)S(1)}, bf16[48,1536]{1,0:T(8,128)(2,1)S(1)}) custom-call(s32[8,128]{1,0:T(8,128)S(1)} %bitcast.31, s32[1]{0:T(128)} %bitcast.8.slab_ref, bf16[8,2,48,256]{3,2,1,0:T(8,128)(2,1)S(1)} %all-to-all-done.6.windows), custom_call_target="tpu_custom_call" | custom-call | tf_op jit(solution)/shard_map/pallas_call | solution.py:45
  114.5 2.0 %collective-permute-start.4 = (bf16[48,1536]{1,0:T(8,128)(2,1)S(1)}, bf16[48,1536]{1,0:T(8,128)(2,1)S(1)}, u32[]{:S(2)}, u32[]{:S(2)}) collective-permute-start(bf16[48,1536]{1,0:T(8,128)(2,1)S(1)} %get-tuple-element.45), channel_id=1, source_target_pairs={{0,8},{8,16},{16,24},{24,0},{1,9},{9,17},{17,25},{25,1},{2,10},{10... | collective-permute-start | bytes 442376 | tf_op jit(solution)/shard_map/ppermute | solution.py:305
  116.6 6.0 %collective-permute-start.5 = (bf16[48,1536]{1,0:T(8,128)(2,1)S(1)}, bf16[48,1536]{1,0:T(8,128)(2,1)S(1)}, u32[]{:S(2)}, u32[]{:S(2)}) collective-permute-start(bf16[48,1536]{1,0:T(8,128)(2,1)S(1)} %get-tuple-element.46), channel_id=1, source_target_pairs={{0,16},{8,24},{16,0},{24,8},{1,17},{9,25},{17,1},{25,9},{2,18},{10... | collective-permute-start | bytes 442376 | tf_op jit(solution)/shard_map/ppermute | solution.py:305
  122.6 1.9 %collective-permute-start.6 = (bf16[48,1536]{1,0:T(8,128)(2,1)S(1)}, bf16[48,1536]{1,0:T(8,128)(2,1)S(1)}, u32[]{:S(2)}, u32[]{:S(2)}) collective-permute-start(bf16[48,1536]{1,0:T(8,128)(2,1)S(1)} %get-tuple-element.47), channel_id=1, source_target_pairs={{0,24},{8,0},{16,8},{24,16},{1,25},{9,1},{17,9},{25,17},{2,26},{10... | collective-permute-start | bytes 442376 | tf_op jit(solution)/shard_map/ppermute | solution.py:305
  124.5 2.7 %collective-permute-done.5 = bf16[48,1536]{1,0:T(8,128)(2,1)S(1)} collective-permute-done((bf16[48,1536]{1,0:T(8,128)(2,1)S(1)}, bf16[48,1536]{1,0:T(8,128)(2,1)S(1)}, u32[]{:S(2)}, u32[]{:S(2)}) %collective-permute-start.5) | collective-permute-done | bytes 147488 | tf_op jit(solution)/shard_map/ppermute | solution.py:305
  128.5 1.9 %collective-permute-start.11 = (bf16[48,1536]{1,0:T(8,128)(2,1)S(1)}, bf16[48,1536]{1,0:T(8,128)(2,1)S(1)}, u32[]{:S(2)}, u32[]{:S(2)}) collective-permute-start(bf16[48,1536]{1,0:T(8,128)(2,1)S(1)} %add_convert_fusion.refs_0_), channel_id=1, source_target_pairs={{0,256},{32,288},{64,320},{96,352},{128,384},{160,416},{192,448},{... | collective-permute-start | bytes 442376 | tf_op jit(solution)/shard_map/ppermute | solution.py:293
  130.5 18.2 %collective-permute-done.11.refs_1_ = bf16[48,1536]{1,0:T(8,128)(2,1)S(1)} collective-permute-done((bf16[48,1536]{1,0:T(8,128)(2,1)S(1)}, bf16[48,1536]{1,0:T(8,128)(2,1)S(1)}, u32[]{:S(2)}, u32[]{:S(2)}) %collective-permute-start.11) | collective-permute-done | bytes 147488 | tf_op jit(solution)/shard_map/ppermute | solution.py:293
  148.7 17.5 %all_to_all.46 = bf16[4,48,1536]{2,1,0:T(8,128)(2,1)S(1)} all-to-all(bf16[4,48,1536]{2,1,0:T(8,128)(2,1)S(1)} %shard_map.97), channel_id=1, replica_groups={{0,64,128,192},{32,96,160,224},{256,320,384,448},{288,352,416,480},{1,6..., dimensions={0} | all-to-all | bytes 1179648 | tf_op jit(solution)/shard_map/all_to_all | solution.py:311
  166.2 3.6 %collective-permute-start.12 = (bf16[192,1536]{1,0:T(8,128)(2,1)S(1)}, bf16[192,1536]{1,0:T(8,128)(2,1)S(1)}, u32[]{:S(2)}, u32[]{:S(2)}) collective-permute-start(bf16[192,1536]{1,0:T(8,128)(2,1)S(1)} %bitcast.24), channel_id=1, source_target_pairs={{0,32},{32,0},{64,96},{96,64},{128,160},{160,128},{192,224},{224,1... | collective-permute-start | bytes 1769480 | tf_op jit(solution)/shard_map/ppermute | solution.py:293
  (35 shorter events, 10.5 us)
Async XLA Ops:
  1.1 25.3 %collective-permute-start = (bf16[48,1536]{1,0:T(8,128)(2,1)S(1)}, bf16[48,1536]{1,0:T(8,128)(2,1)S(1)}, u32[]{:S(2)}, u32[]{:S(2)}) collective-permute-start(bf16[48,1536]{1,0:T(8,128)(2,1)S(1)} %get-tuple-element.58), channel_id=1, source_target_pairs={{1,448},{2,449},{3,450},{4,451},{5,452},{6,453},{7,454},{33,480},{... | collective-permute-start | bytes 442376 | tf_op jit(solution)/shard_map/ppermute | solution.py:302
  2.4 24.0 %collective-permute-start.3 = (bf16[48,1536]{1,0:T(8,128)(2,1)S(1)}, bf16[48,1536]{1,0:T(8,128)(2,1)S(1)}, u32[]{:S(2)}, u32[]{:S(2)}) collective-permute-start(bf16[48,1536]{1,0:T(8,128)(2,1)S(1)} %get-tuple-element.35.refs_0_), channel_id=1, source_target_pairs={{0,24},{8,0},{16,8},{24,16},{1,25},{9,1},{17,9},{25,17},{2,26},{10... | collective-permute-start | bytes 442376 | tf_op jit(solution)/shard_map/ppermute | solution.py:305
  7.6 18.8 %collective-permute-start.2 = (bf16[48,1536]{1,0:T(8,128)(2,1)S(1)}, bf16[48,1536]{1,0:T(8,128)(2,1)S(1)}, u32[]{:S(2)}, u32[]{:S(2)}) collective-permute-start(bf16[48,1536]{1,0:T(8,128)(2,1)S(1)} %get-tuple-element.35.refs_0_), channel_id=1, source_target_pairs={{0,16},{8,24},{16,0},{24,8},{1,17},{9,25},{17,1},{25,9},{2,18},{10... | collective-permute-start | bytes 442376 | tf_op jit(solution)/shard_map/ppermute | solution.py:305
  10.0 16.3 %collective-permute-start.1 = (bf16[48,1536]{1,0:T(8,128)(2,1)S(1)}, bf16[48,1536]{1,0:T(8,128)(2,1)S(1)}, u32[]{:S(2)}, u32[]{:S(2)}) collective-permute-start(bf16[48,1536]{1,0:T(8,128)(2,1)S(1)} %get-tuple-element.35.refs_0_), channel_id=1, source_target_pairs={{0,8},{8,16},{16,24},{24,0},{1,9},{9,17},{17,25},{25,1},{2,10},{10... | collective-permute-start | bytes 442376 | tf_op jit(solution)/shard_map/ppermute | solution.py:305
  13.8 0.7 copy-start.5
  14.5 0.7 copy-start.7
  16.3 12.5 %all-to-all-start.4 = ((s32[8,1,128]{2,1,0:T(1,128)}), s32[8,1,128]{2,1,0:T(1,128)S(1)}, u32[]{:S(2)}, u32[]{:S(2)}) async-start(s32[8,1,128]{2,1,0:T(1,128)} %bitcast.6), calls=%async_computation.4 | async-start | bytes 8192 | tf_op jit(solution)/shard_map/all_to_all | solution.py:308
  29.7 14.3 %all-to-all-start.5 = ((bf16[4,48,1536]{2,1,0:T(8,128)(2,1)}), bf16[4,48,1536]{2,1,0:T(8,128)(2,1)S(1)}, u32[]{:S(2)}, u32[]{:S(2)}) async-start(bf16[4,48,1536]{2,1,0:T(8,128)(2,1)} %broadcast_in_dim.3), calls=%async_computation.5 | async-start | bytes 1179648 | tf_op jit(solution)/shard_map/all_to_all | solution.py:314
  45.8 24.5 %copy-start.1 = (f32[2,256,256]{2,1,0:T(8,128)S(1)}, f32[2,256,256]{2,1,0:T(8,128)}, u32[]{:S(2)}) copy-start(f32[2,256,256]{2,1,0:T(8,128)} %probe.1) | copy-start | bytes 1572868
  45.9 24.5 %copy-start.2 = (bf16[1,1,1,2,256,256]{5,4,3,2,1,0:T(8,128)(2,1)S(1)}, bf16[1,1,1,2,256,256]{5,4,3,2,1,0:T(8,128)(2,1)}, u32[]{:S(2)}) copy-start(bf16[1,1,1,2,256,256]{5,4,3,2,1,0:T(8,128)(2,1)} %param.15) | copy-start | bytes 786436
  45.9 24.4 %copy-start.3 = (bf16[256,256]{1,0:T(8,128)(2,1)S(1)}, bf16[256,256]{1,0:T(8,128)(2,1)}, u32[]{:S(2)}) copy-start(bf16[256,256]{1,0:T(8,128)(2,1)} %constant.105.clone.wi_ref) | copy-start | bytes 393220
  45.9 24.4 %copy-start.4 = (bf16[256,256]{1,0:T(8,128)(2,1)S(1)}, bf16[256,256]{1,0:T(8,128)(2,1)}, u32[]{:S(2)}) copy-start(bf16[256,256]{1,0:T(8,128)(2,1)} %constant.104.clone.wr_ref) | copy-start | bytes 393220
  45.9 24.4 %copy-start.6 = (s32[1,1,1,2]{3,2,1,0:T(1,128)S(1)}, s32[1,1,1,2]{3,2,1,0:T(1,128)}, u32[]{:S(2)}) copy-start(s32[1,1,1,2]{3,2,1,0:T(1,128)} %param.16) | copy-start | bytes 28
  91.0 21.5 %all-to-all-start.6 = ((bf16[8,2,48,256]{3,2,1,0:T(8,128)(2,1)}), bf16[8,2,48,256]{3,2,1,0:T(8,128)(2,1)S(1)}, u32[]{:S(2)}, u32[]{:S(2)}) async-start(bf16[8,2,48,256]{3,2,1,0:T(8,128)(2,1)} %get-tuple-element.43), calls=%async_computation.6 | async-start | bytes 786432 | tf_op jit(solution)/shard_map/all_to_all | solution.py:308
  95.2 74.7 %copy-start = (bf16[2,1,192,1536]{3,2,1,0:T(8,128)(2,1)S(1)}, bf16[2,1,192,1536]{3,2,1,0:T(8,128)(2,1)}, u32[]{:S(2)}) copy-start(bf16[2,1,192,1536]{3,2,1,0:T(8,128)(2,1)} %param.13) | copy-start | bytes 3538948
  97.3 11.6 %collective-permute-start.7 = (bf16[48,1536]{1,0:T(8,128)(2,1)S(1)}, bf16[48,1536]{1,0:T(8,128)(2,1)S(1)}, u32[]{:S(2)}, u32[]{:S(2)}) collective-permute-start(bf16[48,1536]{1,0:T(8,128)(2,1)S(1)} %get-tuple-element.50), channel_id=1, source_target_pairs={{0,8},{8,16},{16,24},{24,0},{1,9},{9,17},{17,25},{25,1},{2,10},{10... | collective-permute-start | bytes 442376 | tf_op jit(solution)/shard_map/ppermute | solution.py:305
  99.2 9.7 %collective-permute-start.8 = (bf16[48,1536]{1,0:T(8,128)(2,1)S(1)}, bf16[48,1536]{1,0:T(8,128)(2,1)S(1)}, u32[]{:S(2)}, u32[]{:S(2)}) collective-permute-start(bf16[48,1536]{1,0:T(8,128)(2,1)S(1)} %get-tuple-element.51), channel_id=1, source_target_pairs={{0,16},{8,24},{16,0},{24,8},{1,17},{9,25},{17,1},{25,9},{2,18},{10... | collective-permute-start | bytes 442376 | tf_op jit(solution)/shard_map/ppermute | solution.py:305
  101.1 9.9 %collective-permute-start.9 = (bf16[48,1536]{1,0:T(8,128)(2,1)S(1)}, bf16[48,1536]{1,0:T(8,128)(2,1)S(1)}, u32[]{:S(2)}, u32[]{:S(2)}) collective-permute-start(bf16[48,1536]{1,0:T(8,128)(2,1)S(1)} %get-tuple-element.52), channel_id=1, source_target_pairs={{0,24},{8,0},{16,8},{24,16},{1,25},{9,1},{17,9},{25,17},{2,26},{10... | collective-permute-start | bytes 442376 | tf_op jit(solution)/shard_map/ppermute | solution.py:305
  111.1 13.4 %collective-permute-start.10 = (bf16[48,1536]{1,0:T(8,128)(2,1)S(1)}, bf16[48,1536]{1,0:T(8,128)(2,1)S(1)}, u32[]{:S(2)}, u32[]{:S(2)}) collective-permute-start(bf16[48,1536]{1,0:T(8,128)(2,1)S(1)} %add_convert_fusion.1), channel_id=1, source_target_pairs={{0,449},{1,450},{2,451},{3,452},{4,453},{5,454},{6,455},{32,481},{... | collective-permute-start | bytes 442376 | tf_op jit(solution)/shard_map/ppermute | solution.py:302
  114.5 10.0 %collective-permute-start.4 = (bf16[48,1536]{1,0:T(8,128)(2,1)S(1)}, bf16[48,1536]{1,0:T(8,128)(2,1)S(1)}, u32[]{:S(2)}, u32[]{:S(2)}) collective-permute-start(bf16[48,1536]{1,0:T(8,128)(2,1)S(1)} %get-tuple-element.45), channel_id=1, source_target_pairs={{0,8},{8,16},{16,24},{24,0},{1,9},{9,17},{17,25},{25,1},{2,10},{10... | collective-permute-start | bytes 442376 | tf_op jit(solution)/shard_map/ppermute | solution.py:305
  116.6 10.7 %collective-permute-start.5 = (bf16[48,1536]{1,0:T(8,128)(2,1)S(1)}, bf16[48,1536]{1,0:T(8,128)(2,1)S(1)}, u32[]{:S(2)}, u32[]{:S(2)}) collective-permute-start(bf16[48,1536]{1,0:T(8,128)(2,1)S(1)} %get-tuple-element.46), channel_id=1, source_target_pairs={{0,16},{8,24},{16,0},{24,8},{1,17},{9,25},{17,1},{25,9},{2,18},{10... | collective-permute-start | bytes 442376 | tf_op jit(solution)/shard_map/ppermute | solution.py:305
  122.6 5.9 %collective-permute-start.6 = (bf16[48,1536]{1,0:T(8,128)(2,1)S(1)}, bf16[48,1536]{1,0:T(8,128)(2,1)S(1)}, u32[]{:S(2)}, u32[]{:S(2)}) collective-permute-start(bf16[48,1536]{1,0:T(8,128)(2,1)S(1)} %get-tuple-element.47), channel_id=1, source_target_pairs={{0,24},{8,0},{16,8},{24,16},{1,25},{9,1},{17,9},{25,17},{2,26},{10... | collective-permute-start | bytes 442376 | tf_op jit(solution)/shard_map/ppermute | solution.py:305
  128.5 20.1 %collective-permute-start.11 = (bf16[48,1536]{1,0:T(8,128)(2,1)S(1)}, bf16[48,1536]{1,0:T(8,128)(2,1)S(1)}, u32[]{:S(2)}, u32[]{:S(2)}) collective-permute-start(bf16[48,1536]{1,0:T(8,128)(2,1)S(1)} %add_convert_fusion.refs_0_), channel_id=1, source_target_pairs={{0,256},{32,288},{64,320},{96,352},{128,384},{160,416},{192,448},{... | collective-permute-start | bytes 442376 | tf_op jit(solution)/shard_map/ppermute | solution.py:293
  166.2 5.2 %collective-permute-start.12 = (bf16[192,1536]{1,0:T(8,128)(2,1)S(1)}, bf16[192,1536]{1,0:T(8,128)(2,1)S(1)}, u32[]{:S(2)}, u32[]{:S(2)}) collective-permute-start(bf16[192,1536]{1,0:T(8,128)(2,1)S(1)} %bitcast.24), channel_id=1, source_target_pairs={{0,32},{32,0},{64,96},{96,64},{128,160},{160,128},{192,224},{224,1... | collective-permute-start | bytes 1769480 | tf_op jit(solution)/shard_map/ppermute | solution.py:293

commit v14 on v12

--- a/solution.py
+++ b/solution.py
@@ -52,7 +52,13 @@
     )(*args)
 
 
-def facts_body(rows_ref, columns_ref, count_ref, index_ref, out):
+def facts_body(rows_in, columns_in, count_in, index_in, out, rows_ref, columns_ref, count_ref, index_ref, sems):
+    pairs = zip((rows_in, columns_in, count_in, index_in), (rows_ref, columns_ref, count_ref, index_ref))
+    copies = [pltpu.make_async_copy(ref, to, sems.at[n]) for n, (ref, to) in enumerate(pairs)]
+    for copy in copies:
+        copy.start()
+    for copy in copies:
+        copy.wait()
     values = []
     for slot in range(rows_ref.shape[0]):
         values += [rows_ref[slot], columns_ref[slot], (slot < count_ref[0]).astype(jnp.int32)]
@@ -61,6 +67,16 @@
     for n, value in enumerate(values + [index_ref[0]]):
         line = jnp.where(lane == n, value, line)
     out[...] = line
+
+
+def facts_line(*args):
+    return pl.pallas_call(
+        facts_body,
+        out_shape=jax.ShapeDtypeStruct((8, LANE), jnp.int32),
+        in_specs=[pl.BlockSpec(memory_space=pltpu.HBM)] * len(args),
+        out_specs=VMEM,
+        scratch_shapes=[pltpu.SMEM(x.shape, jnp.int32) for x in args] + [pltpu.SemaphoreType.DMA((len(args),))],
+    )(*args)
 
 
 class Facts:
@@ -338,8 +354,7 @@
     own = rows_of(place_z)
 
     slot_rows, count = offsets.reshape(slots), counts.reshape(1)
-    line = jax.ShapeDtypeStruct((8, LANE), jnp.int32)
-    meta = call(facts_body, [line], [], slot_rows, column_starts.reshape(slots), count, angle_ids)[0]
+    meta = facts_line(slot_rows, column_starts.reshape(slots), count, angle_ids)
     eight = to_eight(meta)
     facts = (eight, slab.reshape(1).astype(jnp.int32))
     more = jnp.max(eight[:, 5 : 3 * slots : 3]) > 0

time: 169 us -> 168 us (level)
    pallas_call x7 -> x6, Pallas kernels: 13.2 us -> 12.1 us  [call(): pl.pallas_call(body, out_shape=out_shape, in_specs=[smem if x.dtype == jn...]
  transfers between devices with their start and end apart: 14 -> 14, of which waited for: 8 -> 8; matrix products, arithmetic and copies ran while one was open for 1% -> 1% of each run, Pallas kernels for 5% -> 6%
where the time goes in v14:
time: 168 us; the launch traced here: 167 us
  blocking collectives  59.3 us (35%)
  starting transfers between devices  47.2 us (28%)
  waiting for transfers between devices  39.4 us (23%)
  Pallas kernels  15.6 us (9%)
  between operations  2.25 us (1%)
  local copies, waits for them, and re-layouts  1.97 us (1%)
    all_to_all x2, blocking collectives, to_eight(): lax.all_to_all(value, 'angle', 0, 0, axis_index_groups=eight_groups, tile...  41.6 us
    ppermute x6, starting transfers between devices, to_slab(): lax.ppermute(value, 'slab', [(i, (i + by) % slabs) for i in range(slabs)])  18.6 us
    all_to_all x1, blocking collectives, to_four(): lax.all_to_all(value, 'angle', 0, 0, axis_index_groups=four_groups, tiled...  17.7 us
    ppermute x2, waiting for transfers between devices, swap(): return lax.ppermute(value, 'angle', [(i, i ^ by) for i in range(angles)])  14.7 us
    all_to_all x2, waiting for transfers between devices, to_slabs(): return lax.all_to_all(value, 'slab', 0, 0, tiled=True)  13.9 us
    pallas_call x6, Pallas kernels, call(): pl.pallas_call(body, out_shape=out_shape, in_specs=[smem if x.dtype == jn...  12.1 us
    all_to_all x2, starting transfers between devices, to_eight(): lax.all_to_all(value, 'angle', 0, 0, axis_index_groups=eight_groups, tile...  11.9 us
    all_to_all x2, starting transfers between devices, to_slabs(): return lax.all_to_all(value, 'slab', 0, 0, tiled=True)  8.59 us
  transfers between devices with their start and end apart: 14, of which 8 were waited for; matrix products, arithmetic and copies ran while one was open for 1% of the time, Pallas kernels for 6%

profile of v14, /device:TPU:1, one launch (start us, length us, event | category | flops | bytes accessed | tf_op | source)
XLA Modules:
  0.0 166.7 jit_solution(14371396690664780530)
XLA Ops:
  1.1 1.3 collective-permute-start
  2.4 5.2 %collective-permute-start.3 = (bf16[48,1536]{1,0:T(8,128)(2,1)S(1)}, bf16[48,1536]{1,0:T(8,128)(2,1)S(1)}, u32[]{:S(2)}, u32[]{:S(2)}) collective-permute-start(bf16[48,1536]{1,0:T(8,128)(2,1)S(1)} %get-tuple-element.31.refs_0_), channel_id=1, source_target_pairs={{0,24},{8,0},{16,8},{24,16},{1,25},{9,1},{17,9},{25,17},{2,26},{10... | collective-permute-start | bytes 442376 | tf_op jit(solution)/shard_map/ppermute | solution.py:324
  7.6 2.4 %collective-permute-start.2 = (bf16[48,1536]{1,0:T(8,128)(2,1)S(1)}, bf16[48,1536]{1,0:T(8,128)(2,1)S(1)}, u32[]{:S(2)}, u32[]{:S(2)}) collective-permute-start(bf16[48,1536]{1,0:T(8,128)(2,1)S(1)} %get-tuple-element.31.refs_0_), channel_id=1, source_target_pairs={{0,16},{8,24},{16,0},{24,8},{1,17},{9,25},{17,1},{25,9},{2,18},{10... | collective-permute-start | bytes 442376 | tf_op jit(solution)/shard_map/ppermute | solution.py:324
  10.0 2.5 %collective-permute-start.1 = (bf16[48,1536]{1,0:T(8,128)(2,1)S(1)}, bf16[48,1536]{1,0:T(8,128)(2,1)S(1)}, u32[]{:S(2)}, u32[]{:S(2)}) collective-permute-start(bf16[48,1536]{1,0:T(8,128)(2,1)S(1)} %get-tuple-element.31.refs_0_), channel_id=1, source_target_pairs={{0,8},{8,16},{16,24},{24,0},{1,9},{9,17},{17,25},{25,1},{2,10},{10... | collective-permute-start | bytes 442376 | tf_op jit(solution)/shard_map/ppermute | solution.py:324
  13.8 1.3 shard_map.91
  15.2 7.7 %all-to-all-start.4 = ((s32[8,1,128]{2,1,0:T(1,128)}), s32[8,1,128]{2,1,0:T(1,128)S(1)}, u32[]{:S(2)}, u32[]{:S(2)}) async-start(s32[8,1,128]{2,1,0:T(1,128)} %bitcast.34), calls=%async_computation.4 | async-start | bytes 8192 | tf_op jit(solution)/shard_map/all_to_all | solution.py:327
  22.9 3.5 %collective-permute-done = bf16[48,1536]{1,0:T(8,128)(2,1)S(1)} collective-permute-done((bf16[48,1536]{1,0:T(8,128)(2,1)S(1)}, bf16[48,1536]{1,0:T(8,128)(2,1)S(1)}, u32[]{:S(2)}, u32[]{:S(2)}) %collective-permute-start) | collective-permute-done | bytes 147488 | tf_op jit(solution)/shard_map/ppermute | solution.py:321
  26.4 1.3 all-to-all-done.4
  28.6 5.1 %all-to-all-start.5 = ((bf16[4,48,1536]{2,1,0:T(8,128)(2,1)}), bf16[4,48,1536]{2,1,0:T(8,128)(2,1)S(1)}, u32[]{:S(2)}, u32[]{:S(2)}) async-start(bf16[4,48,1536]{2,1,0:T(8,128)(2,1)} %broadcast_in_dim.3), calls=%async_computation.5 | async-start | bytes 1179648 | tf_op jit(solution)/shard_map/all_to_all | solution.py:333
  35.2 1.8 %shard_map.92.done = bf16[8,2,48,256]{3,2,1,0:T(8,128)(2,1)S(1)} custom-call(s32[8,128]{1,0:T(8,128)S(1)} %bitcast.28, s32[1]{0:T(128)} %bitcast.8.slab_ref, bf16[48,1536]{1,0:T(8,128)(2,1)S(1)} %get-tuple-element.31.refs_0_, bf16[48,1536]{1,0:T(8,128)(2,1)S(1)} %collective-permute-done.1.refs_1_, bf16[48,1536]{1,0:T(8,128)(2,1)S(1)} %collective-permute-done.2.refs_2_, ...), custom_call_target="tpu_custom_call" | custom-call | tf_op jit(solution)/shard_map/pallas_call | solution.py:45
  37.0 5.9 %all-to-all-done.5.blocks = bf16[4,48,1536]{2,1,0:T(8,128)(2,1)S(1)} async-done(((bf16[4,48,1536]{2,1,0:T(8,128)(2,1)}), bf16[4,48,1536]{2,1,0:T(8,128)(2,1)S(1)}, u32[]{:S(2)}, u32[]{:S(2)}) %all-to-all-start.5) | async-done | bytes 589856 | tf_op jit(solution)/shard_map/all_to_all | solution.py:333
  42.9 1.8 %shard_map.93 = bf16[8,2,2,48,256]{4,3,2,1,0:T(8,128)(2,1)S(1)} custom-call(s32[8,128]{1,0:T(8,128)S(1)} %bitcast.29, s32[1]{0:T(128)} %bitcast.8.slab_ref, bf16[4,48,1536]{2,1,0:T(8,128)(2,1)S(1)} %all-to-all-done.5.blocks, bf16[8,2,48,256]{3,2,1,0:T(8,128)(2,1)S(1)} %shard_map.92.done), custom_call_target="tpu_custom_call" | custom-call | tf_op jit(solution)/shard_map/pallas_call | solution.py:45
  44.8 24.4 %conditional.2 = (bf16[8,2,2,48,256]{4,3,2,1,0:T(8,128)(2,1)S(1)}) conditional(s32[]{:T(128)} %convert_element_type.25, bf16[8,2,2,48,256]{4,3,2,1,0:T(8,128)(2,1)S(1)} %shard_map.93, bf16[8,2,2,48,256]{4,3,2,1,0:T(8,128)(2,1)S(1)} %shard_map.93), branch_computations={%region_1.2_spmd, %region_2.3_spmd} | conditional | flops 393216 | bytes 3932168 | solution.py:346
  44.8 24.4 %all_to_all.48 = bf16[8,2,2,48,256]{4,3,2,1,0:T(8,128)(2,1)S(1)} all-to-all(bf16[8,2,2,48,256]{4,3,2,1,0:T(8,128)(2,1)S(1)} %param.1), channel_id=1, replica_groups={{0,32,64,96,128,160,192,224},{256,288,320,352,384,416,448,480},{1,33,65..., dimensions={0} | all-to-all | bytes 1572864 | tf_op jit(solution)/shard_map/cond/branch_1_fun/all_to_all | solution.py:327
  69.2 3.4 %shard_map.94 = (bf16[8,2,48,256]{3,2,1,0:T(8,128)(2,1)}, bf16[8,2,48,256]{3,2,1,0:T(8,128)(2,1)S(1)}) custom-call(s32[2]{0:T(128)S(1)} %bitcast.33, s32[1]{0:T(128)} %bitcast.21.count_ref, bf16[8,2,2,48,256]{4,3,2,1,0:T(8,128)(2,1)S(1)} %get-tuple-element.51.windows, f32[2,256,256]{2,1,0:T(8,128)S(1)} %copy-done.1, bf16[2,256,256]{2,1,0:T(8,128)(2,1)S(1)} %bitcast.26, ...), custom_call_target="tpu_custom_call" | custom-call | tf_op jit(solution)/shard_map/pallas_call | solution.py:45
  72.7 17.2 %conditional.3 = (bf16[8,2,48,256]{3,2,1,0:T(8,128)(2,1)S(1)}) conditional(s32[]{:T(128)} %convert_element_type.25, bf16[8,2,48,256]{3,2,1,0:T(8,128)(2,1)S(1)} %get-tuple-element.37, bf16[8,2,48,256]{3,2,1,0:T(8,128)(2,1)S(1)} %get-tuple-element.37), branch_computations={%region_3.4_spmd, %region_4.5_spmd} | conditional | flops 196608 | bytes 1966088 | solution.py:346
  72.7 17.2 %all_to_all.50 = bf16[8,2,48,256]{3,2,1,0:T(8,128)(2,1)S(1)} all-to-all(bf16[8,2,48,256]{3,2,1,0:T(8,128)(2,1)S(1)} %param.3), channel_id=1, replica_groups={{0,32,64,96,128,160,192,224},{256,288,320,352,384,416,448,480},{1,33,65..., dimensions={0} | all-to-all | bytes 786432 | tf_op jit(solution)/shard_map/cond/branch_1_fun/all_to_all | solution.py:327
  89.9 4.2 %all-to-all-start.6 = ((bf16[8,2,48,256]{3,2,1,0:T(8,128)(2,1)}), bf16[8,2,48,256]{3,2,1,0:T(8,128)(2,1)S(1)}, u32[]{:S(2)}, u32[]{:S(2)}) async-start(bf16[8,2,48,256]{3,2,1,0:T(8,128)(2,1)} %get-tuple-element.39), calls=%async_computation.6 | async-start | bytes 786432 | tf_op jit(solution)/shard_map/all_to_all | solution.py:327
  94.1 2.1 %shard_map.96 = (f32[48,1536]{1,0:T(8,128)S(1)}, bf16[48,1536]{1,0:T(8,128)(2,1)S(1)}, bf16[48,1536]{1,0:T(8,128)(2,1)S(1)}, bf16[48,1536]{1,0:T(8,128)(2,1)S(1)}) custom-call(s32[8,128]{1,0:T(8,128)S(1)} %bitcast.30, s32[1]{0:T(128)} %bitcast.8.slab_ref, bf16[8,2,48,256]{3,2,1,0:T(8,128)(2,1)S(1)} %get-tuple-element.52.windows), custom_call_target="tpu_custom_call" | custom-call | tf_op jit(solution)/shard_map/pallas_call | solution.py:45
  96.2 1.9 %collective-permute-start.4 = (bf16[48,1536]{1,0:T(8,128)(2,1)S(1)}, bf16[48,1536]{1,0:T(8,128)(2,1)S(1)}, u32[]{:S(2)}, u32[]{:S(2)}) collective-permute-start(bf16[48,1536]{1,0:T(8,128)(2,1)S(1)} %get-tuple-element.42), channel_id=1, source_target_pairs={{0,8},{8,16},{16,24},{24,0},{1,9},{9,17},{17,25},{25,1},{2,10},{10... | collective-permute-start | bytes 442376 | tf_op jit(solution)/shard_map/ppermute | solution.py:324
  98.2 1.9 %collective-permute-start.5 = (bf16[48,1536]{1,0:T(8,128)(2,1)S(1)}, bf16[48,1536]{1,0:T(8,128)(2,1)S(1)}, u32[]{:S(2)}, u32[]{:S(2)}) collective-permute-start(bf16[48,1536]{1,0:T(8,128)(2,1)S(1)} %get-tuple-element.43), channel_id=1, source_target_pairs={{0,16},{8,24},{16,0},{24,8},{1,17},{9,25},{17,1},{25,9},{2,18},{10... | collective-permute-start | bytes 442376 | tf_op jit(solution)/shard_map/ppermute | solution.py:324
  100.1 4.6 %collective-permute-start.6 = (bf16[48,1536]{1,0:T(8,128)(2,1)S(1)}, bf16[48,1536]{1,0:T(8,128)(2,1)S(1)}, u32[]{:S(2)}, u32[]{:S(2)}) collective-permute-start(bf16[48,1536]{1,0:T(8,128)(2,1)S(1)} %get-tuple-element.44), channel_id=1, source_target_pairs={{0,24},{8,0},{16,8},{24,16},{1,25},{9,1},{17,9},{25,17},{2,26},{10... | collective-permute-start | bytes 442376 | tf_op jit(solution)/shard_map/ppermute | solution.py:324
  104.7 1.1 all-to-all-done.6.windows
  105.8 2.9 %shard_map.95 = bf16[4,48,1536]{2,1,0:T(8,128)(2,1)} custom-call(s32[8,128]{1,0:T(8,128)S(1)} %bitcast.31, s32[1]{0:T(128)} %bitcast.8.slab_ref, bf16[8,2,48,256]{3,2,1,0:T(8,128)(2,1)S(1)} %all-to-all-done.6.windows), custom_call_target="tpu_custom_call" | custom-call | tf_op jit(solution)/shard_map/pallas_call | solution.py:45
  108.7 3.5 %all-to-all-start.7 = ((bf16[4,48,1536]{2,1,0:T(8,128)(2,1)}), bf16[4,48,1536]{2,1,0:T(8,128)(2,1)S(1)}, u32[]{:S(2)}, u32[]{:S(2)}) async-start(bf16[4,48,1536]{2,1,0:T(8,128)(2,1)} %shard_map.95), calls=%async_computation.7 | async-start | bytes 1179648 | tf_op jit(solution)/shard_map/all_to_all | solution.py:333
  112.3 1.3 collective-permute-start.7
  113.6 7.9 %all-to-all-done.7 = bf16[4,48,1536]{2,1,0:T(8,128)(2,1)S(1)} async-done(((bf16[4,48,1536]{2,1,0:T(8,128)(2,1)}), bf16[4,48,1536]{2,1,0:T(8,128)(2,1)S(1)}, u32[]{:S(2)}, u32[]{:S(2)}) %all-to-all-start.7) | async-done | bytes 589856 | tf_op jit(solution)/shard_map/all_to_all | solution.py:333
  121.6 5.0 %collective-permute-done.7 = bf16[48,1536]{1,0:T(8,128)(2,1)S(1)} collective-permute-done((bf16[48,1536]{1,0:T(8,128)(2,1)S(1)}, bf16[48,1536]{1,0:T(8,128)(2,1)S(1)}, u32[]{:S(2)}, u32[]{:S(2)}) %collective-permute-start.7) | collective-permute-done | bytes 147488 | tf_op jit(solution)/shard_map/ppermute | solution.py:321
  126.6 2.1 %collective-permute-start.8 = (bf16[48,1536]{1,0:T(8,128)(2,1)S(1)}, bf16[48,1536]{1,0:T(8,128)(2,1)S(1)}, u32[]{:S(2)}, u32[]{:S(2)}) collective-permute-start(bf16[48,1536]{1,0:T(8,128)(2,1)S(1)} %add_convert_fusion.refs_0_), channel_id=1, source_target_pairs={{0,256},{32,288},{64,320},{96,352},{128,384},{160,416},{192,448},{... | collective-permute-start | bytes 442376 | tf_op jit(solution)/shard_map/ppermute | solution.py:312
  128.7 14.1 %collective-permute-done.8.refs_1_ = bf16[48,1536]{1,0:T(8,128)(2,1)S(1)} collective-permute-done((bf16[48,1536]{1,0:T(8,128)(2,1)S(1)}, bf16[48,1536]{1,0:T(8,128)(2,1)S(1)}, u32[]{:S(2)}, u32[]{:S(2)}) %collective-permute-start.8) | collective-permute-done | bytes 147488 | tf_op jit(solution)/shard_map/ppermute | solution.py:312
  142.9 17.7 %all_to_all.51 = bf16[4,48,1536]{2,1,0:T(8,128)(2,1)S(1)} all-to-all(bf16[4,48,1536]{2,1,0:T(8,128)(2,1)S(1)} %shard_map.97), channel_id=1, replica_groups={{0,64,128,192},{32,96,160,224},{256,320,384,448},{288,352,416,480},{1,6..., dimensions={0} | all-to-all | bytes 1179648 | tf_op jit(solution)/shard_map/all_to_all | solution.py:330
  160.6 3.5 %collective-permute-start.9 = (bf16[192,1536]{1,0:T(8,128)(2,1)S(1)}, bf16[192,1536]{1,0:T(8,128)(2,1)S(1)}, u32[]{:S(2)}, u32[]{:S(2)}) collective-permute-start(bf16[192,1536]{1,0:T(8,128)(2,1)S(1)} %bitcast.24), channel_id=1, source_target_pairs={{0,32},{32,0},{64,96},{96,64},{128,160},{160,128},{192,224},{224,1... | collective-permute-start | bytes 1769480 | tf_op jit(solution)/shard_map/ppermute | solution.py:312
  (28 shorter events, 5.7 us)
Async XLA Ops:
  1.1 25.3 %collective-permute-start = (bf16[48,1536]{1,0:T(8,128)(2,1)S(1)}, bf16[48,1536]{1,0:T(8,128)(2,1)S(1)}, u32[]{:S(2)}, u32[]{:S(2)}) collective-permute-start(bf16[48,1536]{1,0:T(8,128)(2,1)S(1)} %get-tuple-element.50), channel_id=1, source_target_pairs={{1,448},{2,449},{3,450},{4,451},{5,452},{6,453},{7,454},{33,480},{... | collective-permute-start | bytes 442376 | tf_op jit(solution)/shard_map/ppermute | solution.py:321
  2.4 24.0 %collective-permute-start.3 = (bf16[48,1536]{1,0:T(8,128)(2,1)S(1)}, bf16[48,1536]{1,0:T(8,128)(2,1)S(1)}, u32[]{:S(2)}, u32[]{:S(2)}) collective-permute-start(bf16[48,1536]{1,0:T(8,128)(2,1)S(1)} %get-tuple-element.31.refs_0_), channel_id=1, source_target_pairs={{0,24},{8,0},{16,8},{24,16},{1,25},{9,1},{17,9},{25,17},{2,26},{10... | collective-permute-start | bytes 442376 | tf_op jit(solution)/shard_map/ppermute | solution.py:324
  7.6 18.8 %collective-permute-start.2 = (bf16[48,1536]{1,0:T(8,128)(2,1)S(1)}, bf16[48,1536]{1,0:T(8,128)(2,1)S(1)}, u32[]{:S(2)}, u32[]{:S(2)}) collective-permute-start(bf16[48,1536]{1,0:T(8,128)(2,1)S(1)} %get-tuple-element.31.refs_0_), channel_id=1, source_target_pairs={{0,16},{8,24},{16,0},{24,8},{1,17},{9,25},{17,1},{25,9},{2,18},{10... | collective-permute-start | bytes 442376 | tf_op jit(solution)/shard_map/ppermute | solution.py:324
  10.0 16.3 %collective-permute-start.1 = (bf16[48,1536]{1,0:T(8,128)(2,1)S(1)}, bf16[48,1536]{1,0:T(8,128)(2,1)S(1)}, u32[]{:S(2)}, u32[]{:S(2)}) collective-permute-start(bf16[48,1536]{1,0:T(8,128)(2,1)S(1)} %get-tuple-element.31.refs_0_), channel_id=1, source_target_pairs={{0,8},{8,16},{16,24},{24,0},{1,9},{9,17},{17,25},{25,1},{2,10},{10... | collective-permute-start | bytes 442376 | tf_op jit(solution)/shard_map/ppermute | solution.py:324
  15.2 12.5 %all-to-all-start.4 = ((s32[8,1,128]{2,1,0:T(1,128)}), s32[8,1,128]{2,1,0:T(1,128)S(1)}, u32[]{:S(2)}, u32[]{:S(2)}) async-start(s32[8,1,128]{2,1,0:T(1,128)} %bitcast.34), calls=%async_computation.4 | async-start | bytes 8192 | tf_op jit(solution)/shard_map/all_to_all | solution.py:327
  28.6 14.3 %all-to-all-start.5 = ((bf16[4,48,1536]{2,1,0:T(8,128)(2,1)}), bf16[4,48,1536]{2,1,0:T(8,128)(2,1)S(1)}, u32[]{:S(2)}, u32[]{:S(2)}) async-start(bf16[4,48,1536]{2,1,0:T(8,128)(2,1)} %broadcast_in_dim.3), calls=%async_computation.5 | async-start | bytes 1179648 | tf_op jit(solution)/shard_map/all_to_all | solution.py:333
  44.7 24.5 %copy-start.1 = (f32[2,256,256]{2,1,0:T(8,128)S(1)}, f32[2,256,256]{2,1,0:T(8,128)}, u32[]{:S(2)}) copy-start(f32[2,256,256]{2,1,0:T(8,128)} %probe.1) | copy-start | bytes 1572868
  44.7 24.5 %copy-start.2 = (bf16[1,1,1,2,256,256]{5,4,3,2,1,0:T(8,128)(2,1)S(1)}, bf16[1,1,1,2,256,256]{5,4,3,2,1,0:T(8,128)(2,1)}, u32[]{:S(2)}) copy-start(bf16[1,1,1,2,256,256]{5,4,3,2,1,0:T(8,128)(2,1)} %param.15) | copy-start | bytes 786436
  44.8 24.4 %copy-start.3 = (bf16[256,256]{1,0:T(8,128)(2,1)S(1)}, bf16[256,256]{1,0:T(8,128)(2,1)}, u32[]{:S(2)}) copy-start(bf16[256,256]{1,0:T(8,128)(2,1)} %constant.107.clone.wi_ref) | copy-start | bytes 393220
  44.8 24.4 %copy-start.4 = (bf16[256,256]{1,0:T(8,128)(2,1)S(1)}, bf16[256,256]{1,0:T(8,128)(2,1)}, u32[]{:S(2)}) copy-start(bf16[256,256]{1,0:T(8,128)(2,1)} %constant.106.clone.wr_ref) | copy-start | bytes 393220
  44.8 24.4 %copy-start.5 = (s32[1,1,1,2]{3,2,1,0:T(1,128)S(1)}, s32[1,1,1,2]{3,2,1,0:T(1,128)}, u32[]{:S(2)}) copy-start(s32[1,1,1,2]{3,2,1,0:T(1,128)} %param.16) | copy-start | bytes 28
  89.9 15.9 %all-to-all-start.6 = ((bf16[8,2,48,256]{3,2,1,0:T(8,128)(2,1)}), bf16[8,2,48,256]{3,2,1,0:T(8,128)(2,1)S(1)}, u32[]{:S(2)}, u32[]{:S(2)}) async-start(bf16[8,2,48,256]{3,2,1,0:T(8,128)(2,1)} %get-tuple-element.39), calls=%async_computation.6 | async-start | bytes 786432 | tf_op jit(solution)/shard_map/all_to_all | solution.py:327
  96.2 16.0 %collective-permute-start.4 = (bf16[48,1536]{1,0:T(8,128)(2,1)S(1)}, bf16[48,1536]{1,0:T(8,128)(2,1)S(1)}, u32[]{:S(2)}, u32[]{:S(2)}) collective-permute-start(bf16[48,1536]{1,0:T(8,128)(2,1)S(1)} %get-tuple-element.42), channel_id=1, source_target_pairs={{0,8},{8,16},{16,24},{24,0},{1,9},{9,17},{17,25},{25,1},{2,10},{10... | collective-permute-start | bytes 442376 | tf_op jit(solution)/shard_map/ppermute | solution.py:324
  98.2 14.1 %collective-permute-start.5 = (bf16[48,1536]{1,0:T(8,128)(2,1)S(1)}, bf16[48,1536]{1,0:T(8,128)(2,1)S(1)}, u32[]{:S(2)}, u32[]{:S(2)}) collective-permute-start(bf16[48,1536]{1,0:T(8,128)(2,1)S(1)} %get-tuple-element.43), channel_id=1, source_target_pairs={{0,16},{8,24},{16,0},{24,8},{1,17},{9,25},{17,1},{25,9},{2,18},{10... | collective-permute-start | bytes 442376 | tf_op jit(solution)/shard_map/ppermute | solution.py:324
  100.1 12.1 %collective-permute-start.6 = (bf16[48,1536]{1,0:T(8,128)(2,1)S(1)}, bf16[48,1536]{1,0:T(8,128)(2,1)S(1)}, u32[]{:S(2)}, u32[]{:S(2)}) collective-permute-start(bf16[48,1536]{1,0:T(8,128)(2,1)S(1)} %get-tuple-element.44), channel_id=1, source_target_pairs={{0,24},{8,0},{16,8},{24,16},{1,25},{9,1},{17,9},{25,17},{2,26},{10... | collective-permute-start | bytes 442376 | tf_op jit(solution)/shard_map/ppermute | solution.py:324
  108.7 12.8 %all-to-all-start.7 = ((bf16[4,48,1536]{2,1,0:T(8,128)(2,1)}), bf16[4,48,1536]{2,1,0:T(8,128)(2,1)S(1)}, u32[]{:S(2)}, u32[]{:S(2)}) async-start(bf16[4,48,1536]{2,1,0:T(8,128)(2,1)} %shard_map.95), calls=%async_computation.7 | async-start | bytes 1179648 | tf_op jit(solution)/shard_map/all_to_all | solution.py:333
  112.3 14.3 %collective-permute-start.7 = (bf16[48,1536]{1,0:T(8,128)(2,1)S(1)}, bf16[48,1536]{1,0:T(8,128)(2,1)S(1)}, u32[]{:S(2)}, u32[]{:S(2)}) collective-permute-start(bf16[48,1536]{1,0:T(8,128)(2,1)S(1)} %add_convert_fusion.1), channel_id=1, source_target_pairs={{0,449},{1,450},{2,451},{3,452},{4,453},{5,454},{6,455},{32,481},{... | collective-permute-start | bytes 442376 | tf_op jit(solution)/shard_map/ppermute | solution.py:321
  126.6 37.4 %copy-start = (bf16[2,1,192,1536]{3,2,1,0:T(8,128)(2,1)S(1)}, bf16[2,1,192,1536]{3,2,1,0:T(8,128)(2,1)}, u32[]{:S(2)}) copy-start(bf16[2,1,192,1536]{3,2,1,0:T(8,128)(2,1)} %param.13) | copy-start | bytes 3538948
  126.6 16.2 %collective-permute-start.8 = (bf16[48,1536]{1,0:T(8,128)(2,1)S(1)}, bf16[48,1536]{1,0:T(8,128)(2,1)S(1)}, u32[]{:S(2)}, u32[]{:S(2)}) collective-permute-start(bf16[48,1536]{1,0:T(8,128)(2,1)S(1)} %add_convert_fusion.refs_0_), channel_id=1, source_target_pairs={{0,256},{32,288},{64,320},{96,352},{128,384},{160,416},{192,448},{... | collective-permute-start | bytes 442376 | tf_op jit(solution)/shard_map/ppermute | solution.py:312
  160.6 5.1 %collective-permute-start.9 = (bf16[192,1536]{1,0:T(8,128)(2,1)S(1)}, bf16[192,1536]{1,0:T(8,128)(2,1)S(1)}, u32[]{:S(2)}, u32[]{:S(2)}) collective-permute-start(bf16[192,1536]{1,0:T(8,128)(2,1)S(1)} %bitcast.24), channel_id=1, source_target_pairs={{0,32},{32,0},{64,96},{96,64},{128,160},{160,128},{192,224},{224,1... | collective-permute-start | bytes 1769480 | tf_op jit(solution)/shard_map/ppermute | solution.py:312

commit v15 on v14

--- a/solution.py
+++ b/solution.py
@@ -15,6 +15,8 @@
 floor_square = 0.25
 
 LANE = 128
+CHUNK = 16
+FOUR = 4
 
 
 def dft_tables(plane_width):
@@ -105,9 +107,14 @@
         return starts, left & (LANE - 1)
 
 
-def cut_body(absolute, facts_ref, slab_ref, *refs):
+def needed(row, chunk, width, tile_rows):
+    first = chunk * CHUNK
+    return first + CHUNK > row, first + tile_rows < row + width
+
+
+def cut_body(absolute, put, angles, slots, facts_ref, slab_ref, *refs):
     blocks, out = refs[:-1], refs[-1]
-    angles, slots, rows, width = out.shape
+    rows = blocks[0].shape[0]
     facts = Facts(facts_ref, slab_ref, slots, len(blocks), blocks[0].shape[1])
     lane = lax.broadcasted_iota(jnp.int32, (rows, LANE), 1)
     for slot in range(slots):
@@ -125,23 +132,51 @@
                     ]
                     here = lane < LANE - inside
                     total = [t + jnp.where(here, turned[i], turned[i + 1]) for i, t in enumerate(total)]
-                out[angle, slot] = jnp.concatenate(total, axis=1).astype(jnp.bfloat16)
+                put(out, angle, slot, jnp.concatenate(total, axis=1).astype(jnp.bfloat16))
 
 
 def cut_windows(facts, blocks, angles, slots, width):
     out = jax.ShapeDtypeStruct((angles, slots, blocks[0].shape[0], width), jnp.bfloat16)
-    return call(functools.partial(cut_body, False), [out], [], *facts, *blocks)[0]
-
-
-def cut_rest(facts, blocks, done, which):
+
+    def put(out, angle, slot, window):
+        out[angle, slot] = window
+
+    return call(functools.partial(cut_body, False, put, angles, slots), [out], [], *facts, *blocks)[0]
+
+
+def cut_rest(facts, place_z, blocks, done, tile_rows):
     angles, slots, rows, width = done.shape
-    out = jax.ShapeDtypeStruct((angles, 2, slots, rows, width), jnp.bfloat16)
-
-    def body(facts_ref, slab_ref, blocks, done, out):
-        out[:, 1 - which] = done[...]
-        cut_body(True, facts_ref, slab_ref, *(blocks.at[k] for k in range(blocks.shape[0])), out.at[:, which])
-
-    return call(body, [out], [], *facts, blocks, done)[0]
+    chunks = rows // CHUNK
+    out = jax.ShapeDtypeStruct((angles, slots, chunks + 2, CHUNK, width), jnp.bfloat16)
+
+    def body(place_ref, facts_ref, slab_ref, blocks, done, out):
+        facts = Facts(facts_ref, slab_ref, slots, blocks.shape[0], blocks.shape[2])
+
+        def put(out, angle, slot, window):
+            row = facts.slot(angle, slot)[0]
+            extra = chunks
+            for i in range(chunks):
+                own, after = needed(row, place_ref[0] + FOUR * i, width, tile_rows)
+                piece = window[i * CHUNK : (i + 1) * CHUNK]
+                out[angle, slot, i] = done[angle, slot, i * CHUNK : (i + 1) * CHUNK]
+
+                @pl.when(jnp.logical_not(own))
+                def _():
+                    out[angle, slot, i] = piece
+
+                both = jnp.logical_and(own, after)
+
+                @pl.when(both)
+                def _():
+                    out[angle, slot, extra] = piece
+
+                extra = extra + both.astype(jnp.int32)
+
+        cut_body(
+            True, put, angles, slots, facts_ref, slab_ref, *(blocks.at[k] for k in range(blocks.shape[0])), out
+        )
+
+    return call(body, [out], [], place_z, *facts, blocks, done)[0]
 
 
 def cos_sin(angle):
@@ -164,10 +199,11 @@
 
 
 def patch_body(row_ref, count_ref, windows, probe, patterns, wr_ref, wi_ref, own_out, next_out):
-    angles, _, slots, rows, width = windows.shape
+    angles, slots, chunks, _, width = windows.shape
+    chunks = chunks - 2
+    tile_rows = FOUR * chunks * CHUNK
     f32, bf16 = jnp.float32, jnp.bfloat16
-    blocks = angles // 2
-    tall = 2 * blocks * rows
+    tall = 2 * tile_rows
     for slot in range(slots):
         row = row_ref[slot]
 
@@ -175,8 +211,18 @@
         def _():
             pick = one_hot(width, tall, -row)
             window = []
+            after_at = [[None] * FOUR for _ in range(chunks)]
+            for k in range(FOUR):
+                extra = chunks
+                for i in range(chunks):
+                    own, after = needed(row, k + FOUR * i, width, tile_rows)
+                    both = jnp.logical_and(own, after)
+                    after_at[i][k] = jnp.where(both, extra, i)
+                    extra = extra + both.astype(jnp.int32)
             for part in range(2):
-                held = [windows[2 * k + part, tile, slot] for tile in range(2) for k in range(blocks)]
+                order = [(i, k) for i in range(chunks) for k in range(FOUR)]
+                held = [windows[2 * k + part, slot, i] for i, k in order]
+                held += [windows[2 * k + part, slot, after_at[i][k]] for i, k in order]
                 window.append(dot(pick, jnp.concatenate(held, axis=0)))
             phase, absorption = window
             magnitude = jnp.exp(-absorption)
@@ -206,15 +252,16 @@
             put = one_hot(tall, width, row)
             for part, value in enumerate((final_imag, -final_real)):
                 placed = dot(put, value.astype(bf16)).astype(bf16)
-                for k in range(blocks):
-                    own_out[2 * k + part, slot] = placed[k * rows : (k + 1) * rows]
-                    below = placed[(blocks + k) * rows : (blocks + k + 1) * rows]
-                    next_out[2 * (blocks - 1 - k) + part, slot] = below
+                for i, k in order:
+                    at, first = slice(i * CHUNK, (i + 1) * CHUNK), (FOUR * i + k) * CHUNK
+                    own_out[2 * k + part, slot, at] = placed[first : first + CHUNK]
+                    below = placed[tile_rows + first : tile_rows + first + CHUNK]
+                    next_out[2 * (FOUR - 1 - k) + part, slot, at] = below
 
 
 def patch_gradients(slot_rows, count, windows, probe_wave, patterns, tables):
-    angles, _, slots, rows, width = windows.shape
-    out = jax.ShapeDtypeStruct((angles, slots, rows, width), jnp.bfloat16)
+    angles, slots, chunks, _, width = windows.shape
+    out = jax.ShapeDtypeStruct((angles, slots, (chunks - 2) * CHUNK, width), jnp.bfloat16)
     return call(patch_body, [out, out], [], slot_rows, count, windows, probe_wave, patterns, *tables)
 
 
@@ -266,14 +313,16 @@
 def step_body(part_ref, layer, gradient, *refs):
     out, made, sems = refs[-3:]
     part = part_ref[0]
-    size = gradient.shape[0] // 4
+    chunks = gradient.shape[1] // CHUNK
+    size = FOUR * CHUNK
     copies = []
-    for n in range(4):
-        rows = slice(n * size, (n + 1) * size)
-        made[rows] = layer[part, rows].astype(jnp.float32) - step_size * gradient[rows].astype(jnp.float32)
-        copies.append(
-            pltpu.make_async_copy(made.at[pl.ds(n * size, size)], out.at[part, pl.ds(n * size, size)], sems.at[n])
-        )
+    for i in range(chunks):
+        for k in range(FOUR):
+            rows = slice(i * size + k * CHUNK, i * size + (k + 1) * CHUNK)
+            change = gradient[k, i * CHUNK : (i + 1) * CHUNK].astype(jnp.float32)
+            made[rows] = layer[part, rows].astype(jnp.float32) - step_size * change
+        at = pl.ds(i * size, size)
+        copies.append(pltpu.make_async_copy(made.at[at], out.at[part, at], sems.at[i]))
         copies[-1].start()
     for copy in copies:
         copy.wait()
@@ -286,7 +335,7 @@
         in_specs=[pl.BlockSpec(memory_space=pltpu.SMEM), VMEM, VMEM]
         + [pl.BlockSpec(memory_space=pltpu.HBM)] * len(stepped),
         out_specs=pl.BlockSpec(memory_space=pltpu.HBM),
-        scratch_shapes=[pltpu.VMEM(gradient.shape, jnp.float32), pltpu.SemaphoreType.DMA((4,))],
+        scratch_shapes=[pltpu.VMEM(layer.shape[1:], jnp.float32), pltpu.SemaphoreType.DMA((4,))],
         input_output_aliases={3: 0} if stepped else {},
         compiler_params=pltpu.CompilerParams(vmem_limit_bytes=24 * 1024 * 1024),
     )(part.reshape(1).astype(jnp.int32), layer, gradient, *stepped)
@@ -347,8 +396,10 @@
 
     own_part = lax.dynamic_index_in_dim(layer, core, 0, keepdims=False)
 
-    def rows_of(block):
-        return lax.dynamic_slice(own_part, (block * block_rows, 0), (block_rows, columns))
+    own_part = own_part.reshape(-1, FOUR, CHUNK, columns)
+
+    def rows_of(place):
+        return lax.dynamic_index_in_dim(own_part, place, 1, keepdims=False).reshape(block_rows, columns)
 
     after = mirrored(rows_of(3 - place_z), -1)
     own = rows_of(place_z)
@@ -363,7 +414,8 @@
     own = cut_windows(facts, own, 8, slots, width)
     after = to_slabs(jnp.broadcast_to(after, (slabs, *after.shape)))
     after, own = lax.optimization_barrier((after, own))
-    windows = live_to_eight(cut_rest(facts, after, own, 1), 2)
+    place = place_z.reshape(1).astype(jnp.int32)
+    windows = live_to_eight(cut_rest(facts, place, after, own, tile_rows), 1)
 
     own, after = patch_gradients(slot_rows, count, windows, probe_wave, patterns, tables)
     after, own = lax.optimization_barrier((live_to_eight(after, 1), own))
@@ -373,7 +425,7 @@
     own = jnp.sum(own.astype(f32), axis=0)
 
     total = lax.optimization_barrier((own + spill.astype(f32)).astype(bf16))
-    total = to_four(sum_copies([total, swap(total, 8)], 4)).reshape(tile_rows, columns)
+    total = to_four(sum_copies([total, swap(total, 8)], 4))
     new = step(core, layer, total)
     return step(1 - core, layer, swap(total, 1), new).reshape(volume.shape)
 

time: 168 us -> 165 us (0.982)
  blocking collectives: 59.3 us -> 56.4 us
    all_to_all x2, blocking collectives: 41.6 us -> 38.8 us  [to_eight(): lax.all_to_all(value, 'angle', 0, 0, axis_index_groups=eight_groups, tile...]
where the time goes in v15:
time: 165 us; the launch traced here: 164 us
  blocking collectives  56.4 us (34%)
  starting transfers between devices  47.2 us (29%)
  waiting for transfers between devices  39.5 us (24%)
  Pallas kernels  15.8 us (10%)
  between operations  2.21 us (1%)
  local copies, waits for them, and re-layouts  2.03 us (1%)
    all_to_all x2, blocking collectives, to_eight(): lax.all_to_all(value, 'angle', 0, 0, axis_index_groups=eight_groups, tile...  38.8 us
    ppermute x6, starting transfers between devices, to_slab(): lax.ppermute(value, 'slab', [(i, (i + by) % slabs) for i in range(slabs)])  18.6 us
    all_to_all x1, blocking collectives, to_four(): lax.all_to_all(value, 'angle', 0, 0, axis_index_groups=four_groups, tiled...  17.7 us
    ppermute x2, waiting for transfers between devices, swap(): return lax.ppermute(value, 'angle', [(i, i ^ by) for i in range(angles)])  14.6 us
    all_to_all x2, waiting for transfers between devices, to_slabs(): return lax.all_to_all(value, 'slab', 0, 0, tiled=True)  14 us
    pallas_call x6, Pallas kernels, call(): pl.pallas_call(body, out_shape=out_shape, in_specs=[smem if x.dtype == jn...  12.3 us
    all_to_all x2, starting transfers between devices, to_eight(): lax.all_to_all(value, 'angle', 0, 0, axis_index_groups=eight_groups, tile...  11.9 us
    all_to_all x2, starting transfers between devices, to_slabs(): return lax.all_to_all(value, 'slab', 0, 0, tiled=True)  8.59 us
  transfers between devices with their start and end apart: 14, of which 8 were waited for; matrix products, arithmetic and copies ran while one was open for 1% of the time, Pallas kernels for 6%

profile of v15, /device:TPU:1, one launch (start us, length us, event | category | flops | bytes accessed | tf_op | source)
XLA Modules:
  0.0 164.2 jit_solution(9389652045635167548)
XLA Ops:
  1.1 1.3 collective-permute-start
  2.4 5.2 %collective-permute-start.3 = (bf16[48,1536]{1,0:T(8,128)(2,1)S(1)}, bf16[48,1536]{1,0:T(8,128)(2,1)S(1)}, u32[]{:S(2)}, u32[]{:S(2)}) collective-permute-start(bf16[48,1536]{1,0:T(8,128)(2,1)S(1)} %bitcast.23), channel_id=1, source_target_pairs={{0,24},{8,0},{16,8},{24,16},{1,25},{9,1},{17,9},{25,17},{2,26},{10... | collective-permute-start | bytes 442376 | tf_op jit(solution)/shard_map/ppermute | solution.py:373
  7.7 2.4 %collective-permute-start.2 = (bf16[48,1536]{1,0:T(8,128)(2,1)S(1)}, bf16[48,1536]{1,0:T(8,128)(2,1)S(1)}, u32[]{:S(2)}, u32[]{:S(2)}) collective-permute-start(bf16[48,1536]{1,0:T(8,128)(2,1)S(1)} %bitcast.24), channel_id=1, source_target_pairs={{0,16},{8,24},{16,0},{24,8},{1,17},{9,25},{17,1},{25,9},{2,18},{10... | collective-permute-start | bytes 442376 | tf_op jit(solution)/shard_map/ppermute | solution.py:373
  10.1 2.5 %collective-permute-start.1 = (bf16[48,1536]{1,0:T(8,128)(2,1)S(1)}, bf16[48,1536]{1,0:T(8,128)(2,1)S(1)}, u32[]{:S(2)}, u32[]{:S(2)}) collective-permute-start(bf16[48,1536]{1,0:T(8,128)(2,1)S(1)} %bitcast.25), channel_id=1, source_target_pairs={{0,8},{8,16},{16,24},{24,0},{1,9},{9,17},{17,25},{25,1},{2,10},{10... | collective-permute-start | bytes 442376 | tf_op jit(solution)/shard_map/ppermute | solution.py:373
  13.9 1.3 shard_map.91
  15.3 7.7 %all-to-all-start.4 = ((s32[8,1,128]{2,1,0:T(1,128)}), s32[8,1,128]{2,1,0:T(1,128)S(1)}, u32[]{:S(2)}, u32[]{:S(2)}) async-start(s32[8,1,128]{2,1,0:T(1,128)} %bitcast.37), calls=%async_computation.4 | async-start | bytes 8192 | tf_op jit(solution)/shard_map/all_to_all | solution.py:376
  23.0 3.5 %collective-permute-done = bf16[48,1536]{1,0:T(8,128)(2,1)S(1)} collective-permute-done((bf16[48,1536]{1,0:T(8,128)(2,1)S(1)}, bf16[48,1536]{1,0:T(8,128)(2,1)S(1)}, u32[]{:S(2)}, u32[]{:S(2)}) %collective-permute-start) | collective-permute-done | bytes 147488 | tf_op jit(solution)/shard_map/ppermute | solution.py:370
  26.5 1.3 all-to-all-done.4
  28.6 5.1 %all-to-all-start.5 = ((bf16[4,48,1536]{2,1,0:T(8,128)(2,1)}), bf16[4,48,1536]{2,1,0:T(8,128)(2,1)S(1)}, u32[]{:S(2)}, u32[]{:S(2)}) async-start(bf16[4,48,1536]{2,1,0:T(8,128)(2,1)} %broadcast_in_dim.3), calls=%async_computation.5 | async-start | bytes 1179648 | tf_op jit(solution)/shard_map/all_to_all | solution.py:382
  35.1 1.8 %shard_map.92.done = bf16[8,2,48,256]{3,2,1,0:T(8,128)(2,1)S(1)} custom-call(s32[8,128]{1,0:T(8,128)S(1)} %bitcast.29, s32[1]{0:T(128)} %bitcast.8.slab_ref, bf16[48,1536]{1,0:T(8,128)(2,1)S(1)} %bitcast.26, bf16[48,1536]{1,0:T(8,128)(2,1)S(1)} %collective-permute-done.1.refs_1_, bf16[48,1536]{1,0:T(8,128)(2,1)S(1)} %collective-permute-done.2.refs_2_, ...), custom_call_target="tpu_custom_call" | custom-call | tf_op jit(solution)/shard_map/pallas_call | solution.py:47
  36.9 6.1 %all-to-all-done.5.blocks = bf16[4,48,1536]{2,1,0:T(8,128)(2,1)S(1)} async-done(((bf16[4,48,1536]{2,1,0:T(8,128)(2,1)}), bf16[4,48,1536]{2,1,0:T(8,128)(2,1)S(1)}, u32[]{:S(2)}, u32[]{:S(2)}) %all-to-all-start.5) | async-done | bytes 589856 | tf_op jit(solution)/shard_map/all_to_all | solution.py:382
  43.0 2.1 %shard_map.93 = bf16[8,2,5,16,256]{4,3,2,1,0:T(8,128)(2,1)S(1)} custom-call(s32[1]{0:T(128)} %bitcast.9.place_ref, s32[8,128]{1,0:T(8,128)S(1)} %bitcast.30, s32[1]{0:T(128)} %bitcast.8.slab_ref, bf16[4,48,1536]{2,1,0:T(8,128)(2,1)S(1)} %all-to-all-done.5.blocks, bf16[8,2,48,256]{3,2,1,0:T(8,128)(2,1)S(1)} %shard_map.92.done), custom_call_target="tpu_custom_call" | custom-call | tf_op jit(solution)/shard_map/pallas_call | solution.py:47
  45.1 21.7 %conditional.2 = (bf16[8,2,5,16,256]{4,3,2,1,0:T(8,128)(2,1)S(1)}) conditional(s32[]{:T(128)} %convert_element_type.25, bf16[8,2,5,16,256]{4,3,2,1,0:T(8,128)(2,1)S(1)} %shard_map.93, bf16[8,2,5,16,256]{4,3,2,1,0:T(8,128)(2,1)S(1)} %shard_map.93), branch_computations={%region_1.2_spmd, %region_2.3_spmd} | conditional | flops 327680 | bytes 3276808 | solution.py:395
  45.1 21.7 %all_to_all.48 = bf16[8,2,5,16,256]{4,3,2,1,0:T(8,128)(2,1)S(1)} all-to-all(bf16[8,2,5,16,256]{4,3,2,1,0:T(8,128)(2,1)S(1)} %param.1), channel_id=1, replica_groups={{0,32,64,96,128,160,192,224},{256,288,320,352,384,416,448,480},{1,33,65..., dimensions={0} | all-to-all | bytes 1310720 | tf_op jit(solution)/shard_map/cond/branch_1_fun/all_to_all | solution.py:376
  66.9 3.4 %shard_map.94 = (bf16[8,2,48,256]{3,2,1,0:T(8,128)(2,1)}, bf16[8,2,48,256]{3,2,1,0:T(8,128)(2,1)S(1)}) custom-call(s32[2]{0:T(128)S(1)} %bitcast.34, s32[1]{0:T(128)} %bitcast.20.count_ref, bf16[8,2,5,16,256]{4,3,2,1,0:T(8,128)(2,1)S(1)} %get-tuple-element.51.windows, f32[2,256,256]{2,1,0:T(8,128)S(1)} %copy-done.1, bf16[2,256,256]{2,1,0:T(8,128)(2,1)S(1)} %bitcast.27, ...), custom_call_target="tpu_custom_call" | custom-call | tf_op jit(solution)/shard_map/pallas_call | solution.py:47
  70.3 17.1 %conditional.3 = (bf16[8,2,48,256]{3,2,1,0:T(8,128)(2,1)S(1)}) conditional(s32[]{:T(128)} %convert_element_type.25, bf16[8,2,48,256]{3,2,1,0:T(8,128)(2,1)S(1)} %get-tuple-element.37, bf16[8,2,48,256]{3,2,1,0:T(8,128)(2,1)S(1)} %get-tuple-element.37), branch_computations={%region_3.4_spmd, %region_4.5_spmd} | conditional | flops 196608 | bytes 1966088 | solution.py:395
  70.3 17.1 %all_to_all.50 = bf16[8,2,48,256]{3,2,1,0:T(8,128)(2,1)S(1)} all-to-all(bf16[8,2,48,256]{3,2,1,0:T(8,128)(2,1)S(1)} %param.3), channel_id=1, replica_groups={{0,32,64,96,128,160,192,224},{256,288,320,352,384,416,448,480},{1,33,65..., dimensions={0} | all-to-all | bytes 786432 | tf_op jit(solution)/shard_map/cond/branch_1_fun/all_to_all | solution.py:376
  87.4 4.2 %all-to-all-start.6 = ((bf16[8,2,48,256]{3,2,1,0:T(8,128)(2,1)}), bf16[8,2,48,256]{3,2,1,0:T(8,128)(2,1)S(1)}, u32[]{:S(2)}, u32[]{:S(2)}) async-start(bf16[8,2,48,256]{3,2,1,0:T(8,128)(2,1)} %get-tuple-element.39), calls=%async_computation.6 | async-start | bytes 786432 | tf_op jit(solution)/shard_map/all_to_all | solution.py:376
  91.6 2.1 %shard_map.96 = (f32[48,1536]{1,0:T(8,128)S(1)}, bf16[48,1536]{1,0:T(8,128)(2,1)S(1)}, bf16[48,1536]{1,0:T(8,128)(2,1)S(1)}, bf16[48,1536]{1,0:T(8,128)(2,1)S(1)}) custom-call(s32[8,128]{1,0:T(8,128)S(1)} %bitcast.31, s32[1]{0:T(128)} %bitcast.8.slab_ref, bf16[8,2,48,256]{3,2,1,0:T(8,128)(2,1)S(1)} %get-tuple-element.52.windows), custom_call_target="tpu_custom_call" | custom-call | tf_op jit(solution)/shard_map/pallas_call | solution.py:47
  93.7 1.9 %collective-permute-start.4 = (bf16[48,1536]{1,0:T(8,128)(2,1)S(1)}, bf16[48,1536]{1,0:T(8,128)(2,1)S(1)}, u32[]{:S(2)}, u32[]{:S(2)}) collective-permute-start(bf16[48,1536]{1,0:T(8,128)(2,1)S(1)} %get-tuple-element.42), channel_id=1, source_target_pairs={{0,8},{8,16},{16,24},{24,0},{1,9},{9,17},{17,25},{25,1},{2,10},{10... | collective-permute-start | bytes 442376 | tf_op jit(solution)/shard_map/ppermute | solution.py:373
  95.6 1.9 %collective-permute-start.5 = (bf16[48,1536]{1,0:T(8,128)(2,1)S(1)}, bf16[48,1536]{1,0:T(8,128)(2,1)S(1)}, u32[]{:S(2)}, u32[]{:S(2)}) collective-permute-start(bf16[48,1536]{1,0:T(8,128)(2,1)S(1)} %get-tuple-element.43), channel_id=1, source_target_pairs={{0,16},{8,24},{16,0},{24,8},{1,17},{9,25},{17,1},{25,9},{2,18},{10... | collective-permute-start | bytes 442376 | tf_op jit(solution)/shard_map/ppermute | solution.py:373
  97.6 4.6 %collective-permute-start.6 = (bf16[48,1536]{1,0:T(8,128)(2,1)S(1)}, bf16[48,1536]{1,0:T(8,128)(2,1)S(1)}, u32[]{:S(2)}, u32[]{:S(2)}) collective-permute-start(bf16[48,1536]{1,0:T(8,128)(2,1)S(1)} %get-tuple-element.44), channel_id=1, source_target_pairs={{0,24},{8,0},{16,8},{24,16},{1,25},{9,1},{17,9},{25,17},{2,26},{10... | collective-permute-start | bytes 442376 | tf_op jit(solution)/shard_map/ppermute | solution.py:373
  102.2 1.1 all-to-all-done.6.windows
  103.3 2.9 %shard_map.95 = bf16[4,48,1536]{2,1,0:T(8,128)(2,1)} custom-call(s32[8,128]{1,0:T(8,128)S(1)} %bitcast.32, s32[1]{0:T(128)} %bitcast.8.slab_ref, bf16[8,2,48,256]{3,2,1,0:T(8,128)(2,1)S(1)} %all-to-all-done.6.windows), custom_call_target="tpu_custom_call" | custom-call | tf_op jit(solution)/shard_map/pallas_call | solution.py:47
  106.2 3.5 %all-to-all-start.7 = ((bf16[4,48,1536]{2,1,0:T(8,128)(2,1)}), bf16[4,48,1536]{2,1,0:T(8,128)(2,1)S(1)}, u32[]{:S(2)}, u32[]{:S(2)}) async-start(bf16[4,48,1536]{2,1,0:T(8,128)(2,1)} %shard_map.95), calls=%async_computation.7 | async-start | bytes 1179648 | tf_op jit(solution)/shard_map/all_to_all | solution.py:382
  109.8 1.3 collective-permute-start.7
  111.1 7.9 %all-to-all-done.7 = bf16[4,48,1536]{2,1,0:T(8,128)(2,1)S(1)} async-done(((bf16[4,48,1536]{2,1,0:T(8,128)(2,1)}), bf16[4,48,1536]{2,1,0:T(8,128)(2,1)S(1)}, u32[]{:S(2)}, u32[]{:S(2)}) %all-to-all-start.7) | async-done | bytes 589856 | tf_op jit(solution)/shard_map/all_to_all | solution.py:382
  119.1 5.0 %collective-permute-done.7 = bf16[48,1536]{1,0:T(8,128)(2,1)S(1)} collective-permute-done((bf16[48,1536]{1,0:T(8,128)(2,1)S(1)}, bf16[48,1536]{1,0:T(8,128)(2,1)S(1)}, u32[]{:S(2)}, u32[]{:S(2)}) %collective-permute-start.7) | collective-permute-done | bytes 147488 | tf_op jit(solution)/shard_map/ppermute | solution.py:370
  124.1 2.1 %collective-permute-start.8 = (bf16[48,1536]{1,0:T(8,128)(2,1)S(1)}, bf16[48,1536]{1,0:T(8,128)(2,1)S(1)}, u32[]{:S(2)}, u32[]{:S(2)}) collective-permute-start(bf16[48,1536]{1,0:T(8,128)(2,1)S(1)} %add_convert_fusion.refs_0_), channel_id=1, source_target_pairs={{0,256},{32,288},{64,320},{96,352},{128,384},{160,416},{192,448},{... | collective-permute-start | bytes 442376 | tf_op jit(solution)/shard_map/ppermute | solution.py:361
  126.2 14.1 %collective-permute-done.8.refs_1_ = bf16[48,1536]{1,0:T(8,128)(2,1)S(1)} collective-permute-done((bf16[48,1536]{1,0:T(8,128)(2,1)S(1)}, bf16[48,1536]{1,0:T(8,128)(2,1)S(1)}, u32[]{:S(2)}, u32[]{:S(2)}) %collective-permute-start.8) | collective-permute-done | bytes 147488 | tf_op jit(solution)/shard_map/ppermute | solution.py:361
  140.4 17.7 %all_to_all.51.gradient = bf16[4,48,1536]{2,1,0:T(8,128)(2,1)S(1)} all-to-all(bf16[4,48,1536]{2,1,0:T(8,128)(2,1)S(1)} %shard_map.97), channel_id=1, replica_groups={{0,64,128,192},{32,96,160,224},{256,320,384,448},{288,352,416,480},{1,6..., dimensions={0} | all-to-all | bytes 1179648 | tf_op jit(solution)/shard_map/all_to_all | solution.py:379
  158.0 3.5 %collective-permute-start.9 = (bf16[4,48,1536]{2,1,0:T(8,128)(2,1)S(1)}, bf16[4,48,1536]{2,1,0:T(8,128)(2,1)S(1)}, u32[]{:S(2)}, u32[]{:S(2)}) collective-permute-start(bf16[4,48,1536]{2,1,0:T(8,128)(2,1)S(1)} %all_to_all.51.gradient), channel_id=1, source_target_pairs={{0,32},{32,0},{64,96},{96,64},{128,160},{160,128},{192,224},{224,1... | collective-permute-start | bytes 1769480 | tf_op jit(solution)/shard_map/ppermute | solution.py:361
  (29 shorter events, 5.7 us)
Async XLA Ops:
  1.1 25.3 %collective-permute-start = (bf16[48,1536]{1,0:T(8,128)(2,1)S(1)}, bf16[48,1536]{1,0:T(8,128)(2,1)S(1)}, u32[]{:S(2)}, u32[]{:S(2)}) collective-permute-start(bf16[48,1536]{1,0:T(8,128)(2,1)S(1)} %bitcast.36), channel_id=1, source_target_pairs={{1,448},{2,449},{3,450},{4,451},{5,452},{6,453},{7,454},{33,480},{... | collective-permute-start | bytes 442376 | tf_op jit(solution)/shard_map/ppermute | solution.py:370
  2.4 24.0 %collective-permute-start.3 = (bf16[48,1536]{1,0:T(8,128)(2,1)S(1)}, bf16[48,1536]{1,0:T(8,128)(2,1)S(1)}, u32[]{:S(2)}, u32[]{:S(2)}) collective-permute-start(bf16[48,1536]{1,0:T(8,128)(2,1)S(1)} %bitcast.23), channel_id=1, source_target_pairs={{0,24},{8,0},{16,8},{24,16},{1,25},{9,1},{17,9},{25,17},{2,26},{10... | collective-permute-start | bytes 442376 | tf_op jit(solution)/shard_map/ppermute | solution.py:373
  7.7 18.8 %collective-permute-start.2 = (bf16[48,1536]{1,0:T(8,128)(2,1)S(1)}, bf16[48,1536]{1,0:T(8,128)(2,1)S(1)}, u32[]{:S(2)}, u32[]{:S(2)}) collective-permute-start(bf16[48,1536]{1,0:T(8,128)(2,1)S(1)} %bitcast.24), channel_id=1, source_target_pairs={{0,16},{8,24},{16,0},{24,8},{1,17},{9,25},{17,1},{25,9},{2,18},{10... | collective-permute-start | bytes 442376 | tf_op jit(solution)/shard_map/ppermute | solution.py:373
  10.1 16.4 %collective-permute-start.1 = (bf16[48,1536]{1,0:T(8,128)(2,1)S(1)}, bf16[48,1536]{1,0:T(8,128)(2,1)S(1)}, u32[]{:S(2)}, u32[]{:S(2)}) collective-permute-start(bf16[48,1536]{1,0:T(8,128)(2,1)S(1)} %bitcast.25), channel_id=1, source_target_pairs={{0,8},{8,16},{16,24},{24,0},{1,9},{9,17},{17,25},{25,1},{2,10},{10... | collective-permute-start | bytes 442376 | tf_op jit(solution)/shard_map/ppermute | solution.py:373
  15.3 12.5 %all-to-all-start.4 = ((s32[8,1,128]{2,1,0:T(1,128)}), s32[8,1,128]{2,1,0:T(1,128)S(1)}, u32[]{:S(2)}, u32[]{:S(2)}) async-start(s32[8,1,128]{2,1,0:T(1,128)} %bitcast.37), calls=%async_computation.4 | async-start | bytes 8192 | tf_op jit(solution)/shard_map/all_to_all | solution.py:376
  28.6 14.3 %all-to-all-start.5 = ((bf16[4,48,1536]{2,1,0:T(8,128)(2,1)}), bf16[4,48,1536]{2,1,0:T(8,128)(2,1)S(1)}, u32[]{:S(2)}, u32[]{:S(2)}) async-start(bf16[4,48,1536]{2,1,0:T(8,128)(2,1)} %broadcast_in_dim.3), calls=%async_computation.5 | async-start | bytes 1179648 | tf_op jit(solution)/shard_map/all_to_all | solution.py:382
  45.1 21.8 %copy-start.1 = (f32[2,256,256]{2,1,0:T(8,128)S(1)}, f32[2,256,256]{2,1,0:T(8,128)}, u32[]{:S(2)}) copy-start(f32[2,256,256]{2,1,0:T(8,128)} %probe.1) | copy-start | bytes 1572868
  45.1 21.8 %copy-start.2 = (bf16[1,1,1,2,256,256]{5,4,3,2,1,0:T(8,128)(2,1)S(1)}, bf16[1,1,1,2,256,256]{5,4,3,2,1,0:T(8,128)(2,1)}, u32[]{:S(2)}) copy-start(bf16[1,1,1,2,256,256]{5,4,3,2,1,0:T(8,128)(2,1)} %param.15) | copy-start | bytes 786436
  45.1 21.8 %copy-start.3 = (bf16[256,256]{1,0:T(8,128)(2,1)S(1)}, bf16[256,256]{1,0:T(8,128)(2,1)}, u32[]{:S(2)}) copy-start(bf16[256,256]{1,0:T(8,128)(2,1)} %constant.70.clone.wi_ref) | copy-start | bytes 393220
  45.1 21.8 %copy-start.4 = (bf16[256,256]{1,0:T(8,128)(2,1)S(1)}, bf16[256,256]{1,0:T(8,128)(2,1)}, u32[]{:S(2)}) copy-start(bf16[256,256]{1,0:T(8,128)(2,1)} %constant.69.clone.wr_ref) | copy-start | bytes 393220
  45.1 21.8 %copy-start.5 = (s32[1,1,1,2]{3,2,1,0:T(1,128)S(1)}, s32[1,1,1,2]{3,2,1,0:T(1,128)}, u32[]{:S(2)}) copy-start(s32[1,1,1,2]{3,2,1,0:T(1,128)} %param.16) | copy-start | bytes 28
  87.4 15.9 %all-to-all-start.6 = ((bf16[8,2,48,256]{3,2,1,0:T(8,128)(2,1)}), bf16[8,2,48,256]{3,2,1,0:T(8,128)(2,1)S(1)}, u32[]{:S(2)}, u32[]{:S(2)}) async-start(bf16[8,2,48,256]{3,2,1,0:T(8,128)(2,1)} %get-tuple-element.39), calls=%async_computation.6 | async-start | bytes 786432 | tf_op jit(solution)/shard_map/all_to_all | solution.py:376
  93.7 16.0 %collective-permute-start.4 = (bf16[48,1536]{1,0:T(8,128)(2,1)S(1)}, bf16[48,1536]{1,0:T(8,128)(2,1)S(1)}, u32[]{:S(2)}, u32[]{:S(2)}) collective-permute-start(bf16[48,1536]{1,0:T(8,128)(2,1)S(1)} %get-tuple-element.42), channel_id=1, source_target_pairs={{0,8},{8,16},{16,24},{24,0},{1,9},{9,17},{17,25},{25,1},{2,10},{10... | collective-permute-start | bytes 442376 | tf_op jit(solution)/shard_map/ppermute | solution.py:373
  95.6 14.1 %collective-permute-start.5 = (bf16[48,1536]{1,0:T(8,128)(2,1)S(1)}, bf16[48,1536]{1,0:T(8,128)(2,1)S(1)}, u32[]{:S(2)}, u32[]{:S(2)}) collective-permute-start(bf16[48,1536]{1,0:T(8,128)(2,1)S(1)} %get-tuple-element.43), channel_id=1, source_target_pairs={{0,16},{8,24},{16,0},{24,8},{1,17},{9,25},{17,1},{25,9},{2,18},{10... | collective-permute-start | bytes 442376 | tf_op jit(solution)/shard_map/ppermute | solution.py:373
  97.6 12.1 %collective-permute-start.6 = (bf16[48,1536]{1,0:T(8,128)(2,1)S(1)}, bf16[48,1536]{1,0:T(8,128)(2,1)S(1)}, u32[]{:S(2)}, u32[]{:S(2)}) collective-permute-start(bf16[48,1536]{1,0:T(8,128)(2,1)S(1)} %get-tuple-element.44), channel_id=1, source_target_pairs={{0,24},{8,0},{16,8},{24,16},{1,25},{9,1},{17,9},{25,17},{2,26},{10... | collective-permute-start | bytes 442376 | tf_op jit(solution)/shard_map/ppermute | solution.py:373
  106.2 12.8 %all-to-all-start.7 = ((bf16[4,48,1536]{2,1,0:T(8,128)(2,1)}), bf16[4,48,1536]{2,1,0:T(8,128)(2,1)S(1)}, u32[]{:S(2)}, u32[]{:S(2)}) async-start(bf16[4,48,1536]{2,1,0:T(8,128)(2,1)} %shard_map.95), calls=%async_computation.7 | async-start | bytes 1179648 | tf_op jit(solution)/shard_map/all_to_all | solution.py:382
  109.8 14.3 %collective-permute-start.7 = (bf16[48,1536]{1,0:T(8,128)(2,1)S(1)}, bf16[48,1536]{1,0:T(8,128)(2,1)S(1)}, u32[]{:S(2)}, u32[]{:S(2)}) collective-permute-start(bf16[48,1536]{1,0:T(8,128)(2,1)S(1)} %add_convert_fusion.1), channel_id=1, source_target_pairs={{0,449},{1,450},{2,451},{3,452},{4,453},{5,454},{6,455},{32,481},{... | collective-permute-start | bytes 442376 | tf_op jit(solution)/shard_map/ppermute | solution.py:370
  124.1 37.4 %copy-start = (bf16[2,1,192,1536]{3,2,1,0:T(8,128)(2,1)S(1)}, bf16[2,1,192,1536]{3,2,1,0:T(8,128)(2,1)}, u32[]{:S(2)}) copy-start(bf16[2,1,192,1536]{3,2,1,0:T(8,128)(2,1)} %param.13) | copy-start | bytes 3538948
  124.1 16.2 %collective-permute-start.8 = (bf16[48,1536]{1,0:T(8,128)(2,1)S(1)}, bf16[48,1536]{1,0:T(8,128)(2,1)S(1)}, u32[]{:S(2)}, u32[]{:S(2)}) collective-permute-start(bf16[48,1536]{1,0:T(8,128)(2,1)S(1)} %add_convert_fusion.refs_0_), channel_id=1, source_target_pairs={{0,256},{32,288},{64,320},{96,352},{128,384},{160,416},{192,448},{... | collective-permute-start | bytes 442376 | tf_op jit(solution)/shard_map/ppermute | solution.py:361
  158.0 5.1 %collective-permute-start.9 = (bf16[4,48,1536]{2,1,0:T(8,128)(2,1)S(1)}, bf16[4,48,1536]{2,1,0:T(8,128)(2,1)S(1)}, u32[]{:S(2)}, u32[]{:S(2)}) collective-permute-start(bf16[4,48,1536]{2,1,0:T(8,128)(2,1)S(1)} %all_to_all.51.gradient), channel_id=1, source_target_pairs={{0,32},{32,0},{64,96},{96,64},{128,160},{160,128},{192,224},{224,1... | collective-permute-start | bytes 1769480 | tf_op jit(solution)/shard_map/ppermute | solution.py:361

commit v16 on v15

--- a/solution.py
+++ b/solution.py
@@ -127,11 +127,14 @@
                     layer = k if absolute else facts.layer(-k)
                     starts, inside = facts.columns_of(angle, slot, layer)
                     turned = [
-                        pltpu.roll(block[:, pl.ds(start, LANE)].astype(jnp.float32), (LANE - inside) & (LANE - 1), 1)
+                        pltpu.roll(block[:, pl.ds(start, LANE)], (LANE - inside) & (LANE - 1), 1)
                         for start in starts
                     ]
                     here = lane < LANE - inside
-                    total = [t + jnp.where(here, turned[i], turned[i + 1]) for i, t in enumerate(total)]
+                    total = [
+                        t + jnp.where(here, turned[i], turned[i + 1]).astype(jnp.float32)
+                        for i, t in enumerate(total)
+                    ]
                 put(out, angle, slot, jnp.concatenate(total, axis=1).astype(jnp.bfloat16))
 
 
@@ -300,7 +303,9 @@
 
 def sum_body(*refs):
     *terms, out = refs
-    total = sum(term[...].astype(jnp.float32) for term in terms).astype(out.dtype)
+    total = terms[0][...]
+    if len(terms) > 1:
+        total = sum(term[...].astype(jnp.float32) for term in terms).astype(out.dtype)
     for k in range(out.shape[0]):
         out[k] = total
 
@@ -412,7 +417,7 @@
     own = of_slabs(own)
     after, own = lax.optimization_barrier((after, own))
     own = cut_windows(facts, own, 8, slots, width)
-    after = to_slabs(jnp.broadcast_to(after, (slabs, *after.shape)))
+    after = to_slabs(sum_copies([after], slabs))
     after, own = lax.optimization_barrier((after, own))
     place = place_z.reshape(1).astype(jnp.int32)
     windows = live_to_eight(cut_rest(facts, place, after, own, tile_rows), 1)

time: 165 us -> 164 us (level)
    pallas_call x6 -> x7, Pallas kernels: 12.3 us -> 13.1 us  [call(): pl.pallas_call(body, out_shape=out_shape, in_specs=[smem if x.dtype == jn...]
where the time goes in v16:
time: 164 us; the launch traced here: 163 us
  blocking collectives  56.4 us (34%)
  starting transfers between devices  47.3 us (29%)
  waiting for transfers between devices  38.8 us (24%)
  Pallas kernels  16.6 us (10%)
  between operations  2.21 us (1%)
    all_to_all x2, blocking collectives, to_eight(): lax.all_to_all(value, 'angle', 0, 0, axis_index_groups=eight_groups, tile...  38.8 us
    ppermute x6, starting transfers between devices, to_slab(): lax.ppermute(value, 'slab', [(i, (i + by) % slabs) for i in range(slabs)])  18.6 us
    all_to_all x1, blocking collectives, to_four(): lax.all_to_all(value, 'angle', 0, 0, axis_index_groups=four_groups, tiled...  17.7 us
    ppermute x2, waiting for transfers between devices, swap(): return lax.ppermute(value, 'angle', [(i, i ^ by) for i in range(angles)])  14.6 us
    all_to_all x2, waiting for transfers between devices, to_slabs(): return lax.all_to_all(value, 'slab', 0, 0, tiled=True)  14 us
    pallas_call x7, Pallas kernels, call(): pl.pallas_call(body, out_shape=out_shape, in_specs=[smem if x.dtype == jn...  13.1 us
    all_to_all x2, starting transfers between devices, to_eight(): lax.all_to_all(value, 'angle', 0, 0, axis_index_groups=eight_groups, tile...  12 us
    all_to_all x2, starting transfers between devices, to_slabs(): return lax.all_to_all(value, 'slab', 0, 0, tiled=True)  8.59 us
  transfers between devices with their start and end apart: 14, of which 8 were waited for; matrix products, arithmetic and copies ran while one was open for 1% of the time, Pallas kernels for 6%

profile of v16, /device:TPU:1, one launch (start us, length us, event | category | flops | bytes accessed | tf_op | source)
XLA Modules:
  0.0 163.4 jit_solution(5645690525968765252)
XLA Ops:
  0.0 1.1 constant_dynamic-slice_fusion.2
  1.1 1.3 collective-permute-start
  2.4 5.2 %collective-permute-start.3 = (bf16[48,1536]{1,0:T(8,128)(2,1)S(1)}, bf16[48,1536]{1,0:T(8,128)(2,1)S(1)}, u32[]{:S(2)}, u32[]{:S(2)}) collective-permute-start(bf16[48,1536]{1,0:T(8,128)(2,1)S(1)} %bitcast.23), channel_id=1, source_target_pairs={{0,24},{8,0},{16,8},{24,16},{1,25},{9,1},{17,9},{25,17},{2,26},{10... | collective-permute-start | bytes 442376 | tf_op jit(solution)/shard_map/ppermute | solution.py:378
  7.7 2.4 %collective-permute-start.2 = (bf16[48,1536]{1,0:T(8,128)(2,1)S(1)}, bf16[48,1536]{1,0:T(8,128)(2,1)S(1)}, u32[]{:S(2)}, u32[]{:S(2)}) collective-permute-start(bf16[48,1536]{1,0:T(8,128)(2,1)S(1)} %bitcast.24), channel_id=1, source_target_pairs={{0,16},{8,24},{16,0},{24,8},{1,17},{9,25},{17,1},{25,9},{2,18},{10... | collective-permute-start | bytes 442376 | tf_op jit(solution)/shard_map/ppermute | solution.py:378
  10.1 2.5 %collective-permute-start.1 = (bf16[48,1536]{1,0:T(8,128)(2,1)S(1)}, bf16[48,1536]{1,0:T(8,128)(2,1)S(1)}, u32[]{:S(2)}, u32[]{:S(2)}) collective-permute-start(bf16[48,1536]{1,0:T(8,128)(2,1)S(1)} %bitcast.25), channel_id=1, source_target_pairs={{0,8},{8,16},{16,24},{24,0},{1,9},{9,17},{17,25},{25,1},{2,10},{10... | collective-permute-start | bytes 442376 | tf_op jit(solution)/shard_map/ppermute | solution.py:378
  13.9 1.3 shard_map.91
  15.3 7.7 %all-to-all-start.4 = ((s32[8,1,128]{2,1,0:T(1,128)}), s32[8,1,128]{2,1,0:T(1,128)S(1)}, u32[]{:S(2)}, u32[]{:S(2)}) async-start(s32[8,1,128]{2,1,0:T(1,128)} %bitcast.37), calls=%async_computation.4 | async-start | bytes 8192 | tf_op jit(solution)/shard_map/all_to_all | solution.py:381
  23.0 3.5 %collective-permute-done.refs_0_ = bf16[48,1536]{1,0:T(8,128)(2,1)S(1)} collective-permute-done((bf16[48,1536]{1,0:T(8,128)(2,1)S(1)}, bf16[48,1536]{1,0:T(8,128)(2,1)S(1)}, u32[]{:S(2)}, u32[]{:S(2)}) %collective-permute-start) | collective-permute-done | bytes 147488 | tf_op jit(solution)/shard_map/ppermute | solution.py:375
  27.9 5.1 %all-to-all-start.5 = ((bf16[4,48,1536]{2,1,0:T(8,128)(2,1)}), bf16[4,48,1536]{2,1,0:T(8,128)(2,1)S(1)}, u32[]{:S(2)}, u32[]{:S(2)}) async-start(bf16[4,48,1536]{2,1,0:T(8,128)(2,1)} %shard_map.92), calls=%async_computation.5 | async-start | bytes 1179648 | tf_op jit(solution)/shard_map/all_to_all | solution.py:387
  34.4 1.8 %shard_map.93.done = bf16[8,2,48,256]{3,2,1,0:T(8,128)(2,1)S(1)} custom-call(s32[8,128]{1,0:T(8,128)S(1)} %bitcast.29, s32[1]{0:T(128)} %bitcast.8.slab_ref, bf16[48,1536]{1,0:T(8,128)(2,1)S(1)} %bitcast.26, bf16[48,1536]{1,0:T(8,128)(2,1)S(1)} %collective-permute-done.1.refs_1_, bf16[48,1536]{1,0:T(8,128)(2,1)S(1)} %collective-permute-done.2.refs_2_, ...), custom_call_target="tpu_custom_call" | custom-call | tf_op jit(solution)/shard_map/pallas_call | solution.py:47
  36.1 6.1 %all-to-all-done.5.blocks = bf16[4,48,1536]{2,1,0:T(8,128)(2,1)S(1)} async-done(((bf16[4,48,1536]{2,1,0:T(8,128)(2,1)}), bf16[4,48,1536]{2,1,0:T(8,128)(2,1)S(1)}, u32[]{:S(2)}, u32[]{:S(2)}) %all-to-all-start.5) | async-done | bytes 589856 | tf_op jit(solution)/shard_map/all_to_all | solution.py:387
  42.2 2.0 %shard_map.94 = bf16[8,2,5,16,256]{4,3,2,1,0:T(8,128)(2,1)S(1)} custom-call(s32[1]{0:T(128)} %bitcast.9.place_ref, s32[8,128]{1,0:T(8,128)S(1)} %bitcast.30, s32[1]{0:T(128)} %bitcast.8.slab_ref, bf16[4,48,1536]{2,1,0:T(8,128)(2,1)S(1)} %all-to-all-done.5.blocks, bf16[8,2,48,256]{3,2,1,0:T(8,128)(2,1)S(1)} %shard_map.93.done), custom_call_target="tpu_custom_call" | custom-call | tf_op jit(solution)/shard_map/pallas_call | solution.py:47
  44.3 21.7 %conditional.2 = (bf16[8,2,5,16,256]{4,3,2,1,0:T(8,128)(2,1)S(1)}) conditional(s32[]{:T(128)} %convert_element_type.25, bf16[8,2,5,16,256]{4,3,2,1,0:T(8,128)(2,1)S(1)} %shard_map.94, bf16[8,2,5,16,256]{4,3,2,1,0:T(8,128)(2,1)S(1)} %shard_map.94), branch_computations={%region_1.2_spmd, %region_2.3_spmd} | conditional | flops 327680 | bytes 3276808 | solution.py:400
  44.3 21.7 %all_to_all.48 = bf16[8,2,5,16,256]{4,3,2,1,0:T(8,128)(2,1)S(1)} all-to-all(bf16[8,2,5,16,256]{4,3,2,1,0:T(8,128)(2,1)S(1)} %param.1), channel_id=1, replica_groups={{0,32,64,96,128,160,192,224},{256,288,320,352,384,416,448,480},{1,33,65..., dimensions={0} | all-to-all | bytes 1310720 | tf_op jit(solution)/shard_map/cond/branch_1_fun/all_to_all | solution.py:381
  66.1 3.4 %shard_map.95 = (bf16[8,2,48,256]{3,2,1,0:T(8,128)(2,1)}, bf16[8,2,48,256]{3,2,1,0:T(8,128)(2,1)S(1)}) custom-call(s32[2]{0:T(128)S(1)} %bitcast.34, s32[1]{0:T(128)} %bitcast.20.count_ref, bf16[8,2,5,16,256]{4,3,2,1,0:T(8,128)(2,1)S(1)} %get-tuple-element.51.windows, f32[2,256,256]{2,1,0:T(8,128)S(1)} %copy-done.1, bf16[2,256,256]{2,1,0:T(8,128)(2,1)S(1)} %bitcast.27, ...), custom_call_target="tpu_custom_call" | custom-call | tf_op jit(solution)/shard_map/pallas_call | solution.py:47
  69.5 17.1 %conditional.3 = (bf16[8,2,48,256]{3,2,1,0:T(8,128)(2,1)S(1)}) conditional(s32[]{:T(128)} %convert_element_type.25, bf16[8,2,48,256]{3,2,1,0:T(8,128)(2,1)S(1)} %get-tuple-element.37, bf16[8,2,48,256]{3,2,1,0:T(8,128)(2,1)S(1)} %get-tuple-element.37), branch_computations={%region_3.4_spmd, %region_4.5_spmd} | conditional | flops 196608 | bytes 1966088 | solution.py:400
  69.5 17.1 %all_to_all.50 = bf16[8,2,48,256]{3,2,1,0:T(8,128)(2,1)S(1)} all-to-all(bf16[8,2,48,256]{3,2,1,0:T(8,128)(2,1)S(1)} %param.3), channel_id=1, replica_groups={{0,32,64,96,128,160,192,224},{256,288,320,352,384,416,448,480},{1,33,65..., dimensions={0} | all-to-all | bytes 786432 | tf_op jit(solution)/shard_map/cond/branch_1_fun/all_to_all | solution.py:381
  86.6 4.2 %all-to-all-start.6 = ((bf16[8,2,48,256]{3,2,1,0:T(8,128)(2,1)}), bf16[8,2,48,256]{3,2,1,0:T(8,128)(2,1)S(1)}, u32[]{:S(2)}, u32[]{:S(2)}) async-start(bf16[8,2,48,256]{3,2,1,0:T(8,128)(2,1)} %get-tuple-element.39), calls=%async_computation.6 | async-start | bytes 786432 | tf_op jit(solution)/shard_map/all_to_all | solution.py:381
  90.8 2.1 %shard_map.97 = (f32[48,1536]{1,0:T(8,128)S(1)}, bf16[48,1536]{1,0:T(8,128)(2,1)S(1)}, bf16[48,1536]{1,0:T(8,128)(2,1)S(1)}, bf16[48,1536]{1,0:T(8,128)(2,1)S(1)}) custom-call(s32[8,128]{1,0:T(8,128)S(1)} %bitcast.31, s32[1]{0:T(128)} %bitcast.8.slab_ref, bf16[8,2,48,256]{3,2,1,0:T(8,128)(2,1)S(1)} %get-tuple-element.52.windows), custom_call_target="tpu_custom_call" | custom-call | tf_op jit(solution)/shard_map/pallas_call | solution.py:47
  92.9 1.9 %collective-permute-start.4 = (bf16[48,1536]{1,0:T(8,128)(2,1)S(1)}, bf16[48,1536]{1,0:T(8,128)(2,1)S(1)}, u32[]{:S(2)}, u32[]{:S(2)}) collective-permute-start(bf16[48,1536]{1,0:T(8,128)(2,1)S(1)} %get-tuple-element.42), channel_id=1, source_target_pairs={{0,8},{8,16},{16,24},{24,0},{1,9},{9,17},{17,25},{25,1},{2,10},{10... | collective-permute-start | bytes 442376 | tf_op jit(solution)/shard_map/ppermute | solution.py:378
  94.9 1.9 %collective-permute-start.5 = (bf16[48,1536]{1,0:T(8,128)(2,1)S(1)}, bf16[48,1536]{1,0:T(8,128)(2,1)S(1)}, u32[]{:S(2)}, u32[]{:S(2)}) collective-permute-start(bf16[48,1536]{1,0:T(8,128)(2,1)S(1)} %get-tuple-element.43), channel_id=1, source_target_pairs={{0,16},{8,24},{16,0},{24,8},{1,17},{9,25},{17,1},{25,9},{2,18},{10... | collective-permute-start | bytes 442376 | tf_op jit(solution)/shard_map/ppermute | solution.py:378
  96.8 4.6 %collective-permute-start.6 = (bf16[48,1536]{1,0:T(8,128)(2,1)S(1)}, bf16[48,1536]{1,0:T(8,128)(2,1)S(1)}, u32[]{:S(2)}, u32[]{:S(2)}) collective-permute-start(bf16[48,1536]{1,0:T(8,128)(2,1)S(1)} %get-tuple-element.44), channel_id=1, source_target_pairs={{0,24},{8,0},{16,8},{24,16},{1,25},{9,1},{17,9},{25,17},{2,26},{10... | collective-permute-start | bytes 442376 | tf_op jit(solution)/shard_map/ppermute | solution.py:378
  101.4 1.1 all-to-all-done.6.windows
  102.5 2.9 %shard_map.96 = bf16[4,48,1536]{2,1,0:T(8,128)(2,1)} custom-call(s32[8,128]{1,0:T(8,128)S(1)} %bitcast.32, s32[1]{0:T(128)} %bitcast.8.slab_ref, bf16[8,2,48,256]{3,2,1,0:T(8,128)(2,1)S(1)} %all-to-all-done.6.windows), custom_call_target="tpu_custom_call" | custom-call | tf_op jit(solution)/shard_map/pallas_call | solution.py:47
  105.4 3.5 %all-to-all-start.7 = ((bf16[4,48,1536]{2,1,0:T(8,128)(2,1)}), bf16[4,48,1536]{2,1,0:T(8,128)(2,1)S(1)}, u32[]{:S(2)}, u32[]{:S(2)}) async-start(bf16[4,48,1536]{2,1,0:T(8,128)(2,1)} %shard_map.96), calls=%async_computation.7 | async-start | bytes 1179648 | tf_op jit(solution)/shard_map/all_to_all | solution.py:387
  109.0 1.3 collective-permute-start.7
  110.3 7.9 %all-to-all-done.7 = bf16[4,48,1536]{2,1,0:T(8,128)(2,1)S(1)} async-done(((bf16[4,48,1536]{2,1,0:T(8,128)(2,1)}), bf16[4,48,1536]{2,1,0:T(8,128)(2,1)S(1)}, u32[]{:S(2)}, u32[]{:S(2)}) %all-to-all-start.7) | async-done | bytes 589856 | tf_op jit(solution)/shard_map/all_to_all | solution.py:387
  118.3 5.0 %collective-permute-done.7 = bf16[48,1536]{1,0:T(8,128)(2,1)S(1)} collective-permute-done((bf16[48,1536]{1,0:T(8,128)(2,1)S(1)}, bf16[48,1536]{1,0:T(8,128)(2,1)S(1)}, u32[]{:S(2)}, u32[]{:S(2)}) %collective-permute-start.7) | collective-permute-done | bytes 147488 | tf_op jit(solution)/shard_map/ppermute | solution.py:375
  123.3 2.1 %collective-permute-start.8 = (bf16[48,1536]{1,0:T(8,128)(2,1)S(1)}, bf16[48,1536]{1,0:T(8,128)(2,1)S(1)}, u32[]{:S(2)}, u32[]{:S(2)}) collective-permute-start(bf16[48,1536]{1,0:T(8,128)(2,1)S(1)} %add_convert_fusion.refs_0_), channel_id=1, source_target_pairs={{0,256},{32,288},{64,320},{96,352},{128,384},{160,416},{192,448},{... | collective-permute-start | bytes 442376 | tf_op jit(solution)/shard_map/ppermute | solution.py:366
  125.4 14.1 %collective-permute-done.8.refs_1_ = bf16[48,1536]{1,0:T(8,128)(2,1)S(1)} collective-permute-done((bf16[48,1536]{1,0:T(8,128)(2,1)S(1)}, bf16[48,1536]{1,0:T(8,128)(2,1)S(1)}, u32[]{:S(2)}, u32[]{:S(2)}) %collective-permute-start.8) | collective-permute-done | bytes 147488 | tf_op jit(solution)/shard_map/ppermute | solution.py:366
  139.6 17.7 %all_to_all.51.gradient = bf16[4,48,1536]{2,1,0:T(8,128)(2,1)S(1)} all-to-all(bf16[4,48,1536]{2,1,0:T(8,128)(2,1)S(1)} %shard_map.98), channel_id=1, replica_groups={{0,64,128,192},{32,96,160,224},{256,320,384,448},{288,352,416,480},{1,6..., dimensions={0} | all-to-all | bytes 1179648 | tf_op jit(solution)/shard_map/all_to_all | solution.py:384
  157.3 3.5 %collective-permute-start.9 = (bf16[4,48,1536]{2,1,0:T(8,128)(2,1)S(1)}, bf16[4,48,1536]{2,1,0:T(8,128)(2,1)S(1)}, u32[]{:S(2)}, u32[]{:S(2)}) collective-permute-start(bf16[4,48,1536]{2,1,0:T(8,128)(2,1)S(1)} %all_to_all.51.gradient), channel_id=1, source_target_pairs={{0,32},{32,0},{64,96},{96,64},{128,160},{160,128},{192,224},{224,1... | collective-permute-start | bytes 1769480 | tf_op jit(solution)/shard_map/ppermute | solution.py:366
  (29 shorter events, 5.1 us)
Async XLA Ops:
  1.1 25.3 %collective-permute-start = (bf16[48,1536]{1,0:T(8,128)(2,1)S(1)}, bf16[48,1536]{1,0:T(8,128)(2,1)S(1)}, u32[]{:S(2)}, u32[]{:S(2)}) collective-permute-start(bf16[48,1536]{1,0:T(8,128)(2,1)S(1)} %bitcast.36), channel_id=1, source_target_pairs={{1,448},{2,449},{3,450},{4,451},{5,452},{6,453},{7,454},{33,480},{... | collective-permute-start | bytes 442376 | tf_op jit(solution)/shard_map/ppermute | solution.py:375
  2.4 24.0 %collective-permute-start.3 = (bf16[48,1536]{1,0:T(8,128)(2,1)S(1)}, bf16[48,1536]{1,0:T(8,128)(2,1)S(1)}, u32[]{:S(2)}, u32[]{:S(2)}) collective-permute-start(bf16[48,1536]{1,0:T(8,128)(2,1)S(1)} %bitcast.23), channel_id=1, source_target_pairs={{0,24},{8,0},{16,8},{24,16},{1,25},{9,1},{17,9},{25,17},{2,26},{10... | collective-permute-start | bytes 442376 | tf_op jit(solution)/shard_map/ppermute | solution.py:378
  7.7 18.8 %collective-permute-start.2 = (bf16[48,1536]{1,0:T(8,128)(2,1)S(1)}, bf16[48,1536]{1,0:T(8,128)(2,1)S(1)}, u32[]{:S(2)}, u32[]{:S(2)}) collective-permute-start(bf16[48,1536]{1,0:T(8,128)(2,1)S(1)} %bitcast.24), channel_id=1, source_target_pairs={{0,16},{8,24},{16,0},{24,8},{1,17},{9,25},{17,1},{25,9},{2,18},{10... | collective-permute-start | bytes 442376 | tf_op jit(solution)/shard_map/ppermute | solution.py:378
  10.1 16.4 %collective-permute-start.1 = (bf16[48,1536]{1,0:T(8,128)(2,1)S(1)}, bf16[48,1536]{1,0:T(8,128)(2,1)S(1)}, u32[]{:S(2)}, u32[]{:S(2)}) collective-permute-start(bf16[48,1536]{1,0:T(8,128)(2,1)S(1)} %bitcast.25), channel_id=1, source_target_pairs={{0,8},{8,16},{16,24},{24,0},{1,9},{9,17},{17,25},{25,1},{2,10},{10... | collective-permute-start | bytes 442376 | tf_op jit(solution)/shard_map/ppermute | solution.py:378
  15.3 12.6 %all-to-all-start.4 = ((s32[8,1,128]{2,1,0:T(1,128)}), s32[8,1,128]{2,1,0:T(1,128)S(1)}, u32[]{:S(2)}, u32[]{:S(2)}) async-start(s32[8,1,128]{2,1,0:T(1,128)} %bitcast.37), calls=%async_computation.4 | async-start | bytes 8192 | tf_op jit(solution)/shard_map/all_to_all | solution.py:381
  27.9 14.3 %all-to-all-start.5 = ((bf16[4,48,1536]{2,1,0:T(8,128)(2,1)}), bf16[4,48,1536]{2,1,0:T(8,128)(2,1)S(1)}, u32[]{:S(2)}, u32[]{:S(2)}) async-start(bf16[4,48,1536]{2,1,0:T(8,128)(2,1)} %shard_map.92), calls=%async_computation.5 | async-start | bytes 1179648 | tf_op jit(solution)/shard_map/all_to_all | solution.py:387
  44.3 21.8 %copy-start.1 = (f32[2,256,256]{2,1,0:T(8,128)S(1)}, f32[2,256,256]{2,1,0:T(8,128)}, u32[]{:S(2)}) copy-start(f32[2,256,256]{2,1,0:T(8,128)} %probe.1) | copy-start | bytes 1572868
  44.3 21.8 %copy-start.2 = (bf16[1,1,1,2,256,256]{5,4,3,2,1,0:T(8,128)(2,1)S(1)}, bf16[1,1,1,2,256,256]{5,4,3,2,1,0:T(8,128)(2,1)}, u32[]{:S(2)}) copy-start(bf16[1,1,1,2,256,256]{5,4,3,2,1,0:T(8,128)(2,1)} %param.15) | copy-start | bytes 786436
  44.3 21.8 %copy-start.3 = (bf16[256,256]{1,0:T(8,128)(2,1)S(1)}, bf16[256,256]{1,0:T(8,128)(2,1)}, u32[]{:S(2)}) copy-start(bf16[256,256]{1,0:T(8,128)(2,1)} %constant.70.clone.wi_ref) | copy-start | bytes 393220
  44.3 21.8 %copy-start.4 = (bf16[256,256]{1,0:T(8,128)(2,1)S(1)}, bf16[256,256]{1,0:T(8,128)(2,1)}, u32[]{:S(2)}) copy-start(bf16[256,256]{1,0:T(8,128)(2,1)} %constant.69.clone.wr_ref) | copy-start | bytes 393220
  44.3 21.8 %copy-start.5 = (s32[1,1,1,2]{3,2,1,0:T(1,128)S(1)}, s32[1,1,1,2]{3,2,1,0:T(1,128)}, u32[]{:S(2)}) copy-start(s32[1,1,1,2]{3,2,1,0:T(1,128)} %param.16) | copy-start | bytes 28
  86.6 15.9 %all-to-all-start.6 = ((bf16[8,2,48,256]{3,2,1,0:T(8,128)(2,1)}), bf16[8,2,48,256]{3,2,1,0:T(8,128)(2,1)S(1)}, u32[]{:S(2)}, u32[]{:S(2)}) async-start(bf16[8,2,48,256]{3,2,1,0:T(8,128)(2,1)} %get-tuple-element.39), calls=%async_computation.6 | async-start | bytes 786432 | tf_op jit(solution)/shard_map/all_to_all | solution.py:381
  92.9 16.0 %collective-permute-start.4 = (bf16[48,1536]{1,0:T(8,128)(2,1)S(1)}, bf16[48,1536]{1,0:T(8,128)(2,1)S(1)}, u32[]{:S(2)}, u32[]{:S(2)}) collective-permute-start(bf16[48,1536]{1,0:T(8,128)(2,1)S(1)} %get-tuple-element.42), channel_id=1, source_target_pairs={{0,8},{8,16},{16,24},{24,0},{1,9},{9,17},{17,25},{25,1},{2,10},{10... | collective-permute-start | bytes 442376 | tf_op jit(solution)/shard_map/ppermute | solution.py:378
  94.9 14.1 %collective-permute-start.5 = (bf16[48,1536]{1,0:T(8,128)(2,1)S(1)}, bf16[48,1536]{1,0:T(8,128)(2,1)S(1)}, u32[]{:S(2)}, u32[]{:S(2)}) collective-permute-start(bf16[48,1536]{1,0:T(8,128)(2,1)S(1)} %get-tuple-element.43), channel_id=1, source_target_pairs={{0,16},{8,24},{16,0},{24,8},{1,17},{9,25},{17,1},{25,9},{2,18},{10... | collective-permute-start | bytes 442376 | tf_op jit(solution)/shard_map/ppermute | solution.py:378
  96.8 12.1 %collective-permute-start.6 = (bf16[48,1536]{1,0:T(8,128)(2,1)S(1)}, bf16[48,1536]{1,0:T(8,128)(2,1)S(1)}, u32[]{:S(2)}, u32[]{:S(2)}) collective-permute-start(bf16[48,1536]{1,0:T(8,128)(2,1)S(1)} %get-tuple-element.44), channel_id=1, source_target_pairs={{0,24},{8,0},{16,8},{24,16},{1,25},{9,1},{17,9},{25,17},{2,26},{10... | collective-permute-start | bytes 442376 | tf_op jit(solution)/shard_map/ppermute | solution.py:378
  105.4 12.8 %all-to-all-start.7 = ((bf16[4,48,1536]{2,1,0:T(8,128)(2,1)}), bf16[4,48,1536]{2,1,0:T(8,128)(2,1)S(1)}, u32[]{:S(2)}, u32[]{:S(2)}) async-start(bf16[4,48,1536]{2,1,0:T(8,128)(2,1)} %shard_map.96), calls=%async_computation.7 | async-start | bytes 1179648 | tf_op jit(solution)/shard_map/all_to_all | solution.py:387
  109.0 14.3 %collective-permute-start.7 = (bf16[48,1536]{1,0:T(8,128)(2,1)S(1)}, bf16[48,1536]{1,0:T(8,128)(2,1)S(1)}, u32[]{:S(2)}, u32[]{:S(2)}) collective-permute-start(bf16[48,1536]{1,0:T(8,128)(2,1)S(1)} %add_convert_fusion.1), channel_id=1, source_target_pairs={{0,449},{1,450},{2,451},{3,452},{4,453},{5,454},{6,455},{32,481},{... | collective-permute-start | bytes 442376 | tf_op jit(solution)/shard_map/ppermute | solution.py:375
  123.3 37.4 %copy-start = (bf16[2,1,192,1536]{3,2,1,0:T(8,128)(2,1)S(1)}, bf16[2,1,192,1536]{3,2,1,0:T(8,128)(2,1)}, u32[]{:S(2)}) copy-start(bf16[2,1,192,1536]{3,2,1,0:T(8,128)(2,1)} %param.13) | copy-start | bytes 3538948
  123.3 16.2 %collective-permute-start.8 = (bf16[48,1536]{1,0:T(8,128)(2,1)S(1)}, bf16[48,1536]{1,0:T(8,128)(2,1)S(1)}, u32[]{:S(2)}, u32[]{:S(2)}) collective-permute-start(bf16[48,1536]{1,0:T(8,128)(2,1)S(1)} %add_convert_fusion.refs_0_), channel_id=1, source_target_pairs={{0,256},{32,288},{64,320},{96,352},{128,384},{160,416},{192,448},{... | collective-permute-start | bytes 442376 | tf_op jit(solution)/shard_map/ppermute | solution.py:366
  157.3 5.1 %collective-permute-start.9 = (bf16[4,48,1536]{2,1,0:T(8,128)(2,1)S(1)}, bf16[4,48,1536]{2,1,0:T(8,128)(2,1)S(1)}, u32[]{:S(2)}, u32[]{:S(2)}) collective-permute-start(bf16[4,48,1536]{2,1,0:T(8,128)(2,1)S(1)} %all_to_all.51.gradient), channel_id=1, source_target_pairs={{0,32},{32,0},{64,96},{96,64},{128,160},{160,128},{192,224},{224,1... | collective-permute-start | bytes 1769480 | tf_op jit(solution)/shard_map/ppermute | solution.py:366

commit v17 on v16

--- a/solution.py
+++ b/solution.py
@@ -315,16 +315,17 @@
     return call(sum_body, [out], [], *terms)[0]
 
 
-def step_body(part_ref, layer, gradient, *refs):
+def step_body(scalars, layer, *refs):
+    blocks = refs[:FOUR]
     out, made, sems = refs[-3:]
-    part = part_ref[0]
-    chunks = gradient.shape[1] // CHUNK
+    part, place = scalars[0], scalars[1]
+    chunks = blocks[0].shape[0] // CHUNK
     size = FOUR * CHUNK
     copies = []
     for i in range(chunks):
-        for k in range(FOUR):
-            rows = slice(i * size + k * CHUNK, i * size + (k + 1) * CHUNK)
-            change = gradient[k, i * CHUNK : (i + 1) * CHUNK].astype(jnp.float32)
+        for k, block in enumerate(blocks):
+            rows = pl.ds(pl.multiple_of(i * size + (place ^ k) * CHUNK, CHUNK), CHUNK)
+            change = block[i * CHUNK : (i + 1) * CHUNK].astype(jnp.float32)
             made[rows] = layer[part, rows].astype(jnp.float32) - step_size * change
         at = pl.ds(i * size, size)
         copies.append(pltpu.make_async_copy(made.at[at], out.at[part, at], sems.at[i]))
@@ -333,17 +334,17 @@
         copy.wait()
 
 
-def step(part, layer, gradient, *stepped):
+def step(part, place, layer, blocks, *stepped):
     return pl.pallas_call(
         step_body,
         out_shape=jax.ShapeDtypeStruct(layer.shape, jnp.float32),
-        in_specs=[pl.BlockSpec(memory_space=pltpu.SMEM), VMEM, VMEM]
+        in_specs=[pl.BlockSpec(memory_space=pltpu.SMEM)] + [VMEM] * (1 + FOUR)
         + [pl.BlockSpec(memory_space=pltpu.HBM)] * len(stepped),
         out_specs=pl.BlockSpec(memory_space=pltpu.HBM),
         scratch_shapes=[pltpu.VMEM(layer.shape[1:], jnp.float32), pltpu.SemaphoreType.DMA((4,))],
-        input_output_aliases={3: 0} if stepped else {},
+        input_output_aliases={2 + FOUR: 0} if stepped else {},
         compiler_params=pltpu.CompilerParams(vmem_limit_bytes=24 * 1024 * 1024),
-    )(part.reshape(1).astype(jnp.int32), layer, gradient, *stepped)
+    )(jnp.stack([part, place]).astype(jnp.int32), layer, *blocks, *stepped)
 
 
 def per_device(volume, probe_wave, amplitudes, offsets, column_starts, counts, angle_ids):
@@ -430,9 +431,11 @@
     own = jnp.sum(own.astype(f32), axis=0)
 
     total = lax.optimization_barrier((own + spill.astype(f32)).astype(bf16))
-    total = to_four(sum_copies([total, swap(total, 8)], 4))
-    new = step(core, layer, total)
-    return step(1 - core, layer, swap(total, 1), new).reshape(volume.shape)
+    total = sum_copies([total, swap(total, 8)], 1)[0]
+    blocks = [total] + [swap(total, k << 1) for k in range(1, FOUR)]
+    others = [swap(block, 1) for block in blocks]
+    new = step(core, place_z, layer, blocks)
+    return step(1 - core, place_z, layer, others, new).reshape(volume.shape)
 
 
 def solution(mesh):

time: 164 us -> 164 us (level)
  blocking collectives: 56.4 us -> 38.8 us
  starting transfers between devices: 47.3 us -> 62.6 us
    all_to_all x1 -> x0, blocking collectives: 17.7 us -> none  [to_four(): lax.all_to_all(value, 'angle', 0, 0, axis_index_groups=four_groups, tiled...]
    ppermute x2 -> x8, starting transfers between devices: 5.53 us -> 20.7 us  [swap(): return lax.ppermute(value, 'angle', [(i, i ^ by) for i in range(angles)])]
    ppermute x2 -> x8, waiting for transfers between devices: 14.6 us -> 15.4 us  [swap(): return lax.ppermute(value, 'angle', [(i, i ^ by) for i in range(angles)])]
  transfers between devices with their start and end apart: 14 -> 20, of which waited for: 8 -> 8; matrix products, arithmetic and copies ran while one was open for 1% -> 1% of each run, Pallas kernels for 6% -> 7%
where the time goes in v17:
time: 164 us; the launch traced here: 163 us
  starting transfers between devices  62.6 us (38%)
  waiting for transfers between devices  39.6 us (24%)
  blocking collectives  38.8 us (24%)
  Pallas kernels  17.9 us (11%)
  between operations  2.22 us (1%)
    all_to_all x2, blocking collectives, to_eight(): lax.all_to_all(value, 'angle', 0, 0, axis_index_groups=eight_groups, tile...  38.8 us
    ppermute x8, starting transfers between devices, swap(): return lax.ppermute(value, 'angle', [(i, i ^ by) for i in range(angles)])  20.7 us
    ppermute x6, starting transfers between devices, to_slab(): lax.ppermute(value, 'slab', [(i, (i + by) % slabs) for i in range(slabs)])  18.6 us
    ppermute x8, waiting for transfers between devices, swap(): return lax.ppermute(value, 'angle', [(i, i ^ by) for i in range(angles)])  15.4 us
    all_to_all x2, waiting for transfers between devices, to_slabs(): return lax.all_to_all(value, 'slab', 0, 0, tiled=True)  14 us
    pallas_call x7, Pallas kernels, call(): pl.pallas_call(body, out_shape=out_shape, in_specs=[smem if x.dtype == jn...  13.1 us
    all_to_all x2, starting transfers between devices, to_eight(): lax.all_to_all(value, 'angle', 0, 0, axis_index_groups=eight_groups, tile...  12 us
    all_to_all x2, starting transfers between devices, to_slabs(): return lax.all_to_all(value, 'slab', 0, 0, tiled=True)  8.59 us
  transfers between devices with their start and end apart: 20, of which 8 were waited for; matrix products, arithmetic and copies ran while one was open for 1% of the time, Pallas kernels for 7%

profile of v17, /device:TPU:1, one launch (start us, length us, event | category | flops | bytes accessed | tf_op | source)
XLA Modules:
  0.0 163.4 jit_solution(16646178457077916466)
XLA Ops:
  2.4 5.2 %collective-permute-start.3 = (bf16[48,1536]{1,0:T(8,128)(2,1)S(1)}, bf16[48,1536]{1,0:T(8,128)(2,1)S(1)}, u32[]{:S(2)}, u32[]{:S(2)}) collective-permute-start(bf16[48,1536]{1,0:T(8,128)(2,1)S(1)} %bitcast.29), channel_id=1, source_target_pairs={{0,24},{8,0},{16,8},{24,16},{1,25},{9,1},{17,9},{25,17},{2,26},{10... | collective-permute-start | bytes 442376 | tf_op jit(solution)/shard_map/ppermute | solution.py:379
  7.7 2.4 %collective-permute-start.2 = (bf16[48,1536]{1,0:T(8,128)(2,1)S(1)}, bf16[48,1536]{1,0:T(8,128)(2,1)S(1)}, u32[]{:S(2)}, u32[]{:S(2)}) collective-permute-start(bf16[48,1536]{1,0:T(8,128)(2,1)S(1)} %bitcast.30), channel_id=1, source_target_pairs={{0,16},{8,24},{16,0},{24,8},{1,17},{9,25},{17,1},{25,9},{2,18},{10... | collective-permute-start | bytes 442376 | tf_op jit(solution)/shard_map/ppermute | solution.py:379
  10.1 2.5 %collective-permute-start.1 = (bf16[48,1536]{1,0:T(8,128)(2,1)S(1)}, bf16[48,1536]{1,0:T(8,128)(2,1)S(1)}, u32[]{:S(2)}, u32[]{:S(2)}) collective-permute-start(bf16[48,1536]{1,0:T(8,128)(2,1)S(1)} %bitcast.31), channel_id=1, source_target_pairs={{0,8},{8,16},{16,24},{24,0},{1,9},{9,17},{17,25},{25,1},{2,10},{10... | collective-permute-start | bytes 442376 | tf_op jit(solution)/shard_map/ppermute | solution.py:379
  15.3 7.7 %all-to-all-start.4 = ((s32[8,1,128]{2,1,0:T(1,128)}), s32[8,1,128]{2,1,0:T(1,128)S(1)}, u32[]{:S(2)}, u32[]{:S(2)}) async-start(s32[8,1,128]{2,1,0:T(1,128)} %bitcast.43), calls=%async_computation.4 | async-start | bytes 8192 | tf_op jit(solution)/shard_map/all_to_all | solution.py:382
  23.0 3.5 %collective-permute-done.refs_0_ = bf16[48,1536]{1,0:T(8,128)(2,1)S(1)} collective-permute-done((bf16[48,1536]{1,0:T(8,128)(2,1)S(1)}, bf16[48,1536]{1,0:T(8,128)(2,1)S(1)}, u32[]{:S(2)}, u32[]{:S(2)}) %collective-permute-start) | collective-permute-done | bytes 147488 | tf_op jit(solution)/shard_map/ppermute | solution.py:376
  27.9 5.1 %all-to-all-start.5 = ((bf16[4,48,1536]{2,1,0:T(8,128)(2,1)}), bf16[4,48,1536]{2,1,0:T(8,128)(2,1)S(1)}, u32[]{:S(2)}, u32[]{:S(2)}) async-start(bf16[4,48,1536]{2,1,0:T(8,128)(2,1)} %shard_map.92), calls=%async_computation.5 | async-start | bytes 1179648 | tf_op jit(solution)/shard_map/all_to_all | solution.py:388
  34.2 1.8 %shard_map.93.done = bf16[8,2,48,256]{3,2,1,0:T(8,128)(2,1)S(1)} custom-call(s32[8,128]{1,0:T(8,128)S(1)} %bitcast.35, s32[1]{0:T(128)} %bitcast.9.slab_ref, bf16[48,1536]{1,0:T(8,128)(2,1)S(1)} %bitcast.32, bf16[48,1536]{1,0:T(8,128)(2,1)S(1)} %collective-permute-done.1.refs_1_, bf16[48,1536]{1,0:T(8,128)(2,1)S(1)} %collective-permute-done.2.refs_2_, ...), custom_call_target="tpu_custom_call" | custom-call | tf_op jit(solution)/shard_map/pallas_call | solution.py:47
  36.0 6.2 %all-to-all-done.5.blocks = bf16[4,48,1536]{2,1,0:T(8,128)(2,1)S(1)} async-done(((bf16[4,48,1536]{2,1,0:T(8,128)(2,1)}), bf16[4,48,1536]{2,1,0:T(8,128)(2,1)S(1)}, u32[]{:S(2)}, u32[]{:S(2)}) %all-to-all-start.5) | async-done | bytes 589856 | tf_op jit(solution)/shard_map/all_to_all | solution.py:388
  42.2 2.0 %shard_map.94 = bf16[8,2,5,16,256]{4,3,2,1,0:T(8,128)(2,1)S(1)} custom-call(s32[1]{0:T(128)} %bitcast.1.place_ref, s32[8,128]{1,0:T(8,128)S(1)} %bitcast.36, s32[1]{0:T(128)} %bitcast.9.slab_ref, bf16[4,48,1536]{2,1,0:T(8,128)(2,1)S(1)} %all-to-all-done.5.blocks, bf16[8,2,48,256]{3,2,1,0:T(8,128)(2,1)S(1)} %shard_map.93.done), custom_call_target="tpu_custom_call" | custom-call | tf_op jit(solution)/shard_map/pallas_call | solution.py:47
  44.3 21.7 %conditional.2 = (bf16[8,2,5,16,256]{4,3,2,1,0:T(8,128)(2,1)S(1)}) conditional(s32[]{:T(128)} %convert_element_type.25, bf16[8,2,5,16,256]{4,3,2,1,0:T(8,128)(2,1)S(1)} %shard_map.94, bf16[8,2,5,16,256]{4,3,2,1,0:T(8,128)(2,1)S(1)} %shard_map.94), branch_computations={%region_1.2_spmd, %region_2.3_spmd} | conditional | flops 327680 | bytes 3276808 | solution.py:401
  44.3 21.7 %all_to_all.43 = bf16[8,2,5,16,256]{4,3,2,1,0:T(8,128)(2,1)S(1)} all-to-all(bf16[8,2,5,16,256]{4,3,2,1,0:T(8,128)(2,1)S(1)} %param.1), channel_id=1, replica_groups={{0,32,64,96,128,160,192,224},{256,288,320,352,384,416,448,480},{1,33,65..., dimensions={0} | all-to-all | bytes 1310720 | tf_op jit(solution)/shard_map/cond/branch_1_fun/all_to_all | solution.py:382
  66.1 3.4 %shard_map.95 = (bf16[8,2,48,256]{3,2,1,0:T(8,128)(2,1)}, bf16[8,2,48,256]{3,2,1,0:T(8,128)(2,1)S(1)}) custom-call(s32[2]{0:T(128)S(1)} %bitcast.40, s32[1]{0:T(128)} %bitcast.21.count_ref, bf16[8,2,5,16,256]{4,3,2,1,0:T(8,128)(2,1)S(1)} %get-tuple-element.51.windows, f32[2,256,256]{2,1,0:T(8,128)S(1)} %copy-done.1, bf16[2,256,256]{2,1,0:T(8,128)(2,1)S(1)} %bitcast.33, ...), custom_call_target="tpu_custom_call" | custom-call | tf_op jit(solution)/shard_map/pallas_call | solution.py:47
  69.5 17.1 %conditional.3 = (bf16[8,2,48,256]{3,2,1,0:T(8,128)(2,1)S(1)}) conditional(s32[]{:T(128)} %convert_element_type.25, bf16[8,2,48,256]{3,2,1,0:T(8,128)(2,1)S(1)} %get-tuple-element.37, bf16[8,2,48,256]{3,2,1,0:T(8,128)(2,1)S(1)} %get-tuple-element.37), branch_computations={%region_3.4_spmd, %region_4.5_spmd} | conditional | flops 196608 | bytes 1966088 | solution.py:401
  69.5 17.1 %all_to_all.45 = bf16[8,2,48,256]{3,2,1,0:T(8,128)(2,1)S(1)} all-to-all(bf16[8,2,48,256]{3,2,1,0:T(8,128)(2,1)S(1)} %param.3), channel_id=1, replica_groups={{0,32,64,96,128,160,192,224},{256,288,320,352,384,416,448,480},{1,33,65..., dimensions={0} | all-to-all | bytes 786432 | tf_op jit(solution)/shard_map/cond/branch_1_fun/all_to_all | solution.py:382
  86.6 4.2 %all-to-all-start.6 = ((bf16[8,2,48,256]{3,2,1,0:T(8,128)(2,1)}), bf16[8,2,48,256]{3,2,1,0:T(8,128)(2,1)S(1)}, u32[]{:S(2)}, u32[]{:S(2)}) async-start(bf16[8,2,48,256]{3,2,1,0:T(8,128)(2,1)} %get-tuple-element.39), calls=%async_computation.6 | async-start | bytes 786432 | tf_op jit(solution)/shard_map/all_to_all | solution.py:382
  90.8 2.1 %shard_map.97 = (f32[48,1536]{1,0:T(8,128)S(1)}, bf16[48,1536]{1,0:T(8,128)(2,1)S(1)}, bf16[48,1536]{1,0:T(8,128)(2,1)S(1)}, bf16[48,1536]{1,0:T(8,128)(2,1)S(1)}) custom-call(s32[8,128]{1,0:T(8,128)S(1)} %bitcast.37, s32[1]{0:T(128)} %bitcast.9.slab_ref, bf16[8,2,48,256]{3,2,1,0:T(8,128)(2,1)S(1)} %get-tuple-element.52.windows), custom_call_target="tpu_custom_call" | custom-call | tf_op jit(solution)/shard_map/pallas_call | solution.py:47
  92.9 1.9 %collective-permute-start.4 = (bf16[48,1536]{1,0:T(8,128)(2,1)S(1)}, bf16[48,1536]{1,0:T(8,128)(2,1)S(1)}, u32[]{:S(2)}, u32[]{:S(2)}) collective-permute-start(bf16[48,1536]{1,0:T(8,128)(2,1)S(1)} %get-tuple-element.42), channel_id=1, source_target_pairs={{0,8},{8,16},{16,24},{24,0},{1,9},{9,17},{17,25},{25,1},{2,10},{10... | collective-permute-start | bytes 442376 | tf_op jit(solution)/shard_map/ppermute | solution.py:379
  94.9 1.9 %collective-permute-start.5 = (bf16[48,1536]{1,0:T(8,128)(2,1)S(1)}, bf16[48,1536]{1,0:T(8,128)(2,1)S(1)}, u32[]{:S(2)}, u32[]{:S(2)}) collective-permute-start(bf16[48,1536]{1,0:T(8,128)(2,1)S(1)} %get-tuple-element.43), channel_id=1, source_target_pairs={{0,16},{8,24},{16,0},{24,8},{1,17},{9,25},{17,1},{25,9},{2,18},{10... | collective-permute-start | bytes 442376 | tf_op jit(solution)/shard_map/ppermute | solution.py:379
  96.8 4.6 %collective-permute-start.6 = (bf16[48,1536]{1,0:T(8,128)(2,1)S(1)}, bf16[48,1536]{1,0:T(8,128)(2,1)S(1)}, u32[]{:S(2)}, u32[]{:S(2)}) collective-permute-start(bf16[48,1536]{1,0:T(8,128)(2,1)S(1)} %get-tuple-element.44), channel_id=1, source_target_pairs={{0,24},{8,0},{16,8},{24,16},{1,25},{9,1},{17,9},{25,17},{2,26},{10... | collective-permute-start | bytes 442376 | tf_op jit(solution)/shard_map/ppermute | solution.py:379
  102.5 2.9 %shard_map.96 = bf16[4,48,1536]{2,1,0:T(8,128)(2,1)} custom-call(s32[8,128]{1,0:T(8,128)S(1)} %bitcast.38, s32[1]{0:T(128)} %bitcast.9.slab_ref, bf16[8,2,48,256]{3,2,1,0:T(8,128)(2,1)S(1)} %all-to-all-done.6.windows), custom_call_target="tpu_custom_call" | custom-call | tf_op jit(solution)/shard_map/pallas_call | solution.py:47
  105.4 3.5 %all-to-all-start.7 = ((bf16[4,48,1536]{2,1,0:T(8,128)(2,1)}), bf16[4,48,1536]{2,1,0:T(8,128)(2,1)S(1)}, u32[]{:S(2)}, u32[]{:S(2)}) async-start(bf16[4,48,1536]{2,1,0:T(8,128)(2,1)} %shard_map.96), calls=%async_computation.7 | async-start | bytes 1179648 | tf_op jit(solution)/shard_map/all_to_all | solution.py:388
  110.5 7.8 %all-to-all-done.7 = bf16[4,48,1536]{2,1,0:T(8,128)(2,1)S(1)} async-done(((bf16[4,48,1536]{2,1,0:T(8,128)(2,1)}), bf16[4,48,1536]{2,1,0:T(8,128)(2,1)S(1)}, u32[]{:S(2)}, u32[]{:S(2)}) %all-to-all-start.7) | async-done | bytes 589856 | tf_op jit(solution)/shard_map/all_to_all | solution.py:388
  118.3 5.1 %collective-permute-done.7 = bf16[48,1536]{1,0:T(8,128)(2,1)S(1)} collective-permute-done((bf16[48,1536]{1,0:T(8,128)(2,1)S(1)}, bf16[48,1536]{1,0:T(8,128)(2,1)S(1)}, u32[]{:S(2)}, u32[]{:S(2)}) %collective-permute-start.7) | collective-permute-done | bytes 147488 | tf_op jit(solution)/shard_map/ppermute | solution.py:376
  123.5 1.9 %collective-permute-start.8 = (bf16[48,1536]{1,0:T(8,128)(2,1)S(1)}, bf16[48,1536]{1,0:T(8,128)(2,1)S(1)}, u32[]{:S(2)}, u32[]{:S(2)}) collective-permute-start(bf16[48,1536]{1,0:T(8,128)(2,1)S(1)} %add_convert_fusion.refs_0_), channel_id=1, source_target_pairs={{0,256},{32,288},{64,320},{96,352},{128,384},{160,416},{192,448},{... | collective-permute-start | bytes 442376 | tf_op jit(solution)/shard_map/ppermute | solution.py:367
  125.4 14.0 %collective-permute-done.8.refs_1_ = bf16[48,1536]{1,0:T(8,128)(2,1)S(1)} collective-permute-done((bf16[48,1536]{1,0:T(8,128)(2,1)S(1)}, bf16[48,1536]{1,0:T(8,128)(2,1)S(1)}, u32[]{:S(2)}, u32[]{:S(2)}) %collective-permute-start.8) | collective-permute-done | bytes 147488 | tf_op jit(solution)/shard_map/ppermute | solution.py:367
  139.4 1.9 %collective-permute-start.14 = (bf16[48,1536]{1,0:T(8,128)(2,1)S(1)}, bf16[48,1536]{1,0:T(8,128)(2,1)S(1)}, u32[]{:S(2)}, u32[]{:S(2)}) collective-permute-start(bf16[48,1536]{1,0:T(8,128)(2,1)S(1)} %bitcast.24), channel_id=1, source_target_pairs={{0,192},{32,224},{64,128},{96,160},{128,64},{160,96},{192,0},{224,... | collective-permute-start | bytes 442376 | tf_op jit(solution)/shard_map/ppermute | solution.py:367
  141.4 1.9 %collective-permute-start.12 = (bf16[48,1536]{1,0:T(8,128)(2,1)S(1)}, bf16[48,1536]{1,0:T(8,128)(2,1)S(1)}, u32[]{:S(2)}, u32[]{:S(2)}) collective-permute-start(bf16[48,1536]{1,0:T(8,128)(2,1)S(1)} %bitcast.25), channel_id=1, source_target_pairs={{0,128},{32,160},{64,192},{96,224},{128,0},{160,32},{192,64},{224,... | collective-permute-start | bytes 442376 | tf_op jit(solution)/shard_map/ppermute | solution.py:367
  143.3 5.4 %collective-permute-start.10 = (bf16[48,1536]{1,0:T(8,128)(2,1)S(1)}, bf16[48,1536]{1,0:T(8,128)(2,1)S(1)}, u32[]{:S(2)}, u32[]{:S(2)}) collective-permute-start(bf16[48,1536]{1,0:T(8,128)(2,1)S(1)} %bitcast.26), channel_id=1, source_target_pairs={{0,64},{32,96},{64,0},{96,32},{128,192},{160,224},{192,128},{224,1... | collective-permute-start | bytes 442376 | tf_op jit(solution)/shard_map/ppermute | solution.py:367
  148.7 3.2 %collective-permute-start.9 = (bf16[48,1536]{1,0:T(8,128)(2,1)S(1)}, bf16[48,1536]{1,0:T(8,128)(2,1)S(1)}, u32[]{:S(2)}, u32[]{:S(2)}) collective-permute-start(bf16[48,1536]{1,0:T(8,128)(2,1)S(1)} %bitcast.27), channel_id=1, source_target_pairs={{0,32},{32,0},{64,96},{96,64},{128,160},{160,128},{192,224},{224,1... | collective-permute-start | bytes 442376 | tf_op jit(solution)/shard_map/ppermute | solution.py:367
  152.0 1.9 %collective-permute-start.15 = (bf16[48,1536]{1,0:T(8,128)(2,1)S(1)}, bf16[48,1536]{1,0:T(8,128)(2,1)S(1)}, u32[]{:S(2)}, u32[]{:S(2)}) collective-permute-start(bf16[48,1536]{1,0:T(8,128)(2,1)S(1)} %collective-permute-done.14.refs_3_), channel_id=1, source_target_pairs={{0,32},{32,0},{64,96},{96,64},{128,160},{160,128},{192,224},{224,1... | collective-permute-start | bytes 442376 | tf_op jit(solution)/shard_map/ppermute | solution.py:367
  155.3 2.4 %collective-permute-start.13 = (bf16[48,1536]{1,0:T(8,128)(2,1)S(1)}, bf16[48,1536]{1,0:T(8,128)(2,1)S(1)}, u32[]{:S(2)}, u32[]{:S(2)}) collective-permute-start(bf16[48,1536]{1,0:T(8,128)(2,1)S(1)} %collective-permute-done.12.refs_2_), channel_id=1, source_target_pairs={{0,32},{32,0},{64,96},{96,64},{128,160},{160,128},{192,224},{224,1... | collective-permute-start | bytes 442376 | tf_op jit(solution)/shard_map/ppermute | solution.py:367
  157.7 1.9 %collective-permute-start.11 = (bf16[48,1536]{1,0:T(8,128)(2,1)S(1)}, bf16[48,1536]{1,0:T(8,128)(2,1)S(1)}, u32[]{:S(2)}, u32[]{:S(2)}) collective-permute-start(bf16[48,1536]{1,0:T(8,128)(2,1)S(1)} %collective-permute-done.10.refs_1_), channel_id=1, source_target_pairs={{0,32},{32,0},{64,96},{96,64},{128,160},{160,128},{192,224},{224,1... | collective-permute-start | bytes 442376 | tf_op jit(solution)/shard_map/ppermute | solution.py:367
  (42 shorter events, 13.7 us)
Async XLA Ops:
  1.1 25.3 %collective-permute-start = (bf16[48,1536]{1,0:T(8,128)(2,1)S(1)}, bf16[48,1536]{1,0:T(8,128)(2,1)S(1)}, u32[]{:S(2)}, u32[]{:S(2)}) collective-permute-start(bf16[48,1536]{1,0:T(8,128)(2,1)S(1)} %bitcast.42), channel_id=1, source_target_pairs={{1,448},{2,449},{3,450},{4,451},{5,452},{6,453},{7,454},{33,480},{... | collective-permute-start | bytes 442376 | tf_op jit(solution)/shard_map/ppermute | solution.py:376
  2.4 24.0 %collective-permute-start.3 = (bf16[48,1536]{1,0:T(8,128)(2,1)S(1)}, bf16[48,1536]{1,0:T(8,128)(2,1)S(1)}, u32[]{:S(2)}, u32[]{:S(2)}) collective-permute-start(bf16[48,1536]{1,0:T(8,128)(2,1)S(1)} %bitcast.29), channel_id=1, source_target_pairs={{0,24},{8,0},{16,8},{24,16},{1,25},{9,1},{17,9},{25,17},{2,26},{10... | collective-permute-start | bytes 442376 | tf_op jit(solution)/shard_map/ppermute | solution.py:379
  7.7 18.8 %collective-permute-start.2 = (bf16[48,1536]{1,0:T(8,128)(2,1)S(1)}, bf16[48,1536]{1,0:T(8,128)(2,1)S(1)}, u32[]{:S(2)}, u32[]{:S(2)}) collective-permute-start(bf16[48,1536]{1,0:T(8,128)(2,1)S(1)} %bitcast.30), channel_id=1, source_target_pairs={{0,16},{8,24},{16,0},{24,8},{1,17},{9,25},{17,1},{25,9},{2,18},{10... | collective-permute-start | bytes 442376 | tf_op jit(solution)/shard_map/ppermute | solution.py:379
  10.1 16.4 %collective-permute-start.1 = (bf16[48,1536]{1,0:T(8,128)(2,1)S(1)}, bf16[48,1536]{1,0:T(8,128)(2,1)S(1)}, u32[]{:S(2)}, u32[]{:S(2)}) collective-permute-start(bf16[48,1536]{1,0:T(8,128)(2,1)S(1)} %bitcast.31), channel_id=1, source_target_pairs={{0,8},{8,16},{16,24},{24,0},{1,9},{9,17},{17,25},{25,1},{2,10},{10... | collective-permute-start | bytes 442376 | tf_op jit(solution)/shard_map/ppermute | solution.py:379
  15.3 12.6 %all-to-all-start.4 = ((s32[8,1,128]{2,1,0:T(1,128)}), s32[8,1,128]{2,1,0:T(1,128)S(1)}, u32[]{:S(2)}, u32[]{:S(2)}) async-start(s32[8,1,128]{2,1,0:T(1,128)} %bitcast.43), calls=%async_computation.4 | async-start | bytes 8192 | tf_op jit(solution)/shard_map/all_to_all | solution.py:382
  27.9 14.3 %all-to-all-start.5 = ((bf16[4,48,1536]{2,1,0:T(8,128)(2,1)}), bf16[4,48,1536]{2,1,0:T(8,128)(2,1)S(1)}, u32[]{:S(2)}, u32[]{:S(2)}) async-start(bf16[4,48,1536]{2,1,0:T(8,128)(2,1)} %shard_map.92), calls=%async_computation.5 | async-start | bytes 1179648 | tf_op jit(solution)/shard_map/all_to_all | solution.py:388
  44.3 21.8 %copy-start.1 = (f32[2,256,256]{2,1,0:T(8,128)S(1)}, f32[2,256,256]{2,1,0:T(8,128)}, u32[]{:S(2)}) copy-start(f32[2,256,256]{2,1,0:T(8,128)} %probe.1) | copy-start | bytes 1572868
  44.3 21.8 %copy-start.2 = (bf16[1,1,1,2,256,256]{5,4,3,2,1,0:T(8,128)(2,1)S(1)}, bf16[1,1,1,2,256,256]{5,4,3,2,1,0:T(8,128)(2,1)}, u32[]{:S(2)}) copy-start(bf16[1,1,1,2,256,256]{5,4,3,2,1,0:T(8,128)(2,1)} %param.15) | copy-start | bytes 786436
  44.3 21.8 %copy-start.3 = (bf16[256,256]{1,0:T(8,128)(2,1)S(1)}, bf16[256,256]{1,0:T(8,128)(2,1)}, u32[]{:S(2)}) copy-start(bf16[256,256]{1,0:T(8,128)(2,1)} %constant.70.clone.wi_ref) | copy-start | bytes 393220
  44.3 21.8 %copy-start.4 = (bf16[256,256]{1,0:T(8,128)(2,1)S(1)}, bf16[256,256]{1,0:T(8,128)(2,1)}, u32[]{:S(2)}) copy-start(bf16[256,256]{1,0:T(8,128)(2,1)} %constant.69.clone.wr_ref) | copy-start | bytes 393220
  44.3 21.8 %copy-start.5 = (s32[1,1,1,2]{3,2,1,0:T(1,128)S(1)}, s32[1,1,1,2]{3,2,1,0:T(1,128)}, u32[]{:S(2)}) copy-start(s32[1,1,1,2]{3,2,1,0:T(1,128)} %param.16) | copy-start | bytes 28
  86.6 15.9 %all-to-all-start.6 = ((bf16[8,2,48,256]{3,2,1,0:T(8,128)(2,1)}), bf16[8,2,48,256]{3,2,1,0:T(8,128)(2,1)S(1)}, u32[]{:S(2)}, u32[]{:S(2)}) async-start(bf16[8,2,48,256]{3,2,1,0:T(8,128)(2,1)} %get-tuple-element.39), calls=%async_computation.6 | async-start | bytes 786432 | tf_op jit(solution)/shard_map/all_to_all | solution.py:382
  92.9 16.0 %collective-permute-start.4 = (bf16[48,1536]{1,0:T(8,128)(2,1)S(1)}, bf16[48,1536]{1,0:T(8,128)(2,1)S(1)}, u32[]{:S(2)}, u32[]{:S(2)}) collective-permute-start(bf16[48,1536]{1,0:T(8,128)(2,1)S(1)} %get-tuple-element.42), channel_id=1, source_target_pairs={{0,8},{8,16},{16,24},{24,0},{1,9},{9,17},{17,25},{25,1},{2,10},{10... | collective-permute-start | bytes 442376 | tf_op jit(solution)/shard_map/ppermute | solution.py:379
  94.9 14.1 %collective-permute-start.5 = (bf16[48,1536]{1,0:T(8,128)(2,1)S(1)}, bf16[48,1536]{1,0:T(8,128)(2,1)S(1)}, u32[]{:S(2)}, u32[]{:S(2)}) collective-permute-start(bf16[48,1536]{1,0:T(8,128)(2,1)S(1)} %get-tuple-element.43), channel_id=1, source_target_pairs={{0,16},{8,24},{16,0},{24,8},{1,17},{9,25},{17,1},{25,9},{2,18},{10... | collective-permute-start | bytes 442376 | tf_op jit(solution)/shard_map/ppermute | solution.py:379
  96.8 12.1 %collective-permute-start.6 = (bf16[48,1536]{1,0:T(8,128)(2,1)S(1)}, bf16[48,1536]{1,0:T(8,128)(2,1)S(1)}, u32[]{:S(2)}, u32[]{:S(2)}) collective-permute-start(bf16[48,1536]{1,0:T(8,128)(2,1)S(1)} %get-tuple-element.44), channel_id=1, source_target_pairs={{0,24},{8,0},{16,8},{24,16},{1,25},{9,1},{17,9},{25,17},{2,26},{10... | collective-permute-start | bytes 442376 | tf_op jit(solution)/shard_map/ppermute | solution.py:379
  105.4 12.8 %all-to-all-start.7 = ((bf16[4,48,1536]{2,1,0:T(8,128)(2,1)}), bf16[4,48,1536]{2,1,0:T(8,128)(2,1)S(1)}, u32[]{:S(2)}, u32[]{:S(2)}) async-start(bf16[4,48,1536]{2,1,0:T(8,128)(2,1)} %shard_map.96), calls=%async_computation.7 | async-start | bytes 1179648 | tf_op jit(solution)/shard_map/all_to_all | solution.py:388
  109.0 50.8 %copy-start = (bf16[2,1,192,1536]{3,2,1,0:T(8,128)(2,1)S(1)}, bf16[2,1,192,1536]{3,2,1,0:T(8,128)(2,1)}, u32[]{:S(2)}) copy-start(bf16[2,1,192,1536]{3,2,1,0:T(8,128)(2,1)} %param.13) | copy-start | bytes 3538948
  109.0 14.4 %collective-permute-start.7 = (bf16[48,1536]{1,0:T(8,128)(2,1)S(1)}, bf16[48,1536]{1,0:T(8,128)(2,1)S(1)}, u32[]{:S(2)}, u32[]{:S(2)}) collective-permute-start(bf16[48,1536]{1,0:T(8,128)(2,1)S(1)} %add_convert_fusion.1), channel_id=1, source_target_pairs={{0,449},{1,450},{2,451},{3,452},{4,453},{5,454},{6,455},{32,481},{... | collective-permute-start | bytes 442376 | tf_op jit(solution)/shard_map/ppermute | solution.py:376
  123.5 15.9 %collective-permute-start.8 = (bf16[48,1536]{1,0:T(8,128)(2,1)S(1)}, bf16[48,1536]{1,0:T(8,128)(2,1)S(1)}, u32[]{:S(2)}, u32[]{:S(2)}) collective-permute-start(bf16[48,1536]{1,0:T(8,128)(2,1)S(1)} %add_convert_fusion.refs_0_), channel_id=1, source_target_pairs={{0,256},{32,288},{64,320},{96,352},{128,384},{160,416},{192,448},{... | collective-permute-start | bytes 442376 | tf_op jit(solution)/shard_map/ppermute | solution.py:367
  139.4 12.5 %collective-permute-start.14 = (bf16[48,1536]{1,0:T(8,128)(2,1)S(1)}, bf16[48,1536]{1,0:T(8,128)(2,1)S(1)}, u32[]{:S(2)}, u32[]{:S(2)}) collective-permute-start(bf16[48,1536]{1,0:T(8,128)(2,1)S(1)} %bitcast.24), channel_id=1, source_target_pairs={{0,192},{32,224},{64,128},{96,160},{128,64},{160,96},{192,0},{224,... | collective-permute-start | bytes 442376 | tf_op jit(solution)/shard_map/ppermute | solution.py:367
  141.4 13.9 %collective-permute-start.12 = (bf16[48,1536]{1,0:T(8,128)(2,1)S(1)}, bf16[48,1536]{1,0:T(8,128)(2,1)S(1)}, u32[]{:S(2)}, u32[]{:S(2)}) collective-permute-start(bf16[48,1536]{1,0:T(8,128)(2,1)S(1)} %bitcast.25), channel_id=1, source_target_pairs={{0,128},{32,160},{64,192},{96,224},{128,0},{160,32},{192,64},{224,... | collective-permute-start | bytes 442376 | tf_op jit(solution)/shard_map/ppermute | solution.py:367
  143.3 14.4 %collective-permute-start.10 = (bf16[48,1536]{1,0:T(8,128)(2,1)S(1)}, bf16[48,1536]{1,0:T(8,128)(2,1)S(1)}, u32[]{:S(2)}, u32[]{:S(2)}) collective-permute-start(bf16[48,1536]{1,0:T(8,128)(2,1)S(1)} %bitcast.26), channel_id=1, source_target_pairs={{0,64},{32,96},{64,0},{96,32},{128,192},{160,224},{192,128},{224,1... | collective-permute-start | bytes 442376 | tf_op jit(solution)/shard_map/ppermute | solution.py:367
  148.7 12.8 %collective-permute-start.9 = (bf16[48,1536]{1,0:T(8,128)(2,1)S(1)}, bf16[48,1536]{1,0:T(8,128)(2,1)S(1)}, u32[]{:S(2)}, u32[]{:S(2)}) collective-permute-start(bf16[48,1536]{1,0:T(8,128)(2,1)S(1)} %bitcast.27), channel_id=1, source_target_pairs={{0,32},{32,0},{64,96},{96,64},{128,160},{160,128},{192,224},{224,1... | collective-permute-start | bytes 442376 | tf_op jit(solution)/shard_map/ppermute | solution.py:367
  152.0 9.6 %collective-permute-start.15 = (bf16[48,1536]{1,0:T(8,128)(2,1)S(1)}, bf16[48,1536]{1,0:T(8,128)(2,1)S(1)}, u32[]{:S(2)}, u32[]{:S(2)}) collective-permute-start(bf16[48,1536]{1,0:T(8,128)(2,1)S(1)} %collective-permute-done.14.refs_3_), channel_id=1, source_target_pairs={{0,32},{32,0},{64,96},{96,64},{128,160},{160,128},{192,224},{224,1... | collective-permute-start | bytes 442376 | tf_op jit(solution)/shard_map/ppermute | solution.py:367
  155.3 6.3 %collective-permute-start.13 = (bf16[48,1536]{1,0:T(8,128)(2,1)S(1)}, bf16[48,1536]{1,0:T(8,128)(2,1)S(1)}, u32[]{:S(2)}, u32[]{:S(2)}) collective-permute-start(bf16[48,1536]{1,0:T(8,128)(2,1)S(1)} %collective-permute-done.12.refs_2_), channel_id=1, source_target_pairs={{0,32},{32,0},{64,96},{96,64},{128,160},{160,128},{192,224},{224,1... | collective-permute-start | bytes 442376 | tf_op jit(solution)/shard_map/ppermute | solution.py:367
  157.7 3.9 %collective-permute-start.11 = (bf16[48,1536]{1,0:T(8,128)(2,1)S(1)}, bf16[48,1536]{1,0:T(8,128)(2,1)S(1)}, u32[]{:S(2)}, u32[]{:S(2)}) collective-permute-start(bf16[48,1536]{1,0:T(8,128)(2,1)S(1)} %collective-permute-done.10.refs_1_), channel_id=1, source_target_pairs={{0,32},{32,0},{64,96},{96,64},{128,160},{160,128},{192,224},{224,1... | collective-permute-start | bytes 442376 | tf_op jit(solution)/shard_map/ppermute | solution.py:367

commit v18 on v17

--- a/solution.py
+++ b/solution.py
@@ -316,35 +316,34 @@
 
 
 def step_body(scalars, layer, *refs):
-    blocks = refs[:FOUR]
-    out, made, sems = refs[-3:]
-    part, place = scalars[0], scalars[1]
+    blocks, (out, made, sems) = refs[:-3], refs[-3:]
+    core, place = scalars[0], scalars[1]
     chunks = blocks[0].shape[0] // CHUNK
     size = FOUR * CHUNK
     copies = []
-    for i in range(chunks):
-        for k, block in enumerate(blocks):
-            rows = pl.ds(pl.multiple_of(i * size + (place ^ k) * CHUNK, CHUNK), CHUNK)
-            change = block[i * CHUNK : (i + 1) * CHUNK].astype(jnp.float32)
-            made[rows] = layer[part, rows].astype(jnp.float32) - step_size * change
-        at = pl.ds(i * size, size)
-        copies.append(pltpu.make_async_copy(made.at[at], out.at[part, at], sems.at[i]))
-        copies[-1].start()
+    for turn in range(2):
+        part = core ^ turn
+        for i in range(chunks):
+            for k in range(FOUR):
+                rows = pl.ds(pl.multiple_of(i * size + (place ^ k) * CHUNK, CHUNK), CHUNK)
+                change = blocks[turn * FOUR + k][i * CHUNK : (i + 1) * CHUNK].astype(jnp.float32)
+                made[turn, rows] = layer[part, rows].astype(jnp.float32) - step_size * change
+            at = pl.ds(i * size, size)
+            copies.append(pltpu.make_async_copy(made.at[turn, at], out.at[part, at], sems.at[turn, i]))
+            copies[-1].start()
     for copy in copies:
         copy.wait()
 
 
-def step(part, place, layer, blocks, *stepped):
+def step(core, place, layer, blocks):
     return pl.pallas_call(
         step_body,
         out_shape=jax.ShapeDtypeStruct(layer.shape, jnp.float32),
-        in_specs=[pl.BlockSpec(memory_space=pltpu.SMEM)] + [VMEM] * (1 + FOUR)
-        + [pl.BlockSpec(memory_space=pltpu.HBM)] * len(stepped),
+        in_specs=[pl.BlockSpec(memory_space=pltpu.SMEM)] + [VMEM] * (1 + len(blocks)),
         out_specs=pl.BlockSpec(memory_space=pltpu.HBM),
-        scratch_shapes=[pltpu.VMEM(layer.shape[1:], jnp.float32), pltpu.SemaphoreType.DMA((4,))],
-        input_output_aliases={2 + FOUR: 0} if stepped else {},
+        scratch_shapes=[pltpu.VMEM(layer.shape, jnp.float32), pltpu.SemaphoreType.DMA((2, 4))],
         compiler_params=pltpu.CompilerParams(vmem_limit_bytes=24 * 1024 * 1024),
-    )(jnp.stack([part, place]).astype(jnp.int32), layer, *blocks, *stepped)
+    )(jnp.stack([core, place]).astype(jnp.int32), layer, *blocks)
 
 
 def per_device(volume, probe_wave, amplitudes, offsets, column_starts, counts, angle_ids):
@@ -434,8 +433,7 @@
     total = sum_copies([total, swap(total, 8)], 1)[0]
     blocks = [total] + [swap(total, k << 1) for k in range(1, FOUR)]
     others = [swap(block, 1) for block in blocks]
-    new = step(core, place_z, layer, blocks)
-    return step(1 - core, place_z, layer, others, new).reshape(volume.shape)
+    return step(core, place_z, layer, blocks + others).reshape(volume.shape)
 
 
 def solution(mesh):

time: 164 us -> 164 us (level)
    pallas_call x2 -> x1, Pallas kernels: 3.5 us -> 2.31 us  [step(): pl.pallas_call(step_body, out_shape=jax.ShapeDtypeStruct(layer.shape, jnp...]
  transfers between devices with their start and end apart: 20 -> 20, of which waited for: 8 -> 9; matrix products, arithmetic and copies ran while one was open for 1% -> 1% of each run, Pallas kernels for 7% -> 5%
where the time goes in v18:
time: 164 us; the launch traced here: 163 us
  starting transfers between devices  62.6 us (38%)
  waiting for transfers between devices  40.9 us (25%)
  blocking collectives  38.8 us (24%)
  Pallas kernels  16.8 us (10%)
  between operations  2.18 us (1%)
    all_to_all x2, blocking collectives, to_eight(): lax.all_to_all(value, 'angle', 0, 0, axis_index_groups=eight_groups, tile...  38.8 us
    ppermute x8, starting transfers between devices, swap(): return lax.ppermute(value, 'angle', [(i, i ^ by) for i in range(angles)])  20.7 us
    ppermute x6, starting transfers between devices, to_slab(): lax.ppermute(value, 'slab', [(i, (i + by) % slabs) for i in range(slabs)])  18.6 us
    ppermute x8, waiting for transfers between devices, swap(): return lax.ppermute(value, 'angle', [(i, i ^ by) for i in range(angles)])  16.6 us
    all_to_all x2, waiting for transfers between devices, to_slabs(): return lax.all_to_all(value, 'slab', 0, 0, tiled=True)  14 us
    pallas_call x7, Pallas kernels, call(): pl.pallas_call(body, out_shape=out_shape, in_specs=[smem if x.dtype == jn...  13.1 us
    all_to_all x2, starting transfers between devices, to_eight(): lax.all_to_all(value, 'angle', 0, 0, axis_index_groups=eight_groups, tile...  12 us
    all_to_all x2, starting transfers between devices, to_slabs(): return lax.all_to_all(value, 'slab', 0, 0, tiled=True)  8.59 us
  transfers between devices with their start and end apart: 20, of which 9 were waited for; matrix products, arithmetic and copies ran while one was open for 1% of the time, Pallas kernels for 5%

profile of v18, /device:TPU:1, one launch (start us, length us, event | category | flops | bytes accessed | tf_op | source)
XLA Modules:
  0.0 163.3 jit_solution(1450276024045753026)
XLA Ops:
  2.4 5.2 %collective-permute-start.3 = (bf16[48,1536]{1,0:T(8,128)(2,1)S(1)}, bf16[48,1536]{1,0:T(8,128)(2,1)S(1)}, u32[]{:S(2)}, u32[]{:S(2)}) collective-permute-start(bf16[48,1536]{1,0:T(8,128)(2,1)S(1)} %bitcast.27), channel_id=1, source_target_pairs={{0,24},{8,0},{16,8},{24,16},{1,25},{9,1},{17,9},{25,17},{2,26},{10... | collective-permute-start | bytes 442376 | tf_op jit(solution)/shard_map/ppermute | solution.py:378
  7.7 2.4 %collective-permute-start.2 = (bf16[48,1536]{1,0:T(8,128)(2,1)S(1)}, bf16[48,1536]{1,0:T(8,128)(2,1)S(1)}, u32[]{:S(2)}, u32[]{:S(2)}) collective-permute-start(bf16[48,1536]{1,0:T(8,128)(2,1)S(1)} %bitcast.28), channel_id=1, source_target_pairs={{0,16},{8,24},{16,0},{24,8},{1,17},{9,25},{17,1},{25,9},{2,18},{10... | collective-permute-start | bytes 442376 | tf_op jit(solution)/shard_map/ppermute | solution.py:378
  10.1 2.5 %collective-permute-start.1 = (bf16[48,1536]{1,0:T(8,128)(2,1)S(1)}, bf16[48,1536]{1,0:T(8,128)(2,1)S(1)}, u32[]{:S(2)}, u32[]{:S(2)}) collective-permute-start(bf16[48,1536]{1,0:T(8,128)(2,1)S(1)} %bitcast.29), channel_id=1, source_target_pairs={{0,8},{8,16},{16,24},{24,0},{1,9},{9,17},{17,25},{25,1},{2,10},{10... | collective-permute-start | bytes 442376 | tf_op jit(solution)/shard_map/ppermute | solution.py:378
  15.3 7.7 %all-to-all-start.4 = ((s32[8,1,128]{2,1,0:T(1,128)}), s32[8,1,128]{2,1,0:T(1,128)S(1)}, u32[]{:S(2)}, u32[]{:S(2)}) async-start(s32[8,1,128]{2,1,0:T(1,128)} %bitcast.41), calls=%async_computation.4 | async-start | bytes 8192 | tf_op jit(solution)/shard_map/all_to_all | solution.py:381
  23.0 3.5 %collective-permute-done.refs_0_ = bf16[48,1536]{1,0:T(8,128)(2,1)S(1)} collective-permute-done((bf16[48,1536]{1,0:T(8,128)(2,1)S(1)}, bf16[48,1536]{1,0:T(8,128)(2,1)S(1)}, u32[]{:S(2)}, u32[]{:S(2)}) %collective-permute-start) | collective-permute-done | bytes 147488 | tf_op jit(solution)/shard_map/ppermute | solution.py:375
  27.9 5.1 %all-to-all-start.5 = ((bf16[4,48,1536]{2,1,0:T(8,128)(2,1)}), bf16[4,48,1536]{2,1,0:T(8,128)(2,1)S(1)}, u32[]{:S(2)}, u32[]{:S(2)}) async-start(bf16[4,48,1536]{2,1,0:T(8,128)(2,1)} %shard_map.92), calls=%async_computation.5 | async-start | bytes 1179648 | tf_op jit(solution)/shard_map/all_to_all | solution.py:387
  36.0 6.2 %all-to-all-done.5.blocks = bf16[4,48,1536]{2,1,0:T(8,128)(2,1)S(1)} async-done(((bf16[4,48,1536]{2,1,0:T(8,128)(2,1)}), bf16[4,48,1536]{2,1,0:T(8,128)(2,1)S(1)}, u32[]{:S(2)}, u32[]{:S(2)}) %all-to-all-start.5) | async-done | bytes 589856 | tf_op jit(solution)/shard_map/all_to_all | solution.py:387
  42.2 2.0 %shard_map.94 = bf16[8,2,5,16,256]{4,3,2,1,0:T(8,128)(2,1)S(1)} custom-call(s32[1]{0:T(128)} %bitcast.1.place_ref, s32[8,128]{1,0:T(8,128)S(1)} %bitcast.34, s32[1]{0:T(128)} %bitcast.9.slab_ref, bf16[4,48,1536]{2,1,0:T(8,128)(2,1)S(1)} %all-to-all-done.5.blocks, bf16[8,2,48,256]{3,2,1,0:T(8,128)(2,1)S(1)} %shard_map.93.done), custom_call_target="tpu_custom_call" | custom-call | tf_op jit(solution)/shard_map/pallas_call | solution.py:47
  44.3 21.7 %conditional.2 = (bf16[8,2,5,16,256]{4,3,2,1,0:T(8,128)(2,1)S(1)}) conditional(s32[]{:T(128)} %convert_element_type.25, bf16[8,2,5,16,256]{4,3,2,1,0:T(8,128)(2,1)S(1)} %shard_map.94, bf16[8,2,5,16,256]{4,3,2,1,0:T(8,128)(2,1)S(1)} %shard_map.94), branch_computations={%region_1.2_spmd, %region_2.3_spmd} | conditional | flops 327680 | bytes 3276808 | solution.py:400
  44.3 21.7 %all_to_all.43 = bf16[8,2,5,16,256]{4,3,2,1,0:T(8,128)(2,1)S(1)} all-to-all(bf16[8,2,5,16,256]{4,3,2,1,0:T(8,128)(2,1)S(1)} %param.1), channel_id=1, replica_groups={{0,32,64,96,128,160,192,224},{256,288,320,352,384,416,448,480},{1,33,65..., dimensions={0} | all-to-all | bytes 1310720 | tf_op jit(solution)/shard_map/cond/branch_1_fun/all_to_all | solution.py:381
  66.1 3.4 %shard_map.95 = (bf16[8,2,48,256]{3,2,1,0:T(8,128)(2,1)}, bf16[8,2,48,256]{3,2,1,0:T(8,128)(2,1)S(1)}) custom-call(s32[2]{0:T(128)S(1)} %bitcast.38, s32[1]{0:T(128)} %bitcast.20.count_ref, bf16[8,2,5,16,256]{4,3,2,1,0:T(8,128)(2,1)S(1)} %get-tuple-element.51.windows, f32[2,256,256]{2,1,0:T(8,128)S(1)} %copy-done.1, bf16[2,256,256]{2,1,0:T(8,128)(2,1)S(1)} %bitcast.31, ...), custom_call_target="tpu_custom_call" | custom-call | tf_op jit(solution)/shard_map/pallas_call | solution.py:47
  69.5 17.1 %conditional.3 = (bf16[8,2,48,256]{3,2,1,0:T(8,128)(2,1)S(1)}) conditional(s32[]{:T(128)} %convert_element_type.25, bf16[8,2,48,256]{3,2,1,0:T(8,128)(2,1)S(1)} %get-tuple-element.37, bf16[8,2,48,256]{3,2,1,0:T(8,128)(2,1)S(1)} %get-tuple-element.37), branch_computations={%region_3.4_spmd, %region_4.5_spmd} | conditional | flops 196608 | bytes 1966088 | solution.py:400
  69.5 17.1 %all_to_all.45 = bf16[8,2,48,256]{3,2,1,0:T(8,128)(2,1)S(1)} all-to-all(bf16[8,2,48,256]{3,2,1,0:T(8,128)(2,1)S(1)} %param.3), channel_id=1, replica_groups={{0,32,64,96,128,160,192,224},{256,288,320,352,384,416,448,480},{1,33,65..., dimensions={0} | all-to-all | bytes 786432 | tf_op jit(solution)/shard_map/cond/branch_1_fun/all_to_all | solution.py:381
  86.6 4.2 %all-to-all-start.6 = ((bf16[8,2,48,256]{3,2,1,0:T(8,128)(2,1)}), bf16[8,2,48,256]{3,2,1,0:T(8,128)(2,1)S(1)}, u32[]{:S(2)}, u32[]{:S(2)}) async-start(bf16[8,2,48,256]{3,2,1,0:T(8,128)(2,1)} %get-tuple-element.39), calls=%async_computation.6 | async-start | bytes 786432 | tf_op jit(solution)/shard_map/all_to_all | solution.py:381
  90.8 2.1 %shard_map.97 = (f32[48,1536]{1,0:T(8,128)S(1)}, bf16[48,1536]{1,0:T(8,128)(2,1)S(1)}, bf16[48,1536]{1,0:T(8,128)(2,1)S(1)}, bf16[48,1536]{1,0:T(8,128)(2,1)S(1)}) custom-call(s32[8,128]{1,0:T(8,128)S(1)} %bitcast.35, s32[1]{0:T(128)} %bitcast.9.slab_ref, bf16[8,2,48,256]{3,2,1,0:T(8,128)(2,1)S(1)} %get-tuple-element.52.windows), custom_call_target="tpu_custom_call" | custom-call | tf_op jit(solution)/shard_map/pallas_call | solution.py:47
  92.9 1.9 %collective-permute-start.4 = (bf16[48,1536]{1,0:T(8,128)(2,1)S(1)}, bf16[48,1536]{1,0:T(8,128)(2,1)S(1)}, u32[]{:S(2)}, u32[]{:S(2)}) collective-permute-start(bf16[48,1536]{1,0:T(8,128)(2,1)S(1)} %get-tuple-element.42), channel_id=1, source_target_pairs={{0,8},{8,16},{16,24},{24,0},{1,9},{9,17},{17,25},{25,1},{2,10},{10... | collective-permute-start | bytes 442376 | tf_op jit(solution)/shard_map/ppermute | solution.py:378
  94.8 1.9 %collective-permute-start.5 = (bf16[48,1536]{1,0:T(8,128)(2,1)S(1)}, bf16[48,1536]{1,0:T(8,128)(2,1)S(1)}, u32[]{:S(2)}, u32[]{:S(2)}) collective-permute-start(bf16[48,1536]{1,0:T(8,128)(2,1)S(1)} %get-tuple-element.43), channel_id=1, source_target_pairs={{0,16},{8,24},{16,0},{24,8},{1,17},{9,25},{17,1},{25,9},{2,18},{10... | collective-permute-start | bytes 442376 | tf_op jit(solution)/shard_map/ppermute | solution.py:378
  96.8 4.6 %collective-permute-start.6 = (bf16[48,1536]{1,0:T(8,128)(2,1)S(1)}, bf16[48,1536]{1,0:T(8,128)(2,1)S(1)}, u32[]{:S(2)}, u32[]{:S(2)}) collective-permute-start(bf16[48,1536]{1,0:T(8,128)(2,1)S(1)} %get-tuple-element.44), channel_id=1, source_target_pairs={{0,24},{8,0},{16,8},{24,16},{1,25},{9,1},{17,9},{25,17},{2,26},{10... | collective-permute-start | bytes 442376 | tf_op jit(solution)/shard_map/ppermute | solution.py:378
  102.5 2.9 %shard_map.96 = bf16[4,48,1536]{2,1,0:T(8,128)(2,1)} custom-call(s32[8,128]{1,0:T(8,128)S(1)} %bitcast.36, s32[1]{0:T(128)} %bitcast.9.slab_ref, bf16[8,2,48,256]{3,2,1,0:T(8,128)(2,1)S(1)} %all-to-all-done.6.windows), custom_call_target="tpu_custom_call" | custom-call | tf_op jit(solution)/shard_map/pallas_call | solution.py:47
  105.4 3.5 %all-to-all-start.7 = ((bf16[4,48,1536]{2,1,0:T(8,128)(2,1)}), bf16[4,48,1536]{2,1,0:T(8,128)(2,1)S(1)}, u32[]{:S(2)}, u32[]{:S(2)}) async-start(bf16[4,48,1536]{2,1,0:T(8,128)(2,1)} %shard_map.96), calls=%async_computation.7 | async-start | bytes 1179648 | tf_op jit(solution)/shard_map/all_to_all | solution.py:387
  110.5 7.8 %all-to-all-done.7 = bf16[4,48,1536]{2,1,0:T(8,128)(2,1)S(1)} async-done(((bf16[4,48,1536]{2,1,0:T(8,128)(2,1)}), bf16[4,48,1536]{2,1,0:T(8,128)(2,1)S(1)}, u32[]{:S(2)}, u32[]{:S(2)}) %all-to-all-start.7) | async-done | bytes 589856 | tf_op jit(solution)/shard_map/all_to_all | solution.py:387
  118.3 5.1 %collective-permute-done.7 = bf16[48,1536]{1,0:T(8,128)(2,1)S(1)} collective-permute-done((bf16[48,1536]{1,0:T(8,128)(2,1)S(1)}, bf16[48,1536]{1,0:T(8,128)(2,1)S(1)}, u32[]{:S(2)}, u32[]{:S(2)}) %collective-permute-start.7) | collective-permute-done | bytes 147488 | tf_op jit(solution)/shard_map/ppermute | solution.py:375
  123.5 1.9 %collective-permute-start.8 = (bf16[48,1536]{1,0:T(8,128)(2,1)S(1)}, bf16[48,1536]{1,0:T(8,128)(2,1)S(1)}, u32[]{:S(2)}, u32[]{:S(2)}) collective-permute-start(bf16[48,1536]{1,0:T(8,128)(2,1)S(1)} %add_convert_fusion.refs_0_), channel_id=1, source_target_pairs={{0,256},{32,288},{64,320},{96,352},{128,384},{160,416},{192,448},{... | collective-permute-start | bytes 442376 | tf_op jit(solution)/shard_map/ppermute | solution.py:366
  125.4 14.0 %collective-permute-done.8.refs_1_ = bf16[48,1536]{1,0:T(8,128)(2,1)S(1)} collective-permute-done((bf16[48,1536]{1,0:T(8,128)(2,1)S(1)}, bf16[48,1536]{1,0:T(8,128)(2,1)S(1)}, u32[]{:S(2)}, u32[]{:S(2)}) %collective-permute-start.8) | collective-permute-done | bytes 147488 | tf_op jit(solution)/shard_map/ppermute | solution.py:366
  139.4 1.9 %collective-permute-start.11 = (bf16[48,1536]{1,0:T(8,128)(2,1)S(1)}, bf16[48,1536]{1,0:T(8,128)(2,1)S(1)}, u32[]{:S(2)}, u32[]{:S(2)}) collective-permute-start(bf16[48,1536]{1,0:T(8,128)(2,1)S(1)} %bitcast.22), channel_id=1, source_target_pairs={{0,192},{32,224},{64,128},{96,160},{128,64},{160,96},{192,0},{224,... | collective-permute-start | bytes 442376 | tf_op jit(solution)/shard_map/ppermute | solution.py:366
  141.4 1.9 %collective-permute-start.10 = (bf16[48,1536]{1,0:T(8,128)(2,1)S(1)}, bf16[48,1536]{1,0:T(8,128)(2,1)S(1)}, u32[]{:S(2)}, u32[]{:S(2)}) collective-permute-start(bf16[48,1536]{1,0:T(8,128)(2,1)S(1)} %bitcast.23), channel_id=1, source_target_pairs={{0,128},{32,160},{64,192},{96,224},{128,0},{160,32},{192,64},{224,... | collective-permute-start | bytes 442376 | tf_op jit(solution)/shard_map/ppermute | solution.py:366
  143.3 5.4 %collective-permute-start.9 = (bf16[48,1536]{1,0:T(8,128)(2,1)S(1)}, bf16[48,1536]{1,0:T(8,128)(2,1)S(1)}, u32[]{:S(2)}, u32[]{:S(2)}) collective-permute-start(bf16[48,1536]{1,0:T(8,128)(2,1)S(1)} %bitcast.24), channel_id=1, source_target_pairs={{0,64},{32,96},{64,0},{96,32},{128,192},{160,224},{192,128},{224,1... | collective-permute-start | bytes 442376 | tf_op jit(solution)/shard_map/ppermute | solution.py:366
  148.7 3.2 %collective-permute-start.12 = (bf16[48,1536]{1,0:T(8,128)(2,1)S(1)}, bf16[48,1536]{1,0:T(8,128)(2,1)S(1)}, u32[]{:S(2)}, u32[]{:S(2)}) collective-permute-start(bf16[48,1536]{1,0:T(8,128)(2,1)S(1)} %bitcast.25), channel_id=1, source_target_pairs={{0,32},{32,0},{64,96},{96,64},{128,160},{160,128},{192,224},{224,1... | collective-permute-start | bytes 442376 | tf_op jit(solution)/shard_map/ppermute | solution.py:366
  152.0 1.9 %collective-permute-start.15 = (bf16[48,1536]{1,0:T(8,128)(2,1)S(1)}, bf16[48,1536]{1,0:T(8,128)(2,1)S(1)}, u32[]{:S(2)}, u32[]{:S(2)}) collective-permute-start(bf16[48,1536]{1,0:T(8,128)(2,1)S(1)} %collective-permute-done.11.refs_3_), channel_id=1, source_target_pairs={{0,32},{32,0},{64,96},{96,64},{128,160},{160,128},{192,224},{224,1... | collective-permute-start | bytes 442376 | tf_op jit(solution)/shard_map/ppermute | solution.py:366
  155.3 2.4 %collective-permute-start.14 = (bf16[48,1536]{1,0:T(8,128)(2,1)S(1)}, bf16[48,1536]{1,0:T(8,128)(2,1)S(1)}, u32[]{:S(2)}, u32[]{:S(2)}) collective-permute-start(bf16[48,1536]{1,0:T(8,128)(2,1)S(1)} %collective-permute-done.10.refs_2_), channel_id=1, source_target_pairs={{0,32},{32,0},{64,96},{96,64},{128,160},{160,128},{192,224},{224,1... | collective-permute-start | bytes 442376 | tf_op jit(solution)/shard_map/ppermute | solution.py:366
  157.7 1.9 %collective-permute-start.13 = (bf16[48,1536]{1,0:T(8,128)(2,1)S(1)}, bf16[48,1536]{1,0:T(8,128)(2,1)S(1)}, u32[]{:S(2)}, u32[]{:S(2)}) collective-permute-start(bf16[48,1536]{1,0:T(8,128)(2,1)S(1)} %collective-permute-done.9.refs_1_), channel_id=1, source_target_pairs={{0,32},{32,0},{64,96},{96,64},{128,160},{160,128},{192,224},{224,1... | collective-permute-start | bytes 442376 | tf_op jit(solution)/shard_map/ppermute | solution.py:366
  161.0 2.3 %shard_map.99 = f32[2,192,1536]{2,1,0:T(8,128)} custom-call(s32[2]{0:T(128)S(1)} %pad_add_fusion.scalars, bf16[2,192,1536]{2,1,0:T(8,128)(2,1)S(1)} %bitcast.21, bf16[48,1536]{1,0:T(8,128)(2,1)S(1)} %bitcast.26, bf16[48,1536]{1,0:T(8,128)(2,1)S(1)} %collective-permute-done.9.refs_1_, bf16[48,1536]{1,0:T(8,128)(2,1)S(1)} %collective-permute-done.10.refs_2_, ...), custom_call_target="tpu_custom_call" | custom-call | tf_op jit(solution)/shard_map/pallas_call | solution.py:339
  (40 shorter events, 13.2 us)
Async XLA Ops:
  1.1 25.3 %collective-permute-start = (bf16[48,1536]{1,0:T(8,128)(2,1)S(1)}, bf16[48,1536]{1,0:T(8,128)(2,1)S(1)}, u32[]{:S(2)}, u32[]{:S(2)}) collective-permute-start(bf16[48,1536]{1,0:T(8,128)(2,1)S(1)} %bitcast.40), channel_id=1, source_target_pairs={{1,448},{2,449},{3,450},{4,451},{5,452},{6,453},{7,454},{33,480},{... | collective-permute-start | bytes 442376 | tf_op jit(solution)/shard_map/ppermute | solution.py:375
  2.4 24.0 %collective-permute-start.3 = (bf16[48,1536]{1,0:T(8,128)(2,1)S(1)}, bf16[48,1536]{1,0:T(8,128)(2,1)S(1)}, u32[]{:S(2)}, u32[]{:S(2)}) collective-permute-start(bf16[48,1536]{1,0:T(8,128)(2,1)S(1)} %bitcast.27), channel_id=1, source_target_pairs={{0,24},{8,0},{16,8},{24,16},{1,25},{9,1},{17,9},{25,17},{2,26},{10... | collective-permute-start | bytes 442376 | tf_op jit(solution)/shard_map/ppermute | solution.py:378
  7.7 18.8 %collective-permute-start.2 = (bf16[48,1536]{1,0:T(8,128)(2,1)S(1)}, bf16[48,1536]{1,0:T(8,128)(2,1)S(1)}, u32[]{:S(2)}, u32[]{:S(2)}) collective-permute-start(bf16[48,1536]{1,0:T(8,128)(2,1)S(1)} %bitcast.28), channel_id=1, source_target_pairs={{0,16},{8,24},{16,0},{24,8},{1,17},{9,25},{17,1},{25,9},{2,18},{10... | collective-permute-start | bytes 442376 | tf_op jit(solution)/shard_map/ppermute | solution.py:378
  10.1 16.4 %collective-permute-start.1 = (bf16[48,1536]{1,0:T(8,128)(2,1)S(1)}, bf16[48,1536]{1,0:T(8,128)(2,1)S(1)}, u32[]{:S(2)}, u32[]{:S(2)}) collective-permute-start(bf16[48,1536]{1,0:T(8,128)(2,1)S(1)} %bitcast.29), channel_id=1, source_target_pairs={{0,8},{8,16},{16,24},{24,0},{1,9},{9,17},{17,25},{25,1},{2,10},{10... | collective-permute-start | bytes 442376 | tf_op jit(solution)/shard_map/ppermute | solution.py:378
  15.3 12.6 %all-to-all-start.4 = ((s32[8,1,128]{2,1,0:T(1,128)}), s32[8,1,128]{2,1,0:T(1,128)S(1)}, u32[]{:S(2)}, u32[]{:S(2)}) async-start(s32[8,1,128]{2,1,0:T(1,128)} %bitcast.41), calls=%async_computation.4 | async-start | bytes 8192 | tf_op jit(solution)/shard_map/all_to_all | solution.py:381
  27.9 14.3 %all-to-all-start.5 = ((bf16[4,48,1536]{2,1,0:T(8,128)(2,1)}), bf16[4,48,1536]{2,1,0:T(8,128)(2,1)S(1)}, u32[]{:S(2)}, u32[]{:S(2)}) async-start(bf16[4,48,1536]{2,1,0:T(8,128)(2,1)} %shard_map.92), calls=%async_computation.5 | async-start | bytes 1179648 | tf_op jit(solution)/shard_map/all_to_all | solution.py:387
  44.3 21.8 %copy-start.1 = (f32[2,256,256]{2,1,0:T(8,128)S(1)}, f32[2,256,256]{2,1,0:T(8,128)}, u32[]{:S(2)}) copy-start(f32[2,256,256]{2,1,0:T(8,128)} %probe.1) | copy-start | bytes 1572868
  44.3 21.8 %copy-start.2 = (bf16[1,1,1,2,256,256]{5,4,3,2,1,0:T(8,128)(2,1)S(1)}, bf16[1,1,1,2,256,256]{5,4,3,2,1,0:T(8,128)(2,1)}, u32[]{:S(2)}) copy-start(bf16[1,1,1,2,256,256]{5,4,3,2,1,0:T(8,128)(2,1)} %param.15) | copy-start | bytes 786436
  44.3 21.8 %copy-start.3 = (bf16[256,256]{1,0:T(8,128)(2,1)S(1)}, bf16[256,256]{1,0:T(8,128)(2,1)}, u32[]{:S(2)}) copy-start(bf16[256,256]{1,0:T(8,128)(2,1)} %constant.69.clone.wi_ref) | copy-start | bytes 393220
  44.3 21.8 %copy-start.4 = (bf16[256,256]{1,0:T(8,128)(2,1)S(1)}, bf16[256,256]{1,0:T(8,128)(2,1)}, u32[]{:S(2)}) copy-start(bf16[256,256]{1,0:T(8,128)(2,1)} %constant.68.clone.wr_ref) | copy-start | bytes 393220
  44.3 21.8 %copy-start.5 = (s32[1,1,1,2]{3,2,1,0:T(1,128)S(1)}, s32[1,1,1,2]{3,2,1,0:T(1,128)}, u32[]{:S(2)}) copy-start(s32[1,1,1,2]{3,2,1,0:T(1,128)} %param.16) | copy-start | bytes 28
  86.6 15.9 %all-to-all-start.6 = ((bf16[8,2,48,256]{3,2,1,0:T(8,128)(2,1)}), bf16[8,2,48,256]{3,2,1,0:T(8,128)(2,1)S(1)}, u32[]{:S(2)}, u32[]{:S(2)}) async-start(bf16[8,2,48,256]{3,2,1,0:T(8,128)(2,1)} %get-tuple-element.39), calls=%async_computation.6 | async-start | bytes 786432 | tf_op jit(solution)/shard_map/all_to_all | solution.py:381
  92.9 16.0 %collective-permute-start.4 = (bf16[48,1536]{1,0:T(8,128)(2,1)S(1)}, bf16[48,1536]{1,0:T(8,128)(2,1)S(1)}, u32[]{:S(2)}, u32[]{:S(2)}) collective-permute-start(bf16[48,1536]{1,0:T(8,128)(2,1)S(1)} %get-tuple-element.42), channel_id=1, source_target_pairs={{0,8},{8,16},{16,24},{24,0},{1,9},{9,17},{17,25},{25,1},{2,10},{10... | collective-permute-start | bytes 442376 | tf_op jit(solution)/shard_map/ppermute | solution.py:378
  94.8 14.1 %collective-permute-start.5 = (bf16[48,1536]{1,0:T(8,128)(2,1)S(1)}, bf16[48,1536]{1,0:T(8,128)(2,1)S(1)}, u32[]{:S(2)}, u32[]{:S(2)}) collective-permute-start(bf16[48,1536]{1,0:T(8,128)(2,1)S(1)} %get-tuple-element.43), channel_id=1, source_target_pairs={{0,16},{8,24},{16,0},{24,8},{1,17},{9,25},{17,1},{25,9},{2,18},{10... | collective-permute-start | bytes 442376 | tf_op jit(solution)/shard_map/ppermute | solution.py:378
  96.8 12.1 %collective-permute-start.6 = (bf16[48,1536]{1,0:T(8,128)(2,1)S(1)}, bf16[48,1536]{1,0:T(8,128)(2,1)S(1)}, u32[]{:S(2)}, u32[]{:S(2)}) collective-permute-start(bf16[48,1536]{1,0:T(8,128)(2,1)S(1)} %get-tuple-element.44), channel_id=1, source_target_pairs={{0,24},{8,0},{16,8},{24,16},{1,25},{9,1},{17,9},{25,17},{2,26},{10... | collective-permute-start | bytes 442376 | tf_op jit(solution)/shard_map/ppermute | solution.py:378
  105.4 12.8 %all-to-all-start.7 = ((bf16[4,48,1536]{2,1,0:T(8,128)(2,1)}), bf16[4,48,1536]{2,1,0:T(8,128)(2,1)S(1)}, u32[]{:S(2)}, u32[]{:S(2)}) async-start(bf16[4,48,1536]{2,1,0:T(8,128)(2,1)} %shard_map.96), calls=%async_computation.7 | async-start | bytes 1179648 | tf_op jit(solution)/shard_map/all_to_all | solution.py:387
  109.0 52.0 %copy-start = (bf16[2,1,192,1536]{3,2,1,0:T(8,128)(2,1)S(1)}, bf16[2,1,192,1536]{3,2,1,0:T(8,128)(2,1)}, u32[]{:S(2)}) copy-start(bf16[2,1,192,1536]{3,2,1,0:T(8,128)(2,1)} %param.13) | copy-start | bytes 3538948
  109.0 14.4 %collective-permute-start.7 = (bf16[48,1536]{1,0:T(8,128)(2,1)S(1)}, bf16[48,1536]{1,0:T(8,128)(2,1)S(1)}, u32[]{:S(2)}, u32[]{:S(2)}) collective-permute-start(bf16[48,1536]{1,0:T(8,128)(2,1)S(1)} %add_convert_fusion.1), channel_id=1, source_target_pairs={{0,449},{1,450},{2,451},{3,452},{4,453},{5,454},{6,455},{32,481},{... | collective-permute-start | bytes 442376 | tf_op jit(solution)/shard_map/ppermute | solution.py:375
  123.5 15.9 %collective-permute-start.8 = (bf16[48,1536]{1,0:T(8,128)(2,1)S(1)}, bf16[48,1536]{1,0:T(8,128)(2,1)S(1)}, u32[]{:S(2)}, u32[]{:S(2)}) collective-permute-start(bf16[48,1536]{1,0:T(8,128)(2,1)S(1)} %add_convert_fusion.refs_0_), channel_id=1, source_target_pairs={{0,256},{32,288},{64,320},{96,352},{128,384},{160,416},{192,448},{... | collective-permute-start | bytes 442376 | tf_op jit(solution)/shard_map/ppermute | solution.py:366
  139.4 12.5 %collective-permute-start.11 = (bf16[48,1536]{1,0:T(8,128)(2,1)S(1)}, bf16[48,1536]{1,0:T(8,128)(2,1)S(1)}, u32[]{:S(2)}, u32[]{:S(2)}) collective-permute-start(bf16[48,1536]{1,0:T(8,128)(2,1)S(1)} %bitcast.22), channel_id=1, source_target_pairs={{0,192},{32,224},{64,128},{96,160},{128,64},{160,96},{192,0},{224,... | collective-permute-start | bytes 442376 | tf_op jit(solution)/shard_map/ppermute | solution.py:366
  141.4 13.9 %collective-permute-start.10 = (bf16[48,1536]{1,0:T(8,128)(2,1)S(1)}, bf16[48,1536]{1,0:T(8,128)(2,1)S(1)}, u32[]{:S(2)}, u32[]{:S(2)}) collective-permute-start(bf16[48,1536]{1,0:T(8,128)(2,1)S(1)} %bitcast.23), channel_id=1, source_target_pairs={{0,128},{32,160},{64,192},{96,224},{128,0},{160,32},{192,64},{224,... | collective-permute-start | bytes 442376 | tf_op jit(solution)/shard_map/ppermute | solution.py:366
  143.3 14.4 %collective-permute-start.9 = (bf16[48,1536]{1,0:T(8,128)(2,1)S(1)}, bf16[48,1536]{1,0:T(8,128)(2,1)S(1)}, u32[]{:S(2)}, u32[]{:S(2)}) collective-permute-start(bf16[48,1536]{1,0:T(8,128)(2,1)S(1)} %bitcast.24), channel_id=1, source_target_pairs={{0,64},{32,96},{64,0},{96,32},{128,192},{160,224},{192,128},{224,1... | collective-permute-start | bytes 442376 | tf_op jit(solution)/shard_map/ppermute | solution.py:366
  148.7 11.0 %collective-permute-start.12 = (bf16[48,1536]{1,0:T(8,128)(2,1)S(1)}, bf16[48,1536]{1,0:T(8,128)(2,1)S(1)}, u32[]{:S(2)}, u32[]{:S(2)}) collective-permute-start(bf16[48,1536]{1,0:T(8,128)(2,1)S(1)} %bitcast.25), channel_id=1, source_target_pairs={{0,32},{32,0},{64,96},{96,64},{128,160},{160,128},{192,224},{224,1... | collective-permute-start | bytes 442376 | tf_op jit(solution)/shard_map/ppermute | solution.py:366
  152.0 7.8 %collective-permute-start.15 = (bf16[48,1536]{1,0:T(8,128)(2,1)S(1)}, bf16[48,1536]{1,0:T(8,128)(2,1)S(1)}, u32[]{:S(2)}, u32[]{:S(2)}) collective-permute-start(bf16[48,1536]{1,0:T(8,128)(2,1)S(1)} %collective-permute-done.11.refs_3_), channel_id=1, source_target_pairs={{0,32},{32,0},{64,96},{96,64},{128,160},{160,128},{192,224},{224,1... | collective-permute-start | bytes 442376 | tf_op jit(solution)/shard_map/ppermute | solution.py:366
  155.3 4.5 %collective-permute-start.14 = (bf16[48,1536]{1,0:T(8,128)(2,1)S(1)}, bf16[48,1536]{1,0:T(8,128)(2,1)S(1)}, u32[]{:S(2)}, u32[]{:S(2)}) collective-permute-start(bf16[48,1536]{1,0:T(8,128)(2,1)S(1)} %collective-permute-done.10.refs_2_), channel_id=1, source_target_pairs={{0,32},{32,0},{64,96},{96,64},{128,160},{160,128},{192,224},{224,1... | collective-permute-start | bytes 442376 | tf_op jit(solution)/shard_map/ppermute | solution.py:366
  157.7 3.3 %collective-permute-start.13 = (bf16[48,1536]{1,0:T(8,128)(2,1)S(1)}, bf16[48,1536]{1,0:T(8,128)(2,1)S(1)}, u32[]{:S(2)}, u32[]{:S(2)}) collective-permute-start(bf16[48,1536]{1,0:T(8,128)(2,1)S(1)} %collective-permute-done.9.refs_1_), channel_id=1, source_target_pairs={{0,32},{32,0},{64,96},{96,64},{128,160},{160,128},{192,224},{224,1... | collective-permute-start | bytes 442376 | tf_op jit(solution)/shard_map/ppermute | solution.py:366
